TPU v7x, 32 devices: a whole 2x2x4 slice. The times are simulated.
32 devices in a mesh: rep: 2 (over x), exp: 16 (over z, y, core).
Axes of the slice: x: 2, y: 2, z: 4, core: 2. Of those that a mesh axis runs over, the one named last changes fastest.
Arguments:
- tokens: bfloat16 [5120, 512], P(('rep', 'exp')), may hold values from -6 to 6
- gates: bfloat16 [5120, 2], P(('rep', 'exp')), may hold values from 0.19921875 to 1
- routes: int32 [5120, 2], P(('rep', 'exp')), may hold values from 0 to 15, all different within a row; in each aligned block of 160 rows (0 to 159, 160 to 319, ...) at most 30 rows name the same one
- cotangent: bfloat16 [5120, 512], P(('rep', 'exp')), may hold values from -6 to 6
- w_up: bfloat16 [16, 2048, 512], P('exp'), may hold values from -0.25 to 0.25
- w_down: bfloat16 [16, 2048, 512], P('exp'), may hold values from -0.125 to 0.125
Outputs:
- d_tokens: bfloat16 [5120, 512], P(('rep', 'exp'))
- d_gates: bfloat16 [5120, 2], P(('rep', 'exp'))
- grad_up: bfloat16 [16, 2048, 512], P('exp', 'rep')
- grad_down: bfloat16 [16, 2048, 512], P('exp', 'rep')
Inputs may be any that keep to these rules, and one draw needn't show every extreme that they name: `routes`: each row names two different experts. In each aligned block of 160 rows (the rows of one device) no expert is named by more than 30 rows, a bound that some block reaches.
All inputs are finite; a program needn't handle non-finite values.
Results may differ from a plain program's by a relative error of at most 0.014.
Values may be sent and summed in bfloat16 or wider, within the bound.
No kernel may reach another device: no remote copies, remote signals or barrier semaphores. Data moves between devices by JAX's collectives and lax.ppermute only.
A program may use at most 64 MiB of HBM per device.

v0:
```python
import jax
import jax.numpy as jnp
from jax import lax
from jax.sharding import PartitionSpec as P


def silu_parts(preact):
    sigma = jax.nn.sigmoid(preact)
    return (preact * sigma, sigma * (1.0 + preact * (1.0 - sigma)))


def contract_last(left, right):
    return lax.dot_general(
        left, right, (((1,), (1,)), ((), ())), preferred_element_type=jnp.float32
    )


def contract_first(left, right):
    return lax.dot_general(
        left, right, (((0,), (0,)), ((), ())), preferred_element_type=jnp.float32
    )


def local(tokens, gates, routes, cotangent, w_up, w_down):
    tok_rows = tokens.shape[0]
    feat_dim = tokens.shape[1]
    groups = lax.axis_size("exp")
    mirrors = lax.axis_size("rep")
    capacity = max(2, 3 * tok_rows // groups)
    slots_all = groups * capacity
    flat_ids = routes.reshape(-1)
    onehot = (flat_ids[:, None] == jnp.arange(groups, dtype=jnp.int32)[None, :]).astype(jnp.int32)
    slot_pos = jnp.sum((jnp.cumsum(onehot, axis=0) - 1) * onehot, axis=1)
    target = flat_ids * capacity + slot_pos
    gate_flat = gates.reshape(-1)
    select = (jnp.arange(slots_all, dtype=jnp.int32)[:, None] == target[None, :]).astype(
        jnp.bfloat16
    )
    by_row = select.reshape(slots_all, tok_rows, 2).sum(axis=2)
    rows_out = jnp.dot(by_row, tokens, preferred_element_type=jnp.float32).astype(jnp.bfloat16)
    grads_out = jnp.dot(by_row, cotangent, preferred_element_type=jnp.float32).astype(jnp.bfloat16)
    gate_out = jnp.dot(select, gate_flat, preferred_element_type=jnp.float32).astype(jnp.bfloat16)
    rows_in, grad_in, gate_in = (
        lax.all_to_all(
            rows_out.reshape(groups, capacity, feat_dim),
            "exp",
            split_axis=0,
            concat_axis=0,
            tiled=True,
        ),
        lax.all_to_all(
            grads_out.reshape(groups, capacity, feat_dim),
            "exp",
            split_axis=0,
            concat_axis=0,
            tiled=True,
        ),
        lax.all_to_all(
            gate_out.reshape(groups, capacity), "exp", split_axis=0, concat_axis=0, tiled=True
        ),
    )
    rows_in = rows_in.reshape(slots_all, feat_dim)
    grad_in = grad_in.reshape(slots_all, feat_dim)
    gate_in = gate_in.reshape(slots_all)
    up_mat = w_up[0]
    down_mat = w_down[0]
    preact = contract_last(rows_in, up_mat)
    active, slopes = silu_parts(preact)
    hidden = active.astype(jnp.bfloat16)
    output = jnp.dot(hidden, down_mat, preferred_element_type=jnp.float32)
    gate_grad = jnp.sum(grad_in.astype(jnp.float32) * output, axis=1).astype(jnp.bfloat16)
    out_grad = (gate_in.astype(jnp.float32)[:, None] * grad_in.astype(jnp.float32)).astype(
        jnp.bfloat16
    )
    hid_grad = (contract_last(out_grad, down_mat) * slopes).astype(jnp.bfloat16)
    in_grad = jnp.dot(hid_grad, up_mat, preferred_element_type=jnp.float32).astype(jnp.bfloat16)
    ff_share = up_mat.shape[0] // mirrors
    offset = lax.axis_index("rep") * ff_share
    up_slice = lax.dynamic_slice_in_dim(up_mat, offset, ff_share, 0)
    down_slice = lax.dynamic_slice_in_dim(down_mat, offset, ff_share, 0)

    def one_mirror(mirror_rows, mirror_grads):
        part_pre = contract_last(mirror_rows, up_slice)
        part_act, part_slope = silu_parts(part_pre)
        part_hidden = part_act.astype(jnp.bfloat16)
        part_hid_grad = (contract_last(mirror_grads, down_slice) * part_slope).astype(jnp.bfloat16)
        up_part = contract_first(part_hid_grad, mirror_rows).astype(jnp.bfloat16)
        down_part = contract_first(part_hidden, mirror_grads).astype(jnp.bfloat16)
        return (up_part, down_part)

    piece_rows = lax.all_gather(rows_in, "rep", axis=0, tiled=True)
    piece_grads = lax.all_gather(out_grad, "rep", axis=0, tiled=True)
    shards = piece_rows.shape[0] // slots_all
    stacked_rows = piece_rows.reshape(shards, slots_all, feat_dim)
    stacked_grads = piece_grads.reshape(shards, slots_all, feat_dim)
    up_parts, down_parts = jax.vmap(one_mirror)(stacked_rows, stacked_grads)
    up_sum = jnp.sum(up_parts.astype(jnp.float32), axis=0)
    down_sum = jnp.sum(down_parts.astype(jnp.float32), axis=0)
    grad_up = up_sum.astype(jnp.bfloat16)
    grad_down = down_sum.astype(jnp.bfloat16)
    back_grad, back_gate = (
        lax.all_to_all(
            in_grad.reshape(groups, capacity, feat_dim),
            "exp",
            split_axis=0,
            concat_axis=0,
            tiled=True,
        ),
        lax.all_to_all(
            gate_grad.reshape(groups, capacity), "exp", split_axis=0, concat_axis=0, tiled=True
        ),
    )
    back_grad = back_grad.reshape(slots_all, feat_dim)
    back_gate = back_gate.reshape(slots_all)
    d_tokens = contract_first(by_row, back_grad).astype(jnp.bfloat16)
    d_gates = contract_first(select, back_gate).astype(jnp.bfloat16).reshape(tok_rows, 2)
    return (d_tokens, d_gates, grad_up[None], grad_down[None])


def solution(mesh):
    in_specs = (
        P(("rep", "exp"), None),
        P(("rep", "exp"), None),
        P(("rep", "exp"), None),
        P(("rep", "exp"), None),
        P("exp", None, None),
        P("exp", None, None),
    )
    out_specs = (
        P(("rep", "exp"), None),
        P(("rep", "exp"), None),
        P("exp", "rep", None),
        P("exp", "rep", None),
    )
    return jax.shard_map(local, mesh=mesh, in_specs=in_specs, out_specs=out_specs, check_vma=False)
```

profile of v0, /device:TPU:0, one launch (start us, length us, event | category | flops | bytes accessed | tf_op | source)
XLA Modules:
  0.0 122.7 jit_solution(15795308315346128206)
XLA Ops:
  0.6 0.0 copy-start
  0.6 0.0 copy-start.3
  0.7 1.0 copy.45
  1.6 0.1 eq.43
  1.8 0.9 reduce-window.6
  2.7 0.2 slice_reduce_fusion
  2.9 0.1 bitcast_bitcast_fusion
  3.0 0.8 copy.49
  3.8 0.2 reshape.128
  4.0 0.2 fusion.26
  4.3 0.7 all_to_all.25
  5.0 7.4 %all-to-all-start = ((bf16[16,1,30]{2,1,0:T(2,128)(2,1)}), bf16[16,1,30]{2,1,0:T(2,128)(2,1)S(1)}, u32[]{:S(2)}, u32[]{:S(2)}) async-start(bf16[16,1,30]{2,1,0:T(2,128)(2,1)} %all_to_all.25), calls=%async_computation | async-start | bytes 16384 | tf_op jit(solution)/shard_map/all_to_all | solution.py:58
  12.4 0.1 reduce_sum.57
  12.5 0.1 copy.48
  12.6 0.7 multiply_add_fusion.1
  13.3 0.1 fusion.30
  13.4 1.2 %convolution_convert_fusion = bf16[480,512]{1,0:T(8,128)(2,1)S(1)} fusion(bf16[480,160]{0,1:T(8,128)(2,1)S(1)} %fusion.30, bf16[160,512]{1,0:T(8,128)(2,1)} %param.6), kind=kOutput, calls=%fused_computation.18 | convolution fusion | flops 78888960 | bytes 808960 | tf_op jit(solution)/shard_map/dot_general | solution.py:40
  14.7 0.9 reshape.116
  15.6 3.1 %all-to-all-done = bf16[16,1,30]{2,1,0:T(2,128)(2,1)S(1)} async-done(((bf16[16,1,30]{2,1,0:T(2,128)(2,1)}), bf16[16,1,30]{2,1,0:T(2,128)(2,1)S(1)}, u32[]{:S(2)}, u32[]{:S(2)}) %all-to-all-start) | async-done | bytes 992 | tf_op jit(solution)/shard_map/all_to_all | solution.py:58
  18.7 3.6 %all-to-all-start.2 = ((bf16[16,30,512]{2,1,0:T(8,128)(2,1)}), bf16[16,30,512]{2,1,0:T(8,128)(2,1)S(1)}, u32[]{:S(2)}, u32[]{:S(2)}) async-start(bf16[16,30,512]{2,1,0:T(8,128)(2,1)} %reshape.116), calls=%async_computation.2 | async-start | bytes 1048576 | tf_op jit(solution)/shard_map/all_to_all | solution.py:44
  22.3 0.0 copy-done.3
  22.3 0.3 convolution_convert_fusion.1
  22.6 0.9 reshape.115
  23.5 13.2 %all-to-all-done.2 = bf16[16,30,512]{2,1,0:T(8,128)(2,1)S(1)} async-done(((bf16[16,30,512]{2,1,0:T(8,128)(2,1)}), bf16[16,30,512]{2,1,0:T(8,128)(2,1)S(1)}, u32[]{:S(2)}, u32[]{:S(2)}) %all-to-all-start.2) | async-done | bytes 491552 | tf_op jit(solution)/shard_map/all_to_all | solution.py:44
  36.7 0.0 copy-start.2
  36.7 0.8 copy-done.2
  37.5 4.0 %all-to-all-start.1 = ((bf16[16,30,512]{2,1,0:T(8,128)(2,1)}), bf16[16,30,512]{2,1,0:T(8,128)(2,1)S(1)}, u32[]{:S(2)}, u32[]{:S(2)}) async-start(bf16[16,30,512]{2,1,0:T(8,128)(2,1)} %reshape.115), calls=%async_computation.1 | async-start | bytes 1048576 | tf_op jit(solution)/shard_map/all_to_all | solution.py:51
  41.6 0.1 reshape.127
  41.7 1.2 reshape.117
  42.9 14.3 %all_gather.7 = bf16[960,512]{1,0:T(8,128)(2,1)} all-gather(bf16[480,512]{1,0:T(8,128)(2,1)S(1)} %reshape.117), channel_id=1, replica_groups=mesh['rep'=2,'exp'=16] {'rep'}, dimensions={0}, use_global_device_ids=true | all-gather | bytes 1474560 | tf_op jit(solution)/shard_map/all_gather | solution.py:91
  57.2 0.0 copy-done
  57.2 3.1 %fusion.2 = f32[480,2048]{1,0:T(8,128)} fusion(bf16[480,512]{1,0:T(8,128)(2,1)S(1)} %reshape.117, bf16[1,2048,512]{2,1,0:T(8,128)(2,1)S(1)} %copy-done), kind=kOutput, calls=%fused_computation.8 | convolution fusion | flops 1006632960 | bytes 6520832 | tf_op jit(solution)/shard_map/dot_general | solution.py:13
  60.3 0.0 all-to-all-done.1
  60.3 0.2 multiply_convert_fusion.12
  60.5 0.9 convert_element_type.103
  61.4 6.3 %fusion.11 = bf16[480,512]{1,0:T(8,128)(2,1)} fusion(bf16[1,2048,512]{2,1,0:T(8,128)(2,1)S(1)} %copy-done, f32[480,2048]{1,0:T(8,128)} %fusion.2, bf16[480,512]{1,0:T(8,128)(2,1)} %convert_element_type.103, bf16[1,2048,512]{2,1,0:T(8,128)(2,1)} %param.11), kind=kOutput, calls=%fused_computation.17 | convolution fusion | flops 2022359040 | bytes 9109504 | tf_op jit(solution)/shard_map/dot_general | solution.py:76
  67.6 1.1 reshape.126
  68.7 0.0 copy-start.1
  68.7 4.4 %fusion.14 = bf16[480]{0:T(512)(128)(2,1)S(1)} fusion(f32[480,512]{1,0:T(8,128)} %reshape.126, bf16[1,2048,512]{2,1,0:T(8,128)(2,1)} %param.11, f32[480,2048]{1,0:T(8,128)} %fusion.2), kind=kOutput, calls=%fused_computation.20 | convolution fusion | flops 1012039168 | bytes 7013312 | tf_op jit(solution)/shard_map/dot_general | solution.py:70
  73.1 0.7 convert_element_type.124
  73.8 5.7 %all-to-all-start.4 = ((bf16[16,1,30]{2,1,0:T(2,128)(2,1)}), bf16[16,1,30]{2,1,0:T(2,128)(2,1)S(1)}, u32[]{:S(2)}, u32[]{:S(2)}) async-start(bf16[16,1,30]{2,1,0:T(2,128)(2,1)} %convert_element_type.124), calls=%async_computation.4 | async-start | bytes 16384 | tf_op jit(solution)/shard_map/all_to_all | solution.py:109
  79.5 1.3 %multiply_convert_fusion.13 = bf16[480,512]{1,0:T(8,128)(2,1)S(1)} fusion(f32[480,512]{1,0:T(8,128)} %reshape.126, f32[480]{0:T(512)S(1)} %reshape.127), kind=kLoop, calls=%fused_computation.29 | loop fusion | flops 491520 | bytes 1476480 | tf_op jit(solution)/shard_map/convert_element_type | solution.py:72
  80.8 0.0 copy-done.1
  80.8 3.1 %fusion.19 = f32[2,480,1024]{2,1,0:T(8,128)} fusion(bf16[2,480,512]{2,1,0:T(8,128)(2,1)S(1)} %bitcast.61, bf16[1,2048,512]{2,1,0:T(8,128)(2,1)S(1)} %copy-done, s32[]{:T(128)S(6)} %select_n.4), kind=kOutput, calls=%fused_computation.23 | convolution fusion | flops 1006632960 | bytes 5963780 | tf_op jit(solution)/shard_map/vmap()/dot_general | solution.py:13
  83.9 14.3 %all_gather.6 = bf16[960,512]{1,0:T(8,128)(2,1)} all-gather(bf16[480,512]{1,0:T(8,128)(2,1)S(1)} %multiply_convert_fusion.13), channel_id=1, replica_groups=mesh['rep'=2,'exp'=16] {'rep'}, dimensions={0}, use_global_device_ids=true | all-gather | bytes 1474560 | tf_op jit(solution)/shard_map/all_gather | solution.py:92
  98.3 2.0 %reshape.118 = bf16[16,30,512]{2,1,0:T(8,128)(2,1)} reshape(bf16[480,512]{1,0:T(8,128)(2,1)} %fusion.11) | data formatting | bytes 983040 | tf_op jit(solution)/shard_map/reshape | solution.py:103
  100.3 0.0 all-to-all-done.4
  100.3 5.8 %all-to-all-start.3 = ((bf16[16,30,512]{2,1,0:T(8,128)(2,1)}), bf16[16,30,512]{2,1,0:T(8,128)(2,1)}, u32[]{:S(2)}, u32[]{:S(2)}) async-start(bf16[16,30,512]{2,1,0:T(8,128)(2,1)} %reshape.118), calls=%async_computation.3 | async-start | bytes 1048576 | tf_op jit(solution)/shard_map/all_to_all | solution.py:102
  106.1 6.4 %convert_reduce_fusion.1 = bf16[1024,512]{1,0:T(8,128)(2,1)} fusion(bf16[2,480,512]{2,1,0:T(8,128)(2,1)S(1)} %bitcast.62, f32[2,480,1024]{2,1,0:T(8,128)} %fusion.19, bf16[2,480,512]{2,1,0:T(8,128)(2,1)} %bitcast.63, bf16[1,2048,512]{2,1,0:T(8,128)(2,1)} %param.11, s32[]{:T(128)S(6)} %select_n.4), kind=kOutput, calls=%fused_computation.14 | convolution fusion | flops 2023686144 | bytes 7995396 | tf_op jit(solution)/shard_map/vmap()/dot_general | solution.py:19
  112.5 5.0 %convert_reduce_fusion = bf16[1024,512]{1,0:T(8,128)(2,1)} fusion(bf16[2,480,512]{2,1,0:T(8,128)(2,1)} %bitcast.64, f32[2,480,1024]{2,1,0:T(8,128)} %fusion.19), kind=kOutput, calls=%fused_computation.13 | convolution fusion | flops 1013121024 | bytes 5963776 | tf_op jit(solution)/shard_map/vmap()/dot_general | solution.py:19
  117.5 0.1 reshape.130
  117.6 0.3 convolution_reduce_fusion
  117.9 0.2 reshape.121
  118.0 0.7 copy.52
  118.7 1.9 %all-to-all-done.3 = bf16[16,30,512]{2,1,0:T(8,128)(2,1)} async-done(((bf16[16,30,512]{2,1,0:T(8,128)(2,1)}), bf16[16,30,512]{2,1,0:T(8,128)(2,1)}, u32[]{:S(2)}, u32[]{:S(2)}) %all-to-all-start.3) | async-done | bytes 491552 | tf_op jit(solution)/shard_map/all_to_all | solution.py:102
  120.6 1.2 reshape.119
  121.7 0.9 convolution_convert_fusion.2
  (9 shorter events, 0.2 us)
Async XLA Ops:
  0.6 56.6 %copy-start = (bf16[1,2048,512]{2,1,0:T(8,128)(2,1)S(1)}, bf16[1,2048,512]{2,1,0:T(8,128)(2,1)}, u32[]{:S(2)}) copy-start(bf16[1,2048,512]{2,1,0:T(8,128)(2,1)} %param.10) | copy-start | bytes 6291460
  0.6 21.6 %copy-start.3 = (bf16[160,512]{1,0:T(8,128)(2,1)S(1)}, bf16[160,512]{1,0:T(8,128)(2,1)}, u32[]{:S(2)}) copy-start(bf16[160,512]{1,0:T(8,128)(2,1)} %param.9) | copy-start | bytes 491524
  5.0 13.7 %all-to-all-start = ((bf16[16,1,30]{2,1,0:T(2,128)(2,1)}), bf16[16,1,30]{2,1,0:T(2,128)(2,1)S(1)}, u32[]{:S(2)}, u32[]{:S(2)}) async-start(bf16[16,1,30]{2,1,0:T(2,128)(2,1)} %all_to_all.25), calls=%async_computation | async-start | bytes 16384 | tf_op jit(solution)/shard_map/all_to_all | solution.py:58
  18.7 18.0 %all-to-all-start.2 = ((bf16[16,30,512]{2,1,0:T(8,128)(2,1)}), bf16[16,30,512]{2,1,0:T(8,128)(2,1)S(1)}, u32[]{:S(2)}, u32[]{:S(2)}) async-start(bf16[16,30,512]{2,1,0:T(8,128)(2,1)} %reshape.116), calls=%async_computation.2 | async-start | bytes 1048576 | tf_op jit(solution)/shard_map/all_to_all | solution.py:44
  36.7 0.8 copy-start.2
  37.5 22.8 %all-to-all-start.1 = ((bf16[16,30,512]{2,1,0:T(8,128)(2,1)}), bf16[16,30,512]{2,1,0:T(8,128)(2,1)S(1)}, u32[]{:S(2)}, u32[]{:S(2)}) async-start(bf16[16,30,512]{2,1,0:T(8,128)(2,1)} %reshape.115), calls=%async_computation.1 | async-start | bytes 1048576 | tf_op jit(solution)/shard_map/all_to_all | solution.py:51
  68.7 12.1 %copy-start.1 = (bf16[960,512]{1,0:T(8,128)(2,1)S(1)}, bf16[960,512]{1,0:T(8,128)(2,1)}, u32[]{:S(2)}) copy-start(bf16[960,512]{1,0:T(8,128)(2,1)} %all_gather.7) | copy-start | bytes 2949124
  73.8 26.5 %all-to-all-start.4 = ((bf16[16,1,30]{2,1,0:T(2,128)(2,1)}), bf16[16,1,30]{2,1,0:T(2,128)(2,1)S(1)}, u32[]{:S(2)}, u32[]{:S(2)}) async-start(bf16[16,1,30]{2,1,0:T(2,128)(2,1)} %convert_element_type.124), calls=%async_computation.4 | async-start | bytes 16384 | tf_op jit(solution)/shard_map/all_to_all | solution.py:109
  100.3 20.3 %all-to-all-start.3 = ((bf16[16,30,512]{2,1,0:T(8,128)(2,1)}), bf16[16,30,512]{2,1,0:T(8,128)(2,1)}, u32[]{:S(2)}, u32[]{:S(2)}) async-start(bf16[16,30,512]{2,1,0:T(8,128)(2,1)} %reshape.118), calls=%async_computation.3 | async-start | bytes 1048576 | tf_op jit(solution)/shard_map/all_to_all | solution.py:102
where the time goes:
time: 123 us
  matrix products  31.2 us (25%)
  blocking collectives  28.7 us (23%)
  starting transfers between devices  26.5 us (22%)
  waiting for transfers between devices  18.1 us (15%)
  local copies, waits for them, and re-layouts  13.9 us (11%)
  other arithmetic  3.44 us (3%)
    all_gather x1, blocking collectives, local(): piece_rows = lax.all_gather(rows_in, 'rep', axis=0, tiled=True)  14.3 us
    all_gather x1, blocking collectives, local(): piece_grads = lax.all_gather(out_grad, 'rep', axis=0, tiled=True)  14.3 us
    all_to_all x1, waiting for transfers between devices, local(): lax.all_to_all(rows_out.reshape(groups, capacity, feat_dim), 'exp', split...  13.2 us
    dot_general x4, matrix products, contract_first(): lax.dot_general(left, right, (((0,), (0,)), ((), ())), preferred_element_...  12.6 us
    all_to_all x1, starting transfers between devices, local(): lax.all_to_all(gate_out.reshape(groups, capacity), 'exp', split_axis=0, c...  7.39 us
    dot_general x1, matrix products, local(): jnp.dot(hid_grad, up_mat, preferred_element_type=jnp.float32)  6.26 us
    dot_general x2, matrix products, contract_last(): lax.dot_general(left, right, (((1,), (1,)), ((), ())), preferred_element_...  6.2 us
    all_to_all x1, starting transfers between devices, local(): lax.all_to_all(in_grad.reshape(groups, capacity, feat_dim), 'exp', split_...  5.79 us
  transfers between devices with their start and end apart: 5, of which 3 were waited for; matrix products, arithmetic and copies ran while one was open for 23% of the time, Pallas kernels for 0%

commit v1 on v0

v1 whole, which is shorter than its diff:
```python
import functools

import jax
import jax.numpy as jnp
from jax import lax
from jax.experimental import pallas as pl
from jax.experimental.pallas import tpu as pltpu
from jax.sharding import PartitionSpec as P

F32 = jnp.float32
BF16 = jnp.bfloat16
VMEM_LIMIT = 40 * 1024 * 1024


def dot(left, right, left_dim, right_dim):
    return lax.dot_general(
        left, right, (((left_dim,), (right_dim,)), ((), ())), preferred_element_type=F32
    )


def silu_parts(preact):
    sigma = 0.5 * jnp.tanh(0.5 * preact) + 0.5
    active = preact * sigma
    return active, sigma + active * (1.0 - sigma)


def call(body, name, outs, args, flops, transcendentals=0):
    moved = sum(a.size * a.dtype.itemsize for a in (*args, *outs))
    return pl.pallas_call(
        body,
        name=name,
        out_shape=outs,
        in_specs=[pl.BlockSpec(memory_space=pltpu.VMEM)] * len(args),
        out_specs=[pl.BlockSpec(memory_space=pltpu.VMEM)] * len(outs),
        compiler_params=pltpu.CompilerParams(vmem_limit_bytes=VMEM_LIMIT),
        cost_estimate=pl.CostEstimate(
            flops=flops, bytes_accessed=moved, transcendentals=transcendentals
        ),
    )(*args)


def slots_of(routes, groups):
    rows = routes.shape[1]
    expert = lax.broadcasted_iota(jnp.int32, (groups, rows), 0)
    hot = [expert == routes[k : k + 1, :] for k in range(2)]
    as_num = [jnp.where(h, 1.0, 0.0).astype(F32) for h in hot]
    before = jnp.where(
        lax.broadcasted_iota(jnp.int32, (rows, rows), 0)
        < lax.broadcasted_iota(jnp.int32, (rows, rows), 1),
        1.0,
        0.0,
    ).astype(BF16)
    count = [dot(n.astype(BF16), before, 1, 0) for n in as_num]
    total = jnp.sum(as_num[0], axis=1, keepdims=True)
    place = [count[0], count[1] + total]
    slot = [
        jnp.sum(jnp.where(h, p, 0.0), axis=0, keepdims=True).astype(jnp.int32)
        for h, p in zip(hot, place)
    ]
    return hot, slot


def dispatch_kernel(groups, pad, routes_ref, gates_ref, tok_ref, cot_ref, out_ref, pick_ref):
    routes = routes_ref[...]
    gates = gates_ref[...].astype(F32)
    _, slot = slots_of(routes, groups)
    rows = routes.shape[1]
    index = lax.broadcasted_iota(jnp.int32, (groups * pad, rows), 0)
    pick = [index == routes[k : k + 1, :] * pad + slot[k] for k in range(2)]
    plain = jnp.where(pick[0] | pick[1], 1.0, 0.0).astype(BF16)
    scaled = (
        jnp.where(pick[0], gates[0:1, :], 0.0) + jnp.where(pick[1], gates[1:2, :], 0.0)
    ).astype(BF16)
    pick_ref[...] = plain
    feat = tok_ref.shape[1]
    out_ref[:, 0:pad, :] = dot(plain, tok_ref[...], 1, 0).astype(BF16).reshape(groups, pad, feat)
    out_ref[:, pad:, :] = dot(scaled, cot_ref[...], 1, 0).astype(BF16).reshape(groups, pad, feat)


def own_kernel(cap, block, disp_ref, up_ref, down_ref, out_ref, grad_acc, gate_acc):
    groups, both, feat = disp_ref.shape
    pad = both // 2
    slots = groups * pad
    rows = disp_ref[:, 0:pad, :].reshape(slots, feat)
    grads = disp_ref[:, pad:, :].reshape(slots, feat)
    for step in range(up_ref.shape[1] // block):
        part = pl.ds(step * block, block)
        up = up_ref[0, part, :]
        down = down_ref[0, part, :]
        active, slope = silu_parts(dot(rows, up, 1, 1))
        back = dot(grads, down, 1, 1)
        hid_grad = (back * slope).astype(BF16)
        gate = active.astype(BF16).astype(F32) * back
        gate = sum(gate[:, i : i + 128] for i in range(0, block, 128))
        in_grad = dot(hid_grad, up, 1, 0)
        if step == 0:
            grad_acc[...] = in_grad
            gate_acc[...] = gate
        else:
            grad_acc[...] += in_grad
            gate_acc[...] += gate
    gate = jnp.sum(gate_acc[...], axis=1, keepdims=True)
    spot = lax.broadcasted_iota(jnp.int32, (slots, 128), 0) % pad
    lane = lax.broadcasted_iota(jnp.int32, (slots, 128), 1)
    gate = jnp.where(spot == lane, gate, 0.0).reshape(groups, pad, 128)
    gate = jnp.sum(gate, axis=1, keepdims=True)
    grad = grad_acc[...].reshape(groups, pad, feat)
    line = lax.broadcasted_iota(jnp.int32, (groups, pad, 128), 1)
    out_ref[:, :, 0:128] = jnp.where(line == cap, gate, grad[:, :, 0:128]).astype(BF16)
    out_ref[:, :, 128:] = grad[:, :, 128:].astype(BF16)


def weights_kernel(block, share, *refs):
    mirror_refs = refs[:-6]
    up_ref, down_ref, grad_up_ref, grad_down_ref, up_acc, down_acc = refs[-6:]
    base = lax.axis_index("rep") * share
    pairs = []
    own = mirror_refs[0]
    pad = own.shape[1] // 2
    slots = own.shape[0] * pad
    feat = own.shape[2]
    pairs.append((own[:, 0:pad, :].reshape(slots, feat), own[:, pad:, :].reshape(slots, feat)))
    for i in range(1, len(mirror_refs), 2):
        pairs.append((mirror_refs[i][...], mirror_refs[i + 1][...]))
    for number, (rows, grads) in enumerate(pairs):
        for step in range(share // block):
            part = pl.ds(pl.multiple_of(base + step * block, block), block)
            here = pl.ds(step * block, block)
            active, slope = silu_parts(dot(up_ref[0, part, :], rows, 1, 1))
            hid_grad = (dot(down_ref[0, part, :], grads, 1, 1) * slope).astype(BF16)
            up_part = dot(hid_grad, rows, 1, 0)
            down_part = dot(active.astype(BF16), grads, 1, 0)
            if number:
                up_part += up_acc[here, :]
                down_part += down_acc[here, :]
            if number == len(pairs) - 1:
                grad_up_ref[0, here, :] = up_part.astype(BF16)
                grad_down_ref[0, here, :] = down_part.astype(BF16)
            else:
                up_acc[here, :] = up_part
                down_acc[here, :] = down_part


def combine_kernel(cap, routes_ref, gates_ref, pick_ref, back_ref, d_tok_ref, d_gate_ref):
    groups, pad, feat = back_ref.shape
    back = back_ref[...]
    d_tok_ref[...] = dot(pick_ref[...], back.reshape(groups * pad, feat), 0, 0).astype(BF16)
    routes = routes_ref[...]
    gates = gates_ref[...].astype(F32)
    hot, slot = slots_of(routes, groups)
    lane = lax.broadcasted_iota(jnp.int32, (128, routes.shape[1]), 0)
    values = back[:, cap, 0:128]
    for k in range(2):
        spot = jnp.where(lane == slot[k], 1.0, 0.0).astype(BF16)
        found = jnp.where(hot[k], dot(values, spot, 1, 0), 0.0)
        found = jnp.sum(found, axis=0, keepdims=True)
        d_gate_ref[k : k + 1, :] = (found / gates[k : k + 1, :]).astype(BF16)


def local(tokens, gates, routes, cotangent, w_up, w_down):
    rows, feat = tokens.shape
    hidden = w_up.shape[1]
    groups = lax.axis_size("exp")
    mirrors = lax.axis_size("rep")
    cap = max(2, 3 * rows // groups)
    pad = (cap // 16 + 1) * 16
    slots = groups * pad
    share = hidden // mirrors
    routes_t, gates_t = routes.T, gates.T
    shape = jax.ShapeDtypeStruct
    unit = 2 * slots * feat

    out, pick = call(
        functools.partial(dispatch_kernel, groups, pad),
        "dispatch",
        [shape((groups, 2 * pad, feat), BF16), shape((slots, rows), BF16)],
        [routes_t, gates_t, tokens, cotangent],
        2 * unit * rows,
    )
    disp = lax.all_to_all(out, "exp", split_axis=0, concat_axis=0, tiled=True)
    rows_in = disp[:, 0:pad, :].reshape(slots, feat)
    grads_in = disp[:, pad:, :].reshape(slots, feat)
    others = []
    for shift in range(1, mirrors):
        hops = [(i, (i + shift) % mirrors) for i in range(mirrors)]
        others.append(lax.ppermute(rows_in, "rep", hops))
        others.append(lax.ppermute(grads_in, "rep", hops))

    block = min(512, hidden)
    (back,) = pl.pallas_call(
        functools.partial(own_kernel, cap, block),
        name="own_mirror",
        out_shape=[shape((groups, pad, feat), BF16)],
        in_specs=[pl.BlockSpec(memory_space=pltpu.VMEM)] * 3,
        out_specs=[pl.BlockSpec(memory_space=pltpu.VMEM)],
        scratch_shapes=[pltpu.VMEM((slots, feat), F32), pltpu.VMEM((slots, 128), F32)],
        compiler_params=pltpu.CompilerParams(vmem_limit_bytes=VMEM_LIMIT),
        cost_estimate=pl.CostEstimate(
            flops=3 * unit * hidden,
            bytes_accessed=4 * hidden * feat + 6 * slots * feat,
            transcendentals=slots * hidden,
        ),
    )(disp, w_up, w_down)
    back = lax.all_to_all(back, "exp", split_axis=0, concat_axis=0, tiled=True)

    part = min(512, share)
    grad_up, grad_down = pl.pallas_call(
        functools.partial(weights_kernel, part, share),
        name="weight_grads",
        out_shape=[shape((1, share, feat), BF16)] * 2,
        in_specs=[pl.BlockSpec(memory_space=pltpu.VMEM)] * (len(others) + 3),
        out_specs=[pl.BlockSpec(memory_space=pltpu.VMEM)] * 2,
        scratch_shapes=[pltpu.VMEM((share, feat), F32)] * 2,
        compiler_params=pltpu.CompilerParams(vmem_limit_bytes=VMEM_LIMIT),
        cost_estimate=pl.CostEstimate(
            flops=4 * unit * share * mirrors,
            bytes_accessed=8 * hidden * feat,
            transcendentals=slots * hidden,
        ),
    )(disp, *others, w_up, w_down)

    d_tokens, d_gates = call(
        functools.partial(combine_kernel, cap),
        "combine",
        [shape((rows, feat), BF16), shape((2, rows), BF16)],
        [routes_t, gates_t, pick, back],
        unit * rows,
    )
    return d_tokens, d_gates.T, grad_up, grad_down


def solution(mesh):
    by_both = P(("rep", "exp"), None)
    by_expert = P("exp", None, None)
    return jax.shard_map(
        local,
        mesh=mesh,
        in_specs=(by_both, by_both, by_both, by_both, by_expert, by_expert),
        out_specs=(by_both, by_both, P("exp", "rep", None), P("exp", "rep", None)),
        check_vma=False,
    )
```

time: 123 us -> 82.2 us (0.67)
  matrix products: 31.2 us -> 0 us
  starting transfers between devices: 26.5 us -> 7.08 us
  Pallas kernels: 0 us -> 12 us
  local copies, waits for them, and re-layouts: 13.9 us -> 6.46 us
  waiting for transfers between devices: 18.1 us -> 23.5 us
  other arithmetic: 3.44 us -> 0 us
  blocking collectives: 28.7 us -> 32 us
    all_to_all x0 -> x1, blocking collectives: none -> 32 us  [local(): disp = lax.all_to_all(out, 'exp', split_axis=0, concat_axis=0, tiled=True)]
    dot_general x11 -> x0, matrix products: 31.2 us -> none  [the longest x4 12.6 us: contract_first(): lax.dot_general(left, right, (((0,), (0,)), ((), ())), preferred_element_...]
    all_gather x2 -> x0, blocking collectives: 28.7 us -> none  [the longest x1 14.3 us: local(): piece_rows = lax.all_gather(rows_in, 'rep', axis=0, tiled=True)]
    ppermute x0 -> x2, waiting for transfers between devices: none -> 23.5 us  [the longest x1 12.7 us: local(): others.append(lax.ppermute(rows_in, 'rep', hops))]
    all_to_all x5 -> x1, starting transfers between devices: 26.5 us -> 4.99 us  [local(): back = lax.all_to_all(back, 'exp', split_axis=0, concat_axis=0, tiled=True)]
    all_to_all x5 -> x1, waiting for transfers between devices: 18.1 us -> 0.01 us  [local(): back = lax.all_to_all(back, 'exp', split_axis=0, concat_axis=0, tiled=True)]
    pallas_call x0 -> x4, Pallas kernels: none -> 12 us  [the longest x1 5.72 us: local(): pl.pallas_call(functools.partial(weights_kernel, part, share), name='weig...]
    reshape x8 -> x0, local copies, waits for them, and re-layouts: 6.62 us -> none  [the longest x1 1.99 us: local(): in_grad.reshape(groups, capacity, feat_dim)]
  transfers between devices with their start and end apart: 5 -> 3, of which waited for: 3 -> 2; matrix products, arithmetic and copies ran while one was open for 23% -> 0% of each run, Pallas kernels for 0% -> 7%
where the time goes in v1:
time: 82.2 us; the launch traced here: 81.7 us
  blocking collectives  32 us (39%)
  waiting for transfers between devices  23.5 us (29%)
  Pallas kernels  12 us (15%)
  starting transfers between devices  7.08 us (9%)
  local copies, waits for them, and re-layouts  6.46 us (8%)
    all_to_all x1, blocking collectives, local(): disp = lax.all_to_all(out, 'exp', split_axis=0, concat_axis=0, tiled=True)  32 us
    ppermute x1, waiting for transfers between devices, local(): others.append(lax.ppermute(rows_in, 'rep', hops))  12.7 us
    ppermute x1, waiting for transfers between devices, local(): others.append(lax.ppermute(grads_in, 'rep', hops))  10.8 us
    unnamed x20, local copies, waits for them, and re-layouts  6.39 us
    pallas_call x1, Pallas kernels, local(): pl.pallas_call(functools.partial(weights_kernel, part, share), name='weig...  5.72 us
    all_to_all x1, starting transfers between devices, local(): back = lax.all_to_all(back, 'exp', split_axis=0, concat_axis=0, tiled=True)  4.99 us
    pallas_call x1, Pallas kernels, local(): pl.pallas_call(functools.partial(own_kernel, cap, block), name='own_mirro...  4.64 us
    pallas_call x2, Pallas kernels, call(): pl.pallas_call(body, name=name, out_shape=outs, in_specs=[pl.BlockSpec(me...  1.67 us
  transfers between devices with their start and end apart: 3, of which 2 were waited for; matrix products, arithmetic and copies ran while one was open for 0% of the time, Pallas kernels for 7%

profile of v1, /device:TPU:0, one launch (start us, length us, event | category | flops | bytes accessed | tf_op | source)
XLA Modules:
  0.0 81.7 jit_solution(5488093883265240836)
XLA Ops:
  0.6 0.0 copy-start
  0.6 0.7 copy-done
  1.3 0.0 copy-start.2
  1.3 0.7 copy-done.2
  2.0 0.0 copy-start.8
  2.0 0.9 %copy-done.8 = bf16[160,512]{1,0:T(8,128)(2,1)S(1)} copy-done((bf16[160,512]{1,0:T(8,128)(2,1)S(1)}, bf16[160,512]{1,0:T(8,128)(2,1)}, u32[]{:S(2)}) %copy-start.8) | copy-done | bytes 163864
  2.9 0.0 copy-start.9
  2.9 0.9 %copy-done.9 = bf16[160,512]{1,0:T(8,128)(2,1)S(1)} copy-done((bf16[160,512]{1,0:T(8,128)(2,1)S(1)}, bf16[160,512]{1,0:T(8,128)(2,1)}, u32[]{:S(2)}) %copy-start.9) | copy-done | bytes 163864
  3.8 0.0 copy-start.4
  3.8 0.7 dispatch.1
  4.5 32.0 %all_to_all.10.disp_ref.refs_0_ = bf16[16,64,512]{2,1,0:T(8,128)(2,1)S(1)} all-to-all(bf16[16,64,512]{2,1,0:T(8,128)(2,1)S(1)} %get-tuple-element.11), channel_id=1, replica_groups=mesh['rep'=2,'exp'=16] {'exp'}, dimensions={0} | all-to-all | bytes 2097152 | tf_op jit(solution)/shard_map/all_to_all | solution.py:180
  36.5 0.0 copy-done.4
  36.5 0.0 copy-start.6
  36.5 1.6 %copy-done.6 = bf16[1,2048,512]{2,1,0:T(8,128)(2,1)S(1)} copy-done((bf16[1,2048,512]{2,1,0:T(8,128)(2,1)S(1)}, bf16[1,2048,512]{2,1,0:T(8,128)(2,1)}, u32[]{:S(2)}) %copy-start.6) | copy-done | bytes 2097176
  38.1 4.6 %own_mirror.1 = bf16[16,32,512]{2,1,0:T(8,128)(2,1)} custom-call(bf16[16,64,512]{2,1,0:T(8,128)(2,1)S(1)} %all_to_all.10.disp_ref.refs_0_, bf16[1,2048,512]{2,1,0:T(8,128)(2,1)S(1)} %copy-done.4, bf16[1,2048,512]{2,1,0:T(8,128)(2,1)S(1)} %copy-done.6), custom_call_target="tpu_custom_call" | custom-call | flops 3221225472 | bytes 5767168 | tf_op jit(solution)/shard_map/own_mirror/pallas_call | solution.py:190
  42.8 5.0 %all-to-all-start.1 = ((bf16[16,32,512]{2,1,0:T(8,128)(2,1)}), bf16[16,32,512]{2,1,0:T(8,128)(2,1)S(1)}, u32[]{:S(2)}, u32[]{:S(2)}) async-start(bf16[16,32,512]{2,1,0:T(8,128)(2,1)} %own_mirror.1), calls=%async_computation.1 | async-start | bytes 1048576 | tf_op jit(solution)/shard_map/all_to_all | solution.py:204
  47.8 0.0 copy-start.5
  47.8 0.1 fusion
  47.8 1.6 %collective-permute-start = (bf16[512,512]{1,0:T(8,128)(2,1)S(1)}, bf16[512,512]{1,0:T(8,128)(2,1)S(1)}, u32[]{:S(2)}, u32[]{:S(2)}) collective-permute-start(bf16[512,512]{1,0:T(8,128)(2,1)S(1)} %bitcast.10), channel_id=1, source_target_pairs={{0,16},{16,0},{1,17},{17,1},{2,18},{18,2},{3,19},{19,3},{4,20},{20... | collective-permute-start | bytes 1572872 | tf_op jit(solution)/shard_map/ppermute | solution.py:186
  49.4 0.0 copy-start.1
  49.4 0.0 copy-start.3
  49.4 0.5 collective-permute-start.1
  49.9 12.7 %collective-permute-done.refs_1_ = bf16[512,512]{1,0:T(8,128)(2,1)S(1)} collective-permute-done((bf16[512,512]{1,0:T(8,128)(2,1)S(1)}, bf16[512,512]{1,0:T(8,128)(2,1)S(1)}, u32[]{:S(2)}, u32[]{:S(2)}) %collective-permute-start) | collective-permute-done | bytes 524320 | tf_op jit(solution)/shard_map/ppermute | solution.py:186
  62.6 10.8 %collective-permute-done.1.refs_2_ = bf16[512,512]{1,0:T(8,128)(2,1)S(1)} collective-permute-done((bf16[512,512]{1,0:T(8,128)(2,1)S(1)}, bf16[512,512]{1,0:T(8,128)(2,1)S(1)}, u32[]{:S(2)}, u32[]{:S(2)}) %collective-permute-start.1) | collective-permute-done | bytes 524320 | tf_op jit(solution)/shard_map/ppermute | solution.py:187
  73.4 0.0 copy-done.5
  73.4 0.0 copy-start.7
  73.4 1.6 %copy-done.7 = bf16[1,2048,512]{2,1,0:T(8,128)(2,1)S(1)} copy-done((bf16[1,2048,512]{2,1,0:T(8,128)(2,1)S(1)}, bf16[1,2048,512]{2,1,0:T(8,128)(2,1)}, u32[]{:S(2)}) %copy-start.7) | copy-done | bytes 2097176
  75.0 5.7 %weight_grads.1 = (bf16[1,1024,512]{2,1,0:T(8,128)(2,1)}, bf16[1,1024,512]{2,1,0:T(8,128)(2,1)}) custom-call(bf16[16,64,512]{2,1,0:T(8,128)(2,1)S(1)} %all_to_all.10.disp_ref.refs_0_, bf16[512,512]{1,0:T(8,128)(2,1)S(1)} %collective-permute-done.refs_1_, bf16[512,512]{1,0:T(8,128)(2,1)S(1)} %collective-permute-done.1.refs_2_, ...), custom_call_target="tpu_custom_call" | custom-call | flops 4294967296 | bytes 8388608 | tf_op jit(solution)/shard_map/weight_grads/pallas_call | solution.py:207
  80.7 0.0 all-to-all-done.1.back_ref
  80.7 0.0 copy-done.1
  80.7 0.0 copy-done.3
  80.7 1.0 %combine.1 = (bf16[160,512]{1,0:T(8,128)(2,1)}, bf16[2,160]{1,0:T(2,128)(2,1)}) custom-call(s32[2,160]{1,0:T(2,128)S(1)} %bitcast.6, bf16[2,160]{1,0:T(2,128)(2,1)S(1)} %bitcast.8, bf16[512,160]{1,0:T(8,128)(2,1)S(1)} %get-tuple-element.10.pick_ref, bf16[16,32,512]{2,1,0:T(8,128)(2,1)S(1)} %all-to-all-done.1.back_ref), custom_call_target="tpu_custom_call" | custom-call | flops 83886080 | bytes 854528 | tf_op jit(solution)/shard_map/combine/pallas_call | solution.py:29
Async XLA Ops:
  0.6 0.7 copy-start
  1.3 0.7 copy-start.2
  2.0 0.9 %copy-start.8 = (bf16[160,512]{1,0:T(8,128)(2,1)S(1)}, bf16[160,512]{1,0:T(8,128)(2,1)}, u32[]{:S(2)}) copy-start(bf16[160,512]{1,0:T(8,128)(2,1)} %tok_ref.1) | copy-start | bytes 491524
  2.9 0.9 %copy-start.9 = (bf16[160,512]{1,0:T(8,128)(2,1)S(1)}, bf16[160,512]{1,0:T(8,128)(2,1)}, u32[]{:S(2)}) copy-start(bf16[160,512]{1,0:T(8,128)(2,1)} %cot_ref.1) | copy-start | bytes 491524
  3.8 32.7 %copy-start.4 = (bf16[1,2048,512]{2,1,0:T(8,128)(2,1)S(1)}, bf16[1,2048,512]{2,1,0:T(8,128)(2,1)}, u32[]{:S(2)}) copy-start(bf16[1,2048,512]{2,1,0:T(8,128)(2,1)} %refs_3_.1) | copy-start | bytes 6291460
  36.5 1.6 %copy-start.6 = (bf16[1,2048,512]{2,1,0:T(8,128)(2,1)S(1)}, bf16[1,2048,512]{2,1,0:T(8,128)(2,1)}, u32[]{:S(2)}) copy-start(bf16[1,2048,512]{2,1,0:T(8,128)(2,1)} %refs_4_.1) | copy-start | bytes 6291460
  42.8 38.0 %all-to-all-start.1 = ((bf16[16,32,512]{2,1,0:T(8,128)(2,1)}), bf16[16,32,512]{2,1,0:T(8,128)(2,1)S(1)}, u32[]{:S(2)}, u32[]{:S(2)}) async-start(bf16[16,32,512]{2,1,0:T(8,128)(2,1)} %own_mirror.1), calls=%async_computation.1 | async-start | bytes 1048576 | tf_op jit(solution)/shard_map/all_to_all | solution.py:204
  47.8 25.7 %copy-start.5 = (bf16[1,2048,512]{2,1,0:T(8,128)(2,1)S(1)}, bf16[1,2048,512]{2,1,0:T(8,128)(2,1)}, u32[]{:S(2)}) copy-start(bf16[1,2048,512]{2,1,0:T(8,128)(2,1)} %refs_3_.1) | copy-start | bytes 6291460
  47.8 14.8 %collective-permute-start = (bf16[512,512]{1,0:T(8,128)(2,1)S(1)}, bf16[512,512]{1,0:T(8,128)(2,1)S(1)}, u32[]{:S(2)}, u32[]{:S(2)}) collective-permute-start(bf16[512,512]{1,0:T(8,128)(2,1)S(1)} %bitcast.10), channel_id=1, source_target_pairs={{0,16},{16,0},{1,17},{17,1},{2,18},{18,2},{3,19},{19,3},{4,20},{20... | collective-permute-start | bytes 1572872 | tf_op jit(solution)/shard_map/ppermute | solution.py:186
  49.4 31.3 %copy-start.1 = (s32[160,2]{0,1:T(2,128)S(1)}, s32[160,2]{0,1:T(2,128)}, u32[]{:S(2)}) copy-start(s32[160,2]{0,1:T(2,128)} %param.8) | copy-start | bytes 3844
  49.4 31.3 %copy-start.3 = (bf16[160,2]{0,1:T(2,128)(2,1)S(1)}, bf16[160,2]{0,1:T(2,128)(2,1)}, u32[]{:S(2)}) copy-start(bf16[160,2]{0,1:T(2,128)(2,1)} %param.7) | copy-start | bytes 1924
  49.4 24.0 %collective-permute-start.1 = (bf16[512,512]{1,0:T(8,128)(2,1)S(1)}, bf16[512,512]{1,0:T(8,128)(2,1)S(1)}, u32[]{:S(2)}, u32[]{:S(2)}) collective-permute-start(bf16[512,512]{1,0:T(8,128)(2,1)S(1)} %bitcast.9), channel_id=1, source_target_pairs={{0,16},{16,0},{1,17},{17,1},{2,18},{18,2},{3,19},{19,3},{4,20},{20... | collective-permute-start | bytes 1572872 | tf_op jit(solution)/shard_map/ppermute | solution.py:187
  73.4 1.6 %copy-start.7 = (bf16[1,2048,512]{2,1,0:T(8,128)(2,1)S(1)}, bf16[1,2048,512]{2,1,0:T(8,128)(2,1)}, u32[]{:S(2)}) copy-start(bf16[1,2048,512]{2,1,0:T(8,128)(2,1)} %refs_4_.1) | copy-start | bytes 6291460

commit v2 on v1

v2 whole, which is shorter than its diff:
```python
import functools
import itertools

import jax
import jax.numpy as jnp
from jax import lax
from jax.experimental import pallas as pl
from jax.experimental.pallas import tpu as pltpu
from jax.sharding import PartitionSpec as P

F32 = jnp.float32
BF16 = jnp.bfloat16
VMEM_LIMIT = 40 * 1024 * 1024
IN_HBM = pl.BlockSpec(memory_space=pltpu.HBM)
IN_VMEM = pl.BlockSpec(memory_space=pltpu.VMEM)
DMA = pltpu.SemaphoreType.DMA


def dot(left, right, left_dim, right_dim):
    return lax.dot_general(
        left, right, (((left_dim,), (right_dim,)), ((), ())), preferred_element_type=F32
    )


def silu_parts(preact):
    sigma = 0.5 * jnp.tanh(0.5 * preact) + 0.5
    active = preact * sigma
    return active, sigma + active * (1.0 - sigma)


def call(body, name, outs, args, in_specs, scratch, flops, transcendentals=0):
    moved = sum(a.size * a.dtype.itemsize for a in (*args, *outs))
    return pl.pallas_call(
        body,
        name=name,
        out_shape=outs,
        in_specs=in_specs,
        out_specs=[IN_VMEM] * len(outs),
        scratch_shapes=scratch,
        compiler_params=pltpu.CompilerParams(vmem_limit_bytes=VMEM_LIMIT),
        cost_estimate=pl.CostEstimate(
            flops=flops, bytes_accessed=moved, transcendentals=transcendentals
        ),
    )(*args)


def paired(groups):
    return groups & (groups - 1) == 0


def hops_to(groups, k):
    if paired(groups):
        return [(i, i ^ k) for i in range(groups)]
    return [(i, (i + k) % groups) for i in range(groups)]


def issue_order(groups):
    far, near = range(groups // 2, groups), range(1, groups // 2)
    return [k for pair in itertools.zip_longest(far, near) for k in pair if k is not None]


def pieces_of(routes, groups):
    me = lax.axis_index("exp")
    if paired(groups):
        return routes ^ me
    return (routes - me + groups) % groups


def slots_of(pieces, groups):
    rows = pieces.shape[1]
    number = lax.broadcasted_iota(jnp.int32, (groups, rows), 0)
    hot = [number == pieces[k : k + 1, :] for k in range(2)]
    as_num = [jnp.where(h, 1.0, 0.0).astype(F32) for h in hot]
    before = jnp.where(
        lax.broadcasted_iota(jnp.int32, (rows, rows), 0)
        < lax.broadcasted_iota(jnp.int32, (rows, rows), 1),
        1.0,
        0.0,
    ).astype(BF16)
    count = [dot(n.astype(BF16), before, 1, 0) for n in as_num]
    total = jnp.sum(as_num[0], axis=1, keepdims=True)
    place = [count[0], count[1] + total]
    slot = [
        jnp.sum(jnp.where(h, p, 0.0), axis=0, keepdims=True).astype(jnp.int32)
        for h, p in zip(hot, place)
    ]
    return hot, slot


def dispatch_kernel(groups, pad, routes_hbm, gates_hbm, tok_hbm, cot_hbm, *refs):
    out_refs, pick_ref = refs[:groups], refs[groups]
    routes_ref, gates_ref, tok_ref, cot_ref, sems = refs[groups + 1 :]
    copies = [
        pltpu.make_async_copy(src, dst, sems.at[i])
        for i, (src, dst) in enumerate(
            [
                (routes_hbm, routes_ref),
                (gates_hbm, gates_ref),
                (tok_hbm, tok_ref),
                (cot_hbm, cot_ref),
            ]
        )
    ]
    for copy in copies:
        copy.start()
    copies[0].wait()
    copies[1].wait()
    pieces = pieces_of(routes_ref[...], groups)
    gates = gates_ref[...].astype(F32)
    _, slot = slots_of(pieces, groups)
    index = lax.broadcasted_iota(jnp.int32, (groups * pad, pieces.shape[1]), 0)
    pick = [index == pieces[k : k + 1, :] * pad + slot[k] for k in range(2)]
    plain = jnp.where(pick[0] | pick[1], 1.0, 0.0).astype(BF16)
    scaled = (
        jnp.where(pick[0], gates[0:1, :], 0.0) + jnp.where(pick[1], gates[1:2, :], 0.0)
    ).astype(BF16)
    pick_ref[...] = plain
    copies[2].wait()
    copies[3].wait()
    rows = dot(plain, tok_ref[...], 1, 0).astype(BF16)
    grads = dot(scaled, cot_ref[...], 1, 0).astype(BF16)
    for k, out_ref in enumerate(out_refs):
        out_ref[0:pad, :] = rows[k * pad : (k + 1) * pad, :]
        out_ref[pad:, :] = grads[k * pad : (k + 1) * pad, :]


def own_kernel(cap, groups, block, early, *refs):
    piece_refs, refs = refs[early : early + groups], refs[early + groups :]
    up_hbm, down_hbm = refs[:2]
    out_refs, refs = refs[2 : 2 + groups], refs[2 + groups :]
    rows_ref, grads_ref, up_ref, down_ref, grad_acc, gate_acc, sems = refs
    steps = up_ref.shape[0] // block
    slots, feat = rows_ref.shape
    pad = slots // groups
    copies = []
    for step in range(steps):
        part = pl.ds(step * block, block)
        for i, (src, dst) in enumerate([(up_hbm, up_ref), (down_hbm, down_ref)]):
            copies.append(
                pltpu.make_async_copy(src.at[0, part, :], dst.at[part, :], sems.at[2 * step + i])
            )
            copies[-1].start()
    for k, piece_ref in enumerate(piece_refs):
        rows_ref[k * pad : (k + 1) * pad, :] = piece_ref[0:pad, :]
        grads_ref[k * pad : (k + 1) * pad, :] = piece_ref[pad:, :]
    for step in range(steps):
        part = pl.ds(step * block, block)
        copies[2 * step].wait()
        up = up_ref[part, :]
        active, slope = silu_parts(dot(rows_ref[...], up, 1, 1))
        copies[2 * step + 1].wait()
        back = dot(grads_ref[...], down_ref[part, :], 1, 1)
        hid_grad = (back * slope).astype(BF16)
        gate = active.astype(BF16).astype(F32) * back
        gate = sum(gate[:, i : i + 128] for i in range(0, block, 128))
        in_grad = dot(hid_grad, up, 1, 0)
        if step == 0:
            grad_acc[...] = in_grad
            gate_acc[...] = gate
        else:
            grad_acc[...] += in_grad
            gate_acc[...] += gate
    gate = jnp.sum(gate_acc[...], axis=1, keepdims=True)
    spot = lax.broadcasted_iota(jnp.int32, (slots, 128), 0) % pad
    lane = lax.broadcasted_iota(jnp.int32, (slots, 128), 1)
    gate = jnp.where(spot == lane, gate, 0.0).reshape(groups, pad, 128)
    gate = jnp.sum(gate, axis=1, keepdims=True)
    line = lax.broadcasted_iota(jnp.int32, (pad, 128), 0)
    for k, out_ref in enumerate(out_refs):
        here = slice(k * pad, (k + 1) * pad)
        out_ref[:, 0:128] = jnp.where(line == cap, gate[k], grad_acc[here, 0:128]).astype(BF16)
        out_ref[:, 128:] = grad_acc[here, 128:].astype(BF16)


def weight_parts(block, share, rows_ref, grads_ref, up_ref, down_ref, store):
    for step in range(share // block):
        here = pl.ds(step * block, block)
        active, slope = silu_parts(dot(up_ref[here, :], rows_ref[...], 1, 1))
        back = dot(down_ref[here, :], grads_ref[...], 1, 1)
        hid_grad = (back * slope).astype(BF16)
        up_part = dot(hid_grad, rows_ref[...], 1, 0)
        down_part = dot(active.astype(BF16), grads_ref[...], 1, 0)
        store(here, up_part, down_part)


def own_weights_kernel(block, share, rows_ref, grads_ref, up_hbm, down_hbm, *refs):
    up_out, down_out, up_acc, down_acc, up_ref, down_ref, sems = refs
    base = pl.multiple_of(lax.axis_index("rep") * share, share)
    copies = [
        pltpu.make_async_copy(src.at[0, pl.ds(base, share), :], dst, sems.at[i])
        for i, (src, dst) in enumerate([(up_hbm, up_ref), (down_hbm, down_ref)])
    ]
    for copy in copies:
        copy.start()
    for copy in copies:
        copy.wait()
    up_out[...] = up_ref[...]
    down_out[...] = down_ref[...]

    def store(here, up_part, down_part):
        up_acc[here, :] = up_part
        down_acc[here, :] = down_part

    weight_parts(block, share, rows_ref, grads_ref, up_ref, down_ref, store)


def other_weights_kernel(block, share, groups, mirrors, *refs):
    pieces, refs = refs[:-8], refs[-8:]
    up_ref, down_ref, up_acc, down_acc, grad_up_ref, grad_down_ref, rows_ref, grads_ref = refs
    pad = rows_ref.shape[0] // groups
    each = len(pieces) // (mirrors - 1)
    batch = groups // each
    for mirror in range(mirrors - 1):
        for k in range(groups):
            piece = pieces[mirror * each + k // batch]
            at = k % batch * 2 * pad
            here = slice(k * pad, (k + 1) * pad)
            rows_ref[here, :] = piece[at : at + pad, :]
            grads_ref[here, :] = piece[at + pad : at + 2 * pad, :]

        def store(here, up_part, down_part):
            up_part += up_acc[here, :]
            down_part += down_acc[here, :]
            if mirror == mirrors - 2:
                grad_up_ref[0, here, :] = up_part.astype(BF16)
                grad_down_ref[0, here, :] = down_part.astype(BF16)
            else:
                up_acc[here, :] = up_part
                down_acc[here, :] = down_part

        weight_parts(block, share, rows_ref, grads_ref, up_ref, down_ref, store)


def combine_kernel(cap, routes_ref, gates_ref, pick_ref, *refs):
    back_refs, d_tok_ref, d_gate_ref, back_ref = refs[:-3], refs[-3], refs[-2], refs[-1]
    groups = len(back_refs)
    pad = back_refs[0].shape[0]
    for k, ref in enumerate(back_refs):
        back_ref[k * pad : (k + 1) * pad, :] = ref[...]
    d_tok_ref[...] = dot(pick_ref[...], back_ref[...], 0, 0).astype(BF16)
    pieces = pieces_of(routes_ref[...], groups)
    gates = gates_ref[...].astype(F32)
    hot, slot = slots_of(pieces, groups)
    lane = lax.broadcasted_iota(jnp.int32, (128, pieces.shape[1]), 0)
    values = jnp.concatenate([ref[cap : cap + 1, 0:128].astype(F32) for ref in back_refs], axis=0)
    for k in range(2):
        spot = jnp.where(lane == slot[k], 1.0, 0.0).astype(BF16)
        found = jnp.where(hot[k], dot(values.astype(BF16), spot, 1, 0), 0.0)
        found = jnp.sum(found, axis=0, keepdims=True)
        d_gate_ref[k : k + 1, :] = (found / gates[k : k + 1, :]).astype(BF16)


def local(tokens, gates, routes, cotangent, w_up, w_down):
    rows, feat = tokens.shape
    hidden = w_up.shape[1]
    groups = lax.axis_size("exp")
    mirrors = lax.axis_size("rep")
    cap = max(2, 3 * rows // groups)
    pad = (cap // 16 + 1) * 16
    slots = groups * pad
    share = hidden // mirrors
    routes_t, gates_t = routes.T, gates.T
    far = functools.partial(pltpu.with_memory_space_constraint, memory_space=pltpu.HBM)
    shape = jax.ShapeDtypeStruct
    unit = 2 * slots * feat

    *out, pick = call(
        functools.partial(dispatch_kernel, groups, pad),
        "dispatch",
        [shape((2 * pad, feat), BF16)] * groups + [shape((slots, rows), BF16)],
        [far(routes_t), far(gates_t), far(tokens), far(cotangent)],
        [IN_HBM] * 4,
        [
            pltpu.VMEM((2, rows), jnp.int32),
            pltpu.VMEM((2, rows), BF16),
            pltpu.VMEM((rows, feat), BF16),
            pltpu.VMEM((rows, feat), BF16),
            DMA((4,)),
        ],
        2 * unit * rows,
    )
    order = issue_order(groups)
    pieces = {0: out[0]}
    for k in order:
        pieces[k] = lax.ppermute(out[k], "exp", hops_to(groups, k))

    pieces = list(pieces.values())
    batch = max(1, groups // 4)
    others = []
    for shift in range(1, mirrors):
        hops = [(i, (i + shift) % mirrors) for i in range(mirrors)]
        for k in range(0, groups, batch):
            group = jnp.concatenate(pieces[k : k + batch], axis=0)
            others.append(lax.ppermute(group, "rep", hops))

    block = min(512, hidden)
    early = others[:3]
    *back, rows_in, grads_in = pl.pallas_call(
        functools.partial(own_kernel, cap, groups, block, len(early)),
        name="own_mirror",
        out_shape=[shape((pad, feat), BF16)] * groups + [shape((slots, feat), BF16)] * 2,
        in_specs=[pl.BlockSpec(memory_space=pl.ANY)] * len(early) + [IN_VMEM] * groups + [IN_HBM] * 2,
        out_specs=[IN_VMEM] * (groups + 2),
        scratch_shapes=[
            pltpu.VMEM((hidden, feat), BF16),
            pltpu.VMEM((hidden, feat), BF16),
            pltpu.VMEM((slots, feat), F32),
            pltpu.VMEM((slots, 128), F32),
            DMA((2 * hidden // block,)),
        ],
        compiler_params=pltpu.CompilerParams(vmem_limit_bytes=VMEM_LIMIT),
        cost_estimate=pl.CostEstimate(
            flops=3 * unit * hidden,
            bytes_accessed=4 * hidden * feat + 6 * slots * feat,
            transcendentals=slots * hidden,
        ),
    )(*early, *pieces, far(w_up), far(w_down))
    returned = {0: back[0]}
    for number, k in enumerate(order):
        hops = [(j, i) for i, j in hops_to(groups, k)]
        returned[k] = lax.ppermute(back[number + 1], "exp", hops)
    back = [returned[k] for k in range(groups)]

    part = min(512, share)
    weight = shape((share, feat), BF16)
    total = shape((share, feat), F32)
    up_own, down_own, up_sum, down_sum = call(
        functools.partial(own_weights_kernel, part, share),
        "own_weights",
        [weight, weight, total, total],
        [rows_in, grads_in, far(w_up), far(w_down)],
        [IN_VMEM] * 2 + [IN_HBM] * 2,
        [pltpu.VMEM((share, feat), BF16)] * 2 + [DMA((2,))],
        4 * unit * share,
        slots * share,
    )
    if mirrors == 1:
        grad_up, grad_down = up_sum.astype(BF16)[None], down_sum.astype(BF16)[None]
    else:
        grad_up, grad_down = call(
            functools.partial(other_weights_kernel, part, share, groups, mirrors),
            "other_weights",
            [shape((1, share, feat), BF16)] * 2,
            [*others, up_own, down_own, up_sum, down_sum],
            [IN_VMEM] * (len(others) + 4),
            [pltpu.VMEM((slots, feat), BF16)] * 2,
            4 * unit * share * (mirrors - 1),
            slots * share,
        )

    d_tokens, d_gates = call(
        functools.partial(combine_kernel, cap),
        "combine",
        [shape((rows, feat), BF16), shape((2, rows), BF16)],
        [routes_t, gates_t, pick, *back],
        [IN_VMEM] * (3 + groups),
        [pltpu.VMEM((slots, feat), BF16)],
        unit * rows,
    )
    return d_tokens, d_gates.T, grad_up, grad_down


def solution(mesh):
    by_both = P(("rep", "exp"), None)
    by_expert = P("exp", None, None)
    return jax.shard_map(
        local,
        mesh=mesh,
        in_specs=(by_both, by_both, by_both, by_both, by_expert, by_expert),
        out_specs=(by_both, by_both, P("exp", "rep", None), P("exp", "rep", None)),
        check_vma=False,
    )
```

time: 82.2 us -> 78.9 us (0.960)
  starting transfers between devices: 7.08 us -> 48.7 us
  blocking collectives: 32 us -> 0 us
  waiting for transfers between devices: 23.5 us -> 12.5 us
  local copies, waits for them, and re-layouts: 6.46 us -> 0.01 us
  Pallas kernels: 12 us -> 16.7 us
    ppermute x2 -> x34, starting transfers between devices: 2.09 us -> 48.7 us  [the longest x15 23.9 us: local(): pieces[k] = lax.ppermute(out[k], 'exp', hops_to(groups, k))]
    all_to_all x1 -> x0, blocking collectives: 32 us -> none  [local(): disp = lax.all_to_all(out, 'exp', split_axis=0, concat_axis=0, tiled=True)]
    ppermute x2 -> x34, waiting for transfers between devices: 23.5 us -> 12.5 us  [the longest x15 12.4 us: local(): pieces[k] = lax.ppermute(out[k], 'exp', hops_to(groups, k))]
    unnamed x20 -> x4, local copies, waits for them, and re-layouts: 6.39 us -> 0.01 us
    all_to_all x1 -> x0, starting transfers between devices: 4.99 us -> none  [local(): back = lax.all_to_all(back, 'exp', split_axis=0, concat_axis=0, tiled=True)]
    pallas_call x4 -> x5, Pallas kernels: 12 us -> 16.7 us  [the longest x4 10.3 us: call(): pl.pallas_call(body, name=name, out_shape=outs, in_specs=in_specs, out_sp...]
  transfers between devices with their start and end apart: 3 -> 34, of which waited for: 2 -> 5; matrix products, arithmetic and copies ran while one was open for 0% -> 0% of each run, Pallas kernels for 7% -> 18%
where the time goes in v2:
time: 78.9 us; the launch traced here: 78.7 us
  starting transfers between devices  48.7 us (62%)
  Pallas kernels  16.7 us (21%)
  waiting for transfers between devices  12.5 us (16%)
    ppermute x15, starting transfers between devices, local(): pieces[k] = lax.ppermute(out[k], 'exp', hops_to(groups, k))  23.9 us
    ppermute x15, starting transfers between devices, local(): returned[k] = lax.ppermute(back[number + 1], 'exp', hops)  20.6 us
    ppermute x15, waiting for transfers between devices, local(): pieces[k] = lax.ppermute(out[k], 'exp', hops_to(groups, k))  12.4 us
    pallas_call x4, Pallas kernels, call(): pl.pallas_call(body, name=name, out_shape=outs, in_specs=in_specs, out_sp...  10.3 us
    pallas_call x1, Pallas kernels, local(): pl.pallas_call(functools.partial(own_kernel, cap, groups, block, len(earl...  6.39 us
    ppermute x4, starting transfers between devices, local(): others.append(lax.ppermute(group, 'rep', hops))  4.22 us
  transfers between devices with their start and end apart: 34, of which 5 were waited for; matrix products, arithmetic and copies ran while one was open for 0% of the time, Pallas kernels for 18%

profile of v2, /device:TPU:0, one launch (start us, length us, event | category | flops | bytes accessed | tf_op | source)
XLA Modules:
  0.0 78.7 jit_solution(7951709916950162123)
XLA Ops:
  0.6 1.7 %dispatch.1 = (bf16[64,512]{1,0:T(8,128)(2,1)S(1)}, bf16[64,512]{1,0:T(8,128)(2,1)S(1)}, bf16[64,512]{1,0:T(8,128)(2,1)S(1)}, bf16[64,512]{1,0:T(8,128)(2,1)S(1)...) custom-call(s32[2,160]{1,0:T(2,128)} %bitcast.3, ...), custom_call_target="tpu_custom_call" | custom-call | flops 167772160 | bytes 1542016 | tf_op jit(solution)/shard_map/dispatch/pallas_call | solution.py:33
  2.3 4.1 %collective-permute-start = (bf16[64,512]{1,0:T(8,128)(2,1)S(1)}, bf16[64,512]{1,0:T(8,128)(2,1)S(1)}, u32[]{:S(2)}, u32[]{:S(2)}) collective-permute-start(bf16[64,512]{1,0:T(8,128)(2,1)S(1)} %get-tuple-element.49), channel_id=1, source_target_pairs={{0,8},{1,9},{2,10},{3,11},{4,12},{5,13},{6,14},{7,15},{8,0},{9,1},... | collective-permute-start | bytes 196616 | tf_op jit(solution)/shard_map/ppermute | solution.py:285
  6.4 0.0 collective-permute-start.1
  6.4 0.2 collective-permute-start.2
  6.6 1.8 %collective-permute-start.4 = (bf16[64,512]{1,0:T(8,128)(2,1)S(1)}, bf16[64,512]{1,0:T(8,128)(2,1)S(1)}, u32[]{:S(2)}, u32[]{:S(2)}) collective-permute-start(bf16[64,512]{1,0:T(8,128)(2,1)S(1)} %get-tuple-element.52), channel_id=1, source_target_pairs={{0,2},{1,3},{2,0},{3,1},{4,6},{5,7},{6,4},{7,5},{8,10},{9,11},{10,... | collective-permute-start | bytes 196616 | tf_op jit(solution)/shard_map/ppermute | solution.py:285
  8.4 2.5 %collective-permute-start.5 = (bf16[64,512]{1,0:T(8,128)(2,1)S(1)}, bf16[64,512]{1,0:T(8,128)(2,1)S(1)}, u32[]{:S(2)}, u32[]{:S(2)}) collective-permute-start(bf16[64,512]{1,0:T(8,128)(2,1)S(1)} %get-tuple-element.53), channel_id=1, source_target_pairs={{0,10},{1,11},{2,8},{3,9},{4,14},{5,15},{6,12},{7,13},{8,2},{9,3},... | collective-permute-start | bytes 196616 | tf_op jit(solution)/shard_map/ppermute | solution.py:285
  10.9 0.0 collective-permute-done.refs_4_
  10.9 0.6 collective-permute-start.6
  11.5 0.0 collective-permute-done.1.refs_5_
  11.5 1.8 %collective-permute-start.7 = (bf16[64,512]{1,0:T(8,128)(2,1)S(1)}, bf16[64,512]{1,0:T(8,128)(2,1)S(1)}, u32[]{:S(2)}, u32[]{:S(2)}) collective-permute-start(bf16[64,512]{1,0:T(8,128)(2,1)S(1)} %get-tuple-element.55), channel_id=1, source_target_pairs={{0,11},{1,10},{2,9},{3,8},{4,15},{5,14},{6,13},{7,12},{8,3},{9,2},... | collective-permute-start | bytes 196616 | tf_op jit(solution)/shard_map/ppermute | solution.py:285
  13.3 0.0 collective-permute-done.2.refs_6_
  13.3 3.6 %collective-permute-start.9 = (bf16[64,512]{1,0:T(8,128)(2,1)S(1)}, bf16[64,512]{1,0:T(8,128)(2,1)S(1)}, u32[]{:S(2)}, u32[]{:S(2)}) collective-permute-start(bf16[64,512]{1,0:T(8,128)(2,1)S(1)} %get-tuple-element.56), channel_id=1, source_target_pairs={{0,4},{1,5},{2,6},{3,7},{4,0},{5,1},{6,2},{7,3},{8,12},{9,13},{10,... | collective-permute-start | bytes 196616 | tf_op jit(solution)/shard_map/ppermute | solution.py:285
  16.9 0.0 collective-permute-done.4.refs_7_
  16.9 0.6 collective-permute-start.10
  17.5 0.0 collective-permute-done.5.refs_8_
  17.5 0.5 collective-permute-start.11
  18.0 0.0 collective-permute-done.6.refs_9_
  18.0 2.9 %collective-permute-start.12 = (bf16[64,512]{1,0:T(8,128)(2,1)S(1)}, bf16[64,512]{1,0:T(8,128)(2,1)S(1)}, u32[]{:S(2)}, u32[]{:S(2)}) collective-permute-start(bf16[64,512]{1,0:T(8,128)(2,1)S(1)} %get-tuple-element.59), channel_id=1, source_target_pairs={{0,13},{1,12},{2,15},{3,14},{4,9},{5,8},{6,11},{7,10},{8,5},{9,4},... | collective-permute-start | bytes 196616 | tf_op jit(solution)/shard_map/ppermute | solution.py:285
  20.9 0.0 collective-permute-done.7.refs_10_
  20.9 1.5 %collective-permute-start.3 = (bf16[256,512]{1,0:T(8,128)(2,1)S(1)}, bf16[256,512]{1,0:T(8,128)(2,1)S(1)}, u32[]{:S(2)}, u32[]{:S(2)}) collective-permute-start(bf16[256,512]{1,0:T(8,128)(2,1)S(1)} %pad_maximum_fusion), channel_id=1, source_target_pairs={{0,16},{16,0},{1,17},{17,1},{2,18},{18,2},{3,19},{19,3},{4,20},{20... | collective-permute-start | bytes 786440 | tf_op jit(solution)/shard_map/ppermute | solution.py:294
  22.4 0.0 collective-permute-done.9.refs_11_
  22.4 0.6 collective-permute-start.8
  23.0 0.8 %collective-permute-done.10.refs_12_ = bf16[64,512]{1,0:T(8,128)(2,1)S(1)} collective-permute-done((bf16[64,512]{1,0:T(8,128)(2,1)S(1)}, bf16[64,512]{1,0:T(8,128)(2,1)S(1)}, u32[]{:S(2)}, u32[]{:S(2)}) %collective-permute-start.10) | collective-permute-done | bytes 65568 | tf_op jit(solution)/shard_map/ppermute | solution.py:285
  23.8 0.0 collective-permute-done.11.refs_13_
  23.8 0.9 %collective-permute-done.12.refs_14_ = bf16[64,512]{1,0:T(8,128)(2,1)S(1)} collective-permute-done((bf16[64,512]{1,0:T(8,128)(2,1)S(1)}, bf16[64,512]{1,0:T(8,128)(2,1)S(1)}, u32[]{:S(2)}, u32[]{:S(2)}) %collective-permute-start.12) | collective-permute-done | bytes 65568 | tf_op jit(solution)/shard_map/ppermute | solution.py:285
  24.7 1.5 %collective-permute-start.13 = (bf16[256,512]{1,0:T(8,128)(2,1)S(1)}, bf16[256,512]{1,0:T(8,128)(2,1)S(1)}, u32[]{:S(2)}, u32[]{:S(2)}) collective-permute-start(bf16[256,512]{1,0:T(8,128)(2,1)S(1)} %pad_maximum_fusion.2), channel_id=1, source_target_pairs={{0,16},{16,0},{1,17},{17,1},{2,18},{18,2},{3,19},{19,3},{4,20},{20... | collective-permute-start | bytes 786440 | tf_op jit(solution)/shard_map/ppermute | solution.py:294
  26.3 2.7 %collective-permute-start.14 = (bf16[64,512]{1,0:T(8,128)(2,1)S(1)}, bf16[64,512]{1,0:T(8,128)(2,1)S(1)}, u32[]{:S(2)}, u32[]{:S(2)}) collective-permute-start(bf16[64,512]{1,0:T(8,128)(2,1)S(1)} %get-tuple-element.60), channel_id=1, source_target_pairs={{0,6},{1,7},{2,4},{3,5},{4,2},{5,3},{6,0},{7,1},{8,14},{9,15},{10,... | collective-permute-start | bytes 196616 | tf_op jit(solution)/shard_map/ppermute | solution.py:285
  28.9 0.8 %collective-permute-start.15 = (bf16[64,512]{1,0:T(8,128)(2,1)S(1)}, bf16[64,512]{1,0:T(8,128)(2,1)S(1)}, u32[]{:S(2)}, u32[]{:S(2)}) collective-permute-start(bf16[64,512]{1,0:T(8,128)(2,1)S(1)} %get-tuple-element.61), channel_id=1, source_target_pairs={{0,14},{1,15},{2,12},{3,13},{4,10},{5,11},{6,8},{7,9},{8,6},{9,7},... | collective-permute-start | bytes 196616 | tf_op jit(solution)/shard_map/ppermute | solution.py:285
  29.8 1.9 %collective-permute-done.14.refs_15_ = bf16[64,512]{1,0:T(8,128)(2,1)S(1)} collective-permute-done((bf16[64,512]{1,0:T(8,128)(2,1)S(1)}, bf16[64,512]{1,0:T(8,128)(2,1)S(1)}, u32[]{:S(2)}, u32[]{:S(2)}) %collective-permute-start.14) | collective-permute-done | bytes 65568 | tf_op jit(solution)/shard_map/ppermute | solution.py:285
  31.7 0.9 %collective-permute-start.16 = (bf16[64,512]{1,0:T(8,128)(2,1)S(1)}, bf16[64,512]{1,0:T(8,128)(2,1)S(1)}, u32[]{:S(2)}, u32[]{:S(2)}) collective-permute-start(bf16[64,512]{1,0:T(8,128)(2,1)S(1)} %get-tuple-element.62), channel_id=1, source_target_pairs={{0,7},{1,6},{2,5},{3,4},{4,3},{5,2},{6,1},{7,0},{8,15},{9,14},{10,... | collective-permute-start | bytes 196616 | tf_op jit(solution)/shard_map/ppermute | solution.py:285
  32.5 3.4 %collective-permute-done.15.refs_16_ = bf16[64,512]{1,0:T(8,128)(2,1)S(1)} collective-permute-done((bf16[64,512]{1,0:T(8,128)(2,1)S(1)}, bf16[64,512]{1,0:T(8,128)(2,1)S(1)}, u32[]{:S(2)}, u32[]{:S(2)}) %collective-permute-start.15) | collective-permute-done | bytes 65568 | tf_op jit(solution)/shard_map/ppermute | solution.py:285
  35.9 1.0 %collective-permute-start.17 = (bf16[64,512]{1,0:T(8,128)(2,1)S(1)}, bf16[64,512]{1,0:T(8,128)(2,1)S(1)}, u32[]{:S(2)}, u32[]{:S(2)}) collective-permute-start(bf16[64,512]{1,0:T(8,128)(2,1)S(1)} %get-tuple-element.63), channel_id=1, source_target_pairs={{0,15},{1,14},{2,13},{3,12},{4,11},{5,10},{6,9},{7,8},{8,7},{9,6},... | collective-permute-start | bytes 196616 | tf_op jit(solution)/shard_map/ppermute | solution.py:285
  37.0 0.0 collective-permute-done.16.refs_17_
  37.0 5.3 %collective-permute-done.17.refs_18_ = bf16[64,512]{1,0:T(8,128)(2,1)S(1)} collective-permute-done((bf16[64,512]{1,0:T(8,128)(2,1)S(1)}, bf16[64,512]{1,0:T(8,128)(2,1)S(1)}, u32[]{:S(2)}, u32[]{:S(2)}) %collective-permute-start.17) | collective-permute-done | bytes 65568 | tf_op jit(solution)/shard_map/ppermute | solution.py:285
  42.4 0.6 collective-permute-start.33
  42.9 0.0 collective-permute-done.3.refs_0_
  43.0 6.4 %own_mirror.1 = (bf16[32,512]{1,0:T(8,128)(2,1)S(1)}, bf16[32,512]{1,0:T(8,128)(2,1)S(1)}, bf16[32,512]{1,0:T(8,128)(2,1)S(1)}, bf16[32,512]{1,0:T(8,128)(2,1)S(...) custom-call(bf16[256,512]{1,0:T(8,128)(2,1)S(1)} %collective-permute, ...), custom_call_target="tpu_custom_call" | custom-call | flops 3221225472 | bytes 5767168 | tf_op jit(solution)/shard_map/own_mirror/pallas_call | solution.py:298
  49.4 0.1 collective-permute-start.18
  49.4 0.8 %collective-permute-start.19 = (bf16[32,512]{1,0:T(8,128)(2,1)S(1)}, bf16[32,512]{1,0:T(8,128)(2,1)S(1)}, u32[]{:S(2)}, u32[]{:S(2)}) collective-permute-start(bf16[32,512]{1,0:T(8,128)(2,1)S(1)} %get-tuple-element.66), channel_id=1, source_target_pairs={{2,0},{3,1},{0,2},{1,3},{6,4},{7,5},{4,6},{5,7},{10,8},{11,9},{8,1... | collective-permute-start | bytes 98312 | tf_op jit(solution)/shard_map/ppermute | solution.py:321
  50.3 1.0 %collective-permute-start.20 = (bf16[32,512]{1,0:T(8,128)(2,1)S(1)}, bf16[32,512]{1,0:T(8,128)(2,1)S(1)}, u32[]{:S(2)}, u32[]{:S(2)}) collective-permute-start(bf16[32,512]{1,0:T(8,128)(2,1)S(1)} %get-tuple-element.67), channel_id=1, source_target_pairs={{3,0},{2,1},{1,2},{0,3},{7,4},{6,5},{5,6},{4,7},{11,8},{10,9},{9,1... | collective-permute-start | bytes 98312 | tf_op jit(solution)/shard_map/ppermute | solution.py:321
  51.3 0.0 collective-permute-start.21
  51.3 0.0 collective-permute-done.33.refs_3_
  51.3 1.7 %collective-permute-start.22 = (bf16[32,512]{1,0:T(8,128)(2,1)S(1)}, bf16[32,512]{1,0:T(8,128)(2,1)S(1)}, u32[]{:S(2)}, u32[]{:S(2)}) collective-permute-start(bf16[32,512]{1,0:T(8,128)(2,1)S(1)} %get-tuple-element.69), channel_id=1, source_target_pairs={{5,0},{4,1},{7,2},{6,3},{1,4},{0,5},{3,6},{2,7},{13,8},{12,9},{15,... | collective-permute-start | bytes 98312 | tf_op jit(solution)/shard_map/ppermute | solution.py:321
  53.0 0.0 collective-permute-done.18.refs_1_
  53.0 0.6 collective-permute-start.23
  53.6 0.0 collective-permute-done.19.refs_2_
  53.6 2.1 %collective-permute-start.24 = (bf16[32,512]{1,0:T(8,128)(2,1)S(1)}, bf16[32,512]{1,0:T(8,128)(2,1)S(1)}, u32[]{:S(2)}, u32[]{:S(2)}) collective-permute-start(bf16[32,512]{1,0:T(8,128)(2,1)S(1)} %get-tuple-element.71), channel_id=1, source_target_pairs={{7,0},{6,1},{5,2},{4,3},{3,4},{2,5},{1,6},{0,7},{15,8},{14,9},{13,... | collective-permute-start | bytes 98312 | tf_op jit(solution)/shard_map/ppermute | solution.py:321
  55.7 0.4 collective-permute-start.25
  56.1 0.0 collective-permute-done.21.refs_4_
  56.1 2.2 %collective-permute-start.26 = (bf16[32,512]{1,0:T(8,128)(2,1)S(1)}, bf16[32,512]{1,0:T(8,128)(2,1)S(1)}, u32[]{:S(2)}, u32[]{:S(2)}) collective-permute-start(bf16[32,512]{1,0:T(8,128)(2,1)S(1)} %get-tuple-element.73), channel_id=1, source_target_pairs={{9,0},{8,1},{11,2},{10,3},{13,4},{12,5},{15,6},{14,7},{1,8},{0,9},... | collective-permute-start | bytes 98312 | tf_op jit(solution)/shard_map/ppermute | solution.py:321
  58.3 1.1 %collective-permute-start.27 = (bf16[32,512]{1,0:T(8,128)(2,1)S(1)}, bf16[32,512]{1,0:T(8,128)(2,1)S(1)}, u32[]{:S(2)}, u32[]{:S(2)}) collective-permute-start(bf16[32,512]{1,0:T(8,128)(2,1)S(1)} %get-tuple-element.74), channel_id=1, source_target_pairs={{10,0},{11,1},{8,2},{9,3},{14,4},{15,5},{12,6},{13,7},{2,8},{3,9},... | collective-permute-start | bytes 98312 | tf_op jit(solution)/shard_map/ppermute | solution.py:321
  59.4 4.1 %own_weights.1 = (bf16[1024,512]{1,0:T(8,128)(2,1)S(1)}, bf16[1024,512]{1,0:T(8,128)(2,1)S(1)}, f32[1024,512]{1,0:T(8,128)S(1)}, f32[1024,512]{1,0:T(8,128)S(1)}) custom-call(bf16[512,512]{1,0:T(8,128)(2,1)S(1)} %get-tuple-element.82.rows_ref, bf16[512,512]{1,0:T(8,128)(2,1)S(1)} %get-tuple-element.83.grads_ref, bf16[1,2048,512]{2,1,0:T(8,128)(2,1)} %up_hbm.1, ...), custom_call_target="tpu_custom_call" | custom-call | flops 2147483648 | bytes 11534336 | tf_op jit(solution)/shard_map/own_weights/pallas_call | solution.py:33
  63.6 2.6 %collective-permute-start.28 = (bf16[32,512]{1,0:T(8,128)(2,1)S(1)}, bf16[32,512]{1,0:T(8,128)(2,1)S(1)}, u32[]{:S(2)}, u32[]{:S(2)}) collective-permute-start(bf16[32,512]{1,0:T(8,128)(2,1)S(1)} %get-tuple-element.75), channel_id=1, source_target_pairs={{11,0},{10,1},{9,2},{8,3},{15,4},{14,5},{13,6},{12,7},{3,8},{2,9},... | collective-permute-start | bytes 98312 | tf_op jit(solution)/shard_map/ppermute | solution.py:321
  66.1 1.8 %collective-permute-start.29 = (bf16[32,512]{1,0:T(8,128)(2,1)S(1)}, bf16[32,512]{1,0:T(8,128)(2,1)S(1)}, u32[]{:S(2)}, u32[]{:S(2)}) collective-permute-start(bf16[32,512]{1,0:T(8,128)(2,1)S(1)} %get-tuple-element.76), channel_id=1, source_target_pairs={{12,0},{13,1},{14,2},{15,3},{8,4},{9,5},{10,6},{11,7},{4,8},{5,9},... | collective-permute-start | bytes 98312 | tf_op jit(solution)/shard_map/ppermute | solution.py:321
  67.9 0.0 collective-permute-done.25.refs_8_
  67.9 1.7 %collective-permute-start.30 = (bf16[32,512]{1,0:T(8,128)(2,1)S(1)}, bf16[32,512]{1,0:T(8,128)(2,1)S(1)}, u32[]{:S(2)}, u32[]{:S(2)}) collective-permute-start(bf16[32,512]{1,0:T(8,128)(2,1)S(1)} %get-tuple-element.77), channel_id=1, source_target_pairs={{13,0},{12,1},{15,2},{14,3},{9,4},{8,5},{11,6},{10,7},{5,8},{4,9},... | collective-permute-start | bytes 98312 | tf_op jit(solution)/shard_map/ppermute | solution.py:321
  69.6 0.0 collective-permute-done.26.refs_9_
  69.6 1.8 %collective-permute-start.31 = (bf16[32,512]{1,0:T(8,128)(2,1)S(1)}, bf16[32,512]{1,0:T(8,128)(2,1)S(1)}, u32[]{:S(2)}, u32[]{:S(2)}) collective-permute-start(bf16[32,512]{1,0:T(8,128)(2,1)S(1)} %get-tuple-element.78), channel_id=1, source_target_pairs={{14,0},{15,1},{12,2},{13,3},{10,4},{11,5},{8,6},{9,7},{6,8},{7,9},... | collective-permute-start | bytes 98312 | tf_op jit(solution)/shard_map/ppermute | solution.py:321
  71.4 2.7 %collective-permute-start.32 = (bf16[32,512]{1,0:T(8,128)(2,1)S(1)}, bf16[32,512]{1,0:T(8,128)(2,1)S(1)}, u32[]{:S(2)}, u32[]{:S(2)}) collective-permute-start(bf16[32,512]{1,0:T(8,128)(2,1)S(1)} %get-tuple-element.79), channel_id=1, source_target_pairs={{15,0},{14,1},{13,2},{12,3},{11,4},{10,5},{9,6},{8,7},{7,8},{6,9},... | collective-permute-start | bytes 98312 | tf_op jit(solution)/shard_map/ppermute | solution.py:321
  74.1 3.5 %other_weights.1 = (bf16[1,1024,512]{2,1,0:T(8,128)(2,1)}, bf16[1,1024,512]{2,1,0:T(8,128)(2,1)}) custom-call(bf16[256,512]{1,0:T(8,128)(2,1)S(1)} %collective-permute-done.3.refs_0_, bf16[256,512]{1,0:T(8,128)(2,1)S(1)} %collective-permute-done.8.refs_1_, bf16[256,512]{1,0:T(8,128)(2,1)S(1)} %collective-permute-done.13.refs_2_, ...), custom_call_target="tpu_custom_call" | custom-call | flops 2147483648 | bytes 9437184 | tf_op jit(solution)/shard_map/other_weights/pallas_call | solution.py:33
  77.6 0.0 collective-permute-done.29.refs_12_
  77.6 0.0 collective-permute-done.30.refs_13_
  77.6 0.0 collective-permute-done.32.refs_15_
  77.7 1.0 %combine.1 = (bf16[160,512]{1,0:T(8,128)(2,1)}, bf16[2,160]{1,0:T(2,128)(2,1)}) custom-call(s32[2,160]{1,0:T(2,128)S(1)} %bitcast.4, bf16[2,160]{1,0:T(2,128)(2,1)S(1)} %bitcast.6, bf16[512,160]{1,0:T(8,128)(2,1)S(1)} %get-tuple-element.47.pick_ref, bf16[32,512]{1,0:T(8,128)(2,1)S(1)} %get-tuple-element.64.refs_0_, ...), custom_call_target="tpu_custom_call" | custom-call | flops 83886080 | bytes 854528 | tf_op jit(solution)/shard_map/combine/pallas_call | solution.py:33
  (17 shorter events, 0.1 us)
Async XLA Ops:
  2.3 8.6 %collective-permute-start = (bf16[64,512]{1,0:T(8,128)(2,1)S(1)}, bf16[64,512]{1,0:T(8,128)(2,1)S(1)}, u32[]{:S(2)}, u32[]{:S(2)}) collective-permute-start(bf16[64,512]{1,0:T(8,128)(2,1)S(1)} %get-tuple-element.49), channel_id=1, source_target_pairs={{0,8},{1,9},{2,10},{3,11},{4,12},{5,13},{6,14},{7,15},{8,0},{9,1},... | collective-permute-start | bytes 196616 | tf_op jit(solution)/shard_map/ppermute | solution.py:285
  6.4 5.1 %collective-permute-start.1 = (bf16[64,512]{1,0:T(8,128)(2,1)S(1)}, bf16[64,512]{1,0:T(8,128)(2,1)S(1)}, u32[]{:S(2)}, u32[]{:S(2)}) collective-permute-start(bf16[64,512]{1,0:T(8,128)(2,1)S(1)} %get-tuple-element.50), channel_id=1, source_target_pairs={{0,1},{1,0},{2,3},{3,2},{4,5},{5,4},{6,7},{7,6},{8,9},{9,8},{10,11... | collective-permute-start | bytes 196616 | tf_op jit(solution)/shard_map/ppermute | solution.py:285
  6.4 6.9 %collective-permute-start.2 = (bf16[64,512]{1,0:T(8,128)(2,1)S(1)}, bf16[64,512]{1,0:T(8,128)(2,1)S(1)}, u32[]{:S(2)}, u32[]{:S(2)}) collective-permute-start(bf16[64,512]{1,0:T(8,128)(2,1)S(1)} %get-tuple-element.51), channel_id=1, source_target_pairs={{0,9},{1,8},{2,11},{3,10},{4,13},{5,12},{6,15},{7,14},{8,1},{9,0},... | collective-permute-start | bytes 196616 | tf_op jit(solution)/shard_map/ppermute | solution.py:285
  6.6 10.3 %collective-permute-start.4 = (bf16[64,512]{1,0:T(8,128)(2,1)S(1)}, bf16[64,512]{1,0:T(8,128)(2,1)S(1)}, u32[]{:S(2)}, u32[]{:S(2)}) collective-permute-start(bf16[64,512]{1,0:T(8,128)(2,1)S(1)} %get-tuple-element.52), channel_id=1, source_target_pairs={{0,2},{1,3},{2,0},{3,1},{4,6},{5,7},{6,4},{7,5},{8,10},{9,11},{10,... | collective-permute-start | bytes 196616 | tf_op jit(solution)/shard_map/ppermute | solution.py:285
  8.4 9.1 %collective-permute-start.5 = (bf16[64,512]{1,0:T(8,128)(2,1)S(1)}, bf16[64,512]{1,0:T(8,128)(2,1)S(1)}, u32[]{:S(2)}, u32[]{:S(2)}) collective-permute-start(bf16[64,512]{1,0:T(8,128)(2,1)S(1)} %get-tuple-element.53), channel_id=1, source_target_pairs={{0,10},{1,11},{2,8},{3,9},{4,14},{5,15},{6,12},{7,13},{8,2},{9,3},... | collective-permute-start | bytes 196616 | tf_op jit(solution)/shard_map/ppermute | solution.py:285
  10.9 7.1 %collective-permute-start.6 = (bf16[64,512]{1,0:T(8,128)(2,1)S(1)}, bf16[64,512]{1,0:T(8,128)(2,1)S(1)}, u32[]{:S(2)}, u32[]{:S(2)}) collective-permute-start(bf16[64,512]{1,0:T(8,128)(2,1)S(1)} %get-tuple-element.54), channel_id=1, source_target_pairs={{0,3},{1,2},{2,1},{3,0},{4,7},{5,6},{6,5},{7,4},{8,11},{9,10},{10,... | collective-permute-start | bytes 196616 | tf_op jit(solution)/shard_map/ppermute | solution.py:285
  11.5 9.4 %collective-permute-start.7 = (bf16[64,512]{1,0:T(8,128)(2,1)S(1)}, bf16[64,512]{1,0:T(8,128)(2,1)S(1)}, u32[]{:S(2)}, u32[]{:S(2)}) collective-permute-start(bf16[64,512]{1,0:T(8,128)(2,1)S(1)} %get-tuple-element.55), channel_id=1, source_target_pairs={{0,11},{1,10},{2,9},{3,8},{4,15},{5,14},{6,13},{7,12},{8,3},{9,2},... | collective-permute-start | bytes 196616 | tf_op jit(solution)/shard_map/ppermute | solution.py:285
  13.3 9.1 %collective-permute-start.9 = (bf16[64,512]{1,0:T(8,128)(2,1)S(1)}, bf16[64,512]{1,0:T(8,128)(2,1)S(1)}, u32[]{:S(2)}, u32[]{:S(2)}) collective-permute-start(bf16[64,512]{1,0:T(8,128)(2,1)S(1)} %get-tuple-element.56), channel_id=1, source_target_pairs={{0,4},{1,5},{2,6},{3,7},{4,0},{5,1},{6,2},{7,3},{8,12},{9,13},{10,... | collective-permute-start | bytes 196616 | tf_op jit(solution)/shard_map/ppermute | solution.py:285
  16.9 6.9 %collective-permute-start.10 = (bf16[64,512]{1,0:T(8,128)(2,1)S(1)}, bf16[64,512]{1,0:T(8,128)(2,1)S(1)}, u32[]{:S(2)}, u32[]{:S(2)}) collective-permute-start(bf16[64,512]{1,0:T(8,128)(2,1)S(1)} %get-tuple-element.57), channel_id=1, source_target_pairs={{0,12},{1,13},{2,14},{3,15},{4,8},{5,9},{6,10},{7,11},{8,4},{9,5},... | collective-permute-start | bytes 196616 | tf_op jit(solution)/shard_map/ppermute | solution.py:285
  17.5 6.3 %collective-permute-start.11 = (bf16[64,512]{1,0:T(8,128)(2,1)S(1)}, bf16[64,512]{1,0:T(8,128)(2,1)S(1)}, u32[]{:S(2)}, u32[]{:S(2)}) collective-permute-start(bf16[64,512]{1,0:T(8,128)(2,1)S(1)} %get-tuple-element.58), channel_id=1, source_target_pairs={{0,5},{1,4},{2,7},{3,6},{4,1},{5,0},{6,3},{7,2},{8,13},{9,12},{10,... | collective-permute-start | bytes 196616 | tf_op jit(solution)/shard_map/ppermute | solution.py:285
  18.0 6.7 %collective-permute-start.12 = (bf16[64,512]{1,0:T(8,128)(2,1)S(1)}, bf16[64,512]{1,0:T(8,128)(2,1)S(1)}, u32[]{:S(2)}, u32[]{:S(2)}) collective-permute-start(bf16[64,512]{1,0:T(8,128)(2,1)S(1)} %get-tuple-element.59), channel_id=1, source_target_pairs={{0,13},{1,12},{2,15},{3,14},{4,9},{5,8},{6,11},{7,10},{8,5},{9,4},... | collective-permute-start | bytes 196616 | tf_op jit(solution)/shard_map/ppermute | solution.py:285
  20.9 22.1 %collective-permute-start.3 = (bf16[256,512]{1,0:T(8,128)(2,1)S(1)}, bf16[256,512]{1,0:T(8,128)(2,1)S(1)}, u32[]{:S(2)}, u32[]{:S(2)}) collective-permute-start(bf16[256,512]{1,0:T(8,128)(2,1)S(1)} %pad_maximum_fusion), channel_id=1, source_target_pairs={{0,16},{16,0},{1,17},{17,1},{2,18},{18,2},{3,19},{19,3},{4,20},{20... | collective-permute-start | bytes 786440 | tf_op jit(solution)/shard_map/ppermute | solution.py:294
  22.4 20.6 %collective-permute-start.8 = (bf16[256,512]{1,0:T(8,128)(2,1)S(1)}, bf16[256,512]{1,0:T(8,128)(2,1)S(1)}, u32[]{:S(2)}, u32[]{:S(2)}) collective-permute-start(bf16[256,512]{1,0:T(8,128)(2,1)S(1)} %pad_maximum_fusion.1), channel_id=1, source_target_pairs={{0,16},{16,0},{1,17},{17,1},{2,18},{18,2},{3,19},{19,3},{4,20},{20... | collective-permute-start | bytes 786440 | tf_op jit(solution)/shard_map/ppermute | solution.py:294
  24.7 18.2 %collective-permute-start.13 = (bf16[256,512]{1,0:T(8,128)(2,1)S(1)}, bf16[256,512]{1,0:T(8,128)(2,1)S(1)}, u32[]{:S(2)}, u32[]{:S(2)}) collective-permute-start(bf16[256,512]{1,0:T(8,128)(2,1)S(1)} %pad_maximum_fusion.2), channel_id=1, source_target_pairs={{0,16},{16,0},{1,17},{17,1},{2,18},{18,2},{3,19},{19,3},{4,20},{20... | collective-permute-start | bytes 786440 | tf_op jit(solution)/shard_map/ppermute | solution.py:294
  26.3 5.4 %collective-permute-start.14 = (bf16[64,512]{1,0:T(8,128)(2,1)S(1)}, bf16[64,512]{1,0:T(8,128)(2,1)S(1)}, u32[]{:S(2)}, u32[]{:S(2)}) collective-permute-start(bf16[64,512]{1,0:T(8,128)(2,1)S(1)} %get-tuple-element.60), channel_id=1, source_target_pairs={{0,6},{1,7},{2,4},{3,5},{4,2},{5,3},{6,0},{7,1},{8,14},{9,15},{10,... | collective-permute-start | bytes 196616 | tf_op jit(solution)/shard_map/ppermute | solution.py:285
  28.9 7.0 %collective-permute-start.15 = (bf16[64,512]{1,0:T(8,128)(2,1)S(1)}, bf16[64,512]{1,0:T(8,128)(2,1)S(1)}, u32[]{:S(2)}, u32[]{:S(2)}) collective-permute-start(bf16[64,512]{1,0:T(8,128)(2,1)S(1)} %get-tuple-element.61), channel_id=1, source_target_pairs={{0,14},{1,15},{2,12},{3,13},{4,10},{5,11},{6,8},{7,9},{8,6},{9,7},... | collective-permute-start | bytes 196616 | tf_op jit(solution)/shard_map/ppermute | solution.py:285
  31.7 5.3 %collective-permute-start.16 = (bf16[64,512]{1,0:T(8,128)(2,1)S(1)}, bf16[64,512]{1,0:T(8,128)(2,1)S(1)}, u32[]{:S(2)}, u32[]{:S(2)}) collective-permute-start(bf16[64,512]{1,0:T(8,128)(2,1)S(1)} %get-tuple-element.62), channel_id=1, source_target_pairs={{0,7},{1,6},{2,5},{3,4},{4,3},{5,2},{6,1},{7,0},{8,15},{9,14},{10,... | collective-permute-start | bytes 196616 | tf_op jit(solution)/shard_map/ppermute | solution.py:285
  35.9 6.4 %collective-permute-start.17 = (bf16[64,512]{1,0:T(8,128)(2,1)S(1)}, bf16[64,512]{1,0:T(8,128)(2,1)S(1)}, u32[]{:S(2)}, u32[]{:S(2)}) collective-permute-start(bf16[64,512]{1,0:T(8,128)(2,1)S(1)} %get-tuple-element.63), channel_id=1, source_target_pairs={{0,15},{1,14},{2,13},{3,12},{4,11},{5,10},{6,9},{7,8},{8,7},{9,6},... | collective-permute-start | bytes 196616 | tf_op jit(solution)/shard_map/ppermute | solution.py:285
  42.4 8.9 %collective-permute-start.33 = (bf16[256,512]{1,0:T(8,128)(2,1)S(1)}, bf16[256,512]{1,0:T(8,128)(2,1)S(1)}, u32[]{:S(2)}, u32[]{:S(2)}) collective-permute-start(bf16[256,512]{1,0:T(8,128)(2,1)S(1)} %pad_maximum_fusion.3), channel_id=1, source_target_pairs={{0,16},{16,0},{1,17},{17,1},{2,18},{18,2},{3,19},{19,3},{4,20},{20... | collective-permute-start | bytes 786440 | tf_op jit(solution)/shard_map/ppermute | solution.py:294
  49.4 3.6 %collective-permute-start.18 = (bf16[32,512]{1,0:T(8,128)(2,1)S(1)}, bf16[32,512]{1,0:T(8,128)(2,1)S(1)}, u32[]{:S(2)}, u32[]{:S(2)}) collective-permute-start(bf16[32,512]{1,0:T(8,128)(2,1)S(1)} %get-tuple-element.65), channel_id=1, source_target_pairs={{1,0},{0,1},{3,2},{2,3},{5,4},{4,5},{7,6},{6,7},{9,8},{8,9},{11,10... | collective-permute-start | bytes 98312 | tf_op jit(solution)/shard_map/ppermute | solution.py:321
  49.4 4.2 %collective-permute-start.19 = (bf16[32,512]{1,0:T(8,128)(2,1)S(1)}, bf16[32,512]{1,0:T(8,128)(2,1)S(1)}, u32[]{:S(2)}, u32[]{:S(2)}) collective-permute-start(bf16[32,512]{1,0:T(8,128)(2,1)S(1)} %get-tuple-element.66), channel_id=1, source_target_pairs={{2,0},{3,1},{0,2},{1,3},{6,4},{7,5},{4,6},{5,7},{10,8},{11,9},{8,1... | collective-permute-start | bytes 98312 | tf_op jit(solution)/shard_map/ppermute | solution.py:321
  50.3 5.4 %collective-permute-start.20 = (bf16[32,512]{1,0:T(8,128)(2,1)S(1)}, bf16[32,512]{1,0:T(8,128)(2,1)S(1)}, u32[]{:S(2)}, u32[]{:S(2)}) collective-permute-start(bf16[32,512]{1,0:T(8,128)(2,1)S(1)} %get-tuple-element.67), channel_id=1, source_target_pairs={{3,0},{2,1},{1,2},{0,3},{7,4},{6,5},{5,6},{4,7},{11,8},{10,9},{9,1... | collective-permute-start | bytes 98312 | tf_op jit(solution)/shard_map/ppermute | solution.py:321
  51.3 4.8 %collective-permute-start.21 = (bf16[32,512]{1,0:T(8,128)(2,1)S(1)}, bf16[32,512]{1,0:T(8,128)(2,1)S(1)}, u32[]{:S(2)}, u32[]{:S(2)}) collective-permute-start(bf16[32,512]{1,0:T(8,128)(2,1)S(1)} %get-tuple-element.68), channel_id=1, source_target_pairs={{4,0},{5,1},{6,2},{7,3},{0,4},{1,5},{2,6},{3,7},{12,8},{13,9},{14,... | collective-permute-start | bytes 98312 | tf_op jit(solution)/shard_map/ppermute | solution.py:321
  51.3 7.0 %collective-permute-start.22 = (bf16[32,512]{1,0:T(8,128)(2,1)S(1)}, bf16[32,512]{1,0:T(8,128)(2,1)S(1)}, u32[]{:S(2)}, u32[]{:S(2)}) collective-permute-start(bf16[32,512]{1,0:T(8,128)(2,1)S(1)} %get-tuple-element.69), channel_id=1, source_target_pairs={{5,0},{4,1},{7,2},{6,3},{1,4},{0,5},{3,6},{2,7},{13,8},{12,9},{15,... | collective-permute-start | bytes 98312 | tf_op jit(solution)/shard_map/ppermute | solution.py:321
  53.0 10.5 %collective-permute-start.23 = (bf16[32,512]{1,0:T(8,128)(2,1)S(1)}, bf16[32,512]{1,0:T(8,128)(2,1)S(1)}, u32[]{:S(2)}, u32[]{:S(2)}) collective-permute-start(bf16[32,512]{1,0:T(8,128)(2,1)S(1)} %get-tuple-element.70), channel_id=1, source_target_pairs={{6,0},{7,1},{4,2},{5,3},{2,4},{3,5},{0,6},{1,7},{14,8},{15,9},{12,... | collective-permute-start | bytes 98312 | tf_op jit(solution)/shard_map/ppermute | solution.py:321
  53.6 12.5 %collective-permute-start.24 = (bf16[32,512]{1,0:T(8,128)(2,1)S(1)}, bf16[32,512]{1,0:T(8,128)(2,1)S(1)}, u32[]{:S(2)}, u32[]{:S(2)}) collective-permute-start(bf16[32,512]{1,0:T(8,128)(2,1)S(1)} %get-tuple-element.71), channel_id=1, source_target_pairs={{7,0},{6,1},{5,2},{4,3},{3,4},{2,5},{1,6},{0,7},{15,8},{14,9},{13,... | collective-permute-start | bytes 98312 | tf_op jit(solution)/shard_map/ppermute | solution.py:321
  55.7 12.2 %collective-permute-start.25 = (bf16[32,512]{1,0:T(8,128)(2,1)S(1)}, bf16[32,512]{1,0:T(8,128)(2,1)S(1)}, u32[]{:S(2)}, u32[]{:S(2)}) collective-permute-start(bf16[32,512]{1,0:T(8,128)(2,1)S(1)} %get-tuple-element.72), channel_id=1, source_target_pairs={{8,0},{9,1},{10,2},{11,3},{12,4},{13,5},{14,6},{15,7},{0,8},{1,9},... | collective-permute-start | bytes 98312 | tf_op jit(solution)/shard_map/ppermute | solution.py:321
  56.1 13.5 %collective-permute-start.26 = (bf16[32,512]{1,0:T(8,128)(2,1)S(1)}, bf16[32,512]{1,0:T(8,128)(2,1)S(1)}, u32[]{:S(2)}, u32[]{:S(2)}) collective-permute-start(bf16[32,512]{1,0:T(8,128)(2,1)S(1)} %get-tuple-element.73), channel_id=1, source_target_pairs={{9,0},{8,1},{11,2},{10,3},{13,4},{12,5},{15,6},{14,7},{1,8},{0,9},... | collective-permute-start | bytes 98312 | tf_op jit(solution)/shard_map/ppermute | solution.py:321
  58.3 13.1 %collective-permute-start.27 = (bf16[32,512]{1,0:T(8,128)(2,1)S(1)}, bf16[32,512]{1,0:T(8,128)(2,1)S(1)}, u32[]{:S(2)}, u32[]{:S(2)}) collective-permute-start(bf16[32,512]{1,0:T(8,128)(2,1)S(1)} %get-tuple-element.74), channel_id=1, source_target_pairs={{10,0},{11,1},{8,2},{9,3},{14,4},{15,5},{12,6},{13,7},{2,8},{3,9},... | collective-permute-start | bytes 98312 | tf_op jit(solution)/shard_map/ppermute | solution.py:321
  63.6 14.1 %collective-permute-start.28 = (bf16[32,512]{1,0:T(8,128)(2,1)S(1)}, bf16[32,512]{1,0:T(8,128)(2,1)S(1)}, u32[]{:S(2)}, u32[]{:S(2)}) collective-permute-start(bf16[32,512]{1,0:T(8,128)(2,1)S(1)} %get-tuple-element.75), channel_id=1, source_target_pairs={{11,0},{10,1},{9,2},{8,3},{15,4},{14,5},{13,6},{12,7},{3,8},{2,9},... | collective-permute-start | bytes 98312 | tf_op jit(solution)/shard_map/ppermute | solution.py:321
  66.1 11.5 %collective-permute-start.29 = (bf16[32,512]{1,0:T(8,128)(2,1)S(1)}, bf16[32,512]{1,0:T(8,128)(2,1)S(1)}, u32[]{:S(2)}, u32[]{:S(2)}) collective-permute-start(bf16[32,512]{1,0:T(8,128)(2,1)S(1)} %get-tuple-element.76), channel_id=1, source_target_pairs={{12,0},{13,1},{14,2},{15,3},{8,4},{9,5},{10,6},{11,7},{4,8},{5,9},... | collective-permute-start | bytes 98312 | tf_op jit(solution)/shard_map/ppermute | solution.py:321
  67.9 9.7 %collective-permute-start.30 = (bf16[32,512]{1,0:T(8,128)(2,1)S(1)}, bf16[32,512]{1,0:T(8,128)(2,1)S(1)}, u32[]{:S(2)}, u32[]{:S(2)}) collective-permute-start(bf16[32,512]{1,0:T(8,128)(2,1)S(1)} %get-tuple-element.77), channel_id=1, source_target_pairs={{13,0},{12,1},{15,2},{14,3},{9,4},{8,5},{11,6},{10,7},{5,8},{4,9},... | collective-permute-start | bytes 98312 | tf_op jit(solution)/shard_map/ppermute | solution.py:321
  69.6 8.0 %collective-permute-start.31 = (bf16[32,512]{1,0:T(8,128)(2,1)S(1)}, bf16[32,512]{1,0:T(8,128)(2,1)S(1)}, u32[]{:S(2)}, u32[]{:S(2)}) collective-permute-start(bf16[32,512]{1,0:T(8,128)(2,1)S(1)} %get-tuple-element.78), channel_id=1, source_target_pairs={{14,0},{15,1},{12,2},{13,3},{10,4},{11,5},{8,6},{9,7},{6,8},{7,9},... | collective-permute-start | bytes 98312 | tf_op jit(solution)/shard_map/ppermute | solution.py:321
  71.4 6.2 %collective-permute-start.32 = (bf16[32,512]{1,0:T(8,128)(2,1)S(1)}, bf16[32,512]{1,0:T(8,128)(2,1)S(1)}, u32[]{:S(2)}, u32[]{:S(2)}) collective-permute-start(bf16[32,512]{1,0:T(8,128)(2,1)S(1)} %get-tuple-element.79), channel_id=1, source_target_pairs={{15,0},{14,1},{13,2},{12,3},{11,4},{10,5},{9,6},{8,7},{7,8},{6,9},... | collective-permute-start | bytes 98312 | tf_op jit(solution)/shard_map/ppermute | solution.py:321
  74.1 3.5 %copy-start = (s32[160,2]{0,1:T(2,128)S(1)}, s32[160,2]{0,1:T(2,128)}, u32[]{:S(2)}) copy-start(s32[160,2]{0,1:T(2,128)} %param.8) | copy-start | bytes 3844
  74.1 3.5 %copy-start.1 = (bf16[160,2]{0,1:T(2,128)(2,1)S(1)}, bf16[160,2]{0,1:T(2,128)(2,1)}, u32[]{:S(2)}) copy-start(bf16[160,2]{0,1:T(2,128)(2,1)} %param.7) | copy-start | bytes 1924

commit v3 on v1

v3 whole, which is shorter than its diff:
```python
import functools

import jax
import jax.numpy as jnp
from jax import lax
from jax.experimental import pallas as pl
from jax.experimental.pallas import tpu as pltpu
from jax.sharding import PartitionSpec as P

F32 = jnp.float32
BF16 = jnp.bfloat16
VMEM_LIMIT = 32 * 1024 * 1024
IN_HBM = pl.BlockSpec(memory_space=pltpu.HBM)
IN_VMEM = pl.BlockSpec(memory_space=pltpu.VMEM)
DMA = pltpu.SemaphoreType.DMA


def dot(left, right, left_dim, right_dim):
    return lax.dot_general(
        left, right, (((left_dim,), (right_dim,)), ((), ())), preferred_element_type=F32
    )


def silu_parts(preact):
    sigma = 0.5 * jnp.tanh(0.5 * preact) + 0.5
    active = preact * sigma
    return active, sigma + active * (1.0 - sigma)


def call(body, name, outs, args, in_specs, scratch, flops, transcendentals=0):
    moved = sum(a.size * a.dtype.itemsize for a in (*args, *outs))
    return pl.pallas_call(
        body,
        name=name,
        out_shape=outs,
        in_specs=in_specs,
        out_specs=[IN_VMEM] * len(outs),
        scratch_shapes=scratch,
        compiler_params=pltpu.CompilerParams(vmem_limit_bytes=VMEM_LIMIT),
        cost_estimate=pl.CostEstimate(
            flops=flops, bytes_accessed=moved, transcendentals=transcendentals
        ),
    )(*args)


def slots_of(routes, experts, first):
    rows = routes.shape[1]
    number = lax.broadcasted_iota(jnp.int32, (experts, rows), 0) + first
    hot = [number == routes[k : k + 1, :] for k in range(2)]
    as_num = [jnp.where(h, 1.0, 0.0).astype(F32) for h in hot]
    before = jnp.where(
        lax.broadcasted_iota(jnp.int32, (rows, rows), 0)
        < lax.broadcasted_iota(jnp.int32, (rows, rows), 1),
        1.0,
        0.0,
    ).astype(BF16)
    count = [dot(n.astype(BF16), before, 1, 0) for n in as_num]
    total = jnp.sum(as_num[0], axis=1, keepdims=True)
    place = [count[0], count[1] + total]
    slot = [
        jnp.sum(jnp.where(h, p, 0.0), axis=0, keepdims=True).astype(jnp.int32)
        for h, p in zip(hot, place)
    ]
    return hot, slot


def picks_of(routes, experts, first, pad):
    _, slot = slots_of(routes, experts, first)
    index = lax.broadcasted_iota(jnp.int32, (experts * pad, routes.shape[1]), 0)
    return [index == (routes[k : k + 1, :] - first) * pad + slot[k] for k in range(2)]


def fill_slots(routes, gates, tok_ref, cot_ref, out_ref, ready):
    experts, both, feat = out_ref.shape
    pad = both // 2
    first = lax.axis_index("exp") // experts * experts
    pick = picks_of(routes, experts, first, pad)
    gates = gates.astype(F32)
    plain = jnp.where(pick[0] | pick[1], 1.0, 0.0).astype(BF16)
    scaled = (
        jnp.where(pick[0], gates[0:1, :], 0.0) + jnp.where(pick[1], gates[1:2, :], 0.0)
    ).astype(BF16)
    ready()
    out_ref[:, 0:pad, :] = dot(plain, tok_ref[...], 1, 0).astype(BF16).reshape(experts, pad, feat)
    out_ref[:, pad:, :] = dot(scaled, cot_ref[...], 1, 0).astype(BF16).reshape(experts, pad, feat)


def near_kernel(routes_hbm, gates_hbm, tok_hbm, cot_hbm, up_hbm, down_hbm, *refs):
    out_ref, up_ref, down_ref, routes_ref, gates_ref, tok_ref, cot_ref, sems = refs
    pairs = [
        (routes_hbm, routes_ref),
        (gates_hbm, gates_ref),
        (tok_hbm, tok_ref),
        (cot_hbm, cot_ref),
        (up_hbm.at[0], up_ref),
        (down_hbm.at[0], down_ref),
    ]
    copies = [
        pltpu.make_async_copy(src, dst, sems.at[i]) for i, (src, dst) in enumerate(pairs)
    ]
    for copy in copies:
        copy.start()
    copies[0].wait()
    copies[1].wait()

    def ready():
        copies[2].wait()
        copies[3].wait()

    fill_slots(routes_ref[...], gates_ref[...], tok_ref, cot_ref, out_ref, ready)
    copies[4].wait()
    copies[5].wait()


def far_kernel(routes_ref, gates_ref, tok_ref, cot_ref, out_ref):
    fill_slots(routes_ref[...], gates_ref[...], tok_ref, cot_ref, out_ref, lambda: None)


def split_rows(ref):
    experts, both, feat = ref.shape
    pad = both // 2
    return (
        ref[:, 0:pad, :].reshape(experts * pad, feat),
        ref[:, pad:, :].reshape(experts * pad, feat),
    )


def backward(cap, block, disp_ref, up_ref, down_ref, grad_acc, gate_acc, put):
    origins, both, feat = disp_ref.shape
    pad = both // 2
    slots = origins * pad
    rows, grads = split_rows(disp_ref)
    for step in range(up_ref.shape[0] // block):
        part = pl.ds(step * block, block)
        up = up_ref[part, :]
        active, slope = silu_parts(dot(rows, up, 1, 1))
        back = dot(grads, down_ref[part, :], 1, 1)
        hid_grad = (back * slope).astype(BF16)
        gate = active.astype(BF16).astype(F32) * back
        gate = sum(gate[:, i : i + 128] for i in range(0, block, 128))
        in_grad = dot(hid_grad, up, 1, 0)
        if step == 0:
            grad_acc[...] = in_grad
            gate_acc[...] = gate
        else:
            grad_acc[...] += in_grad
            gate_acc[...] += gate
    gate = jnp.sum(gate_acc[...], axis=1, keepdims=True)
    spot = lax.broadcasted_iota(jnp.int32, (slots, 128), 0) % pad
    lane = lax.broadcasted_iota(jnp.int32, (slots, 128), 1)
    gate = jnp.where(spot == lane, gate, 0.0).reshape(origins, pad, 128)
    gate = jnp.sum(gate, axis=1, keepdims=True)
    line = lax.broadcasted_iota(jnp.int32, (pad, 128), 0)
    for k in range(origins):
        here = slice(k * pad, (k + 1) * pad)
        first = jnp.where(line == cap, gate[k], grad_acc[here, 0:128])
        put(k, first.astype(BF16), grad_acc[here, 128:].astype(BF16))


def near_back_kernel(cap, block, routes_ref, disp_ref, up_ref, down_ref, *refs):
    out_ref, pick_ref, grad_acc, gate_acc = refs

    def put(k, first, rest):
        out_ref[k, :, 0:128] = first
        out_ref[k, :, 128:] = rest

    backward(cap, block, disp_ref, up_ref, down_ref, grad_acc, gate_acc, put)
    pad = out_ref.shape[1]
    pick = picks_of(routes_ref[...], pick_ref.shape[0] // pad, 0, pad)
    pick_ref[...] = jnp.where(pick[0] | pick[1], 1.0, 0.0).astype(BF16)


def far_back_kernel(cap, block, near_ref, disp_ref, up_ref, down_ref, *refs):
    out_ref, grad_acc, gate_acc = refs
    half = lax.axis_index("exp") // near_ref.shape[0]
    out_ref[half] = near_ref[...]

    def put(k, first, rest):
        out_ref[1 - half, k, :, 0:128] = first
        out_ref[1 - half, k, :, 128:] = rest

    backward(cap, block, disp_ref, up_ref, down_ref, grad_acc, gate_acc, put)


def weight_parts(block, share, disp_refs, up_ref, down_ref, rows_ref, grads_ref, store):
    size = rows_ref.shape[0] // len(disp_refs)
    for i, ref in enumerate(disp_refs):
        here = slice(i * size, (i + 1) * size)
        rows_ref[here, :], grads_ref[here, :] = split_rows(ref)
    base = lax.axis_index("rep") * share
    for step in range(share // block):
        here = pl.ds(step * block, block)
        part = pl.ds(pl.multiple_of(base + step * block, block), block)
        active, slope = silu_parts(dot(up_ref[part, :], rows_ref[...], 1, 1))
        back = dot(down_ref[part, :], grads_ref[...], 1, 1)
        hid_grad = (back * slope).astype(BF16)
        up_part = dot(hid_grad, rows_ref[...], 1, 0)
        down_part = dot(active.astype(BF16), grads_ref[...], 1, 0)
        store(here, up_part, down_part)


def own_weights_kernel(block, share, near_ref, far_ref, up_ref, down_ref, *refs):
    up_acc, down_acc, rows_ref, grads_ref = refs

    def store(here, up_part, down_part):
        up_acc[here, :] = up_part
        down_acc[here, :] = down_part

    both = [near_ref, far_ref]
    weight_parts(block, share, both, up_ref, down_ref, rows_ref, grads_ref, store)


def other_weights_kernel(block, share, mirrors, *refs):
    pieces, refs = refs[:-8], refs[-8:]
    up_ref, down_ref, up_acc, down_acc, grad_up_ref, grad_down_ref, rows_ref, grads_ref = refs
    for mirror in range(mirrors - 1):

        def store(here, up_part, down_part):
            up_part += up_acc[here, :]
            down_part += down_acc[here, :]
            if mirror == mirrors - 2:
                grad_up_ref[0, here, :] = up_part.astype(BF16)
                grad_down_ref[0, here, :] = down_part.astype(BF16)
            else:
                up_acc[here, :] = up_part
                down_acc[here, :] = down_part

        both = pieces[2 * mirror : 2 * mirror + 2]
        weight_parts(block, share, both, up_ref, down_ref, rows_ref, grads_ref, store)


def combine_kernel(cap, routes_ref, gates_ref, pick_ref, back_ref, d_tok_ref, d_gate_ref):
    groups, pad, feat = back_ref.shape
    back = back_ref[...]
    d_tok_ref[...] = dot(pick_ref[...], back.reshape(groups * pad, feat), 0, 0).astype(BF16)
    routes = routes_ref[...]
    gates = gates_ref[...].astype(F32)
    hot, slot = slots_of(routes, groups, 0)
    lane = lax.broadcasted_iota(jnp.int32, (128, routes.shape[1]), 0)
    values = back[:, cap, 0:128]
    for k in range(2):
        spot = jnp.where(lane == slot[k], 1.0, 0.0).astype(BF16)
        found = jnp.where(hot[k], dot(values, spot, 1, 0), 0.0)
        found = jnp.sum(found, axis=0, keepdims=True)
        d_gate_ref[k : k + 1, :] = (found / gates[k : k + 1, :]).astype(BF16)


def local(tokens, gates, routes, cotangent, w_up, w_down):
    rows, feat = tokens.shape
    hidden = w_up.shape[1]
    groups = lax.axis_size("exp")
    mirrors = lax.axis_size("rep")
    cap = max(2, 3 * rows // groups)
    pad = (cap // 16 + 1) * 16
    half = groups // 2
    slots = half * pad
    share = hidden // mirrors
    routes_t, gates_t = routes.T, gates.T
    far = functools.partial(pltpu.with_memory_space_constraint, memory_space=pltpu.HBM)
    shape = jax.ShapeDtypeStruct
    unit = 2 * slots * feat
    disp_shape = shape((half, 2 * pad, feat), BF16)
    weight = shape((hidden, feat), BF16)

    across = [(i, (i + half) % groups) for i in range(groups)]
    partner = [lax.ppermute(a, "exp", across) for a in (routes_t, gates_t, tokens, cotangent)]

    near_out, up_v, down_v = call(
        near_kernel,
        "near_slots",
        [disp_shape, weight, weight],
        [far(a) for a in (routes_t, gates_t, tokens, cotangent, w_up, w_down)],
        [IN_HBM] * 6,
        [
            pltpu.VMEM((2, rows), jnp.int32),
            pltpu.VMEM((2, rows), BF16),
            pltpu.VMEM((rows, feat), BF16),
            pltpu.VMEM((rows, feat), BF16),
            DMA((6,)),
        ],
        2 * unit * rows,
    )
    halves = [list(range(half)), list(range(half, groups))]
    within = functools.partial(
        lax.all_to_all,
        axis_name="exp",
        split_axis=0,
        concat_axis=0,
        axis_index_groups=halves,
        tiled=True,
    )
    near = within(near_out)
    mirror_hops = [
        [(i, (i + shift) % mirrors) for i in range(mirrors)] for shift in range(1, mirrors)
    ]
    near_others = [lax.ppermute(near, "rep", hops) for hops in mirror_hops]
    (far_out,) = call(
        far_kernel, "far_slots", [disp_shape], partner, [IN_VMEM] * 4, [], 2 * unit * rows
    )
    beyond = within(far_out)
    far_others = [lax.ppermute(beyond, "rep", hops) for hops in mirror_hops]

    block = min(512, hidden)
    scratch = [pltpu.VMEM((slots, feat), F32), pltpu.VMEM((slots, 128), F32)]
    near_back, pick = call(
        functools.partial(near_back_kernel, cap, block),
        "near_backward",
        [shape((half, pad, feat), BF16), shape((groups * pad, rows), BF16)],
        [routes_t, near, up_v, down_v],
        [IN_VMEM] * 4,
        scratch,
        3 * unit * hidden,
        slots * hidden,
    )
    (back,) = call(
        functools.partial(far_back_kernel, cap, block),
        "far_backward",
        [shape((2, half, pad, feat), BF16)],
        [near_back, beyond, up_v, down_v],
        [IN_VMEM] * 4,
        scratch,
        3 * unit * hidden,
        slots * hidden,
    )
    back = lax.all_to_all(
        back.reshape(groups, pad, feat), "exp", split_axis=0, concat_axis=0, tiled=True
    )

    part = min(512, share)
    total = shape((share, feat), F32)
    both_rows = [pltpu.VMEM((2 * slots, feat), BF16)] * 2
    up_sum, down_sum = call(
        functools.partial(own_weights_kernel, part, share),
        "own_weights",
        [total, total],
        [near, beyond, up_v, down_v],
        [IN_VMEM] * 4,
        both_rows,
        8 * unit * share,
        2 * slots * share,
    )
    if mirrors == 1:
        grad_up, grad_down = up_sum.astype(BF16)[None], down_sum.astype(BF16)[None]
    else:
        others = [a for pair in zip(near_others, far_others) for a in pair]
        grad_up, grad_down = call(
            functools.partial(other_weights_kernel, part, share, mirrors),
            "other_weights",
            [shape((1, share, feat), BF16)] * 2,
            [*others, up_v, down_v, up_sum, down_sum],
            [IN_VMEM] * (len(others) + 4),
            both_rows,
            8 * unit * share * (mirrors - 1),
            2 * slots * share,
        )

    d_tokens, d_gates = call(
        functools.partial(combine_kernel, cap),
        "combine",
        [shape((rows, feat), BF16), shape((2, rows), BF16)],
        [routes_t, gates_t, pick, back],
        [IN_VMEM] * 4,
        [],
        2 * unit * rows,
    )
    return d_tokens, d_gates.T, grad_up, grad_down


def solution(mesh):
    by_both = P(("rep", "exp"), None)
    by_expert = P("exp", None, None)
    return jax.shard_map(
        local,
        mesh=mesh,
        in_specs=(by_both, by_both, by_both, by_both, by_expert, by_expert),
        out_specs=(by_both, by_both, P("exp", "rep", None), P("exp", "rep", None)),
        check_vma=False,
    )
```

time: 82.2 us -> 84.1 us (1.023)
  blocking collectives: 32 us -> 0 us
  starting transfers between devices: 7.08 us -> 22 us
  waiting for transfers between devices: 23.5 us -> 34.7 us
  Pallas kernels: 12 us -> 16.2 us
  local copies, waits for them, and re-layouts: 6.46 us -> 9.79 us
    all_to_all x1 -> x0, blocking collectives: 32 us -> none  [local(): disp = lax.all_to_all(out, 'exp', split_axis=0, concat_axis=0, tiled=True)]
    all_to_all x1 -> x3, starting transfers between devices: 4.99 us -> 14 us  [the longest x1 5.29 us: local(): lax.all_to_all(back.reshape(groups, pad, feat), 'exp', split_axis=0, conc...]
    ppermute x2 -> x6, waiting for transfers between devices: 23.5 us -> 30.7 us  [the longest x4 12.3 us: local(): lax.ppermute(a, 'exp', across)]
    ppermute x2 -> x6, starting transfers between devices: 2.09 us -> 8.01 us  [the longest x4 5.91 us: local(): lax.ppermute(a, 'exp', across)]
    pallas_call x4 -> x7, Pallas kernels: 12 us -> 16.2 us  [call(): pl.pallas_call(body, name=name, out_shape=outs, in_specs=in_specs, out_sp...]
    all_to_all x1 -> x3, waiting for transfers between devices: 0.01 us -> 4.04 us  [the longest x1 4.03 us: local(): beyond = within(far_out)]
    unnamed x20 -> x26, local copies, waits for them, and re-layouts: 6.39 us -> 9.79 us
  transfers between devices with their start and end apart: 3 -> 9, of which waited for: 2 -> 4; matrix products, arithmetic and copies ran while one was open for 0% -> 0% of each run, Pallas kernels for 7% -> 12%
where the time goes in v3:
time: 84.1 us; the launch traced here: 83.5 us
  waiting for transfers between devices  34.7 us (41%)
  starting transfers between devices  22 us (26%)
  Pallas kernels  16.2 us (19%)
  local copies, waits for them, and re-layouts  9.79 us (12%)
    pallas_call x7, Pallas kernels, call(): pl.pallas_call(body, name=name, out_shape=outs, in_specs=in_specs, out_sp...  16.2 us
    ppermute x4, waiting for transfers between devices, local(): lax.ppermute(a, 'exp', across)  12.3 us
    ppermute x1, waiting for transfers between devices, local(): far_others = [lax.ppermute(beyond, 'rep', hops) for hops in mirror_hops]  10.7 us
    unnamed x26, local copies, waits for them, and re-layouts  9.79 us
    ppermute x1, waiting for transfers between devices, local(): near_others = [lax.ppermute(near, 'rep', hops) for hops in mirror_hops]  7.65 us
    ppermute x4, starting transfers between devices, local(): lax.ppermute(a, 'exp', across)  5.91 us
    all_to_all x1, starting transfers between devices, local(): lax.all_to_all(back.reshape(groups, pad, feat), 'exp', split_axis=0, conc...  5.29 us
    all_to_all x1, starting transfers between devices, local(): near = within(near_out)  5.26 us
  transfers between devices with their start and end apart: 9, of which 4 were waited for; matrix products, arithmetic and copies ran while one was open for 0% of the time, Pallas kernels for 12%

profile of v3, /device:TPU:0, one launch (start us, length us, event | category | flops | bytes accessed | tf_op | source)
XLA Modules:
  0.0 83.5 jit_solution(11570162489553850963)
XLA Ops:
  0.6 0.0 copy-start.11
  0.6 0.0 copy-start.12
  0.7 0.0 copy-start.7
  0.7 0.0 copy-start.8
  0.7 3.3 %near_slots.1 = (bf16[8,64,512]{2,1,0:T(8,128)(2,1)}, bf16[2048,512]{1,0:T(8,128)(2,1)S(1)}, bf16[2048,512]{1,0:T(8,128)(2,1)S(1)}) custom-call(s32[2,160]{1,0:T(2,128)} %bitcast.5, bf16[2,160]{1,0:T(2,128)(2,1)} %bitcast.9, bf16[160,512]{1,0:T(8,128)(2,1)} %tok_hbm.1, bf16[160,512]{1,0:T(8,128)(2,1)} %cot_hbm.1, bf16[1,2048,512]{2,1,0:T(8,128)(2,1)} %up_hbm.1, ...), custom_call_target="tpu_custom_call" | custom-call | flops 83886080 | bytes 9242496 | tf_op jit(solution)/shard_map/near_slots/pallas_call | solution.py:32
  4.0 0.0 copy-start
  4.0 1.3 %copy-done = bf16[2048,512]{1,0:T(8,128)(2,1)} copy-done((bf16[2048,512]{1,0:T(8,128)(2,1)}, bf16[2048,512]{1,0:T(8,128)(2,1)S(1)}, u32[]{:S(2)}) %copy-start) | copy-done | bytes 2097176
  5.3 5.3 %all-to-all-start = ((bf16[8,64,512]{2,1,0:T(8,128)(2,1)}), bf16[8,64,512]{2,1,0:T(8,128)(2,1)S(1)}, u32[]{:S(2)}, u32[]{:S(2)}) async-start(bf16[8,64,512]{2,1,0:T(8,128)(2,1)} %get-tuple-element.15), calls=%async_computation | async-start | bytes 1048576 | tf_op jit(solution)/shard_map/all_to_all | solution.py:292
  10.6 0.0 copy-done.11
  10.6 2.7 %collective-permute-start.2 = (bf16[160,512]{1,0:T(8,128)(2,1)S(1)}, bf16[160,512]{1,0:T(8,128)(2,1)S(1)}, u32[]{:S(2)}, u32[]{:S(2)}) collective-permute-start(bf16[160,512]{1,0:T(8,128)(2,1)S(1)} %copy-done.11), channel_id=1, source_target_pairs={{0,8},{1,9},{2,10},{3,11},{4,12},{5,13},{6,14},{7,15},{8,0},{9,1},... | collective-permute-start | bytes 491528 | tf_op jit(solution)/shard_map/ppermute | solution.py:266
  13.3 0.0 copy-done.12
  13.3 0.3 collective-permute-start.3
  13.6 0.0 copy-done.7
  13.6 2.6 %collective-permute-start = (s32[2,160]{1,0:T(2,128)S(1)}, s32[2,160]{1,0:T(2,128)S(1)}, u32[]{:S(2)}, u32[]{:S(2)}) collective-permute-start(s32[2,160]{1,0:T(2,128)S(1)} %bitcast.6), channel_id=1, source_target_pairs={{0,8},{1,9},{2,10},{3,11},{4,12},{5,13},{6,14},{7,15},{8,0},{9,1},... | collective-permute-start | bytes 3848 | tf_op jit(solution)/shard_map/ppermute | solution.py:266
  16.2 0.0 copy-done.8
  16.2 0.3 collective-permute-start.1
  16.5 12.3 %collective-permute-done.1.gates_ref = bf16[2,160]{1,0:T(2,128)(2,1)S(1)} collective-permute-done((bf16[2,160]{1,0:T(2,128)(2,1)S(1)}, bf16[2,160]{1,0:T(2,128)(2,1)S(1)}, u32[]{:S(2)}, u32[]{:S(2)}) %collective-permute-start.1) | collective-permute-done | bytes 672 | tf_op jit(solution)/shard_map/ppermute | solution.py:266
  28.9 0.0 collective-permute-done.routes_ref
  28.9 0.0 collective-permute-done.2.tok_ref
  28.9 0.0 collective-permute-done.3.cot_ref
  28.9 1.3 %far_slots.1 = bf16[8,64,512]{2,1,0:T(8,128)(2,1)} custom-call(s32[2,160]{1,0:T(2,128)S(1)} %collective-permute-done.routes_ref, bf16[2,160]{1,0:T(2,128)(2,1)S(1)} %collective-permute-done.1.gates_ref, bf16[160,512]{1,0:T(8,128)(2,1)S(1)} %collective-permute-done.2.tok_ref, bf16[160,512]{1,0:T(8,128)(2,1)S(1)} %collective-permute-done.3.cot_ref), custom_call_target="tpu_custom_call" | custom-call | flops 83886080 | bytes 853888 | tf_op jit(solution)/shard_map/far_slots/pallas_call | solution.py:32
  30.2 0.0 all-to-all-done.disp_ref.near_ref
  30.2 3.5 %all-to-all-start.1 = ((bf16[8,64,512]{2,1,0:T(8,128)(2,1)}), bf16[8,64,512]{2,1,0:T(8,128)(2,1)S(1)}, u32[]{:S(2)}, u32[]{:S(2)}) async-start(bf16[8,64,512]{2,1,0:T(8,128)(2,1)} %far_slots.1), calls=%async_computation.1 | async-start | bytes 1048576 | tf_op jit(solution)/shard_map/all_to_all | solution.py:300
  33.7 0.0 copy-start.1
  33.7 1.6 %copy-done.1 = bf16[2048,512]{1,0:T(8,128)(2,1)S(1)} copy-done((bf16[2048,512]{1,0:T(8,128)(2,1)S(1)}, bf16[2048,512]{1,0:T(8,128)(2,1)}, u32[]{:S(2)}) %copy-start.1) | copy-done | bytes 2097176
  35.3 2.4 %near_backward.1 = (bf16[8,32,512]{2,1,0:T(8,128)(2,1)S(1)}, bf16[512,160]{1,0:T(8,128)(2,1)S(1)}) custom-call(s32[2,160]{1,0:T(2,128)S(1)} %bitcast.7, bf16[8,64,512]{2,1,0:T(8,128)(2,1)S(1)} %all-to-all-done.disp_ref.near_ref, bf16[2048,512]{1,0:T(8,128)(2,1)S(1)} %get-tuple-element.16.up_ref.refs_2_, bf16[2048,512]{1,0:T(8,128)(2,1)S(1)} %copy-done.1), custom_call_target="tpu_custom_call" | custom-call | flops 1610612736 | bytes 5145856 | tf_op jit(solution)/shard_map/near_backward/pallas_call | solution.py:32
  37.7 0.0 copy-start.9
  37.7 0.7 copy-done.9
  38.4 4.0 %all-to-all-done.1.disp_ref.far_ref = bf16[8,64,512]{2,1,0:T(8,128)(2,1)S(1)} async-done(((bf16[8,64,512]{2,1,0:T(8,128)(2,1)}), bf16[8,64,512]{2,1,0:T(8,128)(2,1)S(1)}, u32[]{:S(2)}, u32[]{:S(2)}) %all-to-all-start.1) | async-done | bytes 524320 | tf_op jit(solution)/shard_map/all_to_all | solution.py:300
  42.4 0.0 copy-start.4
  42.4 0.0 copy-start.2
  42.4 1.8 %copy-done.2 = bf16[2048,512]{1,0:T(8,128)(2,1)S(1)} copy-done((bf16[2048,512]{1,0:T(8,128)(2,1)S(1)}, bf16[2048,512]{1,0:T(8,128)(2,1)}, u32[]{:S(2)}) %copy-start.2) | copy-done | bytes 2097176
  44.2 0.0 copy-start.10
  44.2 0.9 %copy-done.10 = bf16[8,32,512]{2,1,0:T(8,128)(2,1)S(1)} copy-done((bf16[8,32,512]{2,1,0:T(8,128)(2,1)S(1)}, bf16[8,32,512]{2,1,0:T(8,128)(2,1)}, u32[]{:S(2)}) %copy-start.10) | copy-done | bytes 262168
  45.2 2.3 %far_backward.1 = bf16[2,8,32,512]{3,2,1,0:T(8,128)(2,1)S(1)} custom-call(bf16[8,32,512]{2,1,0:T(8,128)(2,1)S(1)} %copy-done.10, bf16[8,64,512]{2,1,0:T(8,128)(2,1)S(1)} %all-to-all-done.1.disp_ref.far_ref, bf16[2048,512]{1,0:T(8,128)(2,1)S(1)} %get-tuple-element.16.up_ref.refs_2_, bf16[2048,512]{1,0:T(8,128)(2,1)S(1)} %copy-done.2), custom_call_target="tpu_custom_call" | custom-call | flops 1610612736 | bytes 5505024 | tf_op jit(solution)/shard_map/far_backward/pallas_call | solution.py:32
  47.4 0.0 copy-done.4
  47.5 0.0 copy-start.6
  47.5 0.8 copy-done.6
  48.3 5.3 %all-to-all-start.2 = ((bf16[16,32,512]{2,1,0:T(8,128)(2,1)}), bf16[16,32,512]{2,1,0:T(8,128)(2,1)S(1)}, u32[]{:S(2)}, u32[]{:S(2)}) async-start(bf16[16,32,512]{2,1,0:T(8,128)(2,1)} %bitcast.4), calls=%async_computation.2 | async-start | bytes 1048576 | tf_op jit(solution)/shard_map/all_to_all | solution.py:325
  53.6 1.6 %collective-permute-start.4 = (bf16[8,64,512]{2,1,0:T(8,128)(2,1)S(1)}, bf16[8,64,512]{2,1,0:T(8,128)(2,1)S(1)}, u32[]{:S(2)}, u32[]{:S(2)}) collective-permute-start(bf16[8,64,512]{2,1,0:T(8,128)(2,1)S(1)} %all-to-all-done.disp_ref.near_ref), channel_id=1, source_target_pairs={{0,16},{16,0},{1,17},{17,1},{2,18},{18,2},{3,19},{19,3},{4,20},{20... | collective-permute-start | bytes 1572872 | tf_op jit(solution)/shard_map/ppermute | solution.py:296
  55.1 0.5 collective-permute-start.5
  55.7 0.0 copy-start.3
  55.7 1.6 %copy-done.3 = bf16[2048,512]{1,0:T(8,128)(2,1)S(1)} copy-done((bf16[2048,512]{1,0:T(8,128)(2,1)S(1)}, bf16[2048,512]{1,0:T(8,128)(2,1)}, u32[]{:S(2)}) %copy-start.3) | copy-done | bytes 2097176
  57.3 0.0 copy-start.5
  57.3 1.0 %copy-done.5 = bf16[8,64,512]{2,1,0:T(8,128)(2,1)S(1)} copy-done((bf16[8,64,512]{2,1,0:T(8,128)(2,1)S(1)}, bf16[8,64,512]{2,1,0:T(8,128)(2,1)}, u32[]{:S(2)}) %copy-start.5) | copy-done | bytes 524312
  58.3 2.4 %own_weights.1 = (f32[1024,512]{1,0:T(8,128)S(1)}, f32[1024,512]{1,0:T(8,128)S(1)}) custom-call(bf16[8,64,512]{2,1,0:T(8,128)(2,1)S(1)} %all-to-all-done.disp_ref.near_ref, bf16[8,64,512]{2,1,0:T(8,128)(2,1)S(1)} %copy-done.5, bf16[2048,512]{1,0:T(8,128)(2,1)S(1)} %get-tuple-element.16.up_ref.refs_2_, bf16[2048,512]{1,0:T(8,128)(2,1)S(1)} %copy-done.3), custom_call_target="tpu_custom_call" | custom-call | flops 2147483648 | bytes 9437184 | tf_op jit(solution)/shard_map/own_weights/pallas_call | solution.py:32
  60.7 7.7 %collective-permute-done.4.refs_0_ = bf16[8,64,512]{2,1,0:T(8,128)(2,1)S(1)} collective-permute-done((bf16[8,64,512]{2,1,0:T(8,128)(2,1)S(1)}, bf16[8,64,512]{2,1,0:T(8,128)(2,1)S(1)}, u32[]{:S(2)}, u32[]{:S(2)}) %collective-permute-start.4) | collective-permute-done | bytes 524320 | tf_op jit(solution)/shard_map/ppermute | solution.py:296
  68.4 10.7 %collective-permute-done.5.refs_1_ = bf16[8,64,512]{2,1,0:T(8,128)(2,1)S(1)} collective-permute-done((bf16[8,64,512]{2,1,0:T(8,128)(2,1)}, bf16[8,64,512]{2,1,0:T(8,128)(2,1)S(1)}, u32[]{:S(2)}, u32[]{:S(2)}) %collective-permute-start.5) | collective-permute-done | bytes 524320 | tf_op jit(solution)/shard_map/ppermute | solution.py:301
  79.0 3.5 %other_weights.1 = (bf16[1,1024,512]{2,1,0:T(8,128)(2,1)}, bf16[1,1024,512]{2,1,0:T(8,128)(2,1)}) custom-call(bf16[8,64,512]{2,1,0:T(8,128)(2,1)S(1)} %collective-permute-done.4.refs_0_, bf16[8,64,512]{2,1,0:T(8,128)(2,1)S(1)} %collective-permute-done.5.refs_1_, bf16[2048,512]{1,0:T(8,128)(2,1)S(1)} %get-tuple-element.16.up_ref.refs_2_, ...), custom_call_target="tpu_custom_call" | custom-call | flops 2147483648 | bytes 11534336 | tf_op jit(solution)/shard_map/other_weights/pallas_call | solution.py:32
  82.5 0.0 all-to-all-done.2.back_ref
  82.5 1.0 %combine.1 = (bf16[160,512]{1,0:T(8,128)(2,1)}, bf16[2,160]{1,0:T(2,128)(2,1)}) custom-call(s32[2,160]{1,0:T(2,128)S(1)} %bitcast.8, bf16[2,160]{1,0:T(2,128)(2,1)S(1)} %bitcast.11, bf16[512,160]{1,0:T(8,128)(2,1)S(1)} %get-tuple-element.18.pick_ref, bf16[16,32,512]{2,1,0:T(8,128)(2,1)S(1)} %all-to-all-done.2.back_ref), custom_call_target="tpu_custom_call" | custom-call | flops 83886080 | bytes 854528 | tf_op jit(solution)/shard_map/combine/pallas_call | solution.py:32
Async XLA Ops:
  0.6 10.0 %copy-start.11 = (bf16[160,512]{1,0:T(8,128)(2,1)S(1)}, bf16[160,512]{1,0:T(8,128)(2,1)}, u32[]{:S(2)}) copy-start(bf16[160,512]{1,0:T(8,128)(2,1)} %tok_hbm.1) | copy-start | bytes 491524
  0.6 12.6 %copy-start.12 = (bf16[160,512]{1,0:T(8,128)(2,1)S(1)}, bf16[160,512]{1,0:T(8,128)(2,1)}, u32[]{:S(2)}) copy-start(bf16[160,512]{1,0:T(8,128)(2,1)} %cot_hbm.1) | copy-start | bytes 491524
  0.7 12.9 %copy-start.7 = (s32[160,2]{0,1:T(2,128)S(1)}, s32[160,2]{0,1:T(2,128)}, u32[]{:S(2)}) copy-start(s32[160,2]{0,1:T(2,128)} %param.8) | copy-start | bytes 3844
  0.7 15.5 %copy-start.8 = (bf16[160,2]{0,1:T(2,128)(2,1)S(1)}, bf16[160,2]{0,1:T(2,128)(2,1)}, u32[]{:S(2)}) copy-start(bf16[160,2]{0,1:T(2,128)(2,1)} %param.7) | copy-start | bytes 1924
  4.0 1.3 %copy-start = (bf16[2048,512]{1,0:T(8,128)(2,1)}, bf16[2048,512]{1,0:T(8,128)(2,1)S(1)}, u32[]{:S(2)}) copy-start(bf16[2048,512]{1,0:T(8,128)(2,1)S(1)} %get-tuple-element.17.down_ref.refs_3_) | copy-start | bytes 6291460
  5.3 24.8 %all-to-all-start = ((bf16[8,64,512]{2,1,0:T(8,128)(2,1)}), bf16[8,64,512]{2,1,0:T(8,128)(2,1)S(1)}, u32[]{:S(2)}, u32[]{:S(2)}) async-start(bf16[8,64,512]{2,1,0:T(8,128)(2,1)} %get-tuple-element.15), calls=%async_computation | async-start | bytes 1048576 | tf_op jit(solution)/shard_map/all_to_all | solution.py:292
  10.6 18.3 %collective-permute-start.2 = (bf16[160,512]{1,0:T(8,128)(2,1)S(1)}, bf16[160,512]{1,0:T(8,128)(2,1)S(1)}, u32[]{:S(2)}, u32[]{:S(2)}) collective-permute-start(bf16[160,512]{1,0:T(8,128)(2,1)S(1)} %copy-done.11), channel_id=1, source_target_pairs={{0,8},{1,9},{2,10},{3,11},{4,12},{5,13},{6,14},{7,15},{8,0},{9,1},... | collective-permute-start | bytes 491528 | tf_op jit(solution)/shard_map/ppermute | solution.py:266
  13.3 15.6 %collective-permute-start.3 = (bf16[160,512]{1,0:T(8,128)(2,1)S(1)}, bf16[160,512]{1,0:T(8,128)(2,1)S(1)}, u32[]{:S(2)}, u32[]{:S(2)}) collective-permute-start(bf16[160,512]{1,0:T(8,128)(2,1)S(1)} %copy-done.12), channel_id=1, source_target_pairs={{0,8},{1,9},{2,10},{3,11},{4,12},{5,13},{6,14},{7,15},{8,0},{9,1},... | collective-permute-start | bytes 491528 | tf_op jit(solution)/shard_map/ppermute | solution.py:266
  13.6 15.3 %collective-permute-start = (s32[2,160]{1,0:T(2,128)S(1)}, s32[2,160]{1,0:T(2,128)S(1)}, u32[]{:S(2)}, u32[]{:S(2)}) collective-permute-start(s32[2,160]{1,0:T(2,128)S(1)} %bitcast.6), channel_id=1, source_target_pairs={{0,8},{1,9},{2,10},{3,11},{4,12},{5,13},{6,14},{7,15},{8,0},{9,1},... | collective-permute-start | bytes 3848 | tf_op jit(solution)/shard_map/ppermute | solution.py:266
  16.2 12.7 %collective-permute-start.1 = (bf16[2,160]{1,0:T(2,128)(2,1)S(1)}, bf16[2,160]{1,0:T(2,128)(2,1)S(1)}, u32[]{:S(2)}, u32[]{:S(2)}) collective-permute-start(bf16[2,160]{1,0:T(2,128)(2,1)S(1)} %bitcast.10), channel_id=1, source_target_pairs={{0,8},{1,9},{2,10},{3,11},{4,12},{5,13},{6,14},{7,15},{8,0},{9,1},... | collective-permute-start | bytes 1928 | tf_op jit(solution)/shard_map/ppermute | solution.py:266
  30.2 12.3 %all-to-all-start.1 = ((bf16[8,64,512]{2,1,0:T(8,128)(2,1)}), bf16[8,64,512]{2,1,0:T(8,128)(2,1)S(1)}, u32[]{:S(2)}, u32[]{:S(2)}) async-start(bf16[8,64,512]{2,1,0:T(8,128)(2,1)} %far_slots.1), calls=%async_computation.1 | async-start | bytes 1048576 | tf_op jit(solution)/shard_map/all_to_all | solution.py:300
  33.7 1.6 %copy-start.1 = (bf16[2048,512]{1,0:T(8,128)(2,1)S(1)}, bf16[2048,512]{1,0:T(8,128)(2,1)}, u32[]{:S(2)}) copy-start(bf16[2048,512]{1,0:T(8,128)(2,1)} %copy-done) | copy-start | bytes 6291460
  37.7 0.7 copy-start.9
  42.4 5.0 %copy-start.4 = (bf16[8,64,512]{2,1,0:T(8,128)(2,1)}, bf16[8,64,512]{2,1,0:T(8,128)(2,1)S(1)}, u32[]{:S(2)}) copy-start(bf16[8,64,512]{2,1,0:T(8,128)(2,1)S(1)} %all-to-all-done.1.disp_ref.far_ref) | copy-start | bytes 1572868
  42.4 1.8 %copy-start.2 = (bf16[2048,512]{1,0:T(8,128)(2,1)S(1)}, bf16[2048,512]{1,0:T(8,128)(2,1)}, u32[]{:S(2)}) copy-start(bf16[2048,512]{1,0:T(8,128)(2,1)} %copy-done) | copy-start | bytes 6291460
  44.2 0.9 %copy-start.10 = (bf16[8,32,512]{2,1,0:T(8,128)(2,1)S(1)}, bf16[8,32,512]{2,1,0:T(8,128)(2,1)}, u32[]{:S(2)}) copy-start(bf16[8,32,512]{2,1,0:T(8,128)(2,1)} %copy-done.9) | copy-start | bytes 786436
  47.5 0.8 copy-start.6
  48.3 34.3 %all-to-all-start.2 = ((bf16[16,32,512]{2,1,0:T(8,128)(2,1)}), bf16[16,32,512]{2,1,0:T(8,128)(2,1)S(1)}, u32[]{:S(2)}, u32[]{:S(2)}) async-start(bf16[16,32,512]{2,1,0:T(8,128)(2,1)} %bitcast.4), calls=%async_computation.2 | async-start | bytes 1048576 | tf_op jit(solution)/shard_map/all_to_all | solution.py:325
  53.6 14.8 %collective-permute-start.4 = (bf16[8,64,512]{2,1,0:T(8,128)(2,1)S(1)}, bf16[8,64,512]{2,1,0:T(8,128)(2,1)S(1)}, u32[]{:S(2)}, u32[]{:S(2)}) collective-permute-start(bf16[8,64,512]{2,1,0:T(8,128)(2,1)S(1)} %all-to-all-done.disp_ref.near_ref), channel_id=1, source_target_pairs={{0,16},{16,0},{1,17},{17,1},{2,18},{18,2},{3,19},{19,3},{4,20},{20... | collective-permute-start | bytes 1572872 | tf_op jit(solution)/shard_map/ppermute | solution.py:296
  55.1 23.9 %collective-permute-start.5 = (bf16[8,64,512]{2,1,0:T(8,128)(2,1)}, bf16[8,64,512]{2,1,0:T(8,128)(2,1)S(1)}, u32[]{:S(2)}, u32[]{:S(2)}) collective-permute-start(bf16[8,64,512]{2,1,0:T(8,128)(2,1)} %copy-done.4), channel_id=1, source_target_pairs={{0,16},{16,0},{1,17},{17,1},{2,18},{18,2},{3,19},{19,3},{4,20},{20... | collective-permute-start | bytes 1572872 | tf_op jit(solution)/shard_map/ppermute | solution.py:301
  55.7 1.6 %copy-start.3 = (bf16[2048,512]{1,0:T(8,128)(2,1)S(1)}, bf16[2048,512]{1,0:T(8,128)(2,1)}, u32[]{:S(2)}) copy-start(bf16[2048,512]{1,0:T(8,128)(2,1)} %copy-done) | copy-start | bytes 6291460
  57.3 1.0 %copy-start.5 = (bf16[8,64,512]{2,1,0:T(8,128)(2,1)S(1)}, bf16[8,64,512]{2,1,0:T(8,128)(2,1)}, u32[]{:S(2)}) copy-start(bf16[8,64,512]{2,1,0:T(8,128)(2,1)} %copy-done.4) | copy-start | bytes 1572868

commit v4 on v3

--- a/solution.py
+++ b/solution.py
@@ -9,7 +9,8 @@
 
 F32 = jnp.float32
 BF16 = jnp.bfloat16
-VMEM_LIMIT = 32 * 1024 * 1024
+SMALL, MEDIUM, LARGE = 8 << 20, 12 << 20, 24 << 20
+AHEAD = 10**11
 IN_HBM = pl.BlockSpec(memory_space=pltpu.HBM)
 IN_VMEM = pl.BlockSpec(memory_space=pltpu.VMEM)
 DMA = pltpu.SemaphoreType.DMA
@@ -27,7 +28,7 @@
     return active, sigma + active * (1.0 - sigma)
 
 
-def call(body, name, outs, args, in_specs, scratch, flops, transcendentals=0):
+def call(body, name, outs, args, in_specs, scratch, flops, transcendentals=0, limit=MEDIUM):
     moved = sum(a.size * a.dtype.itemsize for a in (*args, *outs))
     return pl.pallas_call(
         body,
@@ -36,7 +37,7 @@
         in_specs=in_specs,
         out_specs=[IN_VMEM] * len(outs),
         scratch_shapes=scratch,
-        compiler_params=pltpu.CompilerParams(vmem_limit_bytes=VMEM_LIMIT),
+        compiler_params=pltpu.CompilerParams(vmem_limit_bytes=limit),
         cost_estimate=pl.CostEstimate(
             flops=flops, bytes_accessed=moved, transcendentals=transcendentals
         ),
@@ -70,50 +71,25 @@
     return [index == (routes[k : k + 1, :] - first) * pad + slot[k] for k in range(2)]
 
 
-def fill_slots(routes, gates, tok_ref, cot_ref, out_ref, ready):
+def unpack(packed_ref, rows):
+    notes = packed_ref[2 * rows :, :].astype(F32)
+    return notes[0:2, 0:rows].astype(jnp.int32), notes[2:4, 0:rows]
+
+
+def slots_kernel(rows, packed_ref, out_ref):
     experts, both, feat = out_ref.shape
     pad = both // 2
     first = lax.axis_index("exp") // experts * experts
+    routes, gates = unpack(packed_ref, rows)
     pick = picks_of(routes, experts, first, pad)
-    gates = gates.astype(F32)
     plain = jnp.where(pick[0] | pick[1], 1.0, 0.0).astype(BF16)
     scaled = (
         jnp.where(pick[0], gates[0:1, :], 0.0) + jnp.where(pick[1], gates[1:2, :], 0.0)
     ).astype(BF16)
-    ready()
-    out_ref[:, 0:pad, :] = dot(plain, tok_ref[...], 1, 0).astype(BF16).reshape(experts, pad, feat)
-    out_ref[:, pad:, :] = dot(scaled, cot_ref[...], 1, 0).astype(BF16).reshape(experts, pad, feat)
-
-
-def near_kernel(routes_hbm, gates_hbm, tok_hbm, cot_hbm, up_hbm, down_hbm, *refs):
-    out_ref, up_ref, down_ref, routes_ref, gates_ref, tok_ref, cot_ref, sems = refs
-    pairs = [
-        (routes_hbm, routes_ref),
-        (gates_hbm, gates_ref),
-        (tok_hbm, tok_ref),
-        (cot_hbm, cot_ref),
-        (up_hbm.at[0], up_ref),
-        (down_hbm.at[0], down_ref),
-    ]
-    copies = [
-        pltpu.make_async_copy(src, dst, sems.at[i]) for i, (src, dst) in enumerate(pairs)
-    ]
-    for copy in copies:
-        copy.start()
-    copies[0].wait()
-    copies[1].wait()
-
-    def ready():
-        copies[2].wait()
-        copies[3].wait()
-
-    fill_slots(routes_ref[...], gates_ref[...], tok_ref, cot_ref, out_ref, ready)
-    copies[4].wait()
-    copies[5].wait()
-
-
-def far_kernel(routes_ref, gates_ref, tok_ref, cot_ref, out_ref):
-    fill_slots(routes_ref[...], gates_ref[...], tok_ref, cot_ref, out_ref, lambda: None)
+    tok = packed_ref[0:rows, :]
+    cot = packed_ref[rows : 2 * rows, :]
+    out_ref[:, 0:pad, :] = dot(plain, tok, 1, 0).astype(BF16).reshape(experts, pad, feat)
+    out_ref[:, pad:, :] = dot(scaled, cot, 1, 0).astype(BF16).reshape(experts, pad, feat)
 
 
 def split_rows(ref):
@@ -125,15 +101,19 @@
     )
 
 
-def backward(cap, block, disp_ref, up_ref, down_ref, grad_acc, gate_acc, put):
+def backward(cap, block, disp_ref, up_ref, down_ref, grad_acc, gate_acc, put, copies=()):
     origins, both, feat = disp_ref.shape
     pad = both // 2
     slots = origins * pad
     rows, grads = split_rows(disp_ref)
     for step in range(up_ref.shape[0] // block):
         part = pl.ds(step * block, block)
+        if copies:
+            copies[2 * step].wait()
         up = up_ref[part, :]
         active, slope = silu_parts(dot(rows, up, 1, 1))
+        if copies:
+            copies[2 * step + 1].wait()
         back = dot(grads, down_ref[part, :], 1, 1)
         hid_grad = (back * slope).astype(BF16)
         gate = active.astype(BF16).astype(F32) * back
@@ -157,29 +137,41 @@
         put(k, first.astype(BF16), grad_acc[here, 128:].astype(BF16))
 
 
-def near_back_kernel(cap, block, routes_ref, disp_ref, up_ref, down_ref, *refs):
-    out_ref, pick_ref, grad_acc, gate_acc = refs
+def near_back_kernel(cap, block, rows, packed_ref, disp_ref, up_hbm, down_hbm, *refs):
+    out_ref, pick_ref, up_ref, down_ref, grad_acc, gate_acc, sems = refs
+    copies = []
+    for step in range(up_ref.shape[0] // block):
+        part = pl.ds(step * block, block)
+        for i, (src, dst) in enumerate([(up_hbm, up_ref), (down_hbm, down_ref)]):
+            sem = sems.at[2 * step + i]
+            copies.append(pltpu.make_async_copy(src.at[0, part, :], dst.at[part, :], sem))
+            copies[-1].start()
 
     def put(k, first, rest):
         out_ref[k, :, 0:128] = first
         out_ref[k, :, 128:] = rest
 
+    backward(cap, block, disp_ref, up_ref, down_ref, grad_acc, gate_acc, put, copies)
+    pad = out_ref.shape[1]
+    pick = picks_of(unpack(packed_ref, rows)[0], pick_ref.shape[0] // pad, 0, pad)
+    pick_ref[...] = jnp.where(pick[0] | pick[1], 1.0, 0.0).astype(BF16)
+
+
+def far_back_kernel(cap, block, near_ref, disp_ref, up_ref, down_ref, *refs):
+    out_hbm, out_ref, grad_acc, gate_acc, sems = refs
+    half = lax.axis_index("exp") // near_ref.shape[0]
+    near_copy = pltpu.make_async_copy(near_ref, out_hbm.at[half], sems.at[0])
+    near_copy.start()
+
+    def put(k, first, rest):
+        out_ref[k, :, 0:128] = first
+        out_ref[k, :, 128:] = rest
+
     backward(cap, block, disp_ref, up_ref, down_ref, grad_acc, gate_acc, put)
-    pad = out_ref.shape[1]
-    pick = picks_of(routes_ref[...], pick_ref.shape[0] // pad, 0, pad)
-    pick_ref[...] = jnp.where(pick[0] | pick[1], 1.0, 0.0).astype(BF16)
-
-
-def far_back_kernel(cap, block, near_ref, disp_ref, up_ref, down_ref, *refs):
-    out_ref, grad_acc, gate_acc = refs
-    half = lax.axis_index("exp") // near_ref.shape[0]
-    out_ref[half] = near_ref[...]
-
-    def put(k, first, rest):
-        out_ref[1 - half, k, :, 0:128] = first
-        out_ref[1 - half, k, :, 128:] = rest
-
-    backward(cap, block, disp_ref, up_ref, down_ref, grad_acc, gate_acc, put)
+    far_copy = pltpu.make_async_copy(out_ref, out_hbm.at[1 - half], sems.at[1])
+    far_copy.start()
+    near_copy.wait()
+    far_copy.wait()
 
 
 def weight_parts(block, share, disp_refs, up_ref, down_ref, rows_ref, grads_ref, store):
@@ -263,22 +255,14 @@
     weight = shape((hidden, feat), BF16)
 
     across = [(i, (i + half) % groups) for i in range(groups)]
-    partner = [lax.ppermute(a, "exp", across) for a in (routes_t, gates_t, tokens, cotangent)]
-
-    near_out, up_v, down_v = call(
-        near_kernel,
-        "near_slots",
-        [disp_shape, weight, weight],
-        [far(a) for a in (routes_t, gates_t, tokens, cotangent, w_up, w_down)],
-        [IN_HBM] * 6,
-        [
-            pltpu.VMEM((2, rows), jnp.int32),
-            pltpu.VMEM((2, rows), BF16),
-            pltpu.VMEM((rows, feat), BF16),
-            pltpu.VMEM((rows, feat), BF16),
-            DMA((6,)),
-        ],
-        2 * unit * rows,
+    notes = jnp.concatenate([routes_t.astype(BF16), gates_t], axis=0)
+    notes = jnp.pad(notes, ((0, 12), (0, feat - rows)))
+    packed = jnp.concatenate([tokens, cotangent, notes], axis=0)
+    partner = lax.ppermute(packed, "exp", across)
+
+    slots_call = functools.partial(call, functools.partial(slots_kernel, rows))
+    (near_out,) = slots_call(
+        "near_slots", [disp_shape], [packed], [IN_VMEM], [], 2 * unit * rows, 0, SMALL
     )
     halves = [list(range(half)), list(range(half, groups))]
     within = functools.partial(
@@ -294,34 +278,38 @@
         [(i, (i + shift) % mirrors) for i in range(mirrors)] for shift in range(1, mirrors)
     ]
     near_others = [lax.ppermute(near, "rep", hops) for hops in mirror_hops]
-    (far_out,) = call(
-        far_kernel, "far_slots", [disp_shape], partner, [IN_VMEM] * 4, [], 2 * unit * rows
+    (far_out,) = slots_call(
+        "far_slots", [disp_shape], [partner], [IN_VMEM], [], AHEAD, 0, SMALL
     )
     beyond = within(far_out)
     far_others = [lax.ppermute(beyond, "rep", hops) for hops in mirror_hops]
 
     block = min(512, hidden)
     scratch = [pltpu.VMEM((slots, feat), F32), pltpu.VMEM((slots, 128), F32)]
-    near_back, pick = call(
-        functools.partial(near_back_kernel, cap, block),
+    near_back, pick, up_v, down_v = call(
+        functools.partial(near_back_kernel, cap, block, rows),
         "near_backward",
-        [shape((half, pad, feat), BF16), shape((groups * pad, rows), BF16)],
-        [routes_t, near, up_v, down_v],
-        [IN_VMEM] * 4,
-        scratch,
+        [shape((half, pad, feat), BF16), shape((groups * pad, rows), BF16), weight, weight],
+        [packed, near, far(w_up), far(w_down)],
+        [IN_VMEM] * 2 + [IN_HBM] * 2,
+        scratch + [DMA((2 * hidden // block,))],
         3 * unit * hidden,
         slots * hidden,
     )
-    (back,) = call(
+    back = pl.pallas_call(
         functools.partial(far_back_kernel, cap, block),
-        "far_backward",
-        [shape((2, half, pad, feat), BF16)],
-        [near_back, beyond, up_v, down_v],
-        [IN_VMEM] * 4,
-        scratch,
-        3 * unit * hidden,
-        slots * hidden,
-    )
+        name="far_backward",
+        out_shape=pltpu.HBM((2, half, pad, feat), BF16),
+        in_specs=[IN_VMEM] * 4,
+        out_specs=IN_HBM,
+        scratch_shapes=[pltpu.VMEM((half, pad, feat), BF16)] + scratch + [DMA((2,))],
+        compiler_params=pltpu.CompilerParams(vmem_limit_bytes=MEDIUM),
+        cost_estimate=pl.CostEstimate(
+            flops=3 * unit * hidden,
+            bytes_accessed=4 * hidden * feat,
+            transcendentals=slots * hidden,
+        ),
+    )(near_back, beyond, up_v, down_v)
     back = lax.all_to_all(
         back.reshape(groups, pad, feat), "exp", split_axis=0, concat_axis=0, tiled=True
     )
@@ -338,6 +326,7 @@
         both_rows,
         8 * unit * share,
         2 * slots * share,
+        LARGE,
     )
     if mirrors == 1:
         grad_up, grad_down = up_sum.astype(BF16)[None], down_sum.astype(BF16)[None]
@@ -350,8 +339,9 @@
             [*others, up_v, down_v, up_sum, down_sum],
             [IN_VMEM] * (len(others) + 4),
             both_rows,
-            8 * unit * share * (mirrors - 1),
+            AHEAD,
             2 * slots * share,
+            LARGE,
         )
 
     d_tokens, d_gates = call(

time: 84.1 us -> 68.6 us (0.82)
  waiting for transfers between devices: 34.7 us -> 26.2 us
  local copies, waits for them, and re-layouts: 9.79 us -> 3.2 us
  starting transfers between devices: 22 us -> 18.1 us
  other arithmetic: 0 us -> 2.4 us
  Pallas kernels: 16.2 us -> 17.4 us
    ppermute x1, waiting for transfers between devices: 10.7 us -> 0.01 us  [local(): far_others = [lax.ppermute(beyond, 'rep', hops) for hops in mirror_hops]]
    ppermute x1, waiting for transfers between devices: 7.65 us -> 0.01 us  [local(): near_others = [lax.ppermute(near, 'rep', hops) for hops in mirror_hops]]
    unnamed x26 -> x12, local copies, waits for them, and re-layouts: 9.79 us -> 3.2 us
    all_to_all x1, waiting for transfers between devices: 0.01 us -> 5.29 us  [local(): lax.all_to_all(back.reshape(groups, pad, feat), 'exp', split_axis=0, conc...]
    all_to_all x1, waiting for transfers between devices: 0.01 us -> 3.3 us  [local(): near = within(near_out)]
    all_to_all x1, waiting for transfers between devices: 4.03 us -> 7.16 us  [local(): beyond = within(far_out)]
    pallas_call x0 -> x1, Pallas kernels: none -> 3 us  [local(): pl.pallas_call(functools.partial(far_back_kernel, cap, block), name='far_...]
    ppermute x4 -> x1, waiting for transfers between devices: 12.3 us -> 10.4 us  [local(): partner = lax.ppermute(packed, 'exp', across)]
  transfers between devices with their start and end apart: 9 -> 6, of which waited for: 4 -> 4; matrix products, arithmetic and copies ran while one was open for 0% -> 0% of each run, Pallas kernels for 12% -> 24%
where the time goes in v4:
time: 68.6 us; the launch traced here: 68 us
  waiting for transfers between devices  26.2 us (38%)
  starting transfers between devices  18.1 us (26%)
  Pallas kernels  17.4 us (25%)
  local copies, waits for them, and re-layouts  3.2 us (5%)
  other arithmetic  2.4 us (3%)
  between operations  0.75 us (1%)
    pallas_call x6, Pallas kernels, call(): pl.pallas_call(body, name=name, out_shape=outs, in_specs=in_specs, out_sp...  14.4 us
    ppermute x1, waiting for transfers between devices, local(): partner = lax.ppermute(packed, 'exp', across)  10.4 us
    all_to_all x1, waiting for transfers between devices, local(): beyond = within(far_out)  7.16 us
    all_to_all x1, waiting for transfers between devices, local(): lax.all_to_all(back.reshape(groups, pad, feat), 'exp', split_axis=0, conc...  5.29 us
    ppermute x1, starting transfers between devices, local(): partner = lax.ppermute(packed, 'exp', across)  4.1 us
    all_to_all x1, starting transfers between devices, local(): near = within(near_out)  3.81 us
    all_to_all x1, starting transfers between devices, local(): lax.all_to_all(back.reshape(groups, pad, feat), 'exp', split_axis=0, conc...  3.58 us
    all_to_all x1, starting transfers between devices, local(): beyond = within(far_out)  3.49 us
  transfers between devices with their start and end apart: 6, of which 4 were waited for; matrix products, arithmetic and copies ran while one was open for 0% of the time, Pallas kernels for 24%

profile of v4, /device:TPU:0, one launch (start us, length us, event | category | flops | bytes accessed | tf_op | source)
XLA Modules:
  0.0 68.0 jit_solution(2244941164177694556)
XLA Ops:
  0.6 0.7 %bitcast_convert_fusion = bf16[2,160]{1,0:T(2,128)(2,1)S(1)} fusion(s32[160,2]{0,1:T(2,128)} %param.8), kind=kLoop, calls=%fused_computation.9 | loop fusion | flops 320 | bytes 1920 | tf_op jit(solution)/shard_map/convert_element_type | solution.py:258
  1.3 0.7 %fusion.5 = bf16[16,512]{1,0:T(8,128)(2,1)S(1)} fusion(bf16[2,160]{1,0:T(2,128)(2,1)} %bitcast.6, bf16[2,160]{1,0:T(2,128)(2,1)S(1)} %bitcast_convert_fusion), kind=kLoop, calls=%fused_computation.8 | loop fusion | flops 90112 | bytes 17664 | tf_op jit(solution)/shard_map/concatenate | solution.py:258
  2.0 1.0 %pad_maximum_fusion.packed_ref = bf16[336,512]{1,0:T(8,128)(2,1)S(1)} fusion(bf16[16,512]{1,0:T(8,128)(2,1)S(1)} %fusion.5, bf16[160,512]{1,0:T(8,128)(2,1)} %param.9, bf16[160,512]{1,0:T(8,128)(2,1)} %param.6), kind=kLoop, calls=%fused_computation | loop fusion | flops 1032192 | bytes 688128 | tf_op jit(solution)/shard_map/concatenate | solution.py:260
  3.0 4.1 %collective-permute-start = (bf16[336,512]{1,0:T(8,128)(2,1)S(1)}, bf16[336,512]{1,0:T(8,128)(2,1)S(1)}, u32[]{:S(2)}, u32[]{:S(2)}) collective-permute-start(bf16[336,512]{1,0:T(8,128)(2,1)S(1)} %pad_maximum_fusion.packed_ref), channel_id=1, source_target_pairs={{0,8},{1,9},{2,10},{3,11},{4,12},{5,13},{6,14},{7,15},{8,0},{9,1},... | collective-permute-start | bytes 1032200 | tf_op jit(solution)/shard_map/ppermute | solution.py:261
  7.1 1.3 %near_slots.1 = bf16[8,64,512]{2,1,0:T(8,128)(2,1)} custom-call(bf16[336,512]{1,0:T(8,128)(2,1)S(1)} %pad_maximum_fusion.packed_ref), custom_call_target="tpu_custom_call" | custom-call | flops 83886080 | bytes 868352 | tf_op jit(solution)/shard_map/near_slots/pallas_call | solution.py:33
  8.4 3.8 %all-to-all-start = ((bf16[8,64,512]{2,1,0:T(8,128)(2,1)}), bf16[8,64,512]{2,1,0:T(8,128)(2,1)S(1)}, u32[]{:S(2)}, u32[]{:S(2)}) async-start(bf16[8,64,512]{2,1,0:T(8,128)(2,1)} %near_slots.1), calls=%async_computation | async-start | bytes 1048576 | tf_op jit(solution)/shard_map/all_to_all | solution.py:276
  12.2 10.4 %collective-permute-done.packed_ref = bf16[336,512]{1,0:T(8,128)(2,1)S(1)} collective-permute-done((bf16[336,512]{1,0:T(8,128)(2,1)S(1)}, bf16[336,512]{1,0:T(8,128)(2,1)S(1)}, u32[]{:S(2)}, u32[]{:S(2)}) %collective-permute-start) | collective-permute-done | bytes 344096 | tf_op jit(solution)/shard_map/ppermute | solution.py:261
  22.7 1.3 %far_slots.1 = bf16[8,64,512]{2,1,0:T(8,128)(2,1)} custom-call(bf16[336,512]{1,0:T(8,128)(2,1)S(1)} %collective-permute-done.packed_ref), custom_call_target="tpu_custom_call" | custom-call | flops 99999997952 | bytes 868352 | tf_op jit(solution)/shard_map/far_slots/pallas_call | solution.py:33
  23.9 3.3 %all-to-all-done.disp_ref.near_ref = bf16[8,64,512]{2,1,0:T(8,128)(2,1)S(1)} async-done(((bf16[8,64,512]{2,1,0:T(8,128)(2,1)}), bf16[8,64,512]{2,1,0:T(8,128)(2,1)S(1)}, u32[]{:S(2)}, u32[]{:S(2)}) %all-to-all-start) | async-done | bytes 524320 | tf_op jit(solution)/shard_map/all_to_all | solution.py:276
  27.3 3.5 %all-to-all-start.1 = ((bf16[8,64,512]{2,1,0:T(8,128)(2,1)}), bf16[8,64,512]{2,1,0:T(8,128)(2,1)S(1)}, u32[]{:S(2)}, u32[]{:S(2)}) async-start(bf16[8,64,512]{2,1,0:T(8,128)(2,1)} %far_slots.1), calls=%async_computation.1 | async-start | bytes 1048576 | tf_op jit(solution)/shard_map/all_to_all | solution.py:284
  30.8 1.6 %collective-permute-start.1 = (bf16[8,64,512]{2,1,0:T(8,128)(2,1)S(1)}, bf16[8,64,512]{2,1,0:T(8,128)(2,1)S(1)}, u32[]{:S(2)}, u32[]{:S(2)}) collective-permute-start(bf16[8,64,512]{2,1,0:T(8,128)(2,1)S(1)} %all-to-all-done.disp_ref.near_ref), channel_id=1, source_target_pairs={{0,16},{16,0},{1,17},{17,1},{2,18},{18,2},{3,19},{19,3},{4,20},{20... | collective-permute-start | bytes 1572872 | tf_op jit(solution)/shard_map/ppermute | solution.py:280
  32.4 7.2 %all-to-all-done.1.disp_ref.far_ref = bf16[8,64,512]{2,1,0:T(8,128)(2,1)S(1)} async-done(((bf16[8,64,512]{2,1,0:T(8,128)(2,1)}), bf16[8,64,512]{2,1,0:T(8,128)(2,1)S(1)}, u32[]{:S(2)}, u32[]{:S(2)}) %all-to-all-start.1) | async-done | bytes 524320 | tf_op jit(solution)/shard_map/all_to_all | solution.py:284
  39.5 1.5 %collective-permute-start.2 = (bf16[8,64,512]{2,1,0:T(8,128)(2,1)S(1)}, bf16[8,64,512]{2,1,0:T(8,128)(2,1)S(1)}, u32[]{:S(2)}, u32[]{:S(2)}) collective-permute-start(bf16[8,64,512]{2,1,0:T(8,128)(2,1)S(1)} %all-to-all-done.1.disp_ref.far_ref), channel_id=1, source_target_pairs={{0,16},{16,0},{1,17},{17,1},{2,18},{18,2},{3,19},{19,3},{4,20},{20... | collective-permute-start | bytes 1572872 | tf_op jit(solution)/shard_map/ppermute | solution.py:285
  41.1 4.9 %near_backward.1 = (bf16[8,32,512]{2,1,0:T(8,128)(2,1)S(1)}, bf16[512,160]{1,0:T(8,128)(2,1)S(1)}, bf16[2048,512]{1,0:T(8,128)(2,1)S(1)}, bf16[2048,512]{1,0:T(8,128)(2,1)S(1)}) custom-call(bf16[336,512]{1,0:T(8,128)(2,1)S(1)} %pad_maximum_fusion.packed_ref, bf16[8,64,512]{2,1,0:T(8,128)(2,1)S(1)} %all-to-all-done.disp_ref.near_ref, ...), custom_call_target="tpu_custom_call" | custom-call | flops 1610612736 | bytes 9682944 | tf_op jit(solution)/shard_map/near_backward/pallas_call | solution.py:33
  46.0 0.0 copy-start.2
  46.0 0.0 copy-start.4
  46.0 3.0 %far_backward.1 = bf16[2,8,32,512]{3,2,1,0:T(8,128)(2,1)} custom-call(bf16[8,32,512]{2,1,0:T(8,128)(2,1)S(1)} %get-tuple-element.15.near_ref, bf16[8,64,512]{2,1,0:T(8,128)(2,1)S(1)} %all-to-all-done.1.disp_ref.far_ref, bf16[2048,512]{1,0:T(8,128)(2,1)S(1)} %get-tuple-element.16.up_ref.refs_2_, bf16[2048,512]{1,0:T(8,128)(2,1)S(1)} %get-tuple-element.17.down_ref.refs_3_), custom_call_target="tpu_custom_call" | custom-call | flops 1610612736 | bytes 4194304 | tf_op jit(solution)/shard_map/far_backward/pallas_call | solution.py:299
  49.0 0.0 copy-done.2
  49.0 0.0 copy-done.4
  49.0 3.6 %all-to-all-start.2 = ((bf16[16,32,512]{2,1,0:T(8,128)(2,1)}), bf16[16,32,512]{2,1,0:T(8,128)(2,1)S(1)}, u32[]{:S(2)}, u32[]{:S(2)}) async-start(bf16[16,32,512]{2,1,0:T(8,128)(2,1)} %bitcast.8), calls=%async_computation.2 | async-start | bytes 1048576 | tf_op jit(solution)/shard_map/all_to_all | solution.py:313
  52.6 0.0 copy-start.3
  52.6 1.6 %copy-done.3 = bf16[2048,512]{1,0:T(8,128)(2,1)S(1)} copy-done((bf16[2048,512]{1,0:T(8,128)(2,1)S(1)}, bf16[2048,512]{1,0:T(8,128)(2,1)}, u32[]{:S(2)}) %copy-start.3) | copy-done | bytes 2097176
  54.2 0.0 copy-start.5
  54.2 1.6 %copy-done.5 = bf16[2048,512]{1,0:T(8,128)(2,1)S(1)} copy-done((bf16[2048,512]{1,0:T(8,128)(2,1)S(1)}, bf16[2048,512]{1,0:T(8,128)(2,1)}, u32[]{:S(2)}) %copy-start.5) | copy-done | bytes 2097176
  55.8 2.4 %own_weights.1 = (f32[1024,512]{1,0:T(8,128)S(1)}, f32[1024,512]{1,0:T(8,128)S(1)}) custom-call(bf16[8,64,512]{2,1,0:T(8,128)(2,1)S(1)} %all-to-all-done.disp_ref.near_ref, bf16[8,64,512]{2,1,0:T(8,128)(2,1)S(1)} %all-to-all-done.1.disp_ref.far_ref, bf16[2048,512]{1,0:T(8,128)(2,1)S(1)} %copy-done.3, bf16[2048,512]{1,0:T(8,128)(2,1)S(1)} %copy-done.5), custom_call_target="tpu_custom_call" | custom-call | flops 2147483648 | bytes 9437184 | tf_op jit(solution)/shard_map/own_weights/pallas_call | solution.py:33
  58.2 0.0 collective-permute-done.1.refs_0_
  58.2 0.0 collective-permute-done.2.refs_1_
  58.2 0.0 copy-start
  58.3 0.0 copy-start.1
  58.3 3.5 %other_weights.1 = (bf16[1,1024,512]{2,1,0:T(8,128)(2,1)}, bf16[1,1024,512]{2,1,0:T(8,128)(2,1)}) custom-call(bf16[8,64,512]{2,1,0:T(8,128)(2,1)S(1)} %collective-permute-done.1.refs_0_, bf16[8,64,512]{2,1,0:T(8,128)(2,1)S(1)} %collective-permute-done.2.refs_1_, bf16[2048,512]{1,0:T(8,128)(2,1)S(1)} %copy-done.3, bf16[2048,512]{1,0:T(8,128)(2,1)S(1)} %copy-done.5, ...), custom_call_target="tpu_custom_call" | custom-call | flops 99999997952 | bytes 11534336 | tf_op jit(solution)/shard_map/other_weights/pallas_call | solution.py:33
  61.7 5.3 %all-to-all-done.2.back_ref = bf16[16,32,512]{2,1,0:T(8,128)(2,1)S(1)} async-done(((bf16[16,32,512]{2,1,0:T(8,128)(2,1)}), bf16[16,32,512]{2,1,0:T(8,128)(2,1)S(1)}, u32[]{:S(2)}, u32[]{:S(2)}) %all-to-all-start.2) | async-done | bytes 524320 | tf_op jit(solution)/shard_map/all_to_all | solution.py:313
  67.0 0.0 copy-done
  67.0 0.0 copy-done.1
  67.0 1.0 %combine.1 = (bf16[160,512]{1,0:T(8,128)(2,1)}, bf16[2,160]{1,0:T(2,128)(2,1)}) custom-call(s32[2,160]{1,0:T(2,128)S(1)} %bitcast.5, bf16[2,160]{1,0:T(2,128)(2,1)S(1)} %bitcast.7, bf16[512,160]{1,0:T(8,128)(2,1)S(1)} %get-tuple-element.14.pick_ref, bf16[16,32,512]{2,1,0:T(8,128)(2,1)S(1)} %all-to-all-done.2.back_ref), custom_call_target="tpu_custom_call" | custom-call | flops 83886080 | bytes 854528 | tf_op jit(solution)/shard_map/combine/pallas_call | solution.py:33
Async XLA Ops:
  3.0 19.6 %collective-permute-start = (bf16[336,512]{1,0:T(8,128)(2,1)S(1)}, bf16[336,512]{1,0:T(8,128)(2,1)S(1)}, u32[]{:S(2)}, u32[]{:S(2)}) collective-permute-start(bf16[336,512]{1,0:T(8,128)(2,1)S(1)} %pad_maximum_fusion.packed_ref), channel_id=1, source_target_pairs={{0,8},{1,9},{2,10},{3,11},{4,12},{5,13},{6,14},{7,15},{8,0},{9,1},... | collective-permute-start | bytes 1032200 | tf_op jit(solution)/shard_map/ppermute | solution.py:261
  8.4 18.8 %all-to-all-start = ((bf16[8,64,512]{2,1,0:T(8,128)(2,1)}), bf16[8,64,512]{2,1,0:T(8,128)(2,1)S(1)}, u32[]{:S(2)}, u32[]{:S(2)}) async-start(bf16[8,64,512]{2,1,0:T(8,128)(2,1)} %near_slots.1), calls=%async_computation | async-start | bytes 1048576 | tf_op jit(solution)/shard_map/all_to_all | solution.py:276
  27.3 12.3 %all-to-all-start.1 = ((bf16[8,64,512]{2,1,0:T(8,128)(2,1)}), bf16[8,64,512]{2,1,0:T(8,128)(2,1)S(1)}, u32[]{:S(2)}, u32[]{:S(2)}) async-start(bf16[8,64,512]{2,1,0:T(8,128)(2,1)} %far_slots.1), calls=%async_computation.1 | async-start | bytes 1048576 | tf_op jit(solution)/shard_map/all_to_all | solution.py:284
  30.8 27.5 %collective-permute-start.1 = (bf16[8,64,512]{2,1,0:T(8,128)(2,1)S(1)}, bf16[8,64,512]{2,1,0:T(8,128)(2,1)S(1)}, u32[]{:S(2)}, u32[]{:S(2)}) collective-permute-start(bf16[8,64,512]{2,1,0:T(8,128)(2,1)S(1)} %all-to-all-done.disp_ref.near_ref), channel_id=1, source_target_pairs={{0,16},{16,0},{1,17},{17,1},{2,18},{18,2},{3,19},{19,3},{4,20},{20... | collective-permute-start | bytes 1572872 | tf_op jit(solution)/shard_map/ppermute | solution.py:280
  39.5 18.7 %collective-permute-start.2 = (bf16[8,64,512]{2,1,0:T(8,128)(2,1)S(1)}, bf16[8,64,512]{2,1,0:T(8,128)(2,1)S(1)}, u32[]{:S(2)}, u32[]{:S(2)}) collective-permute-start(bf16[8,64,512]{2,1,0:T(8,128)(2,1)S(1)} %all-to-all-done.1.disp_ref.far_ref), channel_id=1, source_target_pairs={{0,16},{16,0},{1,17},{17,1},{2,18},{18,2},{3,19},{19,3},{4,20},{20... | collective-permute-start | bytes 1572872 | tf_op jit(solution)/shard_map/ppermute | solution.py:285
  46.0 3.0 %copy-start.2 = (bf16[2048,512]{1,0:T(8,128)(2,1)}, bf16[2048,512]{1,0:T(8,128)(2,1)S(1)}, u32[]{:S(2)}) copy-start(bf16[2048,512]{1,0:T(8,128)(2,1)S(1)} %get-tuple-element.16.up_ref.refs_2_) | copy-start | bytes 6291460
  46.0 3.0 %copy-start.4 = (bf16[2048,512]{1,0:T(8,128)(2,1)}, bf16[2048,512]{1,0:T(8,128)(2,1)S(1)}, u32[]{:S(2)}) copy-start(bf16[2048,512]{1,0:T(8,128)(2,1)S(1)} %get-tuple-element.17.down_ref.refs_3_) | copy-start | bytes 6291460
  49.0 18.0 %all-to-all-start.2 = ((bf16[16,32,512]{2,1,0:T(8,128)(2,1)}), bf16[16,32,512]{2,1,0:T(8,128)(2,1)S(1)}, u32[]{:S(2)}, u32[]{:S(2)}) async-start(bf16[16,32,512]{2,1,0:T(8,128)(2,1)} %bitcast.8), calls=%async_computation.2 | async-start | bytes 1048576 | tf_op jit(solution)/shard_map/all_to_all | solution.py:313
  52.6 1.6 %copy-start.3 = (bf16[2048,512]{1,0:T(8,128)(2,1)S(1)}, bf16[2048,512]{1,0:T(8,128)(2,1)}, u32[]{:S(2)}) copy-start(bf16[2048,512]{1,0:T(8,128)(2,1)} %copy-done.2) | copy-start | bytes 6291460
  54.2 1.6 %copy-start.5 = (bf16[2048,512]{1,0:T(8,128)(2,1)S(1)}, bf16[2048,512]{1,0:T(8,128)(2,1)}, u32[]{:S(2)}) copy-start(bf16[2048,512]{1,0:T(8,128)(2,1)} %copy-done.4) | copy-start | bytes 6291460
  58.2 8.8 %copy-start = (s32[160,2]{0,1:T(2,128)S(1)}, s32[160,2]{0,1:T(2,128)}, u32[]{:S(2)}) copy-start(s32[160,2]{0,1:T(2,128)} %param.8) | copy-start | bytes 3844
  58.3 8.8 %copy-start.1 = (bf16[160,2]{0,1:T(2,128)(2,1)S(1)}, bf16[160,2]{0,1:T(2,128)(2,1)}, u32[]{:S(2)}) copy-start(bf16[160,2]{0,1:T(2,128)(2,1)} %param.7) | copy-start | bytes 1924

commit v5 on v4

--- a/solution.py
+++ b/solution.py
@@ -74,6 +74,28 @@
 def unpack(packed_ref, rows):
     notes = packed_ref[2 * rows :, :].astype(F32)
     return notes[0:2, 0:rows].astype(jnp.int32), notes[2:4, 0:rows]
+
+
+def pack_kernel(routes_hbm, gates_hbm, tok_hbm, cot_hbm, out_ref, routes_ref, gates_ref, sems):
+    rows, feat = tok_hbm.shape
+    pairs = [
+        (routes_hbm, routes_ref),
+        (gates_hbm, gates_ref),
+        (tok_hbm, out_ref.at[0:rows, :]),
+        (cot_hbm, out_ref.at[rows : 2 * rows, :]),
+    ]
+    copies = [
+        pltpu.make_async_copy(src, dst, sems.at[i]) for i, (src, dst) in enumerate(pairs)
+    ]
+    for copy in copies:
+        copy.start()
+    copies[0].wait()
+    copies[1].wait()
+    notes = [routes_ref[...].astype(F32), gates_ref[...].astype(F32), jnp.zeros((12, rows), F32)]
+    out_ref[2 * rows :, 0:rows] = jnp.concatenate(notes, axis=0).astype(BF16)
+    out_ref[2 * rows :, rows:] = jnp.zeros((16, feat - rows), BF16)
+    copies[2].wait()
+    copies[3].wait()
 
 
 def slots_kernel(rows, packed_ref, out_ref):
@@ -255,9 +277,17 @@
     weight = shape((hidden, feat), BF16)
 
     across = [(i, (i + half) % groups) for i in range(groups)]
-    notes = jnp.concatenate([routes_t.astype(BF16), gates_t], axis=0)
-    notes = jnp.pad(notes, ((0, 12), (0, feat - rows)))
-    packed = jnp.concatenate([tokens, cotangent, notes], axis=0)
+    (packed,) = call(
+        pack_kernel,
+        "pack",
+        [shape((2 * rows + 16, feat), BF16)],
+        [far(a) for a in (routes_t, gates_t, tokens, cotangent)],
+        [IN_HBM] * 4,
+        [pltpu.VMEM((2, rows), jnp.int32), pltpu.VMEM((2, rows), BF16), DMA((4,))],
+        0,
+        0,
+        SMALL,
+    )
     partner = lax.ppermute(packed, "exp", across)
 
     slots_call = functools.partial(call, functools.partial(slots_kernel, rows))
@@ -305,7 +335,7 @@
         scratch_shapes=[pltpu.VMEM((half, pad, feat), BF16)] + scratch + [DMA((2,))],
         compiler_params=pltpu.CompilerParams(vmem_limit_bytes=MEDIUM),
         cost_estimate=pl.CostEstimate(
-            flops=3 * unit * hidden,
+            flops=AHEAD,
             bytes_accessed=4 * hidden * feat,
             transcendentals=slots * hidden,
         ),

time: 68.6 us -> 65.7 us (0.958)
  waiting for transfers between devices: 26.2 us -> 19.1 us
  local copies, waits for them, and re-layouts: 3.2 us -> 9.01 us
  other arithmetic: 2.4 us -> 0 us
  Pallas kernels: 17.4 us -> 18.5 us
    all_to_all x1, waiting for transfers between devices: 7.16 us -> 0.01 us  [local(): beyond = within(far_out)]
    unnamed x12 -> x16, local copies, waits for them, and re-layouts: 3.2 us -> 9.01 us
    concatenate x2 -> x0, other arithmetic: 1.71 us -> none  [the longest x1 1.02 us: local(): packed = jnp.concatenate([tokens, cotangent, notes], axis=0)]
    pallas_call x6 -> x7, Pallas kernels: 14.4 us -> 15.4 us  [call(): pl.pallas_call(body, name=name, out_shape=outs, in_specs=in_specs, out_sp...]
    convert_element_type x1 -> x0, other arithmetic: 0.69 us -> none  [local(): notes = jnp.concatenate([routes_t.astype(BF16), gates_t], axis=0)]
  transfers between devices with their start and end apart: 6 -> 6, of which waited for: 4 -> 3; matrix products, arithmetic and copies ran while one was open for 0% -> 0% of each run, Pallas kernels for 24% -> 25%
where the time goes in v5:
time: 65.7 us; the launch traced here: 65.1 us
  waiting for transfers between devices  19.1 us (29%)
  Pallas kernels  18.5 us (28%)
  starting transfers between devices  17.8 us (27%)
  local copies, waits for them, and re-layouts  9.01 us (14%)
  between operations  0.73 us (1%)
    pallas_call x7, Pallas kernels, call(): pl.pallas_call(body, name=name, out_shape=outs, in_specs=in_specs, out_sp...  15.4 us
    ppermute x1, waiting for transfers between devices, local(): partner = lax.ppermute(packed, 'exp', across)  10.4 us
    unnamed x16, local copies, waits for them, and re-layouts  9.01 us
    all_to_all x1, waiting for transfers between devices, local(): lax.all_to_all(back.reshape(groups, pad, feat), 'exp', split_axis=0, conc...  5.33 us
    ppermute x1, starting transfers between devices, local(): partner = lax.ppermute(packed, 'exp', across)  4.1 us
    all_to_all x1, starting transfers between devices, local(): near = within(near_out)  3.81 us
    all_to_all x1, starting transfers between devices, local(): lax.all_to_all(back.reshape(groups, pad, feat), 'exp', split_axis=0, conc...  3.71 us
    all_to_all x1, starting transfers between devices, local(): beyond = within(far_out)  3.49 us
  transfers between devices with their start and end apart: 6, of which 3 were waited for; matrix products, arithmetic and copies ran while one was open for 0% of the time, Pallas kernels for 25%

profile of v5, /device:TPU:0, one launch (start us, length us, event | category | flops | bytes accessed | tf_op | source)
XLA Modules:
  0.0 65.1 jit_solution(552302283118516390)
XLA Ops:
  0.6 1.1 %pack.1.packed_ref = bf16[336,512]{1,0:T(8,128)(2,1)S(1)} custom-call(s32[2,160]{1,0:T(2,128)} %bitcast.4, bf16[2,160]{1,0:T(2,128)(2,1)} %bitcast.6, bf16[160,512]{1,0:T(8,128)(2,1)} %tok_hbm.1, bf16[160,512]{1,0:T(8,128)(2,1)} %cot_hbm.1), custom_call_target="tpu_custom_call" | custom-call | bytes 673664 | tf_op jit(solution)/shard_map/pack/pallas_call | solution.py:33
  1.7 4.1 %collective-permute-start = (bf16[336,512]{1,0:T(8,128)(2,1)S(1)}, bf16[336,512]{1,0:T(8,128)(2,1)S(1)}, u32[]{:S(2)}, u32[]{:S(2)}) collective-permute-start(bf16[336,512]{1,0:T(8,128)(2,1)S(1)} %pack.1.packed_ref), channel_id=1, source_target_pairs={{0,8},{1,9},{2,10},{3,11},{4,12},{5,13},{6,14},{7,15},{8,0},{9,1},... | collective-permute-start | bytes 1032200 | tf_op jit(solution)/shard_map/ppermute | solution.py:291
  5.8 1.3 %near_slots.1 = bf16[8,64,512]{2,1,0:T(8,128)(2,1)} custom-call(bf16[336,512]{1,0:T(8,128)(2,1)S(1)} %pack.1.packed_ref), custom_call_target="tpu_custom_call" | custom-call | flops 83886080 | bytes 868352 | tf_op jit(solution)/shard_map/near_slots/pallas_call | solution.py:33
  7.1 3.8 %all-to-all-start = ((bf16[8,64,512]{2,1,0:T(8,128)(2,1)}), bf16[8,64,512]{2,1,0:T(8,128)(2,1)S(1)}, u32[]{:S(2)}, u32[]{:S(2)}) async-start(bf16[8,64,512]{2,1,0:T(8,128)(2,1)} %near_slots.1), calls=%async_computation | async-start | bytes 1048576 | tf_op jit(solution)/shard_map/all_to_all | solution.py:306
  10.9 10.4 %collective-permute-done.packed_ref = bf16[336,512]{1,0:T(8,128)(2,1)S(1)} collective-permute-done((bf16[336,512]{1,0:T(8,128)(2,1)S(1)}, bf16[336,512]{1,0:T(8,128)(2,1)S(1)}, u32[]{:S(2)}, u32[]{:S(2)}) %collective-permute-start) | collective-permute-done | bytes 344096 | tf_op jit(solution)/shard_map/ppermute | solution.py:291
  21.3 1.3 %far_slots.1 = bf16[8,64,512]{2,1,0:T(8,128)(2,1)} custom-call(bf16[336,512]{1,0:T(8,128)(2,1)S(1)} %collective-permute-done.packed_ref), custom_call_target="tpu_custom_call" | custom-call | flops 99999997952 | bytes 868352 | tf_op jit(solution)/shard_map/far_slots/pallas_call | solution.py:33
  22.6 3.3 %all-to-all-done.disp_ref.near_ref = bf16[8,64,512]{2,1,0:T(8,128)(2,1)S(1)} async-done(((bf16[8,64,512]{2,1,0:T(8,128)(2,1)}), bf16[8,64,512]{2,1,0:T(8,128)(2,1)S(1)}, u32[]{:S(2)}, u32[]{:S(2)}) %all-to-all-start) | async-done | bytes 524320 | tf_op jit(solution)/shard_map/all_to_all | solution.py:306
  25.9 3.5 %all-to-all-start.1 = ((bf16[8,64,512]{2,1,0:T(8,128)(2,1)}), bf16[8,64,512]{2,1,0:T(8,128)(2,1)S(1)}, u32[]{:S(2)}, u32[]{:S(2)}) async-start(bf16[8,64,512]{2,1,0:T(8,128)(2,1)} %far_slots.1), calls=%async_computation.1 | async-start | bytes 1048576 | tf_op jit(solution)/shard_map/all_to_all | solution.py:314
  29.4 1.6 %collective-permute-start.1 = (bf16[8,64,512]{2,1,0:T(8,128)(2,1)S(1)}, bf16[8,64,512]{2,1,0:T(8,128)(2,1)S(1)}, u32[]{:S(2)}, u32[]{:S(2)}) collective-permute-start(bf16[8,64,512]{2,1,0:T(8,128)(2,1)S(1)} %all-to-all-done.disp_ref.near_ref), channel_id=1, source_target_pairs={{0,16},{16,0},{1,17},{17,1},{2,18},{18,2},{3,19},{19,3},{4,20},{20... | collective-permute-start | bytes 1572872 | tf_op jit(solution)/shard_map/ppermute | solution.py:310
  31.0 4.9 %near_backward.1 = (bf16[8,32,512]{2,1,0:T(8,128)(2,1)S(1)}, bf16[512,160]{1,0:T(8,128)(2,1)S(1)}, bf16[2048,512]{1,0:T(8,128)(2,1)S(1)}, bf16[2048,512]{1,0:T(8,128)(2,1)S(1)}) custom-call(bf16[336,512]{1,0:T(8,128)(2,1)S(1)} %pack.1.packed_ref, bf16[8,64,512]{2,1,0:T(8,128)(2,1)S(1)} %all-to-all-done.disp_ref.near_ref, bf16[1,2048,512]{2,1,0:T(8,128)(2,1)} %up_hbm.1, ...), custom_call_target="tpu_custom_call" | custom-call | flops 1610612736 | bytes 9682944 | tf_op jit(solution)/shard_map/near_backward/pallas_call | solution.py:33
  36.0 0.0 copy-start.2
  36.0 1.3 %copy-done.2 = bf16[2048,512]{1,0:T(8,128)(2,1)} copy-done((bf16[2048,512]{1,0:T(8,128)(2,1)}, bf16[2048,512]{1,0:T(8,128)(2,1)S(1)}, u32[]{:S(2)}) %copy-start.2) | copy-done | bytes 2097176
  37.3 0.0 copy-start.5
  37.3 1.3 %copy-done.5 = bf16[2048,512]{1,0:T(8,128)(2,1)} copy-done((bf16[2048,512]{1,0:T(8,128)(2,1)}, bf16[2048,512]{1,0:T(8,128)(2,1)S(1)}, u32[]{:S(2)}) %copy-start.5) | copy-done | bytes 2097176
  38.6 0.0 all-to-all-done.1.disp_ref.far_ref
  38.6 1.1 %collective-permute-start.2 = (bf16[8,64,512]{2,1,0:T(8,128)(2,1)S(1)}, bf16[8,64,512]{2,1,0:T(8,128)(2,1)S(1)}, u32[]{:S(2)}, u32[]{:S(2)}) collective-permute-start(bf16[8,64,512]{2,1,0:T(8,128)(2,1)S(1)} %all-to-all-done.1.disp_ref.far_ref), channel_id=1, source_target_pairs={{0,16},{16,0},{1,17},{17,1},{2,18},{18,2},{3,19},{19,3},{4,20},{20... | collective-permute-start | bytes 1572872 | tf_op jit(solution)/shard_map/ppermute | solution.py:315
  39.7 0.0 copy-start.3
  39.7 1.6 %copy-done.3 = bf16[2048,512]{1,0:T(8,128)(2,1)S(1)} copy-done((bf16[2048,512]{1,0:T(8,128)(2,1)S(1)}, bf16[2048,512]{1,0:T(8,128)(2,1)}, u32[]{:S(2)}) %copy-start.3) | copy-done | bytes 2097176
  41.3 0.0 copy-start.6
  41.3 1.6 %copy-done.6 = bf16[2048,512]{1,0:T(8,128)(2,1)S(1)} copy-done((bf16[2048,512]{1,0:T(8,128)(2,1)S(1)}, bf16[2048,512]{1,0:T(8,128)(2,1)}, u32[]{:S(2)}) %copy-start.6) | copy-done | bytes 2097176
  42.9 3.0 %far_backward.1 = bf16[2,8,32,512]{3,2,1,0:T(8,128)(2,1)} custom-call(bf16[8,32,512]{2,1,0:T(8,128)(2,1)S(1)} %get-tuple-element.15.near_ref, bf16[8,64,512]{2,1,0:T(8,128)(2,1)S(1)} %all-to-all-done.1.disp_ref.far_ref, bf16[2048,512]{1,0:T(8,128)(2,1)S(1)} %copy-done.3, bf16[2048,512]{1,0:T(8,128)(2,1)S(1)} %copy-done.6), custom_call_target="tpu_custom_call" | custom-call | flops 99999997952 | bytes 4194304 | tf_op jit(solution)/shard_map/far_backward/pallas_call | solution.py:329
  45.9 3.7 %all-to-all-start.2 = ((bf16[16,32,512]{2,1,0:T(8,128)(2,1)}), bf16[16,32,512]{2,1,0:T(8,128)(2,1)S(1)}, u32[]{:S(2)}, u32[]{:S(2)}) async-start(bf16[16,32,512]{2,1,0:T(8,128)(2,1)} %bitcast.8), calls=%async_computation.2 | async-start | bytes 1048576 | tf_op jit(solution)/shard_map/all_to_all | solution.py:343
  49.7 0.0 copy-start.4
  49.7 1.6 %copy-done.4 = bf16[2048,512]{1,0:T(8,128)(2,1)S(1)} copy-done((bf16[2048,512]{1,0:T(8,128)(2,1)S(1)}, bf16[2048,512]{1,0:T(8,128)(2,1)}, u32[]{:S(2)}) %copy-start.4) | copy-done | bytes 2097176
  51.3 0.0 copy-start.7
  51.3 1.6 %copy-done.7 = bf16[2048,512]{1,0:T(8,128)(2,1)S(1)} copy-done((bf16[2048,512]{1,0:T(8,128)(2,1)S(1)}, bf16[2048,512]{1,0:T(8,128)(2,1)}, u32[]{:S(2)}) %copy-start.7) | copy-done | bytes 2097176
  52.8 2.4 %own_weights.1 = (f32[1024,512]{1,0:T(8,128)S(1)}, f32[1024,512]{1,0:T(8,128)S(1)}) custom-call(bf16[8,64,512]{2,1,0:T(8,128)(2,1)S(1)} %all-to-all-done.disp_ref.near_ref, bf16[8,64,512]{2,1,0:T(8,128)(2,1)S(1)} %all-to-all-done.1.disp_ref.far_ref, bf16[2048,512]{1,0:T(8,128)(2,1)S(1)} %copy-done.4, bf16[2048,512]{1,0:T(8,128)(2,1)S(1)} %copy-done.7), custom_call_target="tpu_custom_call" | custom-call | flops 2147483648 | bytes 9437184 | tf_op jit(solution)/shard_map/own_weights/pallas_call | solution.py:33
  55.3 0.0 collective-permute-done.1.refs_0_
  55.3 0.0 collective-permute-done.2.refs_1_
  55.3 0.0 copy-start
  55.3 0.0 copy-start.1
  55.3 3.5 %other_weights.1 = (bf16[1,1024,512]{2,1,0:T(8,128)(2,1)}, bf16[1,1024,512]{2,1,0:T(8,128)(2,1)}) custom-call(bf16[8,64,512]{2,1,0:T(8,128)(2,1)S(1)} %collective-permute-done.1.refs_0_, bf16[8,64,512]{2,1,0:T(8,128)(2,1)S(1)} %collective-permute-done.2.refs_1_, bf16[2048,512]{1,0:T(8,128)(2,1)S(1)} %copy-done.4, bf16[2048,512]{1,0:T(8,128)(2,1)S(1)} %copy-done.7, ...), custom_call_target="tpu_custom_call" | custom-call | flops 99999997952 | bytes 11534336 | tf_op jit(solution)/shard_map/other_weights/pallas_call | solution.py:33
  58.8 5.3 %all-to-all-done.2.back_ref = bf16[16,32,512]{2,1,0:T(8,128)(2,1)S(1)} async-done(((bf16[16,32,512]{2,1,0:T(8,128)(2,1)}), bf16[16,32,512]{2,1,0:T(8,128)(2,1)S(1)}, u32[]{:S(2)}, u32[]{:S(2)}) %all-to-all-start.2) | async-done | bytes 524320 | tf_op jit(solution)/shard_map/all_to_all | solution.py:343
  64.1 0.0 copy-done
  64.1 0.0 copy-done.1
  64.1 1.0 %combine.1 = (bf16[160,512]{1,0:T(8,128)(2,1)}, bf16[2,160]{1,0:T(2,128)(2,1)}) custom-call(s32[2,160]{1,0:T(2,128)S(1)} %bitcast.5, bf16[2,160]{1,0:T(2,128)(2,1)S(1)} %bitcast.7, bf16[512,160]{1,0:T(8,128)(2,1)S(1)} %get-tuple-element.14.pick_ref, bf16[16,32,512]{2,1,0:T(8,128)(2,1)S(1)} %all-to-all-done.2.back_ref), custom_call_target="tpu_custom_call" | custom-call | flops 83886080 | bytes 854528 | tf_op jit(solution)/shard_map/combine/pallas_call | solution.py:33
Async XLA Ops:
  1.7 19.6 %collective-permute-start = (bf16[336,512]{1,0:T(8,128)(2,1)S(1)}, bf16[336,512]{1,0:T(8,128)(2,1)S(1)}, u32[]{:S(2)}, u32[]{:S(2)}) collective-permute-start(bf16[336,512]{1,0:T(8,128)(2,1)S(1)} %pack.1.packed_ref), channel_id=1, source_target_pairs={{0,8},{1,9},{2,10},{3,11},{4,12},{5,13},{6,14},{7,15},{8,0},{9,1},... | collective-permute-start | bytes 1032200 | tf_op jit(solution)/shard_map/ppermute | solution.py:291
  7.1 18.8 %all-to-all-start = ((bf16[8,64,512]{2,1,0:T(8,128)(2,1)}), bf16[8,64,512]{2,1,0:T(8,128)(2,1)S(1)}, u32[]{:S(2)}, u32[]{:S(2)}) async-start(bf16[8,64,512]{2,1,0:T(8,128)(2,1)} %near_slots.1), calls=%async_computation | async-start | bytes 1048576 | tf_op jit(solution)/shard_map/all_to_all | solution.py:306
  25.9 12.7 %all-to-all-start.1 = ((bf16[8,64,512]{2,1,0:T(8,128)(2,1)}), bf16[8,64,512]{2,1,0:T(8,128)(2,1)S(1)}, u32[]{:S(2)}, u32[]{:S(2)}) async-start(bf16[8,64,512]{2,1,0:T(8,128)(2,1)} %far_slots.1), calls=%async_computation.1 | async-start | bytes 1048576 | tf_op jit(solution)/shard_map/all_to_all | solution.py:314
  29.4 25.8 %collective-permute-start.1 = (bf16[8,64,512]{2,1,0:T(8,128)(2,1)S(1)}, bf16[8,64,512]{2,1,0:T(8,128)(2,1)S(1)}, u32[]{:S(2)}, u32[]{:S(2)}) collective-permute-start(bf16[8,64,512]{2,1,0:T(8,128)(2,1)S(1)} %all-to-all-done.disp_ref.near_ref), channel_id=1, source_target_pairs={{0,16},{16,0},{1,17},{17,1},{2,18},{18,2},{3,19},{19,3},{4,20},{20... | collective-permute-start | bytes 1572872 | tf_op jit(solution)/shard_map/ppermute | solution.py:310
  36.0 1.3 %copy-start.2 = (bf16[2048,512]{1,0:T(8,128)(2,1)}, bf16[2048,512]{1,0:T(8,128)(2,1)S(1)}, u32[]{:S(2)}) copy-start(bf16[2048,512]{1,0:T(8,128)(2,1)S(1)} %get-tuple-element.16.up_ref.refs_2_) | copy-start | bytes 6291460
  37.3 1.3 %copy-start.5 = (bf16[2048,512]{1,0:T(8,128)(2,1)}, bf16[2048,512]{1,0:T(8,128)(2,1)S(1)}, u32[]{:S(2)}) copy-start(bf16[2048,512]{1,0:T(8,128)(2,1)S(1)} %get-tuple-element.17.down_ref.refs_3_) | copy-start | bytes 6291460
  38.6 16.7 %collective-permute-start.2 = (bf16[8,64,512]{2,1,0:T(8,128)(2,1)S(1)}, bf16[8,64,512]{2,1,0:T(8,128)(2,1)S(1)}, u32[]{:S(2)}, u32[]{:S(2)}) collective-permute-start(bf16[8,64,512]{2,1,0:T(8,128)(2,1)S(1)} %all-to-all-done.1.disp_ref.far_ref), channel_id=1, source_target_pairs={{0,16},{16,0},{1,17},{17,1},{2,18},{18,2},{3,19},{19,3},{4,20},{20... | collective-permute-start | bytes 1572872 | tf_op jit(solution)/shard_map/ppermute | solution.py:315
  39.7 1.6 %copy-start.3 = (bf16[2048,512]{1,0:T(8,128)(2,1)S(1)}, bf16[2048,512]{1,0:T(8,128)(2,1)}, u32[]{:S(2)}) copy-start(bf16[2048,512]{1,0:T(8,128)(2,1)} %copy-done.2) | copy-start | bytes 6291460
  41.3 1.6 %copy-start.6 = (bf16[2048,512]{1,0:T(8,128)(2,1)S(1)}, bf16[2048,512]{1,0:T(8,128)(2,1)}, u32[]{:S(2)}) copy-start(bf16[2048,512]{1,0:T(8,128)(2,1)} %copy-done.5) | copy-start | bytes 6291460
  45.9 18.2 %all-to-all-start.2 = ((bf16[16,32,512]{2,1,0:T(8,128)(2,1)}), bf16[16,32,512]{2,1,0:T(8,128)(2,1)S(1)}, u32[]{:S(2)}, u32[]{:S(2)}) async-start(bf16[16,32,512]{2,1,0:T(8,128)(2,1)} %bitcast.8), calls=%async_computation.2 | async-start | bytes 1048576 | tf_op jit(solution)/shard_map/all_to_all | solution.py:343
  49.7 1.6 %copy-start.4 = (bf16[2048,512]{1,0:T(8,128)(2,1)S(1)}, bf16[2048,512]{1,0:T(8,128)(2,1)}, u32[]{:S(2)}) copy-start(bf16[2048,512]{1,0:T(8,128)(2,1)} %copy-done.2) | copy-start | bytes 6291460
  51.3 1.6 %copy-start.7 = (bf16[2048,512]{1,0:T(8,128)(2,1)S(1)}, bf16[2048,512]{1,0:T(8,128)(2,1)}, u32[]{:S(2)}) copy-start(bf16[2048,512]{1,0:T(8,128)(2,1)} %copy-done.5) | copy-start | bytes 6291460
  55.3 8.8 %copy-start = (s32[160,2]{0,1:T(2,128)S(1)}, s32[160,2]{0,1:T(2,128)}, u32[]{:S(2)}) copy-start(s32[160,2]{0,1:T(2,128)} %param.8) | copy-start | bytes 3844
  55.3 8.8 %copy-start.1 = (bf16[160,2]{0,1:T(2,128)(2,1)S(1)}, bf16[160,2]{0,1:T(2,128)(2,1)}, u32[]{:S(2)}) copy-start(bf16[160,2]{0,1:T(2,128)(2,1)} %param.7) | copy-start | bytes 1924

commit v6 on v5

--- a/solution.py
+++ b/solution.py
@@ -1,4 +1,5 @@
 import functools
+import math
 
 import jax
 import jax.numpy as jnp
@@ -29,7 +30,7 @@
 
 
 def call(body, name, outs, args, in_specs, scratch, flops, transcendentals=0, limit=MEDIUM):
-    moved = sum(a.size * a.dtype.itemsize for a in (*args, *outs))
+    moved = sum(math.prod(a.shape) * a.dtype.itemsize for a in (*args, *outs))
     return pl.pallas_call(
         body,
         name=name,
@@ -114,6 +115,19 @@
     out_ref[:, pad:, :] = dot(scaled, cot, 1, 0).astype(BF16).reshape(experts, pad, feat)
 
 
+def fetch_kernel(up_hbm, down_hbm, up_ref, down_ref, sems):
+    copies = []
+    for i, (src, dst) in enumerate([(up_hbm, up_ref), (down_hbm, down_ref)]):
+        copies.append(pltpu.make_async_copy(src.at[0], dst, sems.at[i]))
+        copies[i].start()
+    for copy in copies:
+        copy.wait()
+
+
+def far_slots_kernel(rows, packed_ref, _, out_ref):
+    slots_kernel(rows, packed_ref, out_ref)
+
+
 def split_rows(ref):
     experts, both, feat = ref.shape
     pad = both // 2
@@ -123,19 +137,15 @@
     )
 
 
-def backward(cap, block, disp_ref, up_ref, down_ref, grad_acc, gate_acc, put, copies=()):
+def backward(cap, block, disp_ref, up_ref, down_ref, grad_acc, gate_acc, put):
     origins, both, feat = disp_ref.shape
     pad = both // 2
     slots = origins * pad
     rows, grads = split_rows(disp_ref)
     for step in range(up_ref.shape[0] // block):
         part = pl.ds(step * block, block)
-        if copies:
-            copies[2 * step].wait()
         up = up_ref[part, :]
         active, slope = silu_parts(dot(rows, up, 1, 1))
-        if copies:
-            copies[2 * step + 1].wait()
         back = dot(grads, down_ref[part, :], 1, 1)
         hid_grad = (back * slope).astype(BF16)
         gate = active.astype(BF16).astype(F32) * back
@@ -159,21 +169,14 @@
         put(k, first.astype(BF16), grad_acc[here, 128:].astype(BF16))
 
 
-def near_back_kernel(cap, block, rows, packed_ref, disp_ref, up_hbm, down_hbm, *refs):
-    out_ref, pick_ref, up_ref, down_ref, grad_acc, gate_acc, sems = refs
-    copies = []
-    for step in range(up_ref.shape[0] // block):
-        part = pl.ds(step * block, block)
-        for i, (src, dst) in enumerate([(up_hbm, up_ref), (down_hbm, down_ref)]):
-            sem = sems.at[2 * step + i]
-            copies.append(pltpu.make_async_copy(src.at[0, part, :], dst.at[part, :], sem))
-            copies[-1].start()
+def near_back_kernel(cap, block, rows, packed_ref, disp_ref, up_ref, down_ref, *refs):
+    out_ref, pick_ref, grad_acc, gate_acc = refs
 
     def put(k, first, rest):
         out_ref[k, :, 0:128] = first
         out_ref[k, :, 128:] = rest
 
-    backward(cap, block, disp_ref, up_ref, down_ref, grad_acc, gate_acc, put, copies)
+    backward(cap, block, disp_ref, up_ref, down_ref, grad_acc, gate_acc, put)
     pad = out_ref.shape[1]
     pick = picks_of(unpack(packed_ref, rows)[0], pick_ref.shape[0] // pad, 0, pad)
     pick_ref[...] = jnp.where(pick[0] | pick[1], 1.0, 0.0).astype(BF16)
@@ -274,7 +277,8 @@
     shape = jax.ShapeDtypeStruct
     unit = 2 * slots * feat
     disp_shape = shape((half, 2 * pad, feat), BF16)
-    weight = shape((hidden, feat), BF16)
+    weight = pltpu.VMEM((hidden, feat), BF16)
+    close = functools.partial(pltpu.with_memory_space_constraint, memory_space=pltpu.VMEM)
 
     across = [(i, (i + half) % groups) for i in range(groups)]
     (packed,) = call(
@@ -290,10 +294,29 @@
     )
     partner = lax.ppermute(packed, "exp", across)
 
-    slots_call = functools.partial(call, functools.partial(slots_kernel, rows))
-    (near_out,) = slots_call(
-        "near_slots", [disp_shape], [packed], [IN_VMEM], [], 2 * unit * rows, 0, SMALL
-    )
+    (near_out,) = call(
+        functools.partial(slots_kernel, rows),
+        "near_slots",
+        [disp_shape],
+        [packed],
+        [IN_VMEM],
+        [],
+        2 * unit * rows,
+        0,
+        SMALL,
+    )
+    up_v, down_v = call(
+        fetch_kernel,
+        "fetch_weights",
+        [weight, weight],
+        [far(w_up), far(w_down)],
+        [IN_HBM, IN_HBM],
+        [DMA((2,))],
+        0,
+        0,
+        SMALL,
+    )
+    up_v, down_v = close(up_v), close(down_v)
     halves = [list(range(half)), list(range(half, groups))]
     within = functools.partial(
         lax.all_to_all,
@@ -308,21 +331,29 @@
         [(i, (i + shift) % mirrors) for i in range(mirrors)] for shift in range(1, mirrors)
     ]
     near_others = [lax.ppermute(near, "rep", hops) for hops in mirror_hops]
-    (far_out,) = slots_call(
-        "far_slots", [disp_shape], [partner], [IN_VMEM], [], AHEAD, 0, SMALL
+    (far_out,) = call(
+        functools.partial(far_slots_kernel, rows),
+        "far_slots",
+        [disp_shape],
+        [partner, up_v],
+        [IN_VMEM] * 2,
+        [],
+        AHEAD,
+        0,
+        SMALL,
     )
     beyond = within(far_out)
     far_others = [lax.ppermute(beyond, "rep", hops) for hops in mirror_hops]
 
     block = min(512, hidden)
     scratch = [pltpu.VMEM((slots, feat), F32), pltpu.VMEM((slots, 128), F32)]
-    near_back, pick, up_v, down_v = call(
+    near_back, pick = call(
         functools.partial(near_back_kernel, cap, block, rows),
         "near_backward",
-        [shape((half, pad, feat), BF16), shape((groups * pad, rows), BF16), weight, weight],
-        [packed, near, far(w_up), far(w_down)],
-        [IN_VMEM] * 2 + [IN_HBM] * 2,
-        scratch + [DMA((2 * hidden // block,))],
+        [shape((half, pad, feat), BF16), shape((groups * pad, rows), BF16)],
+        [packed, near, up_v, down_v],
+        [IN_VMEM] * 4,
+        scratch,
         3 * unit * hidden,
         slots * hidden,
     )

time: 65.7 us -> 65.6 us (level)
  waiting for transfers between devices: 19.1 us -> 15.7 us
  local copies, waits for them, and re-layouts: 9.01 us -> 12.2 us
    ppermute x1, waiting for transfers between devices: 10.4 us -> 6.87 us  [local(): partner = lax.ppermute(packed, 'exp', across)]
    unnamed x16 -> x20, local copies, waits for them, and re-layouts: 9.01 us -> 12.2 us
    all_to_all x1, waiting for transfers between devices: 0.01 us -> 1.53 us  [local(): beyond = within(far_out)]
    all_to_all x1, waiting for transfers between devices: 3.3 us -> 2.01 us  [local(): near = within(near_out)]
    pallas_call x7 -> x8, Pallas kernels: 15.4 us -> 15.2 us  [call(): pl.pallas_call(body, name=name, out_shape=outs, in_specs=in_specs, out_sp...]
  transfers between devices with their start and end apart: 6 -> 6, of which waited for: 3 -> 4; matrix products, arithmetic and copies ran while one was open for 0% -> 0% of each run, Pallas kernels for 25% -> 25%
where the time goes in v6:
time: 65.6 us; the launch traced here: 65 us
  Pallas kernels  18.2 us (28%)
  starting transfers between devices  18.1 us (28%)
  waiting for transfers between devices  15.7 us (24%)
  local copies, waits for them, and re-layouts  12.2 us (19%)
  between operations  0.74 us (1%)
    pallas_call x8, Pallas kernels, call(): pl.pallas_call(body, name=name, out_shape=outs, in_specs=in_specs, out_sp...  15.2 us
    unnamed x20, local copies, waits for them, and re-layouts  12.2 us
    ppermute x1, waiting for transfers between devices, local(): partner = lax.ppermute(packed, 'exp', across)  6.87 us
    all_to_all x1, waiting for transfers between devices, local(): lax.all_to_all(back.reshape(groups, pad, feat), 'exp', split_axis=0, conc...  5.29 us
    ppermute x1, starting transfers between devices, local(): partner = lax.ppermute(packed, 'exp', across)  4.1 us
    all_to_all x1, starting transfers between devices, local(): near = within(near_out)  3.81 us
    all_to_all x1, starting transfers between devices, local(): lax.all_to_all(back.reshape(groups, pad, feat), 'exp', split_axis=0, conc...  3.58 us
    all_to_all x1, starting transfers between devices, local(): beyond = within(far_out)  3.49 us
  transfers between devices with their start and end apart: 6, of which 4 were waited for; matrix products, arithmetic and copies ran while one was open for 0% of the time, Pallas kernels for 25%

profile of v6, /device:TPU:0, one launch (start us, length us, event | category | flops | bytes accessed | tf_op | source)
XLA Modules:
  0.0 65.0 jit_solution(3915744654200461781)
XLA Ops:
  0.6 1.1 %pack.1.packed_ref = bf16[336,512]{1,0:T(8,128)(2,1)S(1)} custom-call(s32[2,160]{1,0:T(2,128)} %bitcast.4, bf16[2,160]{1,0:T(2,128)(2,1)} %bitcast.6, bf16[160,512]{1,0:T(8,128)(2,1)} %tok_hbm.1, bf16[160,512]{1,0:T(8,128)(2,1)} %cot_hbm.1), custom_call_target="tpu_custom_call" | custom-call | bytes 673664 | tf_op jit(solution)/shard_map/pack/pallas_call | solution.py:34
  1.7 4.1 %collective-permute-start = (bf16[336,512]{1,0:T(8,128)(2,1)S(1)}, bf16[336,512]{1,0:T(8,128)(2,1)S(1)}, u32[]{:S(2)}, u32[]{:S(2)}) collective-permute-start(bf16[336,512]{1,0:T(8,128)(2,1)S(1)} %pack.1.packed_ref), channel_id=1, source_target_pairs={{0,8},{1,9},{2,10},{3,11},{4,12},{5,13},{6,14},{7,15},{8,0},{9,1},... | collective-permute-start | bytes 1032200 | tf_op jit(solution)/shard_map/ppermute | solution.py:295
  5.8 1.3 %near_slots.1 = bf16[8,64,512]{2,1,0:T(8,128)(2,1)} custom-call(bf16[336,512]{1,0:T(8,128)(2,1)S(1)} %pack.1.packed_ref), custom_call_target="tpu_custom_call" | custom-call | flops 83886080 | bytes 868352 | tf_op jit(solution)/shard_map/near_slots/pallas_call | solution.py:34
  7.1 3.8 %all-to-all-start = ((bf16[8,64,512]{2,1,0:T(8,128)(2,1)}), bf16[8,64,512]{2,1,0:T(8,128)(2,1)S(1)}, u32[]{:S(2)}, u32[]{:S(2)}) async-start(bf16[8,64,512]{2,1,0:T(8,128)(2,1)} %near_slots.1), calls=%async_computation | async-start | bytes 1048576 | tf_op jit(solution)/shard_map/all_to_all | solution.py:329
  10.9 2.2 %fetch_weights.1 = (bf16[2048,512]{1,0:T(8,128)(2,1)S(1)}, bf16[2048,512]{1,0:T(8,128)(2,1)S(1)}) custom-call(bf16[1,2048,512]{2,1,0:T(8,128)(2,1)} %up_hbm.1, bf16[1,2048,512]{2,1,0:T(8,128)(2,1)} %down_hbm.1), custom_call_target="tpu_custom_call" | custom-call | bytes 8388608 | tf_op jit(solution)/shard_map/fetch_weights/pallas_call | solution.py:34
  13.1 0.0 copy-start.6
  13.1 1.3 %copy-done.6 = bf16[2048,512]{1,0:T(8,128)(2,1)} copy-done((bf16[2048,512]{1,0:T(8,128)(2,1)}, bf16[2048,512]{1,0:T(8,128)(2,1)S(1)}, u32[]{:S(2)}) %copy-start.6) | copy-done | bytes 2097176
  14.5 6.9 %collective-permute-done.packed_ref = bf16[336,512]{1,0:T(8,128)(2,1)S(1)} collective-permute-done((bf16[336,512]{1,0:T(8,128)(2,1)S(1)}, bf16[336,512]{1,0:T(8,128)(2,1)S(1)}, u32[]{:S(2)}, u32[]{:S(2)}) %collective-permute-start) | collective-permute-done | bytes 344096 | tf_op jit(solution)/shard_map/ppermute | solution.py:295
  21.3 1.3 %far_slots.1 = bf16[8,64,512]{2,1,0:T(8,128)(2,1)} custom-call(bf16[336,512]{1,0:T(8,128)(2,1)S(1)} %collective-permute-done.packed_ref, bf16[2048,512]{1,0:T(8,128)(2,1)S(1)} %get-tuple-element.14.up_ref._.refs_2_), custom_call_target="tpu_custom_call" | custom-call | flops 99999997952 | bytes 2965504 | tf_op jit(solution)/shard_map/far_slots/pallas_call | solution.py:34
  22.6 0.0 copy-start.2
  22.6 1.3 %copy-done.2 = bf16[2048,512]{1,0:T(8,128)(2,1)} copy-done((bf16[2048,512]{1,0:T(8,128)(2,1)}, bf16[2048,512]{1,0:T(8,128)(2,1)S(1)}, u32[]{:S(2)}) %copy-start.2) | copy-done | bytes 2097176
  23.9 2.0 %all-to-all-done.disp_ref.near_ref = bf16[8,64,512]{2,1,0:T(8,128)(2,1)S(1)} async-done(((bf16[8,64,512]{2,1,0:T(8,128)(2,1)}), bf16[8,64,512]{2,1,0:T(8,128)(2,1)S(1)}, u32[]{:S(2)}, u32[]{:S(2)}) %all-to-all-start) | async-done | bytes 524320 | tf_op jit(solution)/shard_map/all_to_all | solution.py:329
  25.9 3.5 %all-to-all-start.1 = ((bf16[8,64,512]{2,1,0:T(8,128)(2,1)}), bf16[8,64,512]{2,1,0:T(8,128)(2,1)S(1)}, u32[]{:S(2)}, u32[]{:S(2)}) async-start(bf16[8,64,512]{2,1,0:T(8,128)(2,1)} %far_slots.1), calls=%async_computation.1 | async-start | bytes 1048576 | tf_op jit(solution)/shard_map/all_to_all | solution.py:345
  29.4 1.6 %collective-permute-start.1 = (bf16[8,64,512]{2,1,0:T(8,128)(2,1)S(1)}, bf16[8,64,512]{2,1,0:T(8,128)(2,1)S(1)}, u32[]{:S(2)}, u32[]{:S(2)}) collective-permute-start(bf16[8,64,512]{2,1,0:T(8,128)(2,1)S(1)} %all-to-all-done.disp_ref.near_ref), channel_id=1, source_target_pairs={{0,16},{16,0},{1,17},{17,1},{2,18},{18,2},{3,19},{19,3},{4,20},{20... | collective-permute-start | bytes 1572872 | tf_op jit(solution)/shard_map/ppermute | solution.py:333
  31.0 0.0 copy-start.3
  31.0 1.6 %copy-done.3 = bf16[2048,512]{1,0:T(8,128)(2,1)S(1)} copy-done((bf16[2048,512]{1,0:T(8,128)(2,1)S(1)}, bf16[2048,512]{1,0:T(8,128)(2,1)}, u32[]{:S(2)}) %copy-start.3) | copy-done | bytes 2097176
  32.6 0.0 copy-start.7
  32.6 1.6 %copy-done.7 = bf16[2048,512]{1,0:T(8,128)(2,1)S(1)} copy-done((bf16[2048,512]{1,0:T(8,128)(2,1)S(1)}, bf16[2048,512]{1,0:T(8,128)(2,1)}, u32[]{:S(2)}) %copy-start.7) | copy-done | bytes 2097176
  34.2 2.4 %near_backward.1 = (bf16[8,32,512]{2,1,0:T(8,128)(2,1)S(1)}, bf16[512,160]{1,0:T(8,128)(2,1)S(1)}) custom-call(bf16[336,512]{1,0:T(8,128)(2,1)S(1)} %pack.1.packed_ref, bf16[8,64,512]{2,1,0:T(8,128)(2,1)S(1)} %all-to-all-done.disp_ref.near_ref, bf16[2048,512]{1,0:T(8,128)(2,1)S(1)} %copy-done.3, bf16[2048,512]{1,0:T(8,128)(2,1)S(1)} %copy-done.7), custom_call_target="tpu_custom_call" | custom-call | flops 1610612736 | bytes 5488640 | tf_op jit(solution)/shard_map/near_backward/pallas_call | solution.py:34
  36.7 1.5 %all-to-all-done.1.disp_ref.far_ref = bf16[8,64,512]{2,1,0:T(8,128)(2,1)S(1)} async-done(((bf16[8,64,512]{2,1,0:T(8,128)(2,1)}), bf16[8,64,512]{2,1,0:T(8,128)(2,1)S(1)}, u32[]{:S(2)}, u32[]{:S(2)}) %all-to-all-start.1) | async-done | bytes 524320 | tf_op jit(solution)/shard_map/all_to_all | solution.py:345
  38.2 1.5 %collective-permute-start.2 = (bf16[8,64,512]{2,1,0:T(8,128)(2,1)S(1)}, bf16[8,64,512]{2,1,0:T(8,128)(2,1)S(1)}, u32[]{:S(2)}, u32[]{:S(2)}) collective-permute-start(bf16[8,64,512]{2,1,0:T(8,128)(2,1)S(1)} %all-to-all-done.1.disp_ref.far_ref), channel_id=1, source_target_pairs={{0,16},{16,0},{1,17},{17,1},{2,18},{18,2},{3,19},{19,3},{4,20},{20... | collective-permute-start | bytes 1572872 | tf_op jit(solution)/shard_map/ppermute | solution.py:346
  39.7 0.0 copy-start.4
  39.7 1.6 %copy-done.4 = bf16[2048,512]{1,0:T(8,128)(2,1)S(1)} copy-done((bf16[2048,512]{1,0:T(8,128)(2,1)S(1)}, bf16[2048,512]{1,0:T(8,128)(2,1)}, u32[]{:S(2)}) %copy-start.4) | copy-done | bytes 2097176
  41.3 0.0 copy-start.8
  41.3 1.6 %copy-done.8 = bf16[2048,512]{1,0:T(8,128)(2,1)S(1)} copy-done((bf16[2048,512]{1,0:T(8,128)(2,1)S(1)}, bf16[2048,512]{1,0:T(8,128)(2,1)}, u32[]{:S(2)}) %copy-start.8) | copy-done | bytes 2097176
  42.9 3.0 %far_backward.1 = bf16[2,8,32,512]{3,2,1,0:T(8,128)(2,1)} custom-call(bf16[8,32,512]{2,1,0:T(8,128)(2,1)S(1)} %get-tuple-element.17.near_ref, bf16[8,64,512]{2,1,0:T(8,128)(2,1)S(1)} %all-to-all-done.1.disp_ref.far_ref, bf16[2048,512]{1,0:T(8,128)(2,1)S(1)} %copy-done.4, bf16[2048,512]{1,0:T(8,128)(2,1)S(1)} %copy-done.8), custom_call_target="tpu_custom_call" | custom-call | flops 99999997952 | bytes 4194304 | tf_op jit(solution)/shard_map/far_backward/pallas_call | solution.py:360
  45.9 3.6 %all-to-all-start.2 = ((bf16[16,32,512]{2,1,0:T(8,128)(2,1)}), bf16[16,32,512]{2,1,0:T(8,128)(2,1)S(1)}, u32[]{:S(2)}, u32[]{:S(2)}) async-start(bf16[16,32,512]{2,1,0:T(8,128)(2,1)} %bitcast.8), calls=%async_computation.2 | async-start | bytes 1048576 | tf_op jit(solution)/shard_map/all_to_all | solution.py:374
  49.5 0.0 copy-start.5
  49.5 1.6 %copy-done.5 = bf16[2048,512]{1,0:T(8,128)(2,1)S(1)} copy-done((bf16[2048,512]{1,0:T(8,128)(2,1)S(1)}, bf16[2048,512]{1,0:T(8,128)(2,1)}, u32[]{:S(2)}) %copy-start.5) | copy-done | bytes 2097176
  51.1 0.0 copy-start.9
  51.1 1.6 %copy-done.9 = bf16[2048,512]{1,0:T(8,128)(2,1)S(1)} copy-done((bf16[2048,512]{1,0:T(8,128)(2,1)S(1)}, bf16[2048,512]{1,0:T(8,128)(2,1)}, u32[]{:S(2)}) %copy-start.9) | copy-done | bytes 2097176
  52.7 2.4 %own_weights.1 = (f32[1024,512]{1,0:T(8,128)S(1)}, f32[1024,512]{1,0:T(8,128)S(1)}) custom-call(bf16[8,64,512]{2,1,0:T(8,128)(2,1)S(1)} %all-to-all-done.disp_ref.near_ref, bf16[8,64,512]{2,1,0:T(8,128)(2,1)S(1)} %all-to-all-done.1.disp_ref.far_ref, bf16[2048,512]{1,0:T(8,128)(2,1)S(1)} %copy-done.5, bf16[2048,512]{1,0:T(8,128)(2,1)S(1)} %copy-done.9), custom_call_target="tpu_custom_call" | custom-call | flops 2147483648 | bytes 9437184 | tf_op jit(solution)/shard_map/own_weights/pallas_call | solution.py:34
  55.1 0.0 collective-permute-done.1.refs_0_
  55.2 0.0 collective-permute-done.2.refs_1_
  55.2 0.0 copy-start
  55.2 0.0 copy-start.1
  55.2 3.5 %other_weights.1 = (bf16[1,1024,512]{2,1,0:T(8,128)(2,1)}, bf16[1,1024,512]{2,1,0:T(8,128)(2,1)}) custom-call(bf16[8,64,512]{2,1,0:T(8,128)(2,1)S(1)} %collective-permute-done.1.refs_0_, bf16[8,64,512]{2,1,0:T(8,128)(2,1)S(1)} %collective-permute-done.2.refs_1_, bf16[2048,512]{1,0:T(8,128)(2,1)S(1)} %copy-done.5, bf16[2048,512]{1,0:T(8,128)(2,1)S(1)} %copy-done.9, ...), custom_call_target="tpu_custom_call" | custom-call | flops 99999997952 | bytes 11534336 | tf_op jit(solution)/shard_map/other_weights/pallas_call | solution.py:34
  58.7 5.3 %all-to-all-done.2.back_ref = bf16[16,32,512]{2,1,0:T(8,128)(2,1)S(1)} async-done(((bf16[16,32,512]{2,1,0:T(8,128)(2,1)}), bf16[16,32,512]{2,1,0:T(8,128)(2,1)S(1)}, u32[]{:S(2)}, u32[]{:S(2)}) %all-to-all-start.2) | async-done | bytes 524320 | tf_op jit(solution)/shard_map/all_to_all | solution.py:374
  64.0 0.0 copy-done
  64.0 0.0 copy-done.1
  64.0 1.0 %combine.1 = (bf16[160,512]{1,0:T(8,128)(2,1)}, bf16[2,160]{1,0:T(2,128)(2,1)}) custom-call(s32[2,160]{1,0:T(2,128)S(1)} %bitcast.5, bf16[2,160]{1,0:T(2,128)(2,1)S(1)} %bitcast.7, bf16[512,160]{1,0:T(8,128)(2,1)S(1)} %get-tuple-element.16.pick_ref, bf16[16,32,512]{2,1,0:T(8,128)(2,1)S(1)} %all-to-all-done.2.back_ref), custom_call_target="tpu_custom_call" | custom-call | flops 83886080 | bytes 854528 | tf_op jit(solution)/shard_map/combine/pallas_call | solution.py:34
Async XLA Ops:
  1.7 19.6 %collective-permute-start = (bf16[336,512]{1,0:T(8,128)(2,1)S(1)}, bf16[336,512]{1,0:T(8,128)(2,1)S(1)}, u32[]{:S(2)}, u32[]{:S(2)}) collective-permute-start(bf16[336,512]{1,0:T(8,128)(2,1)S(1)} %pack.1.packed_ref), channel_id=1, source_target_pairs={{0,8},{1,9},{2,10},{3,11},{4,12},{5,13},{6,14},{7,15},{8,0},{9,1},... | collective-permute-start | bytes 1032200 | tf_op jit(solution)/shard_map/ppermute | solution.py:295
  7.1 18.8 %all-to-all-start = ((bf16[8,64,512]{2,1,0:T(8,128)(2,1)}), bf16[8,64,512]{2,1,0:T(8,128)(2,1)S(1)}, u32[]{:S(2)}, u32[]{:S(2)}) async-start(bf16[8,64,512]{2,1,0:T(8,128)(2,1)} %near_slots.1), calls=%async_computation | async-start | bytes 1048576 | tf_op jit(solution)/shard_map/all_to_all | solution.py:329
  13.1 1.3 %copy-start.6 = (bf16[2048,512]{1,0:T(8,128)(2,1)}, bf16[2048,512]{1,0:T(8,128)(2,1)S(1)}, u32[]{:S(2)}) copy-start(bf16[2048,512]{1,0:T(8,128)(2,1)S(1)} %get-tuple-element.15.down_ref.refs_3_) | copy-start | bytes 6291460
  22.6 1.3 %copy-start.2 = (bf16[2048,512]{1,0:T(8,128)(2,1)}, bf16[2048,512]{1,0:T(8,128)(2,1)S(1)}, u32[]{:S(2)}) copy-start(bf16[2048,512]{1,0:T(8,128)(2,1)S(1)} %get-tuple-element.14.up_ref._.refs_2_) | copy-start | bytes 6291460
  25.9 12.3 %all-to-all-start.1 = ((bf16[8,64,512]{2,1,0:T(8,128)(2,1)}), bf16[8,64,512]{2,1,0:T(8,128)(2,1)S(1)}, u32[]{:S(2)}, u32[]{:S(2)}) async-start(bf16[8,64,512]{2,1,0:T(8,128)(2,1)} %far_slots.1), calls=%async_computation.1 | async-start | bytes 1048576 | tf_op jit(solution)/shard_map/all_to_all | solution.py:345
  29.4 25.7 %collective-permute-start.1 = (bf16[8,64,512]{2,1,0:T(8,128)(2,1)S(1)}, bf16[8,64,512]{2,1,0:T(8,128)(2,1)S(1)}, u32[]{:S(2)}, u32[]{:S(2)}) collective-permute-start(bf16[8,64,512]{2,1,0:T(8,128)(2,1)S(1)} %all-to-all-done.disp_ref.near_ref), channel_id=1, source_target_pairs={{0,16},{16,0},{1,17},{17,1},{2,18},{18,2},{3,19},{19,3},{4,20},{20... | collective-permute-start | bytes 1572872 | tf_op jit(solution)/shard_map/ppermute | solution.py:333
  31.0 1.6 %copy-start.3 = (bf16[2048,512]{1,0:T(8,128)(2,1)S(1)}, bf16[2048,512]{1,0:T(8,128)(2,1)}, u32[]{:S(2)}) copy-start(bf16[2048,512]{1,0:T(8,128)(2,1)} %copy-done.2) | copy-start | bytes 6291460
  32.6 1.6 %copy-start.7 = (bf16[2048,512]{1,0:T(8,128)(2,1)S(1)}, bf16[2048,512]{1,0:T(8,128)(2,1)}, u32[]{:S(2)}) copy-start(bf16[2048,512]{1,0:T(8,128)(2,1)} %copy-done.6) | copy-start | bytes 6291460
  38.2 17.0 %collective-permute-start.2 = (bf16[8,64,512]{2,1,0:T(8,128)(2,1)S(1)}, bf16[8,64,512]{2,1,0:T(8,128)(2,1)S(1)}, u32[]{:S(2)}, u32[]{:S(2)}) collective-permute-start(bf16[8,64,512]{2,1,0:T(8,128)(2,1)S(1)} %all-to-all-done.1.disp_ref.far_ref), channel_id=1, source_target_pairs={{0,16},{16,0},{1,17},{17,1},{2,18},{18,2},{3,19},{19,3},{4,20},{20... | collective-permute-start | bytes 1572872 | tf_op jit(solution)/shard_map/ppermute | solution.py:346
  39.7 1.6 %copy-start.4 = (bf16[2048,512]{1,0:T(8,128)(2,1)S(1)}, bf16[2048,512]{1,0:T(8,128)(2,1)}, u32[]{:S(2)}) copy-start(bf16[2048,512]{1,0:T(8,128)(2,1)} %copy-done.2) | copy-start | bytes 6291460
  41.3 1.6 %copy-start.8 = (bf16[2048,512]{1,0:T(8,128)(2,1)S(1)}, bf16[2048,512]{1,0:T(8,128)(2,1)}, u32[]{:S(2)}) copy-start(bf16[2048,512]{1,0:T(8,128)(2,1)} %copy-done.6) | copy-start | bytes 6291460
  45.9 18.0 %all-to-all-start.2 = ((bf16[16,32,512]{2,1,0:T(8,128)(2,1)}), bf16[16,32,512]{2,1,0:T(8,128)(2,1)S(1)}, u32[]{:S(2)}, u32[]{:S(2)}) async-start(bf16[16,32,512]{2,1,0:T(8,128)(2,1)} %bitcast.8), calls=%async_computation.2 | async-start | bytes 1048576 | tf_op jit(solution)/shard_map/all_to_all | solution.py:374
  49.5 1.6 %copy-start.5 = (bf16[2048,512]{1,0:T(8,128)(2,1)S(1)}, bf16[2048,512]{1,0:T(8,128)(2,1)}, u32[]{:S(2)}) copy-start(bf16[2048,512]{1,0:T(8,128)(2,1)} %copy-done.2) | copy-start | bytes 6291460
  51.1 1.6 %copy-start.9 = (bf16[2048,512]{1,0:T(8,128)(2,1)S(1)}, bf16[2048,512]{1,0:T(8,128)(2,1)}, u32[]{:S(2)}) copy-start(bf16[2048,512]{1,0:T(8,128)(2,1)} %copy-done.6) | copy-start | bytes 6291460
  55.2 8.8 %copy-start = (s32[160,2]{0,1:T(2,128)S(1)}, s32[160,2]{0,1:T(2,128)}, u32[]{:S(2)}) copy-start(s32[160,2]{0,1:T(2,128)} %param.8) | copy-start | bytes 3844
  55.2 8.8 %copy-start.1 = (bf16[160,2]{0,1:T(2,128)(2,1)S(1)}, bf16[160,2]{0,1:T(2,128)(2,1)}, u32[]{:S(2)}) copy-start(bf16[160,2]{0,1:T(2,128)(2,1)} %param.7) | copy-start | bytes 1924

commit v7 on v6

--- a/solution.py
+++ b/solution.py
@@ -115,17 +115,16 @@
     out_ref[:, pad:, :] = dot(scaled, cot, 1, 0).astype(BF16).reshape(experts, pad, feat)
 
 
-def fetch_kernel(up_hbm, down_hbm, up_ref, down_ref, sems):
+def fetch(up_hbm, down_hbm, up_ref, down_ref, sems, base, block):
     copies = []
-    for i, (src, dst) in enumerate([(up_hbm, up_ref), (down_hbm, down_ref)]):
-        copies.append(pltpu.make_async_copy(src.at[0], dst, sems.at[i]))
-        copies[i].start()
-    for copy in copies:
-        copy.wait()
-
-
-def far_slots_kernel(rows, packed_ref, _, out_ref):
-    slots_kernel(rows, packed_ref, out_ref)
+    for step in range(up_ref.shape[0] // block):
+        to = pl.ds(step * block, block)
+        of = pl.ds(pl.multiple_of(base + step * block, block), block)
+        for src, dst in [(up_hbm, up_ref), (down_hbm, down_ref)]:
+            sem = sems.at[len(copies)]
+            copies.append(pltpu.make_async_copy(src.at[0, of, :], dst.at[to, :], sem))
+            copies[-1].start()
+    return copies
 
 
 def split_rows(ref):
@@ -137,15 +136,17 @@
     )
 
 
-def backward(cap, block, disp_ref, up_ref, down_ref, grad_acc, gate_acc, put):
+def backward(cap, block, disp_ref, up_ref, down_ref, grad_acc, gate_acc, put, copies):
     origins, both, feat = disp_ref.shape
     pad = both // 2
     slots = origins * pad
     rows, grads = split_rows(disp_ref)
     for step in range(up_ref.shape[0] // block):
         part = pl.ds(step * block, block)
+        copies[2 * step].wait()
         up = up_ref[part, :]
         active, slope = silu_parts(dot(rows, up, 1, 1))
+        copies[2 * step + 1].wait()
         back = dot(grads, down_ref[part, :], 1, 1)
         hid_grad = (back * slope).astype(BF16)
         gate = active.astype(BF16).astype(F32) * back
@@ -169,21 +170,23 @@
         put(k, first.astype(BF16), grad_acc[here, 128:].astype(BF16))
 
 
-def near_back_kernel(cap, block, rows, packed_ref, disp_ref, up_ref, down_ref, *refs):
-    out_ref, pick_ref, grad_acc, gate_acc = refs
+def near_back_kernel(cap, block, rows, packed_ref, disp_ref, up_hbm, down_hbm, *refs):
+    out_ref, pick_ref, grad_acc, gate_acc, up_ref, down_ref, w_sems = refs
+    copies = fetch(up_hbm, down_hbm, up_ref, down_ref, w_sems, 0, block)
 
     def put(k, first, rest):
         out_ref[k, :, 0:128] = first
         out_ref[k, :, 128:] = rest
 
-    backward(cap, block, disp_ref, up_ref, down_ref, grad_acc, gate_acc, put)
+    backward(cap, block, disp_ref, up_ref, down_ref, grad_acc, gate_acc, put, copies)
     pad = out_ref.shape[1]
     pick = picks_of(unpack(packed_ref, rows)[0], pick_ref.shape[0] // pad, 0, pad)
     pick_ref[...] = jnp.where(pick[0] | pick[1], 1.0, 0.0).astype(BF16)
 
 
-def far_back_kernel(cap, block, near_ref, disp_ref, up_ref, down_ref, *refs):
-    out_hbm, out_ref, grad_acc, gate_acc, sems = refs
+def far_back_kernel(cap, block, near_ref, disp_ref, up_hbm, down_hbm, *refs):
+    out_hbm, grad_acc, gate_acc, up_ref, down_ref, w_sems, out_ref, sems = refs
+    copies = fetch(up_hbm, down_hbm, up_ref, down_ref, w_sems, 0, block)
     half = lax.axis_index("exp") // near_ref.shape[0]
     near_copy = pltpu.make_async_copy(near_ref, out_hbm.at[half], sems.at[0])
     near_copy.start()
@@ -192,44 +195,49 @@
         out_ref[k, :, 0:128] = first
         out_ref[k, :, 128:] = rest
 
-    backward(cap, block, disp_ref, up_ref, down_ref, grad_acc, gate_acc, put)
+    backward(cap, block, disp_ref, up_ref, down_ref, grad_acc, gate_acc, put, copies)
     far_copy = pltpu.make_async_copy(out_ref, out_hbm.at[1 - half], sems.at[1])
     far_copy.start()
     near_copy.wait()
     far_copy.wait()
 
 
-def weight_parts(block, share, disp_refs, up_ref, down_ref, rows_ref, grads_ref, store):
+def weight_parts(block, share, disp_refs, up_ref, down_ref, rows_ref, grads_ref, store, copies):
     size = rows_ref.shape[0] // len(disp_refs)
     for i, ref in enumerate(disp_refs):
         here = slice(i * size, (i + 1) * size)
         rows_ref[here, :], grads_ref[here, :] = split_rows(ref)
-    base = lax.axis_index("rep") * share
     for step in range(share // block):
         here = pl.ds(step * block, block)
-        part = pl.ds(pl.multiple_of(base + step * block, block), block)
-        active, slope = silu_parts(dot(up_ref[part, :], rows_ref[...], 1, 1))
-        back = dot(down_ref[part, :], grads_ref[...], 1, 1)
+        for copy in copies[2 * step : 2 * step + 2]:
+            copy.wait()
+        active, slope = silu_parts(dot(up_ref[here, :], rows_ref[...], 1, 1))
+        back = dot(down_ref[here, :], grads_ref[...], 1, 1)
         hid_grad = (back * slope).astype(BF16)
         up_part = dot(hid_grad, rows_ref[...], 1, 0)
         down_part = dot(active.astype(BF16), grads_ref[...], 1, 0)
         store(here, up_part, down_part)
 
 
-def own_weights_kernel(block, share, near_ref, far_ref, up_ref, down_ref, *refs):
-    up_acc, down_acc, rows_ref, grads_ref = refs
+def own_weights_kernel(block, share, near_ref, far_ref, up_hbm, down_hbm, *refs):
+    up_acc, down_acc, rows_ref, grads_ref, up_ref, down_ref, w_sems = refs
+    base = lax.axis_index("rep") * share
+    copies = fetch(up_hbm, down_hbm, up_ref, down_ref, w_sems, base, block)
 
     def store(here, up_part, down_part):
         up_acc[here, :] = up_part
         down_acc[here, :] = down_part
 
     both = [near_ref, far_ref]
-    weight_parts(block, share, both, up_ref, down_ref, rows_ref, grads_ref, store)
+    weight_parts(block, share, both, up_ref, down_ref, rows_ref, grads_ref, store, copies)
 
 
 def other_weights_kernel(block, share, mirrors, *refs):
-    pieces, refs = refs[:-8], refs[-8:]
-    up_ref, down_ref, up_acc, down_acc, grad_up_ref, grad_down_ref, rows_ref, grads_ref = refs
+    pieces, refs = refs[:-11], refs[-11:]
+    up_hbm, down_hbm, up_acc, down_acc, grad_up_ref, grad_down_ref, rows_ref, grads_ref = refs[:8]
+    up_ref, down_ref, w_sems = refs[8:]
+    base = lax.axis_index("rep") * share
+    copies = fetch(up_hbm, down_hbm, up_ref, down_ref, w_sems, base, block)
     for mirror in range(mirrors - 1):
 
         def store(here, up_part, down_part):
@@ -243,7 +251,8 @@
                 down_acc[here, :] = down_part
 
         both = pieces[2 * mirror : 2 * mirror + 2]
-        weight_parts(block, share, both, up_ref, down_ref, rows_ref, grads_ref, store)
+        copies = copies if mirror == 0 else []
+        weight_parts(block, share, both, up_ref, down_ref, rows_ref, grads_ref, store, copies)
 
 
 def combine_kernel(cap, routes_ref, gates_ref, pick_ref, back_ref, d_tok_ref, d_gate_ref):
@@ -277,9 +286,6 @@
     shape = jax.ShapeDtypeStruct
     unit = 2 * slots * feat
     disp_shape = shape((half, 2 * pad, feat), BF16)
-    weight = pltpu.VMEM((hidden, feat), BF16)
-    close = functools.partial(pltpu.with_memory_space_constraint, memory_space=pltpu.VMEM)
-
     across = [(i, (i + half) % groups) for i in range(groups)]
     (packed,) = call(
         pack_kernel,
@@ -305,18 +311,6 @@
         0,
         SMALL,
     )
-    up_v, down_v = call(
-        fetch_kernel,
-        "fetch_weights",
-        [weight, weight],
-        [far(w_up), far(w_down)],
-        [IN_HBM, IN_HBM],
-        [DMA((2,))],
-        0,
-        0,
-        SMALL,
-    )
-    up_v, down_v = close(up_v), close(down_v)
     halves = [list(range(half)), list(range(half, groups))]
     within = functools.partial(
         lax.all_to_all,
@@ -332,11 +326,11 @@
     ]
     near_others = [lax.ppermute(near, "rep", hops) for hops in mirror_hops]
     (far_out,) = call(
-        functools.partial(far_slots_kernel, rows),
+        functools.partial(slots_kernel, rows),
         "far_slots",
         [disp_shape],
-        [partner, up_v],
-        [IN_VMEM] * 2,
+        [partner],
+        [IN_VMEM],
         [],
         AHEAD,
         0,
@@ -346,13 +340,19 @@
     far_others = [lax.ppermute(beyond, "rep", hops) for hops in mirror_hops]
 
     block = min(512, hidden)
-    scratch = [pltpu.VMEM((slots, feat), F32), pltpu.VMEM((slots, 128), F32)]
+    scratch = [
+        pltpu.VMEM((slots, feat), F32),
+        pltpu.VMEM((slots, 128), F32),
+        pltpu.VMEM((hidden, feat), BF16),
+        pltpu.VMEM((hidden, feat), BF16),
+        DMA((2 * hidden // block,)),
+    ]
     near_back, pick = call(
         functools.partial(near_back_kernel, cap, block, rows),
         "near_backward",
         [shape((half, pad, feat), BF16), shape((groups * pad, rows), BF16)],
-        [packed, near, up_v, down_v],
-        [IN_VMEM] * 4,
+        [packed, near, far(w_up), far(w_down)],
+        [IN_VMEM] * 2 + [IN_HBM] * 2,
         scratch,
         3 * unit * hidden,
         slots * hidden,
@@ -361,29 +361,35 @@
         functools.partial(far_back_kernel, cap, block),
         name="far_backward",
         out_shape=pltpu.HBM((2, half, pad, feat), BF16),
-        in_specs=[IN_VMEM] * 4,
+        in_specs=[IN_VMEM] * 2 + [IN_HBM] * 2,
         out_specs=IN_HBM,
-        scratch_shapes=[pltpu.VMEM((half, pad, feat), BF16)] + scratch + [DMA((2,))],
+        scratch_shapes=scratch + [pltpu.VMEM((half, pad, feat), BF16), DMA((2,))],
         compiler_params=pltpu.CompilerParams(vmem_limit_bytes=MEDIUM),
         cost_estimate=pl.CostEstimate(
             flops=AHEAD,
             bytes_accessed=4 * hidden * feat,
             transcendentals=slots * hidden,
         ),
-    )(near_back, beyond, up_v, down_v)
+    )(near_back, beyond, far(w_up), far(w_down))
     back = lax.all_to_all(
         back.reshape(groups, pad, feat), "exp", split_axis=0, concat_axis=0, tiled=True
     )
 
     part = min(512, share)
     total = shape((share, feat), F32)
-    both_rows = [pltpu.VMEM((2 * slots, feat), BF16)] * 2
+    both_rows = [
+        pltpu.VMEM((2 * slots, feat), BF16),
+        pltpu.VMEM((2 * slots, feat), BF16),
+        pltpu.VMEM((share, feat), BF16),
+        pltpu.VMEM((share, feat), BF16),
+        DMA((2 * share // part,)),
+    ]
     up_sum, down_sum = call(
         functools.partial(own_weights_kernel, part, share),
         "own_weights",
         [total, total],
-        [near, beyond, up_v, down_v],
-        [IN_VMEM] * 4,
+        [near, beyond, far(w_up), far(w_down)],
+        [IN_VMEM] * 2 + [IN_HBM] * 2,
         both_rows,
         8 * unit * share,
         2 * slots * share,
@@ -397,8 +403,8 @@
             functools.partial(other_weights_kernel, part, share, mirrors),
             "other_weights",
             [shape((1, share, feat), BF16)] * 2,
-            [*others, up_v, down_v, up_sum, down_sum],
-            [IN_VMEM] * (len(others) + 4),
+            [*others, far(w_up), far(w_down), up_sum, down_sum],
+            [IN_VMEM] * len(others) + [IN_HBM] * 2 + [IN_VMEM] * 2,
             both_rows,
             AHEAD,
             2 * slots * share,

time: 65.6 us -> 64.8 us (0.988)
  local copies, waits for them, and re-layouts: 12.2 us -> 0.01 us
  Pallas kernels: 18.2 us -> 24 us
  waiting for transfers between devices: 15.7 us -> 21.5 us
    unnamed x20 -> x4, local copies, waits for them, and re-layouts: 12.2 us -> 0.01 us
    ppermute x1, waiting for transfers between devices: 6.87 us -> 10.4 us  [local(): partner = lax.ppermute(packed, 'exp', across)]
    pallas_call x8 -> x7, Pallas kernels: 15.2 us -> 18.4 us  [call(): pl.pallas_call(body, name=name, out_shape=outs, in_specs=in_specs, out_sp...]
    pallas_call x1, Pallas kernels: 3.02 us -> 5.54 us  [local(): pl.pallas_call(functools.partial(far_back_kernel, cap, block), name='far_...]
    ppermute x1, waiting for transfers between devices: 0.01 us -> 2.09 us  [local(): far_others = [lax.ppermute(beyond, 'rep', hops) for hops in mirror_hops]]
    all_to_all x1, waiting for transfers between devices: 5.29 us -> 3.4 us  [local(): lax.all_to_all(back.reshape(groups, pad, feat), 'exp', split_axis=0, conc...]
    all_to_all x1, waiting for transfers between devices: 2.01 us -> 3.3 us  [local(): near = within(near_out)]
    all_to_all x1, waiting for transfers between devices: 1.53 us -> 2.25 us  [local(): beyond = within(far_out)]
  transfers between devices with their start and end apart: 6 -> 6, of which waited for: 4 -> 5; matrix products, arithmetic and copies ran while one was open for 0% -> 0% of each run, Pallas kernels for 25% -> 34%
where the time goes in v7:
time: 64.8 us; the launch traced here: 64.3 us
  Pallas kernels  24 us (37%)
  waiting for transfers between devices  21.5 us (33%)
  starting transfers between devices  18.1 us (28%)
  between operations  0.7 us (1%)
    pallas_call x7, Pallas kernels, call(): pl.pallas_call(body, name=name, out_shape=outs, in_specs=in_specs, out_sp...  18.4 us
    ppermute x1, waiting for transfers between devices, local(): partner = lax.ppermute(packed, 'exp', across)  10.4 us
    pallas_call x1, Pallas kernels, local(): pl.pallas_call(functools.partial(far_back_kernel, cap, block), name='far_...  5.54 us
    ppermute x1, starting transfers between devices, local(): partner = lax.ppermute(packed, 'exp', across)  4.1 us
    all_to_all x1, starting transfers between devices, local(): near = within(near_out)  3.81 us
    all_to_all x1, starting transfers between devices, local(): lax.all_to_all(back.reshape(groups, pad, feat), 'exp', split_axis=0, conc...  3.58 us
    all_to_all x1, starting transfers between devices, local(): beyond = within(far_out)  3.49 us
    all_to_all x1, waiting for transfers between devices, local(): lax.all_to_all(back.reshape(groups, pad, feat), 'exp', split_axis=0, conc...  3.4 us
  transfers between devices with their start and end apart: 6, of which 5 were waited for; matrix products, arithmetic and copies ran while one was open for 0% of the time, Pallas kernels for 34%

profile of v7, /device:TPU:0, one launch (start us, length us, event | category | flops | bytes accessed | tf_op | source)
XLA Modules:
  0.0 64.3 jit_solution(14581978409117946926)
XLA Ops:
  0.6 1.1 %pack.1.packed_ref = bf16[336,512]{1,0:T(8,128)(2,1)S(1)} custom-call(s32[2,160]{1,0:T(2,128)} %bitcast.4, bf16[2,160]{1,0:T(2,128)(2,1)} %bitcast.6, bf16[160,512]{1,0:T(8,128)(2,1)} %tok_hbm.1, bf16[160,512]{1,0:T(8,128)(2,1)} %cot_hbm.1), custom_call_target="tpu_custom_call" | custom-call | bytes 673664 | tf_op jit(solution)/shard_map/pack/pallas_call | solution.py:34
  1.7 4.1 %collective-permute-start = (bf16[336,512]{1,0:T(8,128)(2,1)S(1)}, bf16[336,512]{1,0:T(8,128)(2,1)S(1)}, u32[]{:S(2)}, u32[]{:S(2)}) collective-permute-start(bf16[336,512]{1,0:T(8,128)(2,1)S(1)} %pack.1.packed_ref), channel_id=1, source_target_pairs={{0,8},{1,9},{2,10},{3,11},{4,12},{5,13},{6,14},{7,15},{8,0},{9,1},... | collective-permute-start | bytes 1032200 | tf_op jit(solution)/shard_map/ppermute | solution.py:301
  5.8 1.3 %near_slots.1 = bf16[8,64,512]{2,1,0:T(8,128)(2,1)} custom-call(bf16[336,512]{1,0:T(8,128)(2,1)S(1)} %pack.1.packed_ref), custom_call_target="tpu_custom_call" | custom-call | flops 83886080 | bytes 868352 | tf_op jit(solution)/shard_map/near_slots/pallas_call | solution.py:34
  7.1 3.8 %all-to-all-start = ((bf16[8,64,512]{2,1,0:T(8,128)(2,1)}), bf16[8,64,512]{2,1,0:T(8,128)(2,1)S(1)}, u32[]{:S(2)}, u32[]{:S(2)}) async-start(bf16[8,64,512]{2,1,0:T(8,128)(2,1)} %near_slots.1), calls=%async_computation | async-start | bytes 1048576 | tf_op jit(solution)/shard_map/all_to_all | solution.py:323
  10.9 10.4 %collective-permute-done.packed_ref = bf16[336,512]{1,0:T(8,128)(2,1)S(1)} collective-permute-done((bf16[336,512]{1,0:T(8,128)(2,1)S(1)}, bf16[336,512]{1,0:T(8,128)(2,1)S(1)}, u32[]{:S(2)}, u32[]{:S(2)}) %collective-permute-start) | collective-permute-done | bytes 344096 | tf_op jit(solution)/shard_map/ppermute | solution.py:301
  21.3 1.3 %far_slots.1 = bf16[8,64,512]{2,1,0:T(8,128)(2,1)} custom-call(bf16[336,512]{1,0:T(8,128)(2,1)S(1)} %collective-permute-done.packed_ref), custom_call_target="tpu_custom_call" | custom-call | flops 99999997952 | bytes 868352 | tf_op jit(solution)/shard_map/far_slots/pallas_call | solution.py:34
  22.6 3.3 %all-to-all-done.disp_ref.near_ref = bf16[8,64,512]{2,1,0:T(8,128)(2,1)S(1)} async-done(((bf16[8,64,512]{2,1,0:T(8,128)(2,1)}), bf16[8,64,512]{2,1,0:T(8,128)(2,1)S(1)}, u32[]{:S(2)}, u32[]{:S(2)}) %all-to-all-start) | async-done | bytes 524320 | tf_op jit(solution)/shard_map/all_to_all | solution.py:323
  25.9 3.5 %all-to-all-start.1 = ((bf16[8,64,512]{2,1,0:T(8,128)(2,1)}), bf16[8,64,512]{2,1,0:T(8,128)(2,1)S(1)}, u32[]{:S(2)}, u32[]{:S(2)}) async-start(bf16[8,64,512]{2,1,0:T(8,128)(2,1)} %far_slots.1), calls=%async_computation.1 | async-start | bytes 1048576 | tf_op jit(solution)/shard_map/all_to_all | solution.py:339
  29.4 1.6 %collective-permute-start.1 = (bf16[8,64,512]{2,1,0:T(8,128)(2,1)S(1)}, bf16[8,64,512]{2,1,0:T(8,128)(2,1)S(1)}, u32[]{:S(2)}, u32[]{:S(2)}) collective-permute-start(bf16[8,64,512]{2,1,0:T(8,128)(2,1)S(1)} %all-to-all-done.disp_ref.near_ref), channel_id=1, source_target_pairs={{0,16},{16,0},{1,17},{17,1},{2,18},{18,2},{3,19},{19,3},{4,20},{20... | collective-permute-start | bytes 1572872 | tf_op jit(solution)/shard_map/ppermute | solution.py:327
  31.0 4.9 %near_backward.1 = (bf16[8,32,512]{2,1,0:T(8,128)(2,1)S(1)}, bf16[512,160]{1,0:T(8,128)(2,1)S(1)}) custom-call(bf16[336,512]{1,0:T(8,128)(2,1)S(1)} %pack.1.packed_ref, bf16[8,64,512]{2,1,0:T(8,128)(2,1)S(1)} %all-to-all-done.disp_ref.near_ref, bf16[1,2048,512]{2,1,0:T(8,128)(2,1)} %refs_2_.1, bf16[1,2048,512]{2,1,0:T(8,128)(2,1)} %refs_3_.1), custom_call_target="tpu_custom_call" | custom-call | flops 1610612736 | bytes 5488640 | tf_op jit(solution)/shard_map/near_backward/pallas_call | solution.py:34
  35.9 2.2 %all-to-all-done.1.disp_ref.far_ref = bf16[8,64,512]{2,1,0:T(8,128)(2,1)S(1)} async-done(((bf16[8,64,512]{2,1,0:T(8,128)(2,1)}), bf16[8,64,512]{2,1,0:T(8,128)(2,1)S(1)}, u32[]{:S(2)}, u32[]{:S(2)}) %all-to-all-start.1) | async-done | bytes 524320 | tf_op jit(solution)/shard_map/all_to_all | solution.py:339
  38.2 1.5 %collective-permute-start.2 = (bf16[8,64,512]{2,1,0:T(8,128)(2,1)S(1)}, bf16[8,64,512]{2,1,0:T(8,128)(2,1)S(1)}, u32[]{:S(2)}, u32[]{:S(2)}) collective-permute-start(bf16[8,64,512]{2,1,0:T(8,128)(2,1)S(1)} %all-to-all-done.1.disp_ref.far_ref), channel_id=1, source_target_pairs={{0,16},{16,0},{1,17},{17,1},{2,18},{18,2},{3,19},{19,3},{4,20},{20... | collective-permute-start | bytes 1572872 | tf_op jit(solution)/shard_map/ppermute | solution.py:340
  39.7 5.5 %far_backward.1 = bf16[2,8,32,512]{3,2,1,0:T(8,128)(2,1)} custom-call(bf16[8,32,512]{2,1,0:T(8,128)(2,1)S(1)} %get-tuple-element.13.near_ref, bf16[8,64,512]{2,1,0:T(8,128)(2,1)S(1)} %all-to-all-done.1.disp_ref.far_ref, bf16[1,2048,512]{2,1,0:T(8,128)(2,1)} %refs_2_.1, bf16[1,2048,512]{2,1,0:T(8,128)(2,1)} %refs_3_.1), custom_call_target="tpu_custom_call" | custom-call | flops 99999997952 | bytes 4194304 | tf_op jit(solution)/shard_map/far_backward/pallas_call | solution.py:360
  45.3 3.6 %all-to-all-start.2 = ((bf16[16,32,512]{2,1,0:T(8,128)(2,1)}), bf16[16,32,512]{2,1,0:T(8,128)(2,1)S(1)}, u32[]{:S(2)}, u32[]{:S(2)}) async-start(bf16[16,32,512]{2,1,0:T(8,128)(2,1)} %bitcast.8), calls=%async_computation.2 | async-start | bytes 1048576 | tf_op jit(solution)/shard_map/all_to_all | solution.py:374
  48.9 3.9 %own_weights.1 = (f32[1024,512]{1,0:T(8,128)S(1)}, f32[1024,512]{1,0:T(8,128)S(1)}) custom-call(bf16[8,64,512]{2,1,0:T(8,128)(2,1)S(1)} %all-to-all-done.disp_ref.near_ref, bf16[8,64,512]{2,1,0:T(8,128)(2,1)S(1)} %all-to-all-done.1.disp_ref.far_ref, bf16[1,2048,512]{2,1,0:T(8,128)(2,1)} %refs_2_.1, bf16[1,2048,512]{2,1,0:T(8,128)(2,1)} %refs_3_.1), custom_call_target="tpu_custom_call" | custom-call | flops 2147483648 | bytes 9437184 | tf_op jit(solution)/shard_map/own_weights/pallas_call | solution.py:34
  52.8 0.0 collective-permute-done.1.refs_0_
  52.8 2.1 %collective-permute-done.2.refs_1_ = bf16[8,64,512]{2,1,0:T(8,128)(2,1)S(1)} collective-permute-done((bf16[8,64,512]{2,1,0:T(8,128)(2,1)S(1)}, bf16[8,64,512]{2,1,0:T(8,128)(2,1)S(1)}, u32[]{:S(2)}, u32[]{:S(2)}) %collective-permute-start.2) | collective-permute-done | bytes 524320 | tf_op jit(solution)/shard_map/ppermute | solution.py:340
  54.9 0.0 copy-start
  54.9 0.0 copy-start.1
  54.9 5.0 %other_weights.1 = (bf16[1,1024,512]{2,1,0:T(8,128)(2,1)}, bf16[1,1024,512]{2,1,0:T(8,128)(2,1)}) custom-call(bf16[8,64,512]{2,1,0:T(8,128)(2,1)S(1)} %collective-permute-done.1.refs_0_, bf16[8,64,512]{2,1,0:T(8,128)(2,1)S(1)} %collective-permute-done.2.refs_1_, bf16[1,2048,512]{2,1,0:T(8,128)(2,1)} %refs_2_.1, bf16[1,2048,512]{2,1,0:T(8,128)(2,1)} %refs_3_.1, ...), custom_call_target="tpu_custom_call" | custom-call | flops 99999997952 | bytes 11534336 | tf_op jit(solution)/shard_map/other_weights/pallas_call | solution.py:34
  59.9 3.4 %all-to-all-done.2.back_ref = bf16[16,32,512]{2,1,0:T(8,128)(2,1)S(1)} async-done(((bf16[16,32,512]{2,1,0:T(8,128)(2,1)}), bf16[16,32,512]{2,1,0:T(8,128)(2,1)S(1)}, u32[]{:S(2)}, u32[]{:S(2)}) %all-to-all-start.2) | async-done | bytes 524320 | tf_op jit(solution)/shard_map/all_to_all | solution.py:374
  63.3 0.0 copy-done
  63.3 0.0 copy-done.1
  63.3 1.0 %combine.1 = (bf16[160,512]{1,0:T(8,128)(2,1)}, bf16[2,160]{1,0:T(2,128)(2,1)}) custom-call(s32[2,160]{1,0:T(2,128)S(1)} %bitcast.5, bf16[2,160]{1,0:T(2,128)(2,1)S(1)} %bitcast.7, bf16[512,160]{1,0:T(8,128)(2,1)S(1)} %get-tuple-element.12.pick_ref, bf16[16,32,512]{2,1,0:T(8,128)(2,1)S(1)} %all-to-all-done.2.back_ref), custom_call_target="tpu_custom_call" | custom-call | flops 83886080 | bytes 854528 | tf_op jit(solution)/shard_map/combine/pallas_call | solution.py:34
Async XLA Ops:
  1.7 19.6 %collective-permute-start = (bf16[336,512]{1,0:T(8,128)(2,1)S(1)}, bf16[336,512]{1,0:T(8,128)(2,1)S(1)}, u32[]{:S(2)}, u32[]{:S(2)}) collective-permute-start(bf16[336,512]{1,0:T(8,128)(2,1)S(1)} %pack.1.packed_ref), channel_id=1, source_target_pairs={{0,8},{1,9},{2,10},{3,11},{4,12},{5,13},{6,14},{7,15},{8,0},{9,1},... | collective-permute-start | bytes 1032200 | tf_op jit(solution)/shard_map/ppermute | solution.py:301
  7.1 18.8 %all-to-all-start = ((bf16[8,64,512]{2,1,0:T(8,128)(2,1)}), bf16[8,64,512]{2,1,0:T(8,128)(2,1)S(1)}, u32[]{:S(2)}, u32[]{:S(2)}) async-start(bf16[8,64,512]{2,1,0:T(8,128)(2,1)} %near_slots.1), calls=%async_computation | async-start | bytes 1048576 | tf_op jit(solution)/shard_map/all_to_all | solution.py:323
  25.9 12.3 %all-to-all-start.1 = ((bf16[8,64,512]{2,1,0:T(8,128)(2,1)}), bf16[8,64,512]{2,1,0:T(8,128)(2,1)S(1)}, u32[]{:S(2)}, u32[]{:S(2)}) async-start(bf16[8,64,512]{2,1,0:T(8,128)(2,1)} %far_slots.1), calls=%async_computation.1 | async-start | bytes 1048576 | tf_op jit(solution)/shard_map/all_to_all | solution.py:339
  29.4 23.4 %collective-permute-start.1 = (bf16[8,64,512]{2,1,0:T(8,128)(2,1)S(1)}, bf16[8,64,512]{2,1,0:T(8,128)(2,1)S(1)}, u32[]{:S(2)}, u32[]{:S(2)}) collective-permute-start(bf16[8,64,512]{2,1,0:T(8,128)(2,1)S(1)} %all-to-all-done.disp_ref.near_ref), channel_id=1, source_target_pairs={{0,16},{16,0},{1,17},{17,1},{2,18},{18,2},{3,19},{19,3},{4,20},{20... | collective-permute-start | bytes 1572872 | tf_op jit(solution)/shard_map/ppermute | solution.py:327
  38.2 16.7 %collective-permute-start.2 = (bf16[8,64,512]{2,1,0:T(8,128)(2,1)S(1)}, bf16[8,64,512]{2,1,0:T(8,128)(2,1)S(1)}, u32[]{:S(2)}, u32[]{:S(2)}) collective-permute-start(bf16[8,64,512]{2,1,0:T(8,128)(2,1)S(1)} %all-to-all-done.1.disp_ref.far_ref), channel_id=1, source_target_pairs={{0,16},{16,0},{1,17},{17,1},{2,18},{18,2},{3,19},{19,3},{4,20},{20... | collective-permute-start | bytes 1572872 | tf_op jit(solution)/shard_map/ppermute | solution.py:340
  45.3 18.0 %all-to-all-start.2 = ((bf16[16,32,512]{2,1,0:T(8,128)(2,1)}), bf16[16,32,512]{2,1,0:T(8,128)(2,1)S(1)}, u32[]{:S(2)}, u32[]{:S(2)}) async-start(bf16[16,32,512]{2,1,0:T(8,128)(2,1)} %bitcast.8), calls=%async_computation.2 | async-start | bytes 1048576 | tf_op jit(solution)/shard_map/all_to_all | solution.py:374
  54.9 8.4 %copy-start = (s32[160,2]{0,1:T(2,128)S(1)}, s32[160,2]{0,1:T(2,128)}, u32[]{:S(2)}) copy-start(s32[160,2]{0,1:T(2,128)} %param.8) | copy-start | bytes 3844
  54.9 8.4 %copy-start.1 = (bf16[160,2]{0,1:T(2,128)(2,1)S(1)}, bf16[160,2]{0,1:T(2,128)(2,1)}, u32[]{:S(2)}) copy-start(bf16[160,2]{0,1:T(2,128)(2,1)} %param.7) | copy-start | bytes 1924

commit v8 on v1

v8 whole, which is shorter than its diff:
```python
import functools
import itertools

import jax
import jax.numpy as jnp
from jax import lax
from jax.experimental import pallas as pl
from jax.experimental.pallas import tpu as pltpu
from jax.sharding import PartitionSpec as P

F32 = jnp.float32
BF16 = jnp.bfloat16
SMALL, MEDIUM, LARGE = 8 << 20, 12 << 20, 24 << 20
AHEAD = 10**11
IN_HBM = pl.BlockSpec(memory_space=pltpu.HBM)
IN_VMEM = pl.BlockSpec(memory_space=pltpu.VMEM)
DMA = pltpu.SemaphoreType.DMA


def dot(left, right, left_dim, right_dim):
    return lax.dot_general(
        left, right, (((left_dim,), (right_dim,)), ((), ())), preferred_element_type=F32
    )


def silu_parts(preact):
    sigma = 0.5 * jnp.tanh(0.5 * preact) + 0.5
    active = preact * sigma
    return active, sigma + active * (1.0 - sigma)


def call(body, name, outs, args, in_specs, scratch, flops, transcendentals=0, limit=MEDIUM):
    moved = sum(a.size * a.dtype.itemsize for a in (*args, *outs))
    return pl.pallas_call(
        body,
        name=name,
        out_shape=outs,
        in_specs=in_specs,
        out_specs=[IN_VMEM] * len(outs),
        scratch_shapes=scratch,
        compiler_params=pltpu.CompilerParams(vmem_limit_bytes=limit),
        cost_estimate=pl.CostEstimate(
            flops=flops, bytes_accessed=moved, transcendentals=transcendentals
        ),
    )(*args)


def paired(chips):
    return chips & (chips - 1) == 0


def hops_to(chips, k):
    if paired(chips):
        return [(2 * i + c, 2 * (i ^ k) + c) for i in range(chips) for c in range(2)]
    return [(2 * i + c, 2 * ((i + k) % chips) + c) for i in range(chips) for c in range(2)]


def pieces_of(experts, chips):
    me = lax.axis_index("exp")
    if paired(chips):
        return experts ^ me
    chip = (experts // 2 - me // 2 + chips) % chips
    return 2 * chip + (experts + me) % 2


def origin_of(k, core, chips):
    me = lax.axis_index("exp")
    if paired(chips):
        return me ^ (2 * k + core)
    return 2 * ((me // 2 - k + chips) % chips) + (me + core) % 2


def slots_of(pieces, number_of):
    rows = pieces.shape[1]
    number = lax.broadcasted_iota(jnp.int32, (number_of, rows), 0)
    hot = [number == pieces[k : k + 1, :] for k in range(2)]
    as_num = [jnp.where(h, 1.0, 0.0).astype(F32) for h in hot]
    before = jnp.where(
        lax.broadcasted_iota(jnp.int32, (rows, rows), 0)
        < lax.broadcasted_iota(jnp.int32, (rows, rows), 1),
        1.0,
        0.0,
    ).astype(BF16)
    count = dot(jnp.concatenate(as_num, axis=0).astype(BF16), before, 1, 0)
    total = jnp.sum(as_num[0], axis=1, keepdims=True)
    place = [count[:number_of], count[number_of:] + total]
    slot = [
        jnp.sum(jnp.where(h, p, 0.0), axis=0, keepdims=True).astype(jnp.int32)
        for h, p in zip(hot, place)
    ]
    return hot, slot


def picks_of(pieces, slot, number_of, pad):
    index = lax.broadcasted_iota(jnp.int32, (number_of * pad, pieces.shape[1]), 0)
    return [index == pieces[k : k + 1, :] * pad + slot[k] for k in range(2)]


def slots_kernel(pad, routes_hbm, gates_hbm, tok_hbm, cot_hbm, *refs):
    chips = len(refs) - 5
    out_refs, refs = refs[:chips], refs[chips:]
    routes_ref, gates_ref, tok_ref, cot_ref, sems = refs
    pairs = [
        (routes_hbm, routes_ref),
        (gates_hbm, gates_ref),
        (tok_hbm, tok_ref),
        (cot_hbm, cot_ref),
    ]
    copies = [
        pltpu.make_async_copy(src, dst, sems.at[i]) for i, (src, dst) in enumerate(pairs)
    ]
    for copy in copies:
        copy.start()
    copies[0].wait()
    copies[1].wait()
    pieces = pieces_of(routes_ref[...], chips)
    gates = gates_ref[...].astype(F32)
    _, slot = slots_of(pieces, 2 * chips)
    pick = picks_of(pieces, slot, 2 * chips, pad)
    plain = jnp.where(pick[0] | pick[1], 1.0, 0.0).astype(BF16)
    scaled = (
        jnp.where(pick[0], gates[0:1, :], 0.0) + jnp.where(pick[1], gates[1:2, :], 0.0)
    ).astype(BF16)
    copies[2].wait()
    copies[3].wait()
    rows = dot(plain, tok_ref[...], 1, 0).astype(BF16)
    grads = dot(scaled, cot_ref[...], 1, 0).astype(BF16)
    for k, out_ref in enumerate(out_refs):
        for i in range(2):
            here = slice((2 * k + i) * pad, (2 * k + i + 1) * pad)
            out_ref[2 * i * pad : (2 * i + 1) * pad, :] = rows[here, :]
            out_ref[(2 * i + 1) * pad : (2 * i + 2) * pad, :] = grads[here, :]


class Fetch:
    def __init__(self, up_hbm, down_hbm, up_ref, down_ref, sems, base, block):
        self.pairs = [(up_hbm, up_ref), (down_hbm, down_ref)]
        self.sems, self.base, self.block = sems, base, block
        self.steps = up_ref.shape[0] // block
        self.copies = []
        self.start()

    def start(self):
        step = len(self.copies)
        if step == self.steps:
            return
        to = pl.ds(step * self.block, self.block)
        of = pl.ds(pl.multiple_of(self.base + step * self.block, self.block), self.block)
        self.copies.append([
            pltpu.make_async_copy(src.at[0, of, :], dst.at[to, :], self.sems.at[2 * step + i])
            for i, (src, dst) in enumerate(self.pairs)
        ])
        for copy in self.copies[-1]:
            copy.start()

    def wait(self, step):
        self.start()
        for copy in self.copies[step]:
            copy.wait()


def gather_rows(pad, blocks, rows_ref, grads_ref):
    for i, (ref, at) in enumerate(blocks):
        here = slice(i * pad, (i + 1) * pad)
        rows_ref[here, :] = ref[at : at + pad, :]
        grads_ref[here, :] = ref[at + pad : at + 2 * pad, :]


def backward(cap, pad, block, blocks, weights, scratch, put):
    rows_ref, grads_ref, grad_acc, gate_acc, up_ref, down_ref, sems = scratch
    fetch = Fetch(*weights, up_ref, down_ref, sems, 0, block)
    gather_rows(pad, blocks, rows_ref, grads_ref)
    slots = rows_ref.shape[0]
    for step in range(up_ref.shape[0] // block):
        part = pl.ds(step * block, block)
        fetch.wait(step)
        up = up_ref[part, :]
        active, slope = silu_parts(dot(rows_ref[...], up, 1, 1))
        back = dot(grads_ref[...], down_ref[part, :], 1, 1)
        hid_grad = (back * slope).astype(BF16)
        gate = active.astype(BF16).astype(F32) * back
        gate = sum(gate[:, i : i + 128] for i in range(0, block, 128))
        in_grad = dot(hid_grad, up, 1, 0)
        if step == 0:
            grad_acc[...] = in_grad
            gate_acc[...] = gate
        else:
            grad_acc[...] += in_grad
            gate_acc[...] += gate
    gate = jnp.sum(gate_acc[...], axis=1, keepdims=True)
    spot = lax.broadcasted_iota(jnp.int32, (slots, 128), 0) % pad
    lane = lax.broadcasted_iota(jnp.int32, (slots, 128), 1)
    gate = jnp.where(spot == lane, gate, 0.0).reshape(len(blocks), pad, 128)
    gate = jnp.sum(gate, axis=1, keepdims=True)
    line = lax.broadcasted_iota(jnp.int32, (pad, 128), 0)
    for k in range(len(blocks)):
        here = slice(k * pad, (k + 1) * pad)
        first = jnp.where(line == cap, gate[k], grad_acc[here, 0:128])
        put(k, first.astype(BF16), grad_acc[here, 128:].astype(BF16))


def blocks_of(pad, direct_refs, sibling_refs):
    direct = [(ref, 0) for ref in direct_refs]
    sibling = [(r, at) for r in sibling_refs for at in range(0, r.shape[0], 2 * pad)]
    return direct, sibling


def direct_back_kernel(cap, pad, block, chips, *refs):
    pieces, (up_hbm, down_hbm, out_ref, *scratch) = refs[:chips], refs[chips:]

    def put(k, first, rest):
        out_ref[k, :, 0:128] = first
        out_ref[k, :, 128:] = rest

    direct, _ = blocks_of(pad, pieces, [])
    backward(cap, pad, block, direct, (up_hbm, down_hbm), scratch, put)


def sibling_back_kernel(cap, pad, block, order, *refs):
    sibling_ref, direct_ref, up_hbm, down_hbm, out_hbm, mine_ref, sems, *scratch = refs
    copies = []

    def send(i, core):
        ref = mine_ref if core else direct_ref
        to = out_hbm.at[origin_of(order[i], core, len(order))]
        copies.append(pltpu.make_async_copy(ref.at[i], to, sems.at[2 * i + core]))
        copies[-1].start()

    for i in range(len(order)):
        send(i, 0)

    def put(k, first, rest):
        mine_ref[k, :, 0:128] = first
        mine_ref[k, :, 128:] = rest
        send(k, 1)

    _, sibling = blocks_of(pad, [], [sibling_ref])
    backward(cap, pad, block, sibling, (up_hbm, down_hbm), scratch, put)
    for copy in copies:
        copy.wait()


def weights_kernel(pad, block, share, direct, sibling, begun, *refs):
    refs = list(refs)
    take = lambda number: [refs.pop(0) for _ in range(number)]
    direct_refs, sibling_refs, weights = take(direct), take(sibling), take(2)
    sums = take(2) if begun else None
    notes = None if begun else take(2)
    out_up, out_down = take(2)
    notes_out = None if begun else take(3)
    rows_ref, grads_ref, up_ref, down_ref, sems = refs
    fetch = Fetch(*weights, up_ref, down_ref, sems, lax.axis_index("rep") * share, block)
    blocks = sum(blocks_of(pad, direct_refs, sibling_refs), [])
    gather_rows(pad, blocks, rows_ref, grads_ref)
    for step in range(share // block):
        here = pl.ds(step * block, block)
        fetch.wait(step)
        active, slope = silu_parts(dot(up_ref[here, :], rows_ref[...], 1, 1))
        back = dot(down_ref[here, :], grads_ref[...], 1, 1)
        hid_grad = (back * slope).astype(BF16)
        up_part = dot(hid_grad, rows_ref[...], 1, 0)
        down_part = dot(active.astype(BF16), grads_ref[...], 1, 0)
        if begun:
            up_part += sums[0][0, here, :]
            down_part += sums[1][0, here, :]
        out_up[0, here, :] = up_part.astype(out_up.dtype)
        out_down[0, here, :] = down_part.astype(out_down.dtype)
    if not begun:
        note_routes(pad, *notes, *notes_out)


def note_routes(pad, routes_ref, gates_ref, pick_ref, hot_ref, spot_ref):
    routes = routes_ref[...]
    gates = gates_ref[...].astype(F32)
    groups = pick_ref.shape[0] // pad
    hot, slot = slots_of(routes, groups)
    pick = picks_of(routes, slot, groups, pad)
    pick_ref[...] = jnp.where(pick[0] | pick[1], 1.0, 0.0).astype(BF16)
    lane = lax.broadcasted_iota(jnp.int32, (128, routes.shape[1]), 0)
    for k in range(2):
        hot_ref[k] = jnp.where(hot[k], 1.0 / gates[k : k + 1, :], 0.0)
        spot_ref[k] = jnp.where(lane == slot[k], 1.0, 0.0).astype(BF16)


def combine_kernel(cap, pick_ref, hot_ref, spot_ref, back_ref, d_tok_ref, d_gate_ref):
    groups, pad, feat = back_ref.shape
    back = back_ref[...]
    d_tok_ref[...] = dot(pick_ref[...], back.reshape(groups * pad, feat), 0, 0).astype(BF16)
    values = back[:, cap, 0:128]
    for k in range(2):
        found = dot(values, spot_ref[k], 1, 0) * hot_ref[k]
        d_gate_ref[k : k + 1, :] = jnp.sum(found, axis=0, keepdims=True).astype(BF16)


def local(tokens, gates, routes, cotangent, w_up, w_down):
    rows, feat = tokens.shape
    hidden = w_up.shape[1]
    groups = lax.axis_size("exp")
    mirrors = lax.axis_size("rep")
    chips = groups // 2
    cap = max(2, 3 * rows // groups)
    pad = (cap // 16 + 1) * 16
    slots = chips * pad
    share = hidden // mirrors
    routes_t, gates_t = routes.T, gates.T
    hbm = functools.partial(pltpu.with_memory_space_constraint, memory_space=pltpu.HBM)
    shape = jax.ShapeDtypeStruct
    unit = 2 * slots * feat

    out = call(
        functools.partial(slots_kernel, pad),
        "slots",
        [shape((4 * pad, feat), BF16)] * chips,
        [hbm(a) for a in (routes_t, gates_t, tokens, cotangent)],
        [IN_HBM] * 4,
        [
            pltpu.VMEM((2, rows), jnp.int32),
            pltpu.VMEM((2, rows), BF16),
            pltpu.VMEM((rows, feat), BF16),
            pltpu.VMEM((rows, feat), BF16),
            DMA((4,)),
        ],
        4 * unit * rows,
    )
    near, far = list(range(1, chips // 2)), list(range(chips // 2, chips))
    order = near[:1] + far[:1]
    for pair in itertools.zip_longest(far[1:], near[1:]):
        order += [k for k in pair if k is not None]
    pieces = [out[0]] + [lax.ppermute(out[k], "exp", hops_to(chips, k)) for k in order]

    swap = [(i, i ^ 1) for i in range(groups)]
    around = [[(i, (i + s) % mirrors) for i in range(mirrors)] for s in range(1, mirrors)]
    handed = jnp.concatenate([piece[2 * pad :] for piece in pieces], axis=0)
    sibling = lax.ppermute(handed, "exp", swap)
    arrived = jnp.concatenate([piece[: 2 * pad] for piece in pieces], axis=0)
    others = [lax.ppermute(a, "rep", hops) for hops in around for a in (arrived, sibling)]

    w_up, w_down = hbm(w_up), hbm(w_down)
    block = min(512, hidden)
    scratch = [
        pltpu.VMEM((slots, feat), BF16),
        pltpu.VMEM((slots, feat), BF16),
        pltpu.VMEM((slots, feat), F32),
        pltpu.VMEM((slots, 128), F32),
        pltpu.VMEM((hidden, feat), BF16),
        pltpu.VMEM((hidden, feat), BF16),
        DMA((2 * hidden // block,)),
    ]
    results = (chips, pad, feat)
    (direct,) = call(
        functools.partial(direct_back_kernel, cap, pad, block, chips),
        "direct_backward",
        [shape(results, BF16)],
        [*pieces, w_up, w_down],
        [IN_VMEM] * chips + [IN_HBM] * 2,
        scratch,
        AHEAD,
        slots * hidden,
    )
    back = pl.pallas_call(
        functools.partial(sibling_back_kernel, cap, pad, block, [0, *order]),
        name="sibling_backward",
        out_shape=pltpu.HBM((groups, pad, feat), BF16),
        in_specs=[IN_VMEM] * 2 + [IN_HBM] * 2,
        out_specs=IN_HBM,
        scratch_shapes=[pltpu.VMEM(results, BF16), DMA((groups,)), *scratch],
        compiler_params=pltpu.CompilerParams(vmem_limit_bytes=MEDIUM),
        cost_estimate=pl.CostEstimate(
            flops=AHEAD, bytes_accessed=4 * hidden * feat, transcendentals=slots * hidden
        ),
    )(sibling, direct, w_up, w_down)
    back = lax.all_to_all(back, "exp", split_axis=0, concat_axis=0, tiled=True)

    part = min(512, share)

    def weights_call(name, direct_in, sibling_in, sums, ended, flops):
        begun = bool(sums)
        number = slots * (len(direct_in) // chips + len(sibling_in))
        notes = [] if begun else [
            shape((groups * pad, rows), BF16),
            shape((2, groups, rows), F32),
            shape((2, 128, rows), BF16),
        ]
        kept = BF16 if ended else F32
        return call(
            functools.partial(
                weights_kernel, pad, part, share, len(direct_in), len(sibling_in), begun
            ),
            name,
            [shape((1, share, feat), kept)] * 2 + notes,
            [*direct_in, *sibling_in, w_up, w_down, *(sums or [routes_t, gates_t])],
            [IN_VMEM] * (len(direct_in) + len(sibling_in)) + [IN_HBM] * 2 + [IN_VMEM] * 2,
            [
                pltpu.VMEM((number, feat), BF16),
                pltpu.VMEM((number, feat), BF16),
                pltpu.VMEM((share, feat), BF16),
                pltpu.VMEM((share, feat), BF16),
                DMA((2 * share // part,)),
            ],
            flops,
            number * share,
            LARGE,
        )

    *sums, pick, hot, spot = weights_call(
        "own_weights", pieces, [sibling], [], not others, 8 * unit * share
    )
    for i, other in enumerate(others):
        sums = weights_call("other_weights", [], [other], sums, i == len(others) - 1, AHEAD)
    grad_up, grad_down = sums

    d_tokens, d_gates = call(
        functools.partial(combine_kernel, cap),
        "combine",
        [shape((rows, feat), BF16), shape((2, rows), BF16)],
        [pick, hot, spot, back],
        [IN_VMEM] * 4,
        [],
        4 * unit * rows,
    )
    return d_tokens, d_gates.T, grad_up, grad_down


def solution(mesh):
    by_both = P(("rep", "exp"), None)
    by_expert = P("exp", None, None)
    return jax.shard_map(
        local,
        mesh=mesh,
        in_specs=(by_both, by_both, by_both, by_both, by_expert, by_expert),
        out_specs=(by_both, by_both, P("exp", "rep", None), P("exp", "rep", None)),
        check_vma=False,
    )
```

time: 82.2 us -> 68.6 us (0.83)
  blocking collectives: 32 us -> 0 us
  starting transfers between devices: 7.08 us -> 24 us
  Pallas kernels: 12 us -> 25.4 us
  waiting for transfers between devices: 23.5 us -> 12.8 us
  local copies, waits for them, and re-layouts: 6.46 us -> 5.12 us
    all_to_all x1 -> x0, blocking collectives: 32 us -> none  [local(): disp = lax.all_to_all(out, 'exp', split_axis=0, concat_axis=0, tiled=True)]
    ppermute x2 -> x10, starting transfers between devices: 2.09 us -> 15.7 us  [the longest x7 13.6 us: local(): lax.ppermute(out[k], 'exp', hops_to(chips, k))]
    pallas_call x4 -> x7, Pallas kernels: 12 us -> 25.4 us  [the longest x6 20 us: call(): pl.pallas_call(body, name=name, out_shape=outs, in_specs=in_specs, out_sp...]
    ppermute x2 -> x10, waiting for transfers between devices: 23.5 us -> 12.8 us  [the longest x7 7.27 us: local(): lax.ppermute(out[k], 'exp', hops_to(chips, k))]
    all_to_all x1, starting transfers between devices: 4.99 us -> 8.32 us  [local(): back = lax.all_to_all(back, 'exp', split_axis=0, concat_axis=0, tiled=True)]
    unnamed x20 -> x11, local copies, waits for them, and re-layouts: 6.39 us -> 4.48 us
  transfers between devices with their start and end apart: 3 -> 11, of which waited for: 2 -> 4; matrix products, arithmetic and copies ran while one was open for 0% -> 7% of each run, Pallas kernels for 7% -> 32%
where the time goes in v8:
time: 68.6 us; the launch traced here: 68.1 us
  Pallas kernels  25.4 us (37%)
  starting transfers between devices  24 us (35%)
  waiting for transfers between devices  12.8 us (19%)
  local copies, waits for them, and re-layouts  5.12 us (7%)
  between operations  0.74 us (1%)
    pallas_call x6, Pallas kernels, call(): pl.pallas_call(body, name=name, out_shape=outs, in_specs=in_specs, out_sp...  20 us
    ppermute x7, starting transfers between devices, local(): lax.ppermute(out[k], 'exp', hops_to(chips, k))  13.6 us
    all_to_all x1, starting transfers between devices, local(): back = lax.all_to_all(back, 'exp', split_axis=0, concat_axis=0, tiled=True)  8.32 us
    ppermute x7, waiting for transfers between devices, local(): lax.ppermute(out[k], 'exp', hops_to(chips, k))  7.27 us
    ppermute x2, waiting for transfers between devices, local(): lax.ppermute(a, 'rep', hops)  5.57 us
    pallas_call x1, Pallas kernels, local(): pl.pallas_call(functools.partial(sibling_back_kernel, cap, pad, block, [0...  5.35 us
    unnamed x11, local copies, waits for them, and re-layouts  4.48 us
    ppermute x2, starting transfers between devices, local(): lax.ppermute(a, 'rep', hops)  2.1 us
  transfers between devices with their start and end apart: 11, of which 4 were waited for; matrix products, arithmetic and copies ran while one was open for 7% of the time, Pallas kernels for 32%

profile of v8, /device:TPU:0, one launch (start us, length us, event | category | flops | bytes accessed | tf_op | source)
XLA Modules:
  0.0 68.1 jit_solution(10878487590755992941)
XLA Ops:
  0.6 1.6 %slots.1 = (bf16[128,512]{1,0:T(8,128)(2,1)S(1)}, bf16[128,512]{1,0:T(8,128)(2,1)S(1)}, bf16[128,512]{1,0:T(8,128)(2,1)S(1)}, bf16[128,512]{1,0:T(8,128)(2,1)S(1...) custom-call(s32[2,160]{1,0:T(2,128)} %bitcast.3, ...), custom_call_target="tpu_custom_call" | custom-call | flops 167772160 | bytes 1378176 | tf_op jit(solution)/shard_map/slots/pallas_call | solution.py:34
  2.2 3.0 %collective-permute-start = (bf16[128,512]{1,0:T(8,128)(2,1)S(1)}, bf16[128,512]{1,0:T(8,128)(2,1)S(1)}, u32[]{:S(2)}, u32[]{:S(2)}) collective-permute-start(bf16[128,512]{1,0:T(8,128)(2,1)S(1)} %get-tuple-element.24), channel_id=1, source_target_pairs={{0,2},{1,3},{2,0},{3,1},{4,6},{5,7},{6,4},{7,5},{8,10},{9,11},{10,... | collective-permute-start | bytes 393224 | tf_op jit(solution)/shard_map/ppermute | solution.py:329
  5.3 2.6 %collective-permute-start.1 = (bf16[128,512]{1,0:T(8,128)(2,1)S(1)}, bf16[128,512]{1,0:T(8,128)(2,1)S(1)}, u32[]{:S(2)}, u32[]{:S(2)}) collective-permute-start(bf16[128,512]{1,0:T(8,128)(2,1)S(1)} %get-tuple-element.25), channel_id=1, source_target_pairs={{0,8},{1,9},{2,10},{3,11},{4,12},{5,13},{6,14},{7,15},{8,0},{9,1},... | collective-permute-start | bytes 393224 | tf_op jit(solution)/shard_map/ppermute | solution.py:329
  7.8 0.0 collective-permute-start.2
  7.9 1.9 %collective-permute-start.3 = (bf16[128,512]{1,0:T(8,128)(2,1)S(1)}, bf16[128,512]{1,0:T(8,128)(2,1)S(1)}, u32[]{:S(2)}, u32[]{:S(2)}) collective-permute-start(bf16[128,512]{1,0:T(8,128)(2,1)S(1)} %get-tuple-element.27), channel_id=1, source_target_pairs={{0,4},{1,5},{2,6},{3,7},{4,0},{5,1},{6,2},{7,3},{8,12},{9,13},{10,... | collective-permute-start | bytes 393224 | tf_op jit(solution)/shard_map/ppermute | solution.py:329
  9.7 2.5 %collective-permute-start.4 = (bf16[128,512]{1,0:T(8,128)(2,1)S(1)}, bf16[128,512]{1,0:T(8,128)(2,1)S(1)}, u32[]{:S(2)}, u32[]{:S(2)}) collective-permute-start(bf16[128,512]{1,0:T(8,128)(2,1)S(1)} %get-tuple-element.28), channel_id=1, source_target_pairs={{0,12},{1,13},{2,14},{3,15},{4,8},{5,9},{6,10},{7,11},{8,4},{9,5},... | collective-permute-start | bytes 393224 | tf_op jit(solution)/shard_map/ppermute | solution.py:329
  12.2 0.6 slice_dynamic-update-slice_fusion.14
  12.8 0.0 collective-permute-done.refs_1_
  12.8 1.6 %collective-permute-start.5 = (bf16[128,512]{1,0:T(8,128)(2,1)S(1)}, bf16[128,512]{1,0:T(8,128)(2,1)S(1)}, u32[]{:S(2)}, u32[]{:S(2)}) collective-permute-start(bf16[128,512]{1,0:T(8,128)(2,1)S(1)} %get-tuple-element.29), channel_id=1, source_target_pairs={{0,6},{1,7},{2,4},{3,5},{4,2},{5,3},{6,0},{7,1},{8,14},{9,15},{10,... | collective-permute-start | bytes 393224 | tf_op jit(solution)/shard_map/ppermute | solution.py:329
  14.5 0.6 slice_dynamic-update-slice_fusion.6
  15.1 4.7 %collective-permute-done.1.refs_2_ = bf16[128,512]{1,0:T(8,128)(2,1)S(1)} collective-permute-done((bf16[128,512]{1,0:T(8,128)(2,1)S(1)}, bf16[128,512]{1,0:T(8,128)(2,1)S(1)}, u32[]{:S(2)}, u32[]{:S(2)}) %collective-permute-start.1) | collective-permute-done | bytes 131104 | tf_op jit(solution)/shard_map/ppermute | solution.py:329
  19.8 2.0 %collective-permute-start.6 = (bf16[128,512]{1,0:T(8,128)(2,1)S(1)}, bf16[128,512]{1,0:T(8,128)(2,1)S(1)}, u32[]{:S(2)}, u32[]{:S(2)}) collective-permute-start(bf16[128,512]{1,0:T(8,128)(2,1)S(1)} %get-tuple-element.30), channel_id=1, source_target_pairs={{0,14},{1,15},{2,12},{3,13},{4,10},{5,11},{6,8},{7,9},{8,6},{9,7},... | collective-permute-start | bytes 393224 | tf_op jit(solution)/shard_map/ppermute | solution.py:329
  21.8 0.6 slice_dynamic-update-slice_fusion.5
  22.4 1.8 %collective-permute-done.2.refs_3_ = bf16[128,512]{1,0:T(8,128)(2,1)S(1)} collective-permute-done((bf16[128,512]{1,0:T(8,128)(2,1)S(1)}, bf16[128,512]{1,0:T(8,128)(2,1)S(1)}, u32[]{:S(2)}, u32[]{:S(2)}) %collective-permute-start.2) | collective-permute-done | bytes 131104 | tf_op jit(solution)/shard_map/ppermute | solution.py:329
  24.2 0.6 slice_dynamic-update-slice_fusion.4
  24.9 0.0 collective-permute-done.3.refs_4_
  24.9 0.6 slice_dynamic-update-slice_fusion.3
  25.5 0.0 collective-permute-done.4.refs_5_
  25.5 0.6 slice_dynamic-update-slice_fusion.2
  26.2 0.0 collective-permute-done.5.refs_6_
  26.2 0.6 slice_dynamic-update-slice_fusion.1
  26.8 0.7 %collective-permute-done.6.refs_7_ = bf16[128,512]{1,0:T(8,128)(2,1)S(1)} collective-permute-done((bf16[128,512]{1,0:T(8,128)(2,1)S(1)}, bf16[128,512]{1,0:T(8,128)(2,1)S(1)}, u32[]{:S(2)}, u32[]{:S(2)}) %collective-permute-start.6) | collective-permute-done | bytes 131104 | tf_op jit(solution)/shard_map/ppermute | solution.py:329
  27.6 0.6 slice_dynamic-update-slice_fusion
  28.2 1.5 %collective-permute-start.9 = (bf16[512,512]{1,0:T(8,128)(2,1)}, bf16[512,512]{1,0:T(8,128)(2,1)}, u32[]{:S(2)}, u32[]{:S(2)}) collective-permute-start(bf16[512,512]{1,0:T(8,128)(2,1)} %get-tuple-element.42), channel_id=1, source_target_pairs={{0,16},{16,0},{1,17},{17,1},{2,18},{18,2},{3,19},{19,3},{4,20},{20... | collective-permute-start | bytes 1572872 | tf_op jit(solution)/shard_map/ppermute | solution.py:336
  29.7 0.0 collective-permute-start.7
  29.7 4.4 %direct_backward.1.refs_1_ = bf16[8,32,512]{2,1,0:T(8,128)(2,1)S(1)} custom-call(bf16[128,512]{1,0:T(8,128)(2,1)S(1)} %get-tuple-element.23.refs_0_, bf16[128,512]{1,0:T(8,128)(2,1)S(1)} %collective-permute-done.refs_1_, bf16[128,512]{1,0:T(8,128)(2,1)S(1)} %collective-permute-done.1.refs_2_, bf16[128,512]{1,0:T(8,128)(2,1)S(1)} %collective-permute-done.2.refs_3_, ...), custom_call_target="tpu_custom_call" | custom-call | flops 99999997952 | bytes 5505024 | tf_op jit(solution)/shard_map/direct_backward/pallas_call | solution.py:34
  34.1 0.0 copy-start
  34.2 0.0 copy-start.1
  34.2 0.0 collective-permute-done.7.refs_8_.refs_0_
  34.2 5.4 %sibling_backward.1 = bf16[16,32,512]{2,1,0:T(8,128)(2,1)} custom-call(bf16[512,512]{1,0:T(8,128)(2,1)S(1)} %collective-permute-done.7.refs_8_.refs_0_, bf16[8,32,512]{2,1,0:T(8,128)(2,1)S(1)} %direct_backward.1.refs_1_, bf16[1,2048,512]{2,1,0:T(8,128)(2,1)} %refs_1_.3, bf16[1,2048,512]{2,1,0:T(8,128)(2,1)} %refs_2_.5), custom_call_target="tpu_custom_call" | custom-call | flops 99999997952 | bytes 4194304 | tf_op jit(solution)/shard_map/sibling_backward/pallas_call | solution.py:360
  39.5 8.3 %all-to-all-start = ((bf16[16,32,512]{2,1,0:T(8,128)(2,1)}), bf16[16,32,512]{2,1,0:T(8,128)(2,1)}, u32[]{:S(2)}, u32[]{:S(2)}) async-start(bf16[16,32,512]{2,1,0:T(8,128)(2,1)} %sibling_backward.1), calls=%async_computation | async-start | bytes 1048576 | tf_op jit(solution)/shard_map/all_to_all | solution.py:372
  47.9 0.6 collective-permute-start.8
  48.5 0.0 copy-done
  48.5 0.0 copy-done.1
  48.5 4.1 %own_weights.1 = (f32[1,1024,512]{2,1,0:T(8,128)S(1)}, f32[1,1024,512]{2,1,0:T(8,128)S(1)}, bf16[512,160]{1,0:T(8,128)(2,1)S(1)}, f32[2,16,160]{2,1,0:T(8,128)S(1)}, bf16[2,128,160]{2,1,0:T(8,128)(2,1)S(1)}) custom-call(bf16[128,512]{1,0:T(8,128)(2,1)S(1)} %get-tuple-element.23.refs_0_, bf16[128,512]{1,0:T(8,128)(2,1)S(1)} %collective-permute-done.refs_1_, ...), custom_call_target="tpu_custom_call" | custom-call | flops 2147483648 | bytes 10229632 | tf_op jit(solution)/shard_map/own_weights/pallas_call | solution.py:34
  52.6 0.0 collective-permute-done.9.refs_0_
  52.6 3.9 %other_weights.2 = (f32[1,1024,512]{2,1,0:T(8,128)S(1)}, f32[1,1024,512]{2,1,0:T(8,128)S(1)}) custom-call(bf16[512,512]{1,0:T(8,128)(2,1)} %collective-permute-done.9.refs_0_, bf16[1,2048,512]{2,1,0:T(8,128)(2,1)} %refs_1_.3, bf16[1,2048,512]{2,1,0:T(8,128)(2,1)} %refs_2_.5, f32[1,1024,512]{2,1,0:T(8,128)S(1)} %get-tuple-element.36.refs_3_, ...), custom_call_target="tpu_custom_call" | custom-call | flops 99999997952 | bytes 13107200 | tf_op jit(solution)/shard_map/other_weights/pallas_call | solution.py:34
  56.5 5.6 %collective-permute-done.8.refs_0_ = bf16[512,512]{1,0:T(8,128)(2,1)S(1)} collective-permute-done((bf16[512,512]{1,0:T(8,128)(2,1)S(1)}, bf16[512,512]{1,0:T(8,128)(2,1)S(1)}, u32[]{:S(2)}, u32[]{:S(2)}) %collective-permute-start.8) | collective-permute-done | bytes 524320 | tf_op jit(solution)/shard_map/ppermute | solution.py:336
  62.1 4.0 %other_weights.3 = (bf16[1,1024,512]{2,1,0:T(8,128)(2,1)}, bf16[1,1024,512]{2,1,0:T(8,128)(2,1)}) custom-call(bf16[512,512]{1,0:T(8,128)(2,1)S(1)} %collective-permute-done.8.refs_0_, bf16[1,2048,512]{2,1,0:T(8,128)(2,1)} %refs_1_.3, bf16[1,2048,512]{2,1,0:T(8,128)(2,1)} %refs_2_.5, f32[1,1024,512]{2,1,0:T(8,128)S(1)} %get-tuple-element.38.refs_3_, ...), custom_call_target="tpu_custom_call" | custom-call | flops 99999997952 | bytes 11010048 | tf_op jit(solution)/shard_map/other_weights/pallas_call | solution.py:34
  66.1 0.0 all-to-all-done.back_ref
  66.1 2.0 %combine.1 = (bf16[160,512]{1,0:T(8,128)(2,1)}, bf16[2,160]{1,0:T(2,128)(2,1)}) custom-call(bf16[512,160]{1,0:T(8,128)(2,1)S(1)} %get-tuple-element.31.pick_ref, f32[2,16,160]{2,1,0:T(8,128)S(1)} %get-tuple-element.32.hot_ref, bf16[2,128,160]{2,1,0:T(8,128)(2,1)S(1)} %get-tuple-element.33.spot_ref, bf16[16,32,512]{2,1,0:T(8,128)(2,1)} %all-to-all-done.back_ref), custom_call_target="tpu_custom_call" | custom-call | flops 167772160 | bytes 955008 | tf_op jit(solution)/shard_map/combine/pallas_call | solution.py:34
Async XLA Ops:
  2.2 10.6 %collective-permute-start = (bf16[128,512]{1,0:T(8,128)(2,1)S(1)}, bf16[128,512]{1,0:T(8,128)(2,1)S(1)}, u32[]{:S(2)}, u32[]{:S(2)}) collective-permute-start(bf16[128,512]{1,0:T(8,128)(2,1)S(1)} %get-tuple-element.24), channel_id=1, source_target_pairs={{0,2},{1,3},{2,0},{3,1},{4,6},{5,7},{6,4},{7,5},{8,10},{9,11},{10,... | collective-permute-start | bytes 393224 | tf_op jit(solution)/shard_map/ppermute | solution.py:329
  5.3 14.5 %collective-permute-start.1 = (bf16[128,512]{1,0:T(8,128)(2,1)S(1)}, bf16[128,512]{1,0:T(8,128)(2,1)S(1)}, u32[]{:S(2)}, u32[]{:S(2)}) collective-permute-start(bf16[128,512]{1,0:T(8,128)(2,1)S(1)} %get-tuple-element.25), channel_id=1, source_target_pairs={{0,8},{1,9},{2,10},{3,11},{4,12},{5,13},{6,14},{7,15},{8,0},{9,1},... | collective-permute-start | bytes 393224 | tf_op jit(solution)/shard_map/ppermute | solution.py:329
  7.8 16.4 %collective-permute-start.2 = (bf16[128,512]{1,0:T(8,128)(2,1)S(1)}, bf16[128,512]{1,0:T(8,128)(2,1)S(1)}, u32[]{:S(2)}, u32[]{:S(2)}) collective-permute-start(bf16[128,512]{1,0:T(8,128)(2,1)S(1)} %get-tuple-element.26), channel_id=1, source_target_pairs={{0,10},{1,11},{2,8},{3,9},{4,14},{5,15},{6,12},{7,13},{8,2},{9,3},... | collective-permute-start | bytes 393224 | tf_op jit(solution)/shard_map/ppermute | solution.py:329
  7.9 17.0 %collective-permute-start.3 = (bf16[128,512]{1,0:T(8,128)(2,1)S(1)}, bf16[128,512]{1,0:T(8,128)(2,1)S(1)}, u32[]{:S(2)}, u32[]{:S(2)}) collective-permute-start(bf16[128,512]{1,0:T(8,128)(2,1)S(1)} %get-tuple-element.27), channel_id=1, source_target_pairs={{0,4},{1,5},{2,6},{3,7},{4,0},{5,1},{6,2},{7,3},{8,12},{9,13},{10,... | collective-permute-start | bytes 393224 | tf_op jit(solution)/shard_map/ppermute | solution.py:329
  9.7 15.8 %collective-permute-start.4 = (bf16[128,512]{1,0:T(8,128)(2,1)S(1)}, bf16[128,512]{1,0:T(8,128)(2,1)S(1)}, u32[]{:S(2)}, u32[]{:S(2)}) collective-permute-start(bf16[128,512]{1,0:T(8,128)(2,1)S(1)} %get-tuple-element.28), channel_id=1, source_target_pairs={{0,12},{1,13},{2,14},{3,15},{4,8},{5,9},{6,10},{7,11},{8,4},{9,5},... | collective-permute-start | bytes 393224 | tf_op jit(solution)/shard_map/ppermute | solution.py:329
  12.8 13.3 %collective-permute-start.5 = (bf16[128,512]{1,0:T(8,128)(2,1)S(1)}, bf16[128,512]{1,0:T(8,128)(2,1)S(1)}, u32[]{:S(2)}, u32[]{:S(2)}) collective-permute-start(bf16[128,512]{1,0:T(8,128)(2,1)S(1)} %get-tuple-element.29), channel_id=1, source_target_pairs={{0,6},{1,7},{2,4},{3,5},{4,2},{5,3},{6,0},{7,1},{8,14},{9,15},{10,... | collective-permute-start | bytes 393224 | tf_op jit(solution)/shard_map/ppermute | solution.py:329
  19.8 7.8 %collective-permute-start.6 = (bf16[128,512]{1,0:T(8,128)(2,1)S(1)}, bf16[128,512]{1,0:T(8,128)(2,1)S(1)}, u32[]{:S(2)}, u32[]{:S(2)}) collective-permute-start(bf16[128,512]{1,0:T(8,128)(2,1)S(1)} %get-tuple-element.30), channel_id=1, source_target_pairs={{0,14},{1,15},{2,12},{3,13},{4,10},{5,11},{6,8},{7,9},{8,6},{9,7},... | collective-permute-start | bytes 393224 | tf_op jit(solution)/shard_map/ppermute | solution.py:329
  28.2 24.4 %collective-permute-start.9 = (bf16[512,512]{1,0:T(8,128)(2,1)}, bf16[512,512]{1,0:T(8,128)(2,1)}, u32[]{:S(2)}, u32[]{:S(2)}) collective-permute-start(bf16[512,512]{1,0:T(8,128)(2,1)} %get-tuple-element.42), channel_id=1, source_target_pairs={{0,16},{16,0},{1,17},{17,1},{2,18},{18,2},{3,19},{19,3},{4,20},{20... | collective-permute-start | bytes 1572872 | tf_op jit(solution)/shard_map/ppermute | solution.py:336
  29.7 4.5 %collective-permute-start.7 = (bf16[512,512]{1,0:T(8,128)(2,1)S(1)}, bf16[512,512]{1,0:T(8,128)(2,1)S(1)}, u32[]{:S(2)}, u32[]{:S(2)}) collective-permute-start(bf16[512,512]{1,0:T(8,128)(2,1)S(1)} %get-tuple-element.43), channel_id=1, source_target_pairs={{0,1},{1,0},{2,3},{3,2},{4,5},{5,4},{6,7},{7,6},{8,9},{9,8},{10,11... | collective-permute-start | bytes 1572872 | tf_op jit(solution)/shard_map/ppermute | solution.py:334
  34.1 14.3 %copy-start = (s32[160,2]{0,1:T(2,128)S(1)}, s32[160,2]{0,1:T(2,128)}, u32[]{:S(2)}) copy-start(s32[160,2]{0,1:T(2,128)} %param.8) | copy-start | bytes 3844
  34.2 14.3 %copy-start.1 = (bf16[160,2]{0,1:T(2,128)(2,1)S(1)}, bf16[160,2]{0,1:T(2,128)(2,1)}, u32[]{:S(2)}) copy-start(bf16[160,2]{0,1:T(2,128)(2,1)} %param.7) | copy-start | bytes 1924
  39.5 26.6 %all-to-all-start = ((bf16[16,32,512]{2,1,0:T(8,128)(2,1)}), bf16[16,32,512]{2,1,0:T(8,128)(2,1)}, u32[]{:S(2)}, u32[]{:S(2)}) async-start(bf16[16,32,512]{2,1,0:T(8,128)(2,1)} %sibling_backward.1), calls=%async_computation | async-start | bytes 1048576 | tf_op jit(solution)/shard_map/all_to_all | solution.py:372
  47.9 14.2 %collective-permute-start.8 = (bf16[512,512]{1,0:T(8,128)(2,1)S(1)}, bf16[512,512]{1,0:T(8,128)(2,1)S(1)}, u32[]{:S(2)}, u32[]{:S(2)}) collective-permute-start(bf16[512,512]{1,0:T(8,128)(2,1)S(1)} %collective-permute-done.7.refs_8_.refs_0_), channel_id=1, source_target_pairs={{0,16},{16,0},{1,17},{17,1},{2,18},{18,2},{3,19},{19,3},{4,20},{20... | collective-permute-start | bytes 1572872 | tf_op jit(solution)/shard_map/ppermute | solution.py:336

commit v9 on v8

--- a/solution.py
+++ b/solution.py
@@ -30,7 +30,7 @@
 
 
 def call(body, name, outs, args, in_specs, scratch, flops, transcendentals=0, limit=MEDIUM):
-    moved = sum(a.size * a.dtype.itemsize for a in (*args, *outs))
+    moved = sum(a.size * a.dtype.itemsize for a in (*args, *outs)) if flops else 0
     return pl.pallas_call(
         body,
         name=name,
@@ -40,7 +40,7 @@
         scratch_shapes=scratch,
         compiler_params=pltpu.CompilerParams(vmem_limit_bytes=limit),
         cost_estimate=pl.CostEstimate(
-            flops=flops, bytes_accessed=moved, transcendentals=transcendentals
+            flops=flops, bytes_accessed=moved, transcendentals=transcendentals if flops else 0
         ),
     )(*args)
 
@@ -132,31 +132,48 @@
             out_ref[(2 * i + 1) * pad : (2 * i + 2) * pad, :] = grads[here, :]
 
 
+def steps_of(size, block):
+    half = block // 2
+    return [(0, half), (half, half)] + [(at, block) for at in range(block, size, block)]
+
+
 class Fetch:
-    def __init__(self, up_hbm, down_hbm, up_ref, down_ref, sems, base, block):
+    def __init__(self, up_hbm, down_hbm, up_ref, down_ref, sems, base, steps):
         self.pairs = [(up_hbm, up_ref), (down_hbm, down_ref)]
-        self.sems, self.base, self.block = sems, base, block
-        self.steps = up_ref.shape[0] // block
+        self.sems, self.base, self.steps = sems, base, steps
         self.copies = []
         self.start()
+        self.start()
 
     def start(self):
-        step = len(self.copies)
-        if step == self.steps:
+        number = len(self.copies)
+        if number == len(self.steps):
             return
-        to = pl.ds(step * self.block, self.block)
-        of = pl.ds(pl.multiple_of(self.base + step * self.block, self.block), self.block)
+        at, size = self.steps[number]
+        to, of = pl.ds(at, size), pl.ds(pl.multiple_of(self.base + at, size), size)
         self.copies.append([
-            pltpu.make_async_copy(src.at[0, of, :], dst.at[to, :], self.sems.at[2 * step + i])
+            pltpu.make_async_copy(src.at[0, of, :], dst.at[to, :], self.sems.at[2 * number + i])
             for i, (src, dst) in enumerate(self.pairs)
         ])
         for copy in self.copies[-1]:
             copy.start()
 
-    def wait(self, step):
+    def wait(self, number):
+        for copy in self.copies[number]:
+            copy.wait()
         self.start()
-        for copy in self.copies[step]:
-            copy.wait()
+
+
+def fetch_kernel(up_hbm, down_hbm, up_ref, down_ref, sems):
+    size = up_ref.shape[0]
+    for copy in Fetch(up_hbm, down_hbm, up_ref, down_ref, sems, 0, [(0, size)]).copies[0]:
+        copy.wait()
+
+
+def hand_kernel(pad, at, *refs):
+    piece_refs, out_ref = refs[:-2], refs[-1]
+    for i, ref in enumerate(piece_refs):
+        out_ref[2 * i * pad : 2 * (i + 1) * pad, :] = ref[at : at + 2 * pad, :]
 
 
 def gather_rows(pad, blocks, rows_ref, grads_ref):
@@ -166,14 +183,12 @@
         grads_ref[here, :] = ref[at + pad : at + 2 * pad, :]
 
 
-def backward(cap, pad, block, blocks, weights, scratch, put):
-    rows_ref, grads_ref, grad_acc, gate_acc, up_ref, down_ref, sems = scratch
-    fetch = Fetch(*weights, up_ref, down_ref, sems, 0, block)
+def backward(cap, pad, block, blocks, up_ref, down_ref, scratch, put):
+    rows_ref, grads_ref, grad_acc, gate_acc = scratch
     gather_rows(pad, blocks, rows_ref, grads_ref)
     slots = rows_ref.shape[0]
     for step in range(up_ref.shape[0] // block):
         part = pl.ds(step * block, block)
-        fetch.wait(step)
         up = up_ref[part, :]
         active, slope = silu_parts(dot(rows_ref[...], up, 1, 1))
         back = dot(grads_ref[...], down_ref[part, :], 1, 1)
@@ -199,25 +214,23 @@
         put(k, first.astype(BF16), grad_acc[here, 128:].astype(BF16))
 
 
-def blocks_of(pad, direct_refs, sibling_refs):
-    direct = [(ref, 0) for ref in direct_refs]
-    sibling = [(r, at) for r in sibling_refs for at in range(0, r.shape[0], 2 * pad)]
-    return direct, sibling
+def blocks_of(pad, refs):
+    return [(ref, at) for ref in refs for at in range(0, ref.shape[0], 2 * pad)]
 
 
 def direct_back_kernel(cap, pad, block, chips, *refs):
-    pieces, (up_hbm, down_hbm, out_ref, *scratch) = refs[:chips], refs[chips:]
+    pieces, (up_ref, down_ref, out_ref, *scratch) = refs[:chips], refs[chips:]
 
     def put(k, first, rest):
         out_ref[k, :, 0:128] = first
         out_ref[k, :, 128:] = rest
 
-    direct, _ = blocks_of(pad, pieces, [])
-    backward(cap, pad, block, direct, (up_hbm, down_hbm), scratch, put)
+    blocks = [(ref, 0) for ref in pieces]
+    backward(cap, pad, block, blocks, up_ref, down_ref, scratch, put)
 
 
 def sibling_back_kernel(cap, pad, block, order, *refs):
-    sibling_ref, direct_ref, up_hbm, down_hbm, out_hbm, mine_ref, sems, *scratch = refs
+    sibling_ref, direct_ref, up_ref, down_ref, out_hbm, mine_ref, sems, *scratch = refs
     copies = []
 
     def send(i, core):
@@ -234,26 +247,26 @@
         mine_ref[k, :, 128:] = rest
         send(k, 1)
 
-    _, sibling = blocks_of(pad, [], [sibling_ref])
-    backward(cap, pad, block, sibling, (up_hbm, down_hbm), scratch, put)
+    blocks = blocks_of(pad, [sibling_ref])
+    backward(cap, pad, block, blocks, up_ref, down_ref, scratch, put)
     for copy in copies:
         copy.wait()
 
 
-def weights_kernel(pad, block, share, direct, sibling, begun, *refs):
+def weights_kernel(pad, block, share, number, begun, *refs):
     refs = list(refs)
     take = lambda number: [refs.pop(0) for _ in range(number)]
-    direct_refs, sibling_refs, weights = take(direct), take(sibling), take(2)
+    row_refs, weights = take(number), take(2)
     sums = take(2) if begun else None
     notes = None if begun else take(2)
     out_up, out_down = take(2)
     notes_out = None if begun else take(3)
     rows_ref, grads_ref, up_ref, down_ref, sems = refs
-    fetch = Fetch(*weights, up_ref, down_ref, sems, lax.axis_index("rep") * share, block)
-    blocks = sum(blocks_of(pad, direct_refs, sibling_refs), [])
-    gather_rows(pad, blocks, rows_ref, grads_ref)
-    for step in range(share // block):
-        here = pl.ds(step * block, block)
+    steps = steps_of(share, block)
+    fetch = Fetch(*weights, up_ref, down_ref, sems, lax.axis_index("rep") * share, steps)
+    gather_rows(pad, blocks_of(pad, row_refs), rows_ref, grads_ref)
+    for step, (at, size) in enumerate(steps):
+        here = pl.ds(at, size)
         fetch.wait(step)
         active, slope = silu_parts(dot(up_ref[here, :], rows_ref[...], 1, 1))
         back = dot(down_ref[here, :], grads_ref[...], 1, 1)
@@ -323,36 +336,55 @@
         4 * unit * rows,
     )
     near, far = list(range(1, chips // 2)), list(range(chips // 2, chips))
-    order = near[:1] + far[:1]
-    for pair in itertools.zip_longest(far[1:], near[1:]):
-        order += [k for k in pair if k is not None]
+    order = [k for pair in itertools.zip_longest(far[:-1], near[:-1]) for k in pair if k is not None]
+    order += far[-1:] + near[-1:]
     pieces = [out[0]] + [lax.ppermute(out[k], "exp", hops_to(chips, k)) for k in order]
 
     swap = [(i, i ^ 1) for i in range(groups)]
     around = [[(i, (i + s) % mirrors) for i in range(mirrors)] for s in range(1, mirrors)]
-    handed = jnp.concatenate([piece[2 * pad :] for piece in pieces], axis=0)
+    w_up, w_down = hbm(w_up), hbm(w_down)
+    up_v, down_v = call(
+        fetch_kernel,
+        "fetch_weights",
+        [shape((hidden, feat), BF16)] * 2,
+        [w_up, w_down],
+        [IN_HBM] * 2,
+        [DMA((2,))],
+        0,
+        0,
+        SMALL,
+    )
+    (handed,), (arrived,) = [
+        call(
+            functools.partial(hand_kernel, pad, at),
+            name,
+            [shape((2 * slots, feat), BF16)],
+            [*pieces, up_v],
+            [IN_VMEM] * (chips + 1),
+            [],
+            0,
+            0,
+            SMALL,
+        )
+        for at, name in [(2 * pad, "hand_on"), (0, "arrived_rows")]
+    ]
     sibling = lax.ppermute(handed, "exp", swap)
-    arrived = jnp.concatenate([piece[: 2 * pad] for piece in pieces], axis=0)
     others = [lax.ppermute(a, "rep", hops) for hops in around for a in (arrived, sibling)]
 
-    w_up, w_down = hbm(w_up), hbm(w_down)
     block = min(512, hidden)
     scratch = [
         pltpu.VMEM((slots, feat), BF16),
         pltpu.VMEM((slots, feat), BF16),
         pltpu.VMEM((slots, feat), F32),
         pltpu.VMEM((slots, 128), F32),
-        pltpu.VMEM((hidden, feat), BF16),
-        pltpu.VMEM((hidden, feat), BF16),
-        DMA((2 * hidden // block,)),
     ]
     results = (chips, pad, feat)
     (direct,) = call(
         functools.partial(direct_back_kernel, cap, pad, block, chips),
         "direct_backward",
         [shape(results, BF16)],
-        [*pieces, w_up, w_down],
-        [IN_VMEM] * chips + [IN_HBM] * 2,
+        [*pieces, up_v, down_v],
+        [IN_VMEM] * (chips + 2),
         scratch,
         AHEAD,
         slots * hidden,
@@ -361,21 +393,21 @@
         functools.partial(sibling_back_kernel, cap, pad, block, [0, *order]),
         name="sibling_backward",
         out_shape=pltpu.HBM((groups, pad, feat), BF16),
-        in_specs=[IN_VMEM] * 2 + [IN_HBM] * 2,
+        in_specs=[IN_VMEM] * 4,
         out_specs=IN_HBM,
         scratch_shapes=[pltpu.VMEM(results, BF16), DMA((groups,)), *scratch],
         compiler_params=pltpu.CompilerParams(vmem_limit_bytes=MEDIUM),
         cost_estimate=pl.CostEstimate(
             flops=AHEAD, bytes_accessed=4 * hidden * feat, transcendentals=slots * hidden
         ),
-    )(sibling, direct, w_up, w_down)
+    )(sibling, direct, up_v, down_v)
     back = lax.all_to_all(back, "exp", split_axis=0, concat_axis=0, tiled=True)
 
     part = min(512, share)
 
-    def weights_call(name, direct_in, sibling_in, sums, ended, flops):
+    def weights_call(name, row_ins, sums, ended, flops):
         begun = bool(sums)
-        number = slots * (len(direct_in) // chips + len(sibling_in))
+        number = slots * len(row_ins)
         notes = [] if begun else [
             shape((groups * pad, rows), BF16),
             shape((2, groups, rows), F32),
@@ -383,30 +415,27 @@
         ]
         kept = BF16 if ended else F32
         return call(
-            functools.partial(
-                weights_kernel, pad, part, share, len(direct_in), len(sibling_in), begun
-            ),
+            functools.partial(weights_kernel, pad, part, share, len(row_ins), begun),
             name,
             [shape((1, share, feat), kept)] * 2 + notes,
-            [*direct_in, *sibling_in, w_up, w_down, *(sums or [routes_t, gates_t])],
-            [IN_VMEM] * (len(direct_in) + len(sibling_in)) + [IN_HBM] * 2 + [IN_VMEM] * 2,
+            [*row_ins, w_up, w_down, *(sums or [routes_t, gates_t])],
+            [IN_VMEM] * len(row_ins) + [IN_HBM] * 2 + [IN_VMEM] * 2,
             [
                 pltpu.VMEM((number, feat), BF16),
                 pltpu.VMEM((number, feat), BF16),
                 pltpu.VMEM((share, feat), BF16),
                 pltpu.VMEM((share, feat), BF16),
-                DMA((2 * share // part,)),
+                DMA((2 * share // part + 2,)),
             ],
             flops,
             number * share,
             LARGE,
         )
 
-    *sums, pick, hot, spot = weights_call(
-        "own_weights", pieces, [sibling], [], not others, 8 * unit * share
-    )
+    *sums, pick, hot, spot = weights_call("own_weights", [arrived, sibling], [], not others, 0)
     for i, other in enumerate(others):
-        sums = weights_call("other_weights", [], [other], sums, i == len(others) - 1, AHEAD)
+        ended = i == len(others) - 1
+        sums = weights_call("other_weights", [other], sums, ended, AHEAD if ended else 0)
     grad_up, grad_down = sums
 
     d_tokens, d_gates = call(
@@ -417,6 +446,8 @@
         [IN_VMEM] * 4,
         [],
         4 * unit * rows,
+        0,
+        SMALL,
     )
     return d_tokens, d_gates.T, grad_up, grad_down
 

time: 68.6 us -> 61.5 us (0.90)
  local copies, waits for them, and re-layouts: 5.12 us -> 0.01 us
  waiting for transfers between devices: 12.8 us -> 11.5 us
  Pallas kernels: 25.4 us -> 24.7 us
    unnamed x11 -> x4, local copies, waits for them, and re-layouts: 4.48 us -> 0.01 us
    all_to_all x1, starting transfers between devices: 8.32 us -> 5.72 us  [local(): back = lax.all_to_all(back, 'exp', split_axis=0, concat_axis=0, tiled=True)]
    ppermute x2, waiting for transfers between devices: 5.57 us -> 3.07 us  [local(): lax.ppermute(a, 'rep', hops)]
    ppermute x7, starting transfers between devices: 13.6 us -> 15.9 us  [local(): lax.ppermute(out[k], 'exp', hops_to(chips, k))]
    pallas_call x1, Pallas kernels: 5.35 us -> 3.07 us  [local(): pl.pallas_call(functools.partial(sibling_back_kernel, cap, pad, block, [0...]
    pallas_call x6 -> x9, Pallas kernels: 20 us -> 21.7 us  [call(): pl.pallas_call(body, name=name, out_shape=outs, in_specs=in_specs, out_sp...]
    ppermute x7, waiting for transfers between devices: 7.27 us -> 8.43 us  [local(): lax.ppermute(out[k], 'exp', hops_to(chips, k))]
  transfers between devices with their start and end apart: 11 -> 11, of which waited for: 4 -> 4; matrix products, arithmetic and copies ran while one was open for 7% -> 0% of each run, Pallas kernels for 32% -> 36%
where the time goes in v9:
time: 61.5 us; the launch traced here: 60.8 us
  Pallas kernels  24.7 us (40%)
  starting transfers between devices  23.8 us (39%)
  waiting for transfers between devices  11.5 us (19%)
  between operations  0.79 us (1%)
    pallas_call x9, Pallas kernels, call(): pl.pallas_call(body, name=name, out_shape=outs, in_specs=in_specs, out_sp...  21.7 us
    ppermute x7, starting transfers between devices, local(): lax.ppermute(out[k], 'exp', hops_to(chips, k))  15.9 us
    ppermute x7, waiting for transfers between devices, local(): lax.ppermute(out[k], 'exp', hops_to(chips, k))  8.43 us
    all_to_all x1, starting transfers between devices, local(): back = lax.all_to_all(back, 'exp', split_axis=0, concat_axis=0, tiled=True)  5.72 us
    pallas_call x1, Pallas kernels, local(): pl.pallas_call(functools.partial(sibling_back_kernel, cap, pad, block, [0...  3.07 us
    ppermute x2, waiting for transfers between devices, local(): lax.ppermute(a, 'rep', hops)  3.07 us
    ppermute x2, starting transfers between devices, local(): lax.ppermute(a, 'rep', hops)  2.09 us
  transfers between devices with their start and end apart: 11, of which 4 were waited for; matrix products, arithmetic and copies ran while one was open for 0% of the time, Pallas kernels for 36%

profile of v9, /device:TPU:0, one launch (start us, length us, event | category | flops | bytes accessed | tf_op | source)
XLA Modules:
  0.0 60.8 jit_solution(14643860418433026285)
XLA Ops:
  0.6 1.6 %slots.1 = (bf16[128,512]{1,0:T(8,128)(2,1)S(1)}, bf16[128,512]{1,0:T(8,128)(2,1)S(1)}, bf16[128,512]{1,0:T(8,128)(2,1)S(1)}, bf16[128,512]{1,0:T(8,128)(2,1)S(1...) custom-call(s32[2,160]{1,0:T(2,128)} %bitcast.3, ...), custom_call_target="tpu_custom_call" | custom-call | flops 167772160 | bytes 1378176 | tf_op jit(solution)/shard_map/slots/pallas_call | solution.py:34
  2.2 4.1 %collective-permute-start = (bf16[128,512]{1,0:T(8,128)(2,1)S(1)}, bf16[128,512]{1,0:T(8,128)(2,1)S(1)}, u32[]{:S(2)}, u32[]{:S(2)}) collective-permute-start(bf16[128,512]{1,0:T(8,128)(2,1)S(1)} %get-tuple-element.26), channel_id=1, source_target_pairs={{0,8},{1,9},{2,10},{3,11},{4,12},{5,13},{6,14},{7,15},{8,0},{9,1},... | collective-permute-start | bytes 393224 | tf_op jit(solution)/shard_map/ppermute | solution.py:341
  6.3 1.5 %collective-permute-start.1 = (bf16[128,512]{1,0:T(8,128)(2,1)S(1)}, bf16[128,512]{1,0:T(8,128)(2,1)S(1)}, u32[]{:S(2)}, u32[]{:S(2)}) collective-permute-start(bf16[128,512]{1,0:T(8,128)(2,1)S(1)} %get-tuple-element.27), channel_id=1, source_target_pairs={{0,2},{1,3},{2,0},{3,1},{4,6},{5,7},{6,4},{7,5},{8,10},{9,11},{10,... | collective-permute-start | bytes 393224 | tf_op jit(solution)/shard_map/ppermute | solution.py:341
  7.8 0.0 collective-permute-start.2
  7.9 1.8 %collective-permute-start.3 = (bf16[128,512]{1,0:T(8,128)(2,1)S(1)}, bf16[128,512]{1,0:T(8,128)(2,1)S(1)}, u32[]{:S(2)}, u32[]{:S(2)}) collective-permute-start(bf16[128,512]{1,0:T(8,128)(2,1)S(1)} %get-tuple-element.29), channel_id=1, source_target_pairs={{0,4},{1,5},{2,6},{3,7},{4,0},{5,1},{6,2},{7,3},{8,12},{9,13},{10,... | collective-permute-start | bytes 393224 | tf_op jit(solution)/shard_map/ppermute | solution.py:341
  9.7 2.5 %collective-permute-start.4 = (bf16[128,512]{1,0:T(8,128)(2,1)S(1)}, bf16[128,512]{1,0:T(8,128)(2,1)S(1)}, u32[]{:S(2)}, u32[]{:S(2)}) collective-permute-start(bf16[128,512]{1,0:T(8,128)(2,1)S(1)} %get-tuple-element.30), channel_id=1, source_target_pairs={{0,12},{1,13},{2,14},{3,15},{4,8},{5,9},{6,10},{7,11},{8,4},{9,5},... | collective-permute-start | bytes 393224 | tf_op jit(solution)/shard_map/ppermute | solution.py:341
  12.2 4.8 %collective-permute-done.refs_1_ = bf16[128,512]{1,0:T(8,128)(2,1)S(1)} collective-permute-done((bf16[128,512]{1,0:T(8,128)(2,1)S(1)}, bf16[128,512]{1,0:T(8,128)(2,1)S(1)}, u32[]{:S(2)}, u32[]{:S(2)}) %collective-permute-start) | collective-permute-done | bytes 131104 | tf_op jit(solution)/shard_map/ppermute | solution.py:341
  17.0 5.9 %collective-permute-start.5 = (bf16[128,512]{1,0:T(8,128)(2,1)S(1)}, bf16[128,512]{1,0:T(8,128)(2,1)S(1)}, u32[]{:S(2)}, u32[]{:S(2)}) collective-permute-start(bf16[128,512]{1,0:T(8,128)(2,1)S(1)} %get-tuple-element.31), channel_id=1, source_target_pairs={{0,14},{1,15},{2,12},{3,13},{4,10},{5,11},{6,8},{7,9},{8,6},{9,7},... | collective-permute-start | bytes 393224 | tf_op jit(solution)/shard_map/ppermute | solution.py:341
  22.9 0.0 collective-permute-done.1.refs_2_
  22.9 0.0 collective-permute-start.6
  22.9 2.2 %fetch_weights.1 = (bf16[2048,512]{1,0:T(8,128)(2,1)S(1)}, bf16[2048,512]{1,0:T(8,128)(2,1)S(1)}) custom-call(bf16[1,2048,512]{2,1,0:T(8,128)(2,1)} %refs_1_.3, bf16[1,2048,512]{2,1,0:T(8,128)(2,1)} %refs_2_.5), custom_call_target="tpu_custom_call" | custom-call | tf_op jit(solution)/shard_map/fetch_weights/pallas_call | solution.py:34
  25.2 0.0 collective-permute-done.2.refs_3_
  25.2 0.0 collective-permute-done.3.refs_4_
  25.2 0.0 collective-permute-done.4.refs_5_
  25.2 1.0 %collective-permute-done.5.refs_6_ = bf16[128,512]{1,0:T(8,128)(2,1)S(1)} collective-permute-done((bf16[128,512]{1,0:T(8,128)(2,1)S(1)}, bf16[128,512]{1,0:T(8,128)(2,1)S(1)}, u32[]{:S(2)}, u32[]{:S(2)}) %collective-permute-start.5) | collective-permute-done | bytes 131104 | tf_op jit(solution)/shard_map/ppermute | solution.py:341
  26.3 2.5 %collective-permute-done.6.refs_7_ = bf16[128,512]{1,0:T(8,128)(2,1)S(1)} collective-permute-done((bf16[128,512]{1,0:T(8,128)(2,1)S(1)}, bf16[128,512]{1,0:T(8,128)(2,1)S(1)}, u32[]{:S(2)}, u32[]{:S(2)}) %collective-permute-start.6) | collective-permute-done | bytes 131104 | tf_op jit(solution)/shard_map/ppermute | solution.py:341
  28.8 0.1 collective-permute-start.7
  28.9 0.8 %arrived_rows.1.refs_0_ = bf16[512,512]{1,0:T(8,128)(2,1)} custom-call(bf16[128,512]{1,0:T(8,128)(2,1)S(1)} %get-tuple-element.25.refs_0_, bf16[128,512]{1,0:T(8,128)(2,1)S(1)} %collective-permute-done.refs_1_, bf16[128,512]{1,0:T(8,128)(2,1)S(1)} %collective-permute-done.1.refs_2_, bf16[128,512]{1,0:T(8,128)(2,1)S(1)} %collective-permute-done.2.refs_3_, ...), custom_call_target="tpu_custom_call" | custom-call | tf_op jit(solution)/shard_map/arrived_rows/pallas_call | solution.py:34
  29.8 1.5 %collective-permute-start.9 = (bf16[512,512]{1,0:T(8,128)(2,1)}, bf16[512,512]{1,0:T(8,128)(2,1)}, u32[]{:S(2)}, u32[]{:S(2)}) collective-permute-start(bf16[512,512]{1,0:T(8,128)(2,1)} %arrived_rows.1.refs_0_), channel_id=1, source_target_pairs={{0,16},{16,0},{1,17},{17,1},{2,18},{18,2},{3,19},{19,3},{4,20},{20... | collective-permute-start | bytes 1572872 | tf_op jit(solution)/shard_map/ppermute | solution.py:372
  31.2 2.3 %direct_backward.1.refs_1_ = bf16[8,32,512]{2,1,0:T(8,128)(2,1)S(1)} custom-call(bf16[128,512]{1,0:T(8,128)(2,1)S(1)} %get-tuple-element.25.refs_0_, bf16[128,512]{1,0:T(8,128)(2,1)S(1)} %collective-permute-done.refs_1_, bf16[128,512]{1,0:T(8,128)(2,1)S(1)} %collective-permute-done.1.refs_2_, bf16[128,512]{1,0:T(8,128)(2,1)S(1)} %collective-permute-done.2.refs_3_, ...), custom_call_target="tpu_custom_call" | custom-call | flops 99999997952 | bytes 5505024 | tf_op jit(solution)/shard_map/direct_backward/pallas_call | solution.py:34
  33.5 0.0 copy-start
  33.5 0.0 copy-start.1
  33.6 0.0 collective-permute-done.7.refs_1_.refs_0_
  33.6 0.6 collective-permute-start.8
  34.2 3.1 %sibling_backward.1 = bf16[16,32,512]{2,1,0:T(8,128)(2,1)} custom-call(bf16[512,512]{1,0:T(8,128)(2,1)S(1)} %collective-permute-done.7.refs_1_.refs_0_, bf16[8,32,512]{2,1,0:T(8,128)(2,1)S(1)} %direct_backward.1.refs_1_, bf16[2048,512]{1,0:T(8,128)(2,1)S(1)} %get-tuple-element.33.refs_8_.refs_2_, bf16[2048,512]{1,0:T(8,128)(2,1)S(1)} %get-tuple-element.37.refs_9_.refs_3_), custom_call_target="tpu_custom_call" | custom-call | flops 99999997952 | bytes 4194304 | tf_op jit(solution)/shard_map/sibling_backward/pallas_call | solution.py:392
  37.3 5.7 %all-to-all-start = ((bf16[16,32,512]{2,1,0:T(8,128)(2,1)}), bf16[16,32,512]{2,1,0:T(8,128)(2,1)S(1)}, u32[]{:S(2)}, u32[]{:S(2)}) async-start(bf16[16,32,512]{2,1,0:T(8,128)(2,1)} %sibling_backward.1), calls=%async_computation | async-start | bytes 1048576 | tf_op jit(solution)/shard_map/all_to_all | solution.py:404
  43.0 0.0 copy-done
  43.0 0.0 copy-done.1
  43.0 5.3 %own_weights.1 = (f32[1,1024,512]{2,1,0:T(8,128)S(1)}, f32[1,1024,512]{2,1,0:T(8,128)S(1)}, bf16[512,160]{1,0:T(8,128)(2,1)S(1)}, f32[2,16,160]{2,1,0:T(8,128)S(1)}, bf16[2,128,160]{2,1,0:T(8,128)(2,1)S(1)}) custom-call(bf16[512,512]{1,0:T(8,128)(2,1)} %arrived_rows.1.refs_0_, bf16[512,512]{1,0:T(8,128)(2,1)S(1)} %collective-permute-done.7.refs_1_.refs_0_, ...), custom_call_target="tpu_custom_call" | custom-call | tf_op jit(solution)/shard_map/own_weights/pallas_call | solution.py:34
  48.3 0.0 collective-permute-done.9.refs_0_
  48.3 4.2 %other_weights.2 = (f32[1,1024,512]{2,1,0:T(8,128)S(1)}, f32[1,1024,512]{2,1,0:T(8,128)S(1)}) custom-call(bf16[512,512]{1,0:T(8,128)(2,1)} %collective-permute-done.9.refs_0_, bf16[1,2048,512]{2,1,0:T(8,128)(2,1)} %refs_1_.3, bf16[1,2048,512]{2,1,0:T(8,128)(2,1)} %refs_2_.5, f32[1,1024,512]{2,1,0:T(8,128)S(1)} %get-tuple-element.40.refs_3_, ...), custom_call_target="tpu_custom_call" | custom-call | tf_op jit(solution)/shard_map/other_weights/pallas_call | solution.py:34
  52.5 3.1 %collective-permute-done.8.refs_0_ = bf16[512,512]{1,0:T(8,128)(2,1)S(1)} collective-permute-done((bf16[512,512]{1,0:T(8,128)(2,1)S(1)}, bf16[512,512]{1,0:T(8,128)(2,1)S(1)}, u32[]{:S(2)}, u32[]{:S(2)}) %collective-permute-start.8) | collective-permute-done | bytes 524320 | tf_op jit(solution)/shard_map/ppermute | solution.py:372
  55.5 4.3 %other_weights.3 = (bf16[1,1024,512]{2,1,0:T(8,128)(2,1)}, bf16[1,1024,512]{2,1,0:T(8,128)(2,1)}) custom-call(bf16[512,512]{1,0:T(8,128)(2,1)S(1)} %collective-permute-done.8.refs_0_, bf16[1,2048,512]{2,1,0:T(8,128)(2,1)} %refs_1_.3, bf16[1,2048,512]{2,1,0:T(8,128)(2,1)} %refs_2_.5, f32[1,1024,512]{2,1,0:T(8,128)S(1)} %get-tuple-element.42.refs_3_, ...), custom_call_target="tpu_custom_call" | custom-call | flops 99999997952 | bytes 11010048 | tf_op jit(solution)/shard_map/other_weights/pallas_call | solution.py:34
  59.8 0.0 all-to-all-done.back_ref
  59.9 0.9 %combine.1 = (bf16[160,512]{1,0:T(8,128)(2,1)}, bf16[2,160]{1,0:T(2,128)(2,1)}) custom-call(bf16[512,160]{1,0:T(8,128)(2,1)S(1)} %get-tuple-element.34.pick_ref, f32[2,16,160]{2,1,0:T(8,128)S(1)} %get-tuple-element.35.hot_ref, bf16[2,128,160]{2,1,0:T(8,128)(2,1)S(1)} %get-tuple-element.36.spot_ref, bf16[16,32,512]{2,1,0:T(8,128)(2,1)S(1)} %all-to-all-done.back_ref), custom_call_target="tpu_custom_call" | custom-call | flops 167772160 | bytes 955008 | tf_op jit(solution)/shard_map/combine/pallas_call | solution.py:34
  (1 shorter events, 0.0 us)
Async XLA Ops:
  2.2 14.8 %collective-permute-start = (bf16[128,512]{1,0:T(8,128)(2,1)S(1)}, bf16[128,512]{1,0:T(8,128)(2,1)S(1)}, u32[]{:S(2)}, u32[]{:S(2)}) collective-permute-start(bf16[128,512]{1,0:T(8,128)(2,1)S(1)} %get-tuple-element.26), channel_id=1, source_target_pairs={{0,8},{1,9},{2,10},{3,11},{4,12},{5,13},{6,14},{7,15},{8,0},{9,1},... | collective-permute-start | bytes 393224 | tf_op jit(solution)/shard_map/ppermute | solution.py:341
  6.3 16.6 %collective-permute-start.1 = (bf16[128,512]{1,0:T(8,128)(2,1)S(1)}, bf16[128,512]{1,0:T(8,128)(2,1)S(1)}, u32[]{:S(2)}, u32[]{:S(2)}) collective-permute-start(bf16[128,512]{1,0:T(8,128)(2,1)S(1)} %get-tuple-element.27), channel_id=1, source_target_pairs={{0,2},{1,3},{2,0},{3,1},{4,6},{5,7},{6,4},{7,5},{8,10},{9,11},{10,... | collective-permute-start | bytes 393224 | tf_op jit(solution)/shard_map/ppermute | solution.py:341
  7.8 17.3 %collective-permute-start.2 = (bf16[128,512]{1,0:T(8,128)(2,1)S(1)}, bf16[128,512]{1,0:T(8,128)(2,1)S(1)}, u32[]{:S(2)}, u32[]{:S(2)}) collective-permute-start(bf16[128,512]{1,0:T(8,128)(2,1)S(1)} %get-tuple-element.28), channel_id=1, source_target_pairs={{0,10},{1,11},{2,8},{3,9},{4,14},{5,15},{6,12},{7,13},{8,2},{9,3},... | collective-permute-start | bytes 393224 | tf_op jit(solution)/shard_map/ppermute | solution.py:341
  7.9 17.3 %collective-permute-start.3 = (bf16[128,512]{1,0:T(8,128)(2,1)S(1)}, bf16[128,512]{1,0:T(8,128)(2,1)S(1)}, u32[]{:S(2)}, u32[]{:S(2)}) collective-permute-start(bf16[128,512]{1,0:T(8,128)(2,1)S(1)} %get-tuple-element.29), channel_id=1, source_target_pairs={{0,4},{1,5},{2,6},{3,7},{4,0},{5,1},{6,2},{7,3},{8,12},{9,13},{10,... | collective-permute-start | bytes 393224 | tf_op jit(solution)/shard_map/ppermute | solution.py:341
  9.7 15.5 %collective-permute-start.4 = (bf16[128,512]{1,0:T(8,128)(2,1)S(1)}, bf16[128,512]{1,0:T(8,128)(2,1)S(1)}, u32[]{:S(2)}, u32[]{:S(2)}) collective-permute-start(bf16[128,512]{1,0:T(8,128)(2,1)S(1)} %get-tuple-element.30), channel_id=1, source_target_pairs={{0,12},{1,13},{2,14},{3,15},{4,8},{5,9},{6,10},{7,11},{8,4},{9,5},... | collective-permute-start | bytes 393224 | tf_op jit(solution)/shard_map/ppermute | solution.py:341
  17.0 9.2 %collective-permute-start.5 = (bf16[128,512]{1,0:T(8,128)(2,1)S(1)}, bf16[128,512]{1,0:T(8,128)(2,1)S(1)}, u32[]{:S(2)}, u32[]{:S(2)}) collective-permute-start(bf16[128,512]{1,0:T(8,128)(2,1)S(1)} %get-tuple-element.31), channel_id=1, source_target_pairs={{0,14},{1,15},{2,12},{3,13},{4,10},{5,11},{6,8},{7,9},{8,6},{9,7},... | collective-permute-start | bytes 393224 | tf_op jit(solution)/shard_map/ppermute | solution.py:341
  22.9 5.9 %collective-permute-start.6 = (bf16[128,512]{1,0:T(8,128)(2,1)S(1)}, bf16[128,512]{1,0:T(8,128)(2,1)S(1)}, u32[]{:S(2)}, u32[]{:S(2)}) collective-permute-start(bf16[128,512]{1,0:T(8,128)(2,1)S(1)} %get-tuple-element.32), channel_id=1, source_target_pairs={{0,6},{1,7},{2,4},{3,5},{4,2},{5,3},{6,0},{7,1},{8,14},{9,15},{10,... | collective-permute-start | bytes 393224 | tf_op jit(solution)/shard_map/ppermute | solution.py:341
  28.8 4.7 %collective-permute-start.7 = (bf16[512,512]{1,0:T(8,128)(2,1)S(1)}, bf16[512,512]{1,0:T(8,128)(2,1)S(1)}, u32[]{:S(2)}, u32[]{:S(2)}) collective-permute-start(bf16[512,512]{1,0:T(8,128)(2,1)S(1)} %hand_on.1), channel_id=1, source_target_pairs={{0,1},{1,0},{2,3},{3,2},{4,5},{5,4},{6,7},{7,6},{8,9},{9,8},{10,11... | collective-permute-start | bytes 1572872 | tf_op jit(solution)/shard_map/ppermute | solution.py:371
  29.8 18.5 %collective-permute-start.9 = (bf16[512,512]{1,0:T(8,128)(2,1)}, bf16[512,512]{1,0:T(8,128)(2,1)}, u32[]{:S(2)}, u32[]{:S(2)}) collective-permute-start(bf16[512,512]{1,0:T(8,128)(2,1)} %arrived_rows.1.refs_0_), channel_id=1, source_target_pairs={{0,16},{16,0},{1,17},{17,1},{2,18},{18,2},{3,19},{19,3},{4,20},{20... | collective-permute-start | bytes 1572872 | tf_op jit(solution)/shard_map/ppermute | solution.py:372
  33.5 9.4 %copy-start = (s32[160,2]{0,1:T(2,128)S(1)}, s32[160,2]{0,1:T(2,128)}, u32[]{:S(2)}) copy-start(s32[160,2]{0,1:T(2,128)} %param.8) | copy-start | bytes 3844
  33.5 9.4 %copy-start.1 = (bf16[160,2]{0,1:T(2,128)(2,1)S(1)}, bf16[160,2]{0,1:T(2,128)(2,1)}, u32[]{:S(2)}) copy-start(bf16[160,2]{0,1:T(2,128)(2,1)} %param.7) | copy-start | bytes 1924
  33.6 22.0 %collective-permute-start.8 = (bf16[512,512]{1,0:T(8,128)(2,1)S(1)}, bf16[512,512]{1,0:T(8,128)(2,1)S(1)}, u32[]{:S(2)}, u32[]{:S(2)}) collective-permute-start(bf16[512,512]{1,0:T(8,128)(2,1)S(1)} %collective-permute-done.7.refs_1_.refs_0_), channel_id=1, source_target_pairs={{0,16},{16,0},{1,17},{17,1},{2,18},{18,2},{3,19},{19,3},{4,20},{20... | collective-permute-start | bytes 1572872 | tf_op jit(solution)/shard_map/ppermute | solution.py:372
  37.3 22.6 %all-to-all-start = ((bf16[16,32,512]{2,1,0:T(8,128)(2,1)}), bf16[16,32,512]{2,1,0:T(8,128)(2,1)S(1)}, u32[]{:S(2)}, u32[]{:S(2)}) async-start(bf16[16,32,512]{2,1,0:T(8,128)(2,1)} %sibling_backward.1), calls=%async_computation | async-start | bytes 1048576 | tf_op jit(solution)/shard_map/all_to_all | solution.py:404

commit v10 on v9

--- a/solution.py
+++ b/solution.py
@@ -1,5 +1,5 @@
 import functools
-import itertools
+import math
 
 import jax
 import jax.numpy as jnp
@@ -29,14 +29,14 @@
     return active, sigma + active * (1.0 - sigma)
 
 
-def call(body, name, outs, args, in_specs, scratch, flops, transcendentals=0, limit=MEDIUM):
-    moved = sum(a.size * a.dtype.itemsize for a in (*args, *outs)) if flops else 0
+def call(body, name, outs, args, in_specs, scratch, flops, transcendentals=0, limit=MEDIUM, out_specs=None):
+    moved = sum(math.prod(a.shape) * a.dtype.itemsize for a in (*args, *outs)) if flops else 0
     return pl.pallas_call(
         body,
         name=name,
         out_shape=outs,
         in_specs=in_specs,
-        out_specs=[IN_VMEM] * len(outs),
+        out_specs=out_specs or [IN_VMEM] * len(outs),
         scratch_shapes=scratch,
         compiler_params=pltpu.CompilerParams(vmem_limit_bytes=limit),
         cost_estimate=pl.CostEstimate(
@@ -96,9 +96,9 @@
     return [index == pieces[k : k + 1, :] * pad + slot[k] for k in range(2)]
 
 
-def slots_kernel(pad, routes_hbm, gates_hbm, tok_hbm, cot_hbm, *refs):
-    chips = len(refs) - 5
-    out_refs, refs = refs[:chips], refs[chips:]
+def slots_kernel(pad, chips, twice, routes_hbm, gates_hbm, tok_hbm, cot_hbm, *refs):
+    order = [*range(chips), *twice]
+    out_refs, refs = refs[: len(order)], refs[len(order) :]
     routes_ref, gates_ref, tok_ref, cot_ref, sems = refs
     pairs = [
         (routes_hbm, routes_ref),
@@ -125,7 +125,7 @@
     copies[3].wait()
     rows = dot(plain, tok_ref[...], 1, 0).astype(BF16)
     grads = dot(scaled, cot_ref[...], 1, 0).astype(BF16)
-    for k, out_ref in enumerate(out_refs):
+    for k, out_ref in zip(order, out_refs):
         for i in range(2):
             here = slice((2 * k + i) * pad, (2 * k + i + 1) * pad)
             out_ref[2 * i * pad : (2 * i + 1) * pad, :] = rows[here, :]
@@ -170,10 +170,11 @@
         copy.wait()
 
 
-def hand_kernel(pad, at, *refs):
-    piece_refs, out_ref = refs[:-2], refs[-1]
-    for i, ref in enumerate(piece_refs):
-        out_ref[2 * i * pad : 2 * (i + 1) * pad, :] = ref[at : at + 2 * pad, :]
+def join_kernel(size, lists, *refs):
+    out_refs = refs[len(refs) - len(lists) :]
+    for blocks, out_ref in zip(lists, out_refs):
+        for i, (number, at) in enumerate(blocks):
+            out_ref[i * size : (i + 1) * size, :] = refs[number][at : at + size, :]
 
 
 def gather_rows(pad, blocks, rows_ref, grads_ref):
@@ -253,33 +254,40 @@
         copy.wait()
 
 
-def weights_kernel(pad, block, share, number, begun, *refs):
+def weights_kernel(pad, block, share, number, places, begun, ended, *refs):
     refs = list(refs)
     take = lambda number: [refs.pop(0) for _ in range(number)]
     row_refs, weights = take(number), take(2)
     sums = take(2) if begun else None
     notes = None if begun else take(2)
-    out_up, out_down = take(2)
+    outs = take(2)
     notes_out = None if begun else take(3)
-    rows_ref, grads_ref, up_ref, down_ref, sems = refs
+    rows_ref, grads_ref, up_ref, down_ref, sems, *kept = refs
     steps = steps_of(share, block)
     fetch = Fetch(*weights, up_ref, down_ref, sems, lax.axis_index("rep") * share, steps)
-    gather_rows(pad, blocks_of(pad, row_refs), rows_ref, grads_ref)
+    gather_rows(pad, [(row_refs[i], at) for i, at in places], rows_ref, grads_ref)
+    copies = []
     for step, (at, size) in enumerate(steps):
         here = pl.ds(at, size)
         fetch.wait(step)
         active, slope = silu_parts(dot(up_ref[here, :], rows_ref[...], 1, 1))
         back = dot(down_ref[here, :], grads_ref[...], 1, 1)
         hid_grad = (back * slope).astype(BF16)
-        up_part = dot(hid_grad, rows_ref[...], 1, 0)
-        down_part = dot(active.astype(BF16), grads_ref[...], 1, 0)
-        if begun:
-            up_part += sums[0][0, here, :]
-            down_part += sums[1][0, here, :]
-        out_up[0, here, :] = up_part.astype(out_up.dtype)
-        out_down[0, here, :] = down_part.astype(out_down.dtype)
+        parts = [dot(hid_grad, rows_ref[...], 1, 0), dot(active.astype(BF16), grads_ref[...], 1, 0)]
+        for i, part in enumerate(parts):
+            if begun:
+                part += sums[i][0, here, :]
+            if not ended:
+                outs[i][0, here, :] = part
+                continue
+            kept[i][here, :] = part.astype(BF16)
+            sem = kept[2].at[2 * step + i]
+            copies.append(pltpu.make_async_copy(kept[i].at[here, :], outs[i].at[0, here, :], sem))
+            copies[-1].start()
     if not begun:
         note_routes(pad, *notes, *notes_out)
+    for copy in copies:
+        copy.wait()
 
 
 def note_routes(pad, routes_ref, gates_ref, pick_ref, hot_ref, spot_ref):
@@ -320,10 +328,13 @@
     shape = jax.ShapeDtypeStruct
     unit = 2 * slots * feat
 
+    near, far = list(range(1, chips // 2)), list(range(chips // 2, chips))
+    order = near[:1] + far + near[1:]
+    twice = [0, order[0]] if mirrors > 1 else []
     out = call(
-        functools.partial(slots_kernel, pad),
+        functools.partial(slots_kernel, pad, chips, twice),
         "slots",
-        [shape((4 * pad, feat), BF16)] * chips,
+        [shape((4 * pad, feat), BF16)] * (chips + len(twice)),
         [hbm(a) for a in (routes_t, gates_t, tokens, cotangent)],
         [IN_HBM] * 4,
         [
@@ -335,13 +346,19 @@
         ],
         4 * unit * rows,
     )
-    near, far = list(range(1, chips // 2)), list(range(chips // 2, chips))
-    order = [k for pair in itertools.zip_longest(far[:-1], near[:-1]) for k in pair if k is not None]
-    order += far[-1:] + near[-1:]
     pieces = [out[0]] + [lax.ppermute(out[k], "exp", hops_to(chips, k)) for k in order]
-
     swap = [(i, i ^ 1) for i in range(groups)]
     around = [[(i, (i + s) % mirrors) for i in range(mirrors)] for s in range(1, mirrors)]
+
+    def crossed(piece, k, hops):
+        moves = hops_to(chips, k) if k else [(i, i) for i in range(groups)]
+        pairs = [(m * groups + i, n * groups + j) for m, n in hops for i, j in moves]
+        return lax.ppermute(piece, ("rep", "exp"), pairs)
+
+    doubles = list(zip(out[chips:], twice))
+    straight = [[crossed(piece, k, hops) for hops in around] for piece, k in doubles]
+    arrivals = [*pieces[:2], *sum(straight[:1], []), *pieces[2:], *sum(straight[1:], [])]
+
     w_up, w_down = hbm(w_up), hbm(w_down)
     up_v, down_v = call(
         fetch_kernel,
@@ -354,22 +371,36 @@
         0,
         SMALL,
     )
-    (handed,), (arrived,) = [
-        call(
-            functools.partial(hand_kernel, pad, at),
+    whole = 2 * pad
+
+    def join(name, arrays, *lists):
+        return call(
+            functools.partial(join_kernel, whole, lists),
             name,
-            [shape((2 * slots, feat), BF16)],
-            [*pieces, up_v],
-            [IN_VMEM] * (chips + 1),
+            [shape((len(blocks) * whole, feat), BF16) for blocks in lists],
+            arrays,
+            [IN_VMEM] * len(arrays),
             [],
             0,
             0,
             SMALL,
         )
-        for at, name in [(2 * pad, "hand_on"), (0, "arrived_rows")]
-    ]
+
+    def places_in(arrays):
+        return [next(i for i, a in enumerate(arrivals) if a is array) for array in arrays]
+
+    own, flat = places_in(pieces), places_in(sum(straight, []))
+    (handed,) = join("hand_on", [*arrivals, up_v], [(i, whole) for i in own])
     sibling = lax.ppermute(handed, "exp", swap)
-    others = [lax.ppermute(a, "rep", hops) for hops in around for a in (arrived, sibling)]
+    lists = [[(i, 0) for i in own[2:]], [(i, 0) for i in own[:2] + flat]]
+    if flat:
+        lists.append([(i, whole) for i in flat])
+    arrived, early, *mirrored = join("arrived_rows", [*arrivals, handed], *lists)
+    firsts = [lax.ppermute(arrived, "rep", hops) for hops in around]
+    later = range(2, chips)
+    (passed,) = join("sibling_rows", [sibling], [(0, i * whole) for i in later])
+    seconds = [lax.ppermute(passed, "rep", hops) for hops in around]
+    seconds += [lax.ppermute(a, "exp", swap) for a in mirrored]
 
     block = min(512, hidden)
     scratch = [
@@ -405,37 +436,51 @@
 
     part = min(512, share)
 
-    def weights_call(name, row_ins, sums, ended, flops):
+    def weights_call(name, arrays, places, sums, ended, flops):
         begun = bool(sums)
-        number = slots * len(row_ins)
+        number = len(places) * pad
         notes = [] if begun else [
             shape((groups * pad, rows), BF16),
             shape((2, groups, rows), F32),
             shape((2, 128, rows), BF16),
         ]
-        kept = BF16 if ended else F32
+        grad = pltpu.HBM((1, share, feat), BF16) if ended else shape((1, share, feat), F32)
+        steps = len(steps_of(share, part))
+        scratch = [
+            pltpu.VMEM((number, feat), BF16),
+            pltpu.VMEM((number, feat), BF16),
+            pltpu.VMEM((share, feat), BF16),
+            pltpu.VMEM((share, feat), BF16),
+            DMA((2 * steps,)),
+        ]
+        if ended:
+            scratch += [pltpu.VMEM((share, feat), BF16)] * 2 + [DMA((2 * steps,))]
         return call(
-            functools.partial(weights_kernel, pad, part, share, len(row_ins), begun),
+            functools.partial(
+                weights_kernel, pad, part, share, len(arrays), places, begun, ended
+            ),
             name,
-            [shape((1, share, feat), kept)] * 2 + notes,
-            [*row_ins, w_up, w_down, *(sums or [routes_t, gates_t])],
-            [IN_VMEM] * len(row_ins) + [IN_HBM] * 2 + [IN_VMEM] * 2,
-            [
-                pltpu.VMEM((number, feat), BF16),
-                pltpu.VMEM((number, feat), BF16),
-                pltpu.VMEM((share, feat), BF16),
-                pltpu.VMEM((share, feat), BF16),
-                DMA((2 * share // part + 2,)),
-            ],
+            [grad] * 2 + notes,
+            [*arrays, w_up, w_down, *(sums or [routes_t, gates_t])],
+            [IN_VMEM] * len(arrays) + [IN_HBM] * 2 + [IN_VMEM] * 2,
+            scratch,
             flops,
             number * share,
             LARGE,
+            [IN_HBM if ended else IN_VMEM] * 2 + [IN_VMEM] * len(notes),
         )
 
-    *sums, pick, hot, spot = weights_call("own_weights", [arrived, sibling], [], not others, 0)
-    for i, other in enumerate(others):
-        ended = i == len(others) - 1
-        sums = weights_call("other_weights", [other], sums, ended, AHEAD if ended else 0)
+    def places_of(arrays, first=0):
+        return [
+            (first + i, at) for i, a in enumerate(arrays) for at in range(0, a.shape[0], whole)
+        ]
+
+    joined = [sibling, arrived, early, *firsts]
+    *sums, pick, hot, spot = weights_call(
+        "first_weights", joined, places_of(joined), [], not seconds, 0
+    )
+    if seconds:
+        sums = weights_call("last_weights", seconds, places_of(seconds), sums, True, AHEAD)
     grad_up, grad_down = sums
 
     d_tokens, d_gates = call(

time: 61.5 us -> 64.5 us (1.049)
  waiting for transfers between devices: 11.5 us -> 18.3 us
  Pallas kernels: 24.7 us -> 22.3 us
  starting transfers between devices: 23.8 us -> 22.7 us
    ppermute x7, waiting for transfers between devices: 8.43 us -> 13.7 us  [local(): lax.ppermute(out[k], 'exp', hops_to(chips, k))]
    ppermute x7, starting transfers between devices: 15.9 us -> 10.7 us  [local(): lax.ppermute(out[k], 'exp', hops_to(chips, k))]
    ppermute x2 -> x5, starting transfers between devices: 2.09 us -> 5.61 us  [the longest x2 3.03 us: crossed(): return lax.ppermute(piece, ('rep', 'exp'), pairs)]
    all_to_all x1, waiting for transfers between devices: 0.01 us -> 3.2 us  [local(): back = lax.all_to_all(back, 'exp', split_axis=0, concat_axis=0, tiled=True)]
    pallas_call x9, Pallas kernels: 21.7 us -> 19.2 us  [call(): pl.pallas_call(body, name=name, out_shape=outs, in_specs=in_specs, out_sp...]
    ppermute x2 -> x5, waiting for transfers between devices: 3.07 us -> 1.49 us  [the longest x2 1.48 us: crossed(): return lax.ppermute(piece, ('rep', 'exp'), pairs)]
  transfers between devices with their start and end apart: 11 -> 14, of which waited for: 4 -> 5; matrix products, arithmetic and copies ran while one was open for 0% -> 0% of each run, Pallas kernels for 36% -> 31%
where the time goes in v10:
time: 64.5 us; the launch traced here: 64.2 us
  starting transfers between devices  22.7 us (35%)
  Pallas kernels  22.3 us (35%)
  waiting for transfers between devices  18.3 us (28%)
  between operations  0.8 us (1%)
    pallas_call x9, Pallas kernels, call(): pl.pallas_call(body, name=name, out_shape=outs, in_specs=in_specs, out_sp...  19.2 us
    ppermute x7, waiting for transfers between devices, local(): lax.ppermute(out[k], 'exp', hops_to(chips, k))  13.7 us
    ppermute x7, starting transfers between devices, local(): lax.ppermute(out[k], 'exp', hops_to(chips, k))  10.7 us
    all_to_all x1, starting transfers between devices, local(): back = lax.all_to_all(back, 'exp', split_axis=0, concat_axis=0, tiled=True)  6.35 us
    all_to_all x1, waiting for transfers between devices, local(): back = lax.all_to_all(back, 'exp', split_axis=0, concat_axis=0, tiled=True)  3.2 us
    pallas_call x1, Pallas kernels, local(): pl.pallas_call(functools.partial(sibling_back_kernel, cap, pad, block, [0...  3.12 us
    ppermute x2, starting transfers between devices, crossed(): return lax.ppermute(piece, ('rep', 'exp'), pairs)  3.03 us
    ppermute x1, starting transfers between devices, local(): seconds = [lax.ppermute(passed, 'rep', hops) for hops in around]  1.56 us
  transfers between devices with their start and end apart: 14, of which 5 were waited for; matrix products, arithmetic and copies ran while one was open for 0% of the time, Pallas kernels for 31%

profile of v10, /device:TPU:0, one launch (start us, length us, event | category | flops | bytes accessed | tf_op | source)
XLA Modules:
  0.0 64.2 jit_solution(10268510502419294243)
XLA Ops:
  0.6 1.6 %slots.1 = (bf16[128,512]{1,0:T(8,128)(2,1)S(1)}, bf16[128,512]{1,0:T(8,128)(2,1)S(1)}, bf16[128,512]{1,0:T(8,128)(2,1)S(1)}, bf16[128,512]{1,0:T(8,128)(2,1)S(1...) custom-call(s32[2,160]{1,0:T(2,128)} %bitcast.3, ...), custom_call_target="tpu_custom_call" | custom-call | flops 167772160 | bytes 1640320 | tf_op jit(solution)/shard_map/slots/pallas_call | solution.py:34
  2.2 3.0 %collective-permute-start = (bf16[128,512]{1,0:T(8,128)(2,1)S(1)}, bf16[128,512]{1,0:T(8,128)(2,1)S(1)}, u32[]{:S(2)}, u32[]{:S(2)}) collective-permute-start(bf16[128,512]{1,0:T(8,128)(2,1)S(1)} %get-tuple-element.29), channel_id=1, source_target_pairs={{0,2},{1,3},{2,0},{3,1},{4,6},{5,7},{6,4},{7,5},{8,10},{9,11},{10,... | collective-permute-start | bytes 393224 | tf_op jit(solution)/shard_map/ppermute | solution.py:349
  5.3 1.5 %collective-permute-start.1 = (bf16[128,512]{1,0:T(8,128)(2,1)S(1)}, bf16[128,512]{1,0:T(8,128)(2,1)S(1)}, u32[]{:S(2)}, u32[]{:S(2)}) collective-permute-start(bf16[128,512]{1,0:T(8,128)(2,1)S(1)} %get-tuple-element.30), channel_id=1, source_target_pairs={{0,16},{1,17},{2,18},{3,19},{4,20},{5,21},{6,22},{7,23},{8,24},{9,... | collective-permute-start | bytes 393224 | tf_op jit(solution)/shard_map/ppermute | solution.py:356
  6.8 2.6 %collective-permute-start.2 = (bf16[128,512]{1,0:T(8,128)(2,1)S(1)}, bf16[128,512]{1,0:T(8,128)(2,1)S(1)}, u32[]{:S(2)}, u32[]{:S(2)}) collective-permute-start(bf16[128,512]{1,0:T(8,128)(2,1)S(1)} %get-tuple-element.31), channel_id=1, source_target_pairs={{0,8},{1,9},{2,10},{3,11},{4,12},{5,13},{6,14},{7,15},{8,0},{9,1},... | collective-permute-start | bytes 393224 | tf_op jit(solution)/shard_map/ppermute | solution.py:349
  9.3 0.3 collective-permute-start.3
  9.6 3.6 %collective-permute-start.4 = (bf16[128,512]{1,0:T(8,128)(2,1)S(1)}, bf16[128,512]{1,0:T(8,128)(2,1)S(1)}, u32[]{:S(2)}, u32[]{:S(2)}) collective-permute-start(bf16[128,512]{1,0:T(8,128)(2,1)S(1)} %get-tuple-element.33), channel_id=1, source_target_pairs={{0,12},{1,13},{2,14},{3,15},{4,8},{5,9},{6,10},{7,11},{8,4},{9,5},... | collective-permute-start | bytes 393224 | tf_op jit(solution)/shard_map/ppermute | solution.py:349
  13.2 0.0 collective-permute-done.refs_1_
  13.2 1.2 %collective-permute-start.5 = (bf16[128,512]{1,0:T(8,128)(2,1)S(1)}, bf16[128,512]{1,0:T(8,128)(2,1)S(1)}, u32[]{:S(2)}, u32[]{:S(2)}) collective-permute-start(bf16[128,512]{1,0:T(8,128)(2,1)S(1)} %get-tuple-element.34), channel_id=1, source_target_pairs={{0,14},{1,15},{2,12},{3,13},{4,10},{5,11},{6,8},{7,9},{8,6},{9,7},... | collective-permute-start | bytes 393224 | tf_op jit(solution)/shard_map/ppermute | solution.py:349
  14.4 0.0 collective-permute-done.1.refs_2_
  14.4 0.0 collective-permute-start.6
  14.4 10.4 %collective-permute-done.2.refs_3_.refs_2_ = bf16[128,512]{1,0:T(8,128)(2,1)S(1)} collective-permute-done((bf16[128,512]{1,0:T(8,128)(2,1)S(1)}, bf16[128,512]{1,0:T(8,128)(2,1)S(1)}, u32[]{:S(2)}, u32[]{:S(2)}) %collective-permute-start.2) | collective-permute-done | bytes 131104 | tf_op jit(solution)/shard_map/ppermute | solution.py:349
  24.8 0.0 collective-permute-start.7
  24.8 2.6 %collective-permute-done.3.refs_4_.refs_3_ = bf16[128,512]{1,0:T(8,128)(2,1)S(1)} collective-permute-done((bf16[128,512]{1,0:T(8,128)(2,1)S(1)}, bf16[128,512]{1,0:T(8,128)(2,1)S(1)}, u32[]{:S(2)}, u32[]{:S(2)}) %collective-permute-start.3) | collective-permute-done | bytes 131104 | tf_op jit(solution)/shard_map/ppermute | solution.py:349
  27.5 1.5 %collective-permute-start.8 = (bf16[128,512]{1,0:T(8,128)(2,1)S(1)}, bf16[128,512]{1,0:T(8,128)(2,1)S(1)}, u32[]{:S(2)}, u32[]{:S(2)}) collective-permute-start(bf16[128,512]{1,0:T(8,128)(2,1)S(1)} %get-tuple-element.37), channel_id=1, source_target_pairs={{0,18},{1,19},{2,16},{3,17},{4,22},{5,23},{6,20},{7,21},{8,26},{9,... | collective-permute-start | bytes 393224 | tf_op jit(solution)/shard_map/ppermute | solution.py:356
  29.0 2.2 %fetch_weights.1 = (bf16[2048,512]{1,0:T(8,128)(2,1)S(1)}, bf16[2048,512]{1,0:T(8,128)(2,1)S(1)}) custom-call(bf16[1,2048,512]{2,1,0:T(8,128)(2,1)} %refs_2_.1, bf16[1,2048,512]{2,1,0:T(8,128)(2,1)} %refs_3_.1), custom_call_target="tpu_custom_call" | custom-call | tf_op jit(solution)/shard_map/fetch_weights/pallas_call | solution.py:34
  31.3 0.0 collective-permute-done.4.refs_5_.refs_4_
  31.3 0.0 collective-permute-done.5.refs_6_.refs_5_
  31.3 0.0 collective-permute-done.6.refs_7_.refs_6_
  31.3 0.6 collective-permute-done.7.refs_8_.refs_7_
  31.9 1.5 %collective-permute-done.8.refs_9_ = bf16[128,512]{1,0:T(8,128)(2,1)S(1)} collective-permute-done((bf16[128,512]{1,0:T(8,128)(2,1)S(1)}, bf16[128,512]{1,0:T(8,128)(2,1)S(1)}, u32[]{:S(2)}, u32[]{:S(2)}) %collective-permute-start.8) | collective-permute-done | bytes 131104 | tf_op jit(solution)/shard_map/ppermute | solution.py:356
  33.4 0.1 collective-permute-start.9
  33.5 0.8 %arrived_rows.1 = (bf16[384,512]{1,0:T(8,128)(2,1)}, bf16[256,512]{1,0:T(8,128)(2,1)S(1)}, bf16[128,512]{1,0:T(8,128)(2,1)}) custom-call(bf16[128,512]{1,0:T(8,128)(2,1)S(1)} %get-tuple-element.28.refs_0_, bf16[128,512]{1,0:T(8,128)(2,1)S(1)} %collective-permute-done.refs_1_, bf16[128,512]{1,0:T(8,128)(2,1)S(1)} %collective-permute-done.1.refs_2_, ...), custom_call_target="tpu_custom_call" | custom-call | tf_op jit(solution)/shard_map/arrived_rows/pallas_call | solution.py:34
  34.3 0.5 collective-permute-start.12
  34.8 0.5 collective-permute-start.10
  35.3 2.3 %direct_backward.1.refs_1_ = bf16[8,32,512]{2,1,0:T(8,128)(2,1)S(1)} custom-call(bf16[128,512]{1,0:T(8,128)(2,1)S(1)} %get-tuple-element.28.refs_0_, bf16[128,512]{1,0:T(8,128)(2,1)S(1)} %collective-permute-done.refs_1_, bf16[128,512]{1,0:T(8,128)(2,1)S(1)} %collective-permute-done.2.refs_3_.refs_2_, ...), custom_call_target="tpu_custom_call" | custom-call | flops 99999997952 | bytes 5505024 | tf_op jit(solution)/shard_map/direct_backward/pallas_call | solution.py:34
  37.6 0.0 collective-permute-done.9.refs_0_
  37.7 0.0 copy-start
  37.7 0.0 copy-start.1
  37.7 1.6 %collective-permute-start.11 = (bf16[384,512]{1,0:T(8,128)(2,1)S(1)}, bf16[384,512]{1,0:T(8,128)(2,1)S(1)}, u32[]{:S(2)}, u32[]{:S(2)}) collective-permute-start(bf16[384,512]{1,0:T(8,128)(2,1)S(1)} %sibling_rows.1), channel_id=1, source_target_pairs={{0,16},{16,0},{1,17},{17,1},{2,18},{18,2},{3,19},{19,3},{4,20},{20... | collective-permute-start | bytes 1179656 | tf_op jit(solution)/shard_map/ppermute | solution.py:402
  39.3 3.1 %sibling_backward.1 = bf16[16,32,512]{2,1,0:T(8,128)(2,1)} custom-call(bf16[512,512]{1,0:T(8,128)(2,1)S(1)} %collective-permute-done.9.refs_0_, bf16[8,32,512]{2,1,0:T(8,128)(2,1)S(1)} %direct_backward.1.refs_1_, bf16[2048,512]{1,0:T(8,128)(2,1)S(1)} %get-tuple-element.38.refs_10_.refs_8_.refs_2_, bf16[2048,512]{1,0:T(8,128)(2,1)S(1)} %get-tuple-element.44.refs_9_.refs_3_), custom_call_target="tpu_custom_call" | custom-call | flops 99999997952 | bytes 4194304 | tf_op jit(solution)/shard_map/sibling_backward/pallas_call | solution.py:423
  42.4 6.4 %all-to-all-start = ((bf16[16,32,512]{2,1,0:T(8,128)(2,1)}), bf16[16,32,512]{2,1,0:T(8,128)(2,1)S(1)}, u32[]{:S(2)}, u32[]{:S(2)}) async-start(bf16[16,32,512]{2,1,0:T(8,128)(2,1)} %sibling_backward.1), calls=%async_computation | async-start | bytes 1048576 | tf_op jit(solution)/shard_map/all_to_all | solution.py:435
  48.7 0.0 collective-permute-done.10.refs_3_
  48.8 0.0 copy-done
  48.8 0.0 copy-done.1
  48.8 6.3 %first_weights.1 = (f32[1,1024,512]{2,1,0:T(8,128)S(1)}, f32[1,1024,512]{2,1,0:T(8,128)S(1)}, bf16[512,160]{1,0:T(8,128)(2,1)S(1)}, f32[2,16,160]{2,1,0:T(8,128)S(1)}, bf16[2,128,160]{2,1,0:T(8,128)(2,1)S(1)}) custom-call(bf16[512,512]{1,0:T(8,128)(2,1)S(1)} %collective-permute-done.9.refs_0_, bf16[384,512]{1,0:T(8,128)(2,1)} %get-tuple-element.39.refs_1_, ...), custom_call_target="tpu_custom_call" | custom-call | tf_op jit(solution)/shard_map/first_weights/pallas_call | solution.py:34
  55.1 0.0 collective-permute-done.12.refs_1_
  55.1 0.0 collective-permute-done.11.refs_0_
  55.1 4.9 %last_weights.1 = (bf16[1,1024,512]{2,1,0:T(8,128)(2,1)}, bf16[1,1024,512]{2,1,0:T(8,128)(2,1)}) custom-call(bf16[384,512]{1,0:T(8,128)(2,1)S(1)} %collective-permute-done.11.refs_0_, bf16[128,512]{1,0:T(8,128)(2,1)} %collective-permute-done.12.refs_1_, bf16[1,2048,512]{2,1,0:T(8,128)(2,1)} %refs_2_.1, bf16[1,2048,512]{2,1,0:T(8,128)(2,1)} %refs_3_.1, ...), custom_call_target="tpu_custom_call" | custom-call | flops 99999997952 | bytes 11010048 | tf_op jit(solution)/shard_map/last_weights/pallas_call | solution.py:34
  60.0 3.2 %all-to-all-done.back_ref = bf16[16,32,512]{2,1,0:T(8,128)(2,1)S(1)} async-done(((bf16[16,32,512]{2,1,0:T(8,128)(2,1)}), bf16[16,32,512]{2,1,0:T(8,128)(2,1)S(1)}, u32[]{:S(2)}, u32[]{:S(2)}) %all-to-all-start) | async-done | bytes 524320 | tf_op jit(solution)/shard_map/all_to_all | solution.py:435
  63.2 0.9 %combine.1 = (bf16[160,512]{1,0:T(8,128)(2,1)}, bf16[2,160]{1,0:T(2,128)(2,1)}) custom-call(bf16[512,160]{1,0:T(8,128)(2,1)S(1)} %get-tuple-element.41.pick_ref, f32[2,16,160]{2,1,0:T(8,128)S(1)} %get-tuple-element.42.hot_ref, bf16[2,128,160]{2,1,0:T(8,128)(2,1)S(1)} %get-tuple-element.43.spot_ref, bf16[16,32,512]{2,1,0:T(8,128)(2,1)S(1)} %all-to-all-done.back_ref), custom_call_target="tpu_custom_call" | custom-call | flops 167772160 | bytes 955008 | tf_op jit(solution)/shard_map/combine/pallas_call | solution.py:34
  (2 shorter events, 0.1 us)
Async XLA Ops:
  2.2 11.0 %collective-permute-start = (bf16[128,512]{1,0:T(8,128)(2,1)S(1)}, bf16[128,512]{1,0:T(8,128)(2,1)S(1)}, u32[]{:S(2)}, u32[]{:S(2)}) collective-permute-start(bf16[128,512]{1,0:T(8,128)(2,1)S(1)} %get-tuple-element.29), channel_id=1, source_target_pairs={{0,2},{1,3},{2,0},{3,1},{4,6},{5,7},{6,4},{7,5},{8,10},{9,11},{10,... | collective-permute-start | bytes 393224 | tf_op jit(solution)/shard_map/ppermute | solution.py:349
  5.3 9.1 %collective-permute-start.1 = (bf16[128,512]{1,0:T(8,128)(2,1)S(1)}, bf16[128,512]{1,0:T(8,128)(2,1)S(1)}, u32[]{:S(2)}, u32[]{:S(2)}) collective-permute-start(bf16[128,512]{1,0:T(8,128)(2,1)S(1)} %get-tuple-element.30), channel_id=1, source_target_pairs={{0,16},{1,17},{2,18},{3,19},{4,20},{5,21},{6,22},{7,23},{8,24},{9,... | collective-permute-start | bytes 393224 | tf_op jit(solution)/shard_map/ppermute | solution.py:356
  6.8 18.1 %collective-permute-start.2 = (bf16[128,512]{1,0:T(8,128)(2,1)S(1)}, bf16[128,512]{1,0:T(8,128)(2,1)S(1)}, u32[]{:S(2)}, u32[]{:S(2)}) collective-permute-start(bf16[128,512]{1,0:T(8,128)(2,1)S(1)} %get-tuple-element.31), channel_id=1, source_target_pairs={{0,8},{1,9},{2,10},{3,11},{4,12},{5,13},{6,14},{7,15},{8,0},{9,1},... | collective-permute-start | bytes 393224 | tf_op jit(solution)/shard_map/ppermute | solution.py:349
  9.3 18.1 %collective-permute-start.3 = (bf16[128,512]{1,0:T(8,128)(2,1)S(1)}, bf16[128,512]{1,0:T(8,128)(2,1)S(1)}, u32[]{:S(2)}, u32[]{:S(2)}) collective-permute-start(bf16[128,512]{1,0:T(8,128)(2,1)S(1)} %get-tuple-element.32), channel_id=1, source_target_pairs={{0,10},{1,11},{2,8},{3,9},{4,14},{5,15},{6,12},{7,13},{8,2},{9,3},... | collective-permute-start | bytes 393224 | tf_op jit(solution)/shard_map/ppermute | solution.py:349
  9.6 21.6 %collective-permute-start.4 = (bf16[128,512]{1,0:T(8,128)(2,1)S(1)}, bf16[128,512]{1,0:T(8,128)(2,1)S(1)}, u32[]{:S(2)}, u32[]{:S(2)}) collective-permute-start(bf16[128,512]{1,0:T(8,128)(2,1)S(1)} %get-tuple-element.33), channel_id=1, source_target_pairs={{0,12},{1,13},{2,14},{3,15},{4,8},{5,9},{6,10},{7,11},{8,4},{9,5},... | collective-permute-start | bytes 393224 | tf_op jit(solution)/shard_map/ppermute | solution.py:349
  13.2 18.1 %collective-permute-start.5 = (bf16[128,512]{1,0:T(8,128)(2,1)S(1)}, bf16[128,512]{1,0:T(8,128)(2,1)S(1)}, u32[]{:S(2)}, u32[]{:S(2)}) collective-permute-start(bf16[128,512]{1,0:T(8,128)(2,1)S(1)} %get-tuple-element.34), channel_id=1, source_target_pairs={{0,14},{1,15},{2,12},{3,13},{4,10},{5,11},{6,8},{7,9},{8,6},{9,7},... | collective-permute-start | bytes 393224 | tf_op jit(solution)/shard_map/ppermute | solution.py:349
  14.4 16.9 %collective-permute-start.6 = (bf16[128,512]{1,0:T(8,128)(2,1)S(1)}, bf16[128,512]{1,0:T(8,128)(2,1)S(1)}, u32[]{:S(2)}, u32[]{:S(2)}) collective-permute-start(bf16[128,512]{1,0:T(8,128)(2,1)S(1)} %get-tuple-element.35), channel_id=1, source_target_pairs={{0,4},{1,5},{2,6},{3,7},{4,0},{5,1},{6,2},{7,3},{8,12},{9,13},{10,... | collective-permute-start | bytes 393224 | tf_op jit(solution)/shard_map/ppermute | solution.py:349
  24.8 7.0 %collective-permute-start.7 = (bf16[128,512]{1,0:T(8,128)(2,1)S(1)}, bf16[128,512]{1,0:T(8,128)(2,1)S(1)}, u32[]{:S(2)}, u32[]{:S(2)}) collective-permute-start(bf16[128,512]{1,0:T(8,128)(2,1)S(1)} %get-tuple-element.36), channel_id=1, source_target_pairs={{0,6},{1,7},{2,4},{3,5},{4,2},{5,3},{6,0},{7,1},{8,14},{9,15},{10,... | collective-permute-start | bytes 393224 | tf_op jit(solution)/shard_map/ppermute | solution.py:349
  27.5 5.9 %collective-permute-start.8 = (bf16[128,512]{1,0:T(8,128)(2,1)S(1)}, bf16[128,512]{1,0:T(8,128)(2,1)S(1)}, u32[]{:S(2)}, u32[]{:S(2)}) collective-permute-start(bf16[128,512]{1,0:T(8,128)(2,1)S(1)} %get-tuple-element.37), channel_id=1, source_target_pairs={{0,18},{1,19},{2,16},{3,17},{4,22},{5,23},{6,20},{7,21},{8,26},{9,... | collective-permute-start | bytes 393224 | tf_op jit(solution)/shard_map/ppermute | solution.py:356
  33.4 4.2 %collective-permute-start.9 = (bf16[512,512]{1,0:T(8,128)(2,1)S(1)}, bf16[512,512]{1,0:T(8,128)(2,1)S(1)}, u32[]{:S(2)}, u32[]{:S(2)}) collective-permute-start(bf16[512,512]{1,0:T(8,128)(2,1)S(1)} %hand_on.1.refs_10_), channel_id=1, source_target_pairs={{0,1},{1,0},{2,3},{3,2},{4,5},{5,4},{6,7},{7,6},{8,9},{9,8},{10,11... | collective-permute-start | bytes 1572872 | tf_op jit(solution)/shard_map/ppermute | solution.py:394
  34.3 20.8 %collective-permute-start.12 = (bf16[128,512]{1,0:T(8,128)(2,1)}, bf16[128,512]{1,0:T(8,128)(2,1)}, u32[]{:S(2)}, u32[]{:S(2)}) collective-permute-start(bf16[128,512]{1,0:T(8,128)(2,1)} %get-tuple-element.47), channel_id=1, source_target_pairs={{0,1},{1,0},{2,3},{3,2},{4,5},{5,4},{6,7},{7,6},{8,9},{9,8},{10,11... | collective-permute-start | bytes 393224 | tf_op jit(solution)/shard_map/ppermute | solution.py:403
  34.8 13.9 %collective-permute-start.10 = (bf16[384,512]{1,0:T(8,128)(2,1)}, bf16[384,512]{1,0:T(8,128)(2,1)}, u32[]{:S(2)}, u32[]{:S(2)}) collective-permute-start(bf16[384,512]{1,0:T(8,128)(2,1)} %get-tuple-element.39.refs_1_), channel_id=1, source_target_pairs={{0,16},{16,0},{1,17},{17,1},{2,18},{18,2},{3,19},{19,3},{4,20},{20... | collective-permute-start | bytes 1179656 | tf_op jit(solution)/shard_map/ppermute | solution.py:399
  37.7 11.1 %copy-start = (s32[160,2]{0,1:T(2,128)S(1)}, s32[160,2]{0,1:T(2,128)}, u32[]{:S(2)}) copy-start(s32[160,2]{0,1:T(2,128)} %param.8) | copy-start | bytes 3844
  37.7 11.1 %copy-start.1 = (bf16[160,2]{0,1:T(2,128)(2,1)S(1)}, bf16[160,2]{0,1:T(2,128)(2,1)}, u32[]{:S(2)}) copy-start(bf16[160,2]{0,1:T(2,128)(2,1)} %param.7) | copy-start | bytes 1924
  37.7 17.4 %collective-permute-start.11 = (bf16[384,512]{1,0:T(8,128)(2,1)S(1)}, bf16[384,512]{1,0:T(8,128)(2,1)S(1)}, u32[]{:S(2)}, u32[]{:S(2)}) collective-permute-start(bf16[384,512]{1,0:T(8,128)(2,1)S(1)} %sibling_rows.1), channel_id=1, source_target_pairs={{0,16},{16,0},{1,17},{17,1},{2,18},{18,2},{3,19},{19,3},{4,20},{20... | collective-permute-start | bytes 1179656 | tf_op jit(solution)/shard_map/ppermute | solution.py:402
  42.4 20.8 %all-to-all-start = ((bf16[16,32,512]{2,1,0:T(8,128)(2,1)}), bf16[16,32,512]{2,1,0:T(8,128)(2,1)S(1)}, u32[]{:S(2)}, u32[]{:S(2)}) async-start(bf16[16,32,512]{2,1,0:T(8,128)(2,1)} %sibling_backward.1), calls=%async_computation | async-start | bytes 1048576 | tf_op jit(solution)/shard_map/all_to_all | solution.py:435

commit v11 on v10

--- a/solution.py
+++ b/solution.py
@@ -330,7 +330,7 @@
 
     near, far = list(range(1, chips // 2)), list(range(chips // 2, chips))
     order = near[:1] + far + near[1:]
-    twice = [0, order[0]] if mirrors > 1 else []
+    twice = [0] if mirrors > 1 else []
     out = call(
         functools.partial(slots_kernel, pad, chips, twice),
         "slots",
@@ -357,7 +357,7 @@
 
     doubles = list(zip(out[chips:], twice))
     straight = [[crossed(piece, k, hops) for hops in around] for piece, k in doubles]
-    arrivals = [*pieces[:2], *sum(straight[:1], []), *pieces[2:], *sum(straight[1:], [])]
+    arrivals = [*pieces, *sum(straight, [])]
 
     w_up, w_down = hbm(w_up), hbm(w_down)
     up_v, down_v = call(
@@ -392,15 +392,12 @@
     own, flat = places_in(pieces), places_in(sum(straight, []))
     (handed,) = join("hand_on", [*arrivals, up_v], [(i, whole) for i in own])
     sibling = lax.ppermute(handed, "exp", swap)
-    lists = [[(i, 0) for i in own[2:]], [(i, 0) for i in own[:2] + flat]]
-    if flat:
-        lists.append([(i, whole) for i in flat])
-    arrived, early, *mirrored = join("arrived_rows", [*arrivals, handed], *lists)
+    lists = [[(i, 0) for i in own[1:]], [(i, 0) for i in own[:1] + flat]]
+    arrived, early = join("arrived_rows", [*arrivals, handed], *lists)
     firsts = [lax.ppermute(arrived, "rep", hops) for hops in around]
-    later = range(2, chips)
+    later = range(1, chips)
     (passed,) = join("sibling_rows", [sibling], [(0, i * whole) for i in later])
     seconds = [lax.ppermute(passed, "rep", hops) for hops in around]
-    seconds += [lax.ppermute(a, "exp", swap) for a in mirrored]
 
     block = min(512, hidden)
     scratch = [
@@ -433,6 +430,12 @@
         ),
     )(sibling, direct, up_v, down_v)
     back = lax.all_to_all(back, "exp", split_axis=0, concat_axis=0, tiled=True)
+
+    if flat:
+        crossers = sum(straight, [])
+        blocks = [(i, whole) for i in range(len(crossers))]
+        (mirrored,) = join("hand_on_mirror", [*crossers, direct], blocks)
+        seconds.append(lax.ppermute(mirrored, "exp", swap))
 
     part = min(512, share)
 

time: 64.5 us -> 62.7 us (0.972)
  waiting for transfers between devices: 18.3 us -> 21 us
  starting transfers between devices: 22.7 us -> 20.3 us
  Pallas kernels: 22.3 us -> 20.3 us
    ppermute x1, waiting for transfers between devices: 0.01 us -> 3.71 us  [local(): seconds = [lax.ppermute(passed, 'rep', hops) for hops in around]]
    all_to_all x1, waiting for transfers between devices: 3.2 us -> 0.01 us  [local(): back = lax.all_to_all(back, 'exp', split_axis=0, concat_axis=0, tiled=True)]
    ppermute x1, waiting for transfers between devices: 0.01 us -> 2.87 us  [local(): firsts = [lax.ppermute(arrived, 'rep', hops) for hops in around]]
    pallas_call x9 -> x10, Pallas kernels: 19.2 us -> 17.2 us  [call(): pl.pallas_call(body, name=name, out_shape=outs, in_specs=in_specs, out_sp...]
    ppermute x2 -> x1, starting transfers between devices: 3.03 us -> 1.57 us  [crossed(): return lax.ppermute(piece, ('rep', 'exp'), pairs)]
    ppermute x1, starting transfers between devices: 0.53 us -> 1.64 us  [local(): firsts = [lax.ppermute(arrived, 'rep', hops) for hops in around]]
    all_to_all x1, starting transfers between devices: 6.35 us -> 5.24 us  [local(): back = lax.all_to_all(back, 'exp', split_axis=0, concat_axis=0, tiled=True)]
    ppermute x1, starting transfers between devices: 1.56 us -> 0.52 us  [local(): seconds = [lax.ppermute(passed, 'rep', hops) for hops in around]]
  transfers between devices with their start and end apart: 14 -> 13, of which waited for: 5 -> 5; matrix products, arithmetic and copies ran while one was open for 0% -> 0% of each run, Pallas kernels for 31% -> 28%
where the time goes in v11:
time: 62.7 us; the launch traced here: 62.3 us
  waiting for transfers between devices  21 us (33%)
  Pallas kernels  20.3 us (32%)
  starting transfers between devices  20.3 us (32%)
  between operations  0.78 us (1%)
    pallas_call x10, Pallas kernels, call(): pl.pallas_call(body, name=name, out_shape=outs, in_specs=in_specs, out_sp...  17.2 us
    ppermute x7, waiting for transfers between devices, local(): lax.ppermute(out[k], 'exp', hops_to(chips, k))  13.3 us
    ppermute x7, starting transfers between devices, local(): lax.ppermute(out[k], 'exp', hops_to(chips, k))  10.7 us
    all_to_all x1, starting transfers between devices, local(): back = lax.all_to_all(back, 'exp', split_axis=0, concat_axis=0, tiled=True)  5.24 us
    ppermute x1, waiting for transfers between devices, local(): seconds = [lax.ppermute(passed, 'rep', hops) for hops in around]  3.71 us
    pallas_call x1, Pallas kernels, local(): pl.pallas_call(functools.partial(sibling_back_kernel, cap, pad, block, [0...  3.09 us
    ppermute x1, waiting for transfers between devices, local(): firsts = [lax.ppermute(arrived, 'rep', hops) for hops in around]  2.87 us
    ppermute x1, starting transfers between devices, local(): firsts = [lax.ppermute(arrived, 'rep', hops) for hops in around]  1.64 us
  transfers between devices with their start and end apart: 13, of which 5 were waited for; matrix products, arithmetic and copies ran while one was open for 0% of the time, Pallas kernels for 28%

profile of v11, /device:TPU:0, one launch (start us, length us, event | category | flops | bytes accessed | tf_op | source)
XLA Modules:
  0.0 62.3 jit_solution(4216636607294886742)
XLA Ops:
  0.6 1.6 %slots.1 = (bf16[128,512]{1,0:T(8,128)(2,1)S(1)}, bf16[128,512]{1,0:T(8,128)(2,1)S(1)}, bf16[128,512]{1,0:T(8,128)(2,1)S(1)}, bf16[128,512]{1,0:T(8,128)(2,1)S(1...) custom-call(s32[2,160]{1,0:T(2,128)} %bitcast.3, ...), custom_call_target="tpu_custom_call" | custom-call | flops 167772160 | bytes 1509248 | tf_op jit(solution)/shard_map/slots/pallas_call | solution.py:34
  2.2 3.0 %collective-permute-start = (bf16[128,512]{1,0:T(8,128)(2,1)S(1)}, bf16[128,512]{1,0:T(8,128)(2,1)S(1)}, u32[]{:S(2)}, u32[]{:S(2)}) collective-permute-start(bf16[128,512]{1,0:T(8,128)(2,1)S(1)} %get-tuple-element.27), channel_id=1, source_target_pairs={{0,2},{1,3},{2,0},{3,1},{4,6},{5,7},{6,4},{7,5},{8,10},{9,11},{10,... | collective-permute-start | bytes 393224 | tf_op jit(solution)/shard_map/ppermute | solution.py:349
  5.3 2.6 %collective-permute-start.1 = (bf16[128,512]{1,0:T(8,128)(2,1)S(1)}, bf16[128,512]{1,0:T(8,128)(2,1)S(1)}, u32[]{:S(2)}, u32[]{:S(2)}) collective-permute-start(bf16[128,512]{1,0:T(8,128)(2,1)S(1)} %get-tuple-element.28), channel_id=1, source_target_pairs={{0,8},{1,9},{2,10},{3,11},{4,12},{5,13},{6,14},{7,15},{8,0},{9,1},... | collective-permute-start | bytes 393224 | tf_op jit(solution)/shard_map/ppermute | solution.py:349
  7.8 0.0 collective-permute-start.2
  7.9 3.9 %collective-permute-start.3 = (bf16[128,512]{1,0:T(8,128)(2,1)S(1)}, bf16[128,512]{1,0:T(8,128)(2,1)S(1)}, u32[]{:S(2)}, u32[]{:S(2)}) collective-permute-start(bf16[128,512]{1,0:T(8,128)(2,1)S(1)} %get-tuple-element.30), channel_id=1, source_target_pairs={{0,12},{1,13},{2,14},{3,15},{4,8},{5,9},{6,10},{7,11},{8,4},{9,5},... | collective-permute-start | bytes 393224 | tf_op jit(solution)/shard_map/ppermute | solution.py:349
  11.7 1.2 %collective-permute-start.4 = (bf16[128,512]{1,0:T(8,128)(2,1)S(1)}, bf16[128,512]{1,0:T(8,128)(2,1)S(1)}, u32[]{:S(2)}, u32[]{:S(2)}) collective-permute-start(bf16[128,512]{1,0:T(8,128)(2,1)S(1)} %get-tuple-element.31), channel_id=1, source_target_pairs={{0,14},{1,15},{2,12},{3,13},{4,10},{5,11},{6,8},{7,9},{8,6},{9,7},... | collective-permute-start | bytes 393224 | tf_op jit(solution)/shard_map/ppermute | solution.py:349
  12.9 0.0 collective-permute-done.refs_1_
  12.9 0.0 collective-permute-start.5
  12.9 10.7 %collective-permute-done.1.refs_2_ = bf16[128,512]{1,0:T(8,128)(2,1)S(1)} collective-permute-done((bf16[128,512]{1,0:T(8,128)(2,1)S(1)}, bf16[128,512]{1,0:T(8,128)(2,1)S(1)}, u32[]{:S(2)}, u32[]{:S(2)}) %collective-permute-start.1) | collective-permute-done | bytes 131104 | tf_op jit(solution)/shard_map/ppermute | solution.py:349
  23.6 0.0 collective-permute-start.6
  23.6 2.6 %collective-permute-done.2.refs_3_ = bf16[128,512]{1,0:T(8,128)(2,1)S(1)} collective-permute-done((bf16[128,512]{1,0:T(8,128)(2,1)S(1)}, bf16[128,512]{1,0:T(8,128)(2,1)S(1)}, u32[]{:S(2)}, u32[]{:S(2)}) %collective-permute-start.2) | collective-permute-done | bytes 131104 | tf_op jit(solution)/shard_map/ppermute | solution.py:349
  26.2 1.6 %collective-permute-start.7 = (bf16[128,512]{1,0:T(8,128)(2,1)S(1)}, bf16[128,512]{1,0:T(8,128)(2,1)S(1)}, u32[]{:S(2)}, u32[]{:S(2)}) collective-permute-start(bf16[128,512]{1,0:T(8,128)(2,1)S(1)} %get-tuple-element.34), channel_id=1, source_target_pairs={{0,16},{1,17},{2,18},{3,19},{4,20},{5,21},{6,22},{7,23},{8,24},{9,... | collective-permute-start | bytes 393224 | tf_op jit(solution)/shard_map/ppermute | solution.py:356
  27.8 2.2 %fetch_weights.1 = (bf16[2048,512]{1,0:T(8,128)(2,1)S(1)}, bf16[2048,512]{1,0:T(8,128)(2,1)S(1)}) custom-call(bf16[1,2048,512]{2,1,0:T(8,128)(2,1)} %refs_2_.1, bf16[1,2048,512]{2,1,0:T(8,128)(2,1)} %refs_3_.1), custom_call_target="tpu_custom_call" | custom-call | tf_op jit(solution)/shard_map/fetch_weights/pallas_call | solution.py:34
  30.0 0.0 collective-permute-done.3.refs_4_
  30.0 0.0 collective-permute-done.4.refs_5_
  30.0 0.0 collective-permute-done.5.refs_6_
  30.0 0.0 collective-permute-done.6.refs_7_
  30.0 1.1 %collective-permute-done.7.refs_8_.refs_0_ = bf16[128,512]{1,0:T(8,128)(2,1)S(1)} collective-permute-done((bf16[128,512]{1,0:T(8,128)(2,1)S(1)}, bf16[128,512]{1,0:T(8,128)(2,1)S(1)}, u32[]{:S(2)}, u32[]{:S(2)}) %collective-permute-start.7) | collective-permute-done | bytes 131104 | tf_op jit(solution)/shard_map/ppermute | solution.py:356
  31.2 0.1 collective-permute-start.8
  31.3 2.3 %direct_backward.1.refs_1_ = bf16[8,32,512]{2,1,0:T(8,128)(2,1)S(1)} custom-call(bf16[128,512]{1,0:T(8,128)(2,1)S(1)} %get-tuple-element.26.refs_0_, bf16[128,512]{1,0:T(8,128)(2,1)S(1)} %collective-permute-done.refs_1_, bf16[128,512]{1,0:T(8,128)(2,1)S(1)} %collective-permute-done.1.refs_2_, bf16[128,512]{1,0:T(8,128)(2,1)S(1)} %collective-permute-done.2.refs_3_, ...), custom_call_target="tpu_custom_call" | custom-call | flops 99999997952 | bytes 5505024 | tf_op jit(solution)/shard_map/direct_backward/pallas_call | solution.py:34
  33.6 0.6 collective-permute-start.11
  34.2 1.6 %collective-permute-start.9 = (bf16[448,512]{1,0:T(8,128)(2,1)S(1)}, bf16[448,512]{1,0:T(8,128)(2,1)S(1)}, u32[]{:S(2)}, u32[]{:S(2)}) collective-permute-start(bf16[448,512]{1,0:T(8,128)(2,1)S(1)} %get-tuple-element.36.refs_1_), channel_id=1, source_target_pairs={{0,16},{16,0},{1,17},{17,1},{2,18},{18,2},{3,19},{19,3},{4,20},{20... | collective-permute-start | bytes 1376264 | tf_op jit(solution)/shard_map/ppermute | solution.py:397
  35.8 0.0 collective-permute-done.8.refs_0_
  35.9 0.0 copy-start
  35.9 0.0 copy-start.1
  35.9 0.5 collective-permute-start.10
  36.4 3.1 %sibling_backward.1 = bf16[16,32,512]{2,1,0:T(8,128)(2,1)} custom-call(bf16[512,512]{1,0:T(8,128)(2,1)S(1)} %collective-permute-done.8.refs_0_, bf16[8,32,512]{2,1,0:T(8,128)(2,1)S(1)} %direct_backward.1.refs_1_, bf16[2048,512]{1,0:T(8,128)(2,1)S(1)} %get-tuple-element.35.refs_9_.refs_8_.refs_2_, bf16[2048,512]{1,0:T(8,128)(2,1)S(1)} %get-tuple-element.41.refs_9_.refs_3_), custom_call_target="tpu_custom_call" | custom-call | flops 99999997952 | bytes 4194304 | tf_op jit(solution)/shard_map/sibling_backward/pallas_call | solution.py:420
  39.5 5.2 %all-to-all-start = ((bf16[16,32,512]{2,1,0:T(8,128)(2,1)}), bf16[16,32,512]{2,1,0:T(8,128)(2,1)S(1)}, u32[]{:S(2)}, u32[]{:S(2)}) async-start(bf16[16,32,512]{2,1,0:T(8,128)(2,1)} %sibling_backward.1), calls=%async_computation | async-start | bytes 1048576 | tf_op jit(solution)/shard_map/all_to_all | solution.py:432
  44.7 2.9 %collective-permute-done.9.refs_3_ = bf16[448,512]{1,0:T(8,128)(2,1)S(1)} collective-permute-done((bf16[448,512]{1,0:T(8,128)(2,1)S(1)}, bf16[448,512]{1,0:T(8,128)(2,1)S(1)}, u32[]{:S(2)}, u32[]{:S(2)}) %collective-permute-start.9) | collective-permute-done | bytes 458784 | tf_op jit(solution)/shard_map/ppermute | solution.py:397
  47.6 0.0 copy-done
  47.6 0.0 copy-done.1
  47.6 5.2 %first_weights.1 = (f32[1,1024,512]{2,1,0:T(8,128)S(1)}, f32[1,1024,512]{2,1,0:T(8,128)S(1)}, bf16[512,160]{1,0:T(8,128)(2,1)S(1)}, f32[2,16,160]{2,1,0:T(8,128)S(1)}, bf16[2,128,160]{2,1,0:T(8,128)(2,1)S(1)}) custom-call(bf16[512,512]{1,0:T(8,128)(2,1)S(1)} %collective-permute-done.8.refs_0_, bf16[448,512]{1,0:T(8,128)(2,1)S(1)} %get-tuple-element.36.refs_1_, ...), custom_call_target="tpu_custom_call" | custom-call | tf_op jit(solution)/shard_map/first_weights/pallas_call | solution.py:34
  52.8 0.0 collective-permute-done.11.refs_1_
  52.8 3.7 %collective-permute-done.10.refs_0_ = bf16[448,512]{1,0:T(8,128)(2,1)S(1)} collective-permute-done((bf16[448,512]{1,0:T(8,128)(2,1)S(1)}, bf16[448,512]{1,0:T(8,128)(2,1)S(1)}, u32[]{:S(2)}, u32[]{:S(2)}) %collective-permute-start.10) | collective-permute-done | bytes 458784 | tf_op jit(solution)/shard_map/ppermute | solution.py:400
  56.5 4.8 %last_weights.1 = (bf16[1,1024,512]{2,1,0:T(8,128)(2,1)}, bf16[1,1024,512]{2,1,0:T(8,128)(2,1)}) custom-call(bf16[448,512]{1,0:T(8,128)(2,1)S(1)} %collective-permute-done.10.refs_0_, bf16[64,512]{1,0:T(8,128)(2,1)} %collective-permute-done.11.refs_1_, bf16[1,2048,512]{2,1,0:T(8,128)(2,1)} %refs_2_.1, bf16[1,2048,512]{2,1,0:T(8,128)(2,1)} %refs_3_.1, ...), custom_call_target="tpu_custom_call" | custom-call | flops 99999997952 | bytes 11010048 | tf_op jit(solution)/shard_map/last_weights/pallas_call | solution.py:34
  61.4 0.0 all-to-all-done.back_ref
  61.4 0.9 %combine.1 = (bf16[160,512]{1,0:T(8,128)(2,1)}, bf16[2,160]{1,0:T(2,128)(2,1)}) custom-call(bf16[512,160]{1,0:T(8,128)(2,1)S(1)} %get-tuple-element.38.pick_ref, f32[2,16,160]{2,1,0:T(8,128)S(1)} %get-tuple-element.39.hot_ref, bf16[2,128,160]{2,1,0:T(8,128)(2,1)S(1)} %get-tuple-element.40.spot_ref, bf16[16,32,512]{2,1,0:T(8,128)(2,1)S(1)} %all-to-all-done.back_ref), custom_call_target="tpu_custom_call" | custom-call | flops 167772160 | bytes 955008 | tf_op jit(solution)/shard_map/combine/pallas_call | solution.py:34
  (4 shorter events, 0.1 us)
Async XLA Ops:
  2.2 10.7 %collective-permute-start = (bf16[128,512]{1,0:T(8,128)(2,1)S(1)}, bf16[128,512]{1,0:T(8,128)(2,1)S(1)}, u32[]{:S(2)}, u32[]{:S(2)}) collective-permute-start(bf16[128,512]{1,0:T(8,128)(2,1)S(1)} %get-tuple-element.27), channel_id=1, source_target_pairs={{0,2},{1,3},{2,0},{3,1},{4,6},{5,7},{6,4},{7,5},{8,10},{9,11},{10,... | collective-permute-start | bytes 393224 | tf_op jit(solution)/shard_map/ppermute | solution.py:349
  5.3 18.4 %collective-permute-start.1 = (bf16[128,512]{1,0:T(8,128)(2,1)S(1)}, bf16[128,512]{1,0:T(8,128)(2,1)S(1)}, u32[]{:S(2)}, u32[]{:S(2)}) collective-permute-start(bf16[128,512]{1,0:T(8,128)(2,1)S(1)} %get-tuple-element.28), channel_id=1, source_target_pairs={{0,8},{1,9},{2,10},{3,11},{4,12},{5,13},{6,14},{7,15},{8,0},{9,1},... | collective-permute-start | bytes 393224 | tf_op jit(solution)/shard_map/ppermute | solution.py:349
  7.8 18.3 %collective-permute-start.2 = (bf16[128,512]{1,0:T(8,128)(2,1)S(1)}, bf16[128,512]{1,0:T(8,128)(2,1)S(1)}, u32[]{:S(2)}, u32[]{:S(2)}) collective-permute-start(bf16[128,512]{1,0:T(8,128)(2,1)S(1)} %get-tuple-element.29), channel_id=1, source_target_pairs={{0,10},{1,11},{2,8},{3,9},{4,14},{5,15},{6,12},{7,13},{8,2},{9,3},... | collective-permute-start | bytes 393224 | tf_op jit(solution)/shard_map/ppermute | solution.py:349
  7.9 22.2 %collective-permute-start.3 = (bf16[128,512]{1,0:T(8,128)(2,1)S(1)}, bf16[128,512]{1,0:T(8,128)(2,1)S(1)}, u32[]{:S(2)}, u32[]{:S(2)}) collective-permute-start(bf16[128,512]{1,0:T(8,128)(2,1)S(1)} %get-tuple-element.30), channel_id=1, source_target_pairs={{0,12},{1,13},{2,14},{3,15},{4,8},{5,9},{6,10},{7,11},{8,4},{9,5},... | collective-permute-start | bytes 393224 | tf_op jit(solution)/shard_map/ppermute | solution.py:349
  11.7 18.3 %collective-permute-start.4 = (bf16[128,512]{1,0:T(8,128)(2,1)S(1)}, bf16[128,512]{1,0:T(8,128)(2,1)S(1)}, u32[]{:S(2)}, u32[]{:S(2)}) collective-permute-start(bf16[128,512]{1,0:T(8,128)(2,1)S(1)} %get-tuple-element.31), channel_id=1, source_target_pairs={{0,14},{1,15},{2,12},{3,13},{4,10},{5,11},{6,8},{7,9},{8,6},{9,7},... | collective-permute-start | bytes 393224 | tf_op jit(solution)/shard_map/ppermute | solution.py:349
  12.9 17.1 %collective-permute-start.5 = (bf16[128,512]{1,0:T(8,128)(2,1)S(1)}, bf16[128,512]{1,0:T(8,128)(2,1)S(1)}, u32[]{:S(2)}, u32[]{:S(2)}) collective-permute-start(bf16[128,512]{1,0:T(8,128)(2,1)S(1)} %get-tuple-element.32), channel_id=1, source_target_pairs={{0,4},{1,5},{2,6},{3,7},{4,0},{5,1},{6,2},{7,3},{8,12},{9,13},{10,... | collective-permute-start | bytes 393224 | tf_op jit(solution)/shard_map/ppermute | solution.py:349
  23.6 6.4 %collective-permute-start.6 = (bf16[128,512]{1,0:T(8,128)(2,1)S(1)}, bf16[128,512]{1,0:T(8,128)(2,1)S(1)}, u32[]{:S(2)}, u32[]{:S(2)}) collective-permute-start(bf16[128,512]{1,0:T(8,128)(2,1)S(1)} %get-tuple-element.33), channel_id=1, source_target_pairs={{0,6},{1,7},{2,4},{3,5},{4,2},{5,3},{6,0},{7,1},{8,14},{9,15},{10,... | collective-permute-start | bytes 393224 | tf_op jit(solution)/shard_map/ppermute | solution.py:349
  26.2 5.0 %collective-permute-start.7 = (bf16[128,512]{1,0:T(8,128)(2,1)S(1)}, bf16[128,512]{1,0:T(8,128)(2,1)S(1)}, u32[]{:S(2)}, u32[]{:S(2)}) collective-permute-start(bf16[128,512]{1,0:T(8,128)(2,1)S(1)} %get-tuple-element.34), channel_id=1, source_target_pairs={{0,16},{1,17},{2,18},{3,19},{4,20},{5,21},{6,22},{7,23},{8,24},{9,... | collective-permute-start | bytes 393224 | tf_op jit(solution)/shard_map/ppermute | solution.py:356
  31.2 4.6 %collective-permute-start.8 = (bf16[512,512]{1,0:T(8,128)(2,1)S(1)}, bf16[512,512]{1,0:T(8,128)(2,1)S(1)}, u32[]{:S(2)}, u32[]{:S(2)}) collective-permute-start(bf16[512,512]{1,0:T(8,128)(2,1)S(1)} %hand_on.1.refs_9_), channel_id=1, source_target_pairs={{0,1},{1,0},{2,3},{3,2},{4,5},{5,4},{6,7},{7,6},{8,9},{9,8},{10,11... | collective-permute-start | bytes 1572872 | tf_op jit(solution)/shard_map/ppermute | solution.py:394
  33.6 19.2 %collective-permute-start.11 = (bf16[64,512]{1,0:T(8,128)(2,1)S(1)}, bf16[64,512]{1,0:T(8,128)(2,1)}, u32[]{:S(2)}, u32[]{:S(2)}) collective-permute-start(bf16[64,512]{1,0:T(8,128)(2,1)S(1)} %hand_on_mirror.1), channel_id=1, source_target_pairs={{0,1},{1,0},{2,3},{3,2},{4,5},{5,4},{6,7},{7,6},{8,9},{9,8},{10,11... | collective-permute-start | bytes 196616 | tf_op jit(solution)/shard_map/ppermute | solution.py:438
  34.2 13.4 %collective-permute-start.9 = (bf16[448,512]{1,0:T(8,128)(2,1)S(1)}, bf16[448,512]{1,0:T(8,128)(2,1)S(1)}, u32[]{:S(2)}, u32[]{:S(2)}) collective-permute-start(bf16[448,512]{1,0:T(8,128)(2,1)S(1)} %get-tuple-element.36.refs_1_), channel_id=1, source_target_pairs={{0,16},{16,0},{1,17},{17,1},{2,18},{18,2},{3,19},{19,3},{4,20},{20... | collective-permute-start | bytes 1376264 | tf_op jit(solution)/shard_map/ppermute | solution.py:397
  35.9 11.8 %copy-start = (s32[160,2]{0,1:T(2,128)S(1)}, s32[160,2]{0,1:T(2,128)}, u32[]{:S(2)}) copy-start(s32[160,2]{0,1:T(2,128)} %param.8) | copy-start | bytes 3844
  35.9 11.8 %copy-start.1 = (bf16[160,2]{0,1:T(2,128)(2,1)S(1)}, bf16[160,2]{0,1:T(2,128)(2,1)}, u32[]{:S(2)}) copy-start(bf16[160,2]{0,1:T(2,128)(2,1)} %param.7) | copy-start | bytes 1924
  35.9 20.6 %collective-permute-start.10 = (bf16[448,512]{1,0:T(8,128)(2,1)S(1)}, bf16[448,512]{1,0:T(8,128)(2,1)S(1)}, u32[]{:S(2)}, u32[]{:S(2)}) collective-permute-start(bf16[448,512]{1,0:T(8,128)(2,1)S(1)} %sibling_rows.1), channel_id=1, source_target_pairs={{0,16},{16,0},{1,17},{17,1},{2,18},{18,2},{3,19},{19,3},{4,20},{20... | collective-permute-start | bytes 1376264 | tf_op jit(solution)/shard_map/ppermute | solution.py:400
  39.5 21.9 %all-to-all-start = ((bf16[16,32,512]{2,1,0:T(8,128)(2,1)}), bf16[16,32,512]{2,1,0:T(8,128)(2,1)S(1)}, u32[]{:S(2)}, u32[]{:S(2)}) async-start(bf16[16,32,512]{2,1,0:T(8,128)(2,1)} %sibling_backward.1), calls=%async_computation | async-start | bytes 1048576 | tf_op jit(solution)/shard_map/all_to_all | solution.py:432

commit v12 on v11

--- a/solution.py
+++ b/solution.py
@@ -14,6 +14,7 @@
 AHEAD = 10**11
 IN_HBM = pl.BlockSpec(memory_space=pltpu.HBM)
 IN_VMEM = pl.BlockSpec(memory_space=pltpu.VMEM)
+ANYWHERE = pl.BlockSpec(memory_space=pl.ANY)
 DMA = pltpu.SemaphoreType.DMA
 
 
@@ -134,7 +135,7 @@
 
 def steps_of(size, block):
     half = block // 2
-    return [(0, half), (half, half)] + [(at, block) for at in range(block, size, block)]
+    return [(0, half)] + [(at, block) for at in range(half, size - half, block)] + [(size - half, half)]
 
 
 class Fetch:
@@ -220,7 +221,7 @@
 
 
 def direct_back_kernel(cap, pad, block, chips, *refs):
-    pieces, (up_ref, down_ref, out_ref, *scratch) = refs[:chips], refs[chips:]
+    pieces, (up_ref, down_ref, _, out_ref, *scratch) = refs[:chips], refs[chips:]
 
     def put(k, first, rest):
         out_ref[k, :, 0:128] = first
@@ -260,16 +261,20 @@
     row_refs, weights = take(number), take(2)
     sums = take(2) if begun else None
     notes = None if begun else take(2)
+    take(1)
     outs = take(2)
     notes_out = None if begun else take(3)
-    rows_ref, grads_ref, up_ref, down_ref, sems, *kept = refs
+    up_ref, down_ref = weights if begun else take(2)
+    rows_ref, grads_ref, sems, *kept = refs
     steps = steps_of(share, block)
-    fetch = Fetch(*weights, up_ref, down_ref, sems, lax.axis_index("rep") * share, steps)
+    if not begun:
+        fetch = Fetch(*weights, up_ref, down_ref, sems, lax.axis_index("rep") * share, steps)
     gather_rows(pad, [(row_refs[i], at) for i, at in places], rows_ref, grads_ref)
     copies = []
     for step, (at, size) in enumerate(steps):
         here = pl.ds(at, size)
-        fetch.wait(step)
+        if not begun:
+            fetch.wait(step)
         active, slope = silu_parts(dot(up_ref[here, :], rows_ref[...], 1, 1))
         back = dot(down_ref[here, :], grads_ref[...], 1, 1)
         hid_grad = (back * slope).astype(BF16)
@@ -329,7 +334,7 @@
     unit = 2 * slots * feat
 
     near, far = list(range(1, chips // 2)), list(range(chips // 2, chips))
-    order = near[:1] + far + near[1:]
+    order = far[:2] + near[:1] + far[2:] + near[1:]
     twice = [0] if mirrors > 1 else []
     out = call(
         functools.partial(slots_kernel, pad, chips, twice),
@@ -357,7 +362,7 @@
 
     doubles = list(zip(out[chips:], twice))
     straight = [[crossed(piece, k, hops) for hops in around] for piece, k in doubles]
-    arrivals = [*pieces, *sum(straight, [])]
+    arrivals = [*pieces[:2], *sum(straight, []), *pieces[2:]]
 
     w_up, w_down = hbm(w_up), hbm(w_down)
     up_v, down_v = call(
@@ -373,13 +378,13 @@
     )
     whole = 2 * pad
 
-    def join(name, arrays, *lists):
+    def join(name, arrays, *lists, after=()):
         return call(
             functools.partial(join_kernel, whole, lists),
             name,
             [shape((len(blocks) * whole, feat), BF16) for blocks in lists],
-            arrays,
-            [IN_VMEM] * len(arrays),
+            [*arrays, *after],
+            [IN_VMEM] * len(arrays) + [ANYWHERE] * len(after),
             [],
             0,
             0,
@@ -411,8 +416,8 @@
         functools.partial(direct_back_kernel, cap, pad, block, chips),
         "direct_backward",
         [shape(results, BF16)],
-        [*pieces, up_v, down_v],
-        [IN_VMEM] * (chips + 2),
+        [*pieces, up_v, down_v, arrived],
+        [IN_VMEM] * (chips + 2) + [ANYWHERE],
         scratch,
         AHEAD,
         slots * hidden,
@@ -429,31 +434,26 @@
             flops=AHEAD, bytes_accessed=4 * hidden * feat, transcendentals=slots * hidden
         ),
     )(sibling, direct, up_v, down_v)
+    results_out = hbm(back)
     back = lax.all_to_all(back, "exp", split_axis=0, concat_axis=0, tiled=True)
 
-    if flat:
-        crossers = sum(straight, [])
-        blocks = [(i, whole) for i in range(len(crossers))]
-        (mirrored,) = join("hand_on_mirror", [*crossers, direct], blocks)
-        seconds.append(lax.ppermute(mirrored, "exp", swap))
-
     part = min(512, share)
 
-    def weights_call(name, arrays, places, sums, ended, flops):
+    def weights_call(name, arrays, places, weights, sums, ended, flops):
         begun = bool(sums)
         number = len(places) * pad
         notes = [] if begun else [
             shape((groups * pad, rows), BF16),
             shape((2, groups, rows), F32),
             shape((2, 128, rows), BF16),
+            shape((share, feat), BF16),
+            shape((share, feat), BF16),
         ]
         grad = pltpu.HBM((1, share, feat), BF16) if ended else shape((1, share, feat), F32)
         steps = len(steps_of(share, part))
         scratch = [
             pltpu.VMEM((number, feat), BF16),
             pltpu.VMEM((number, feat), BF16),
-            pltpu.VMEM((share, feat), BF16),
-            pltpu.VMEM((share, feat), BF16),
             DMA((2 * steps,)),
         ]
         if ended:
@@ -464,8 +464,11 @@
             ),
             name,
             [grad] * 2 + notes,
-            [*arrays, w_up, w_down, *(sums or [routes_t, gates_t])],
-            [IN_VMEM] * len(arrays) + [IN_HBM] * 2 + [IN_VMEM] * 2,
+            [*arrays, *weights, *(sums or [routes_t, gates_t]), results_out],
+            [IN_VMEM] * len(arrays)
+            + [IN_VMEM if begun else IN_HBM] * 2
+            + [IN_VMEM] * 2
+            + [IN_HBM],
             scratch,
             flops,
             number * share,
@@ -479,11 +482,18 @@
         ]
 
     joined = [sibling, arrived, early, *firsts]
-    *sums, pick, hot, spot = weights_call(
-        "first_weights", joined, places_of(joined), [], not seconds, 0
-    )
+    *sums, pick, hot, spot, up_v, down_v = weights_call(
+        "first_weights", joined, places_of(joined), [w_up, w_down], [], not seconds, 0
+    )
+    if flat:
+        crossers = sum(straight, [])
+        blocks = [(i, whole) for i in range(len(crossers))]
+        (mirrored,) = join("hand_on_mirror", crossers, blocks, after=sums[:1])
+        seconds.append(lax.ppermute(mirrored, "exp", swap))
     if seconds:
-        sums = weights_call("last_weights", seconds, places_of(seconds), sums, True, AHEAD)
+        sums = weights_call(
+            "last_weights", seconds, places_of(seconds), [up_v, down_v], sums, True, AHEAD
+        )
     grad_up, grad_down = sums
 
     d_tokens, d_gates = call(

time: 62.7 us -> 76.8 us (1.22)
  local copies, waits for them, and re-layouts: 0.01 us -> 7.33 us
  waiting for transfers between devices: 21 us -> 24.3 us
  starting transfers between devices: 20.3 us -> 23.1 us
    unnamed x4 -> x24, local copies, waits for them, and re-layouts: 0.01 us -> 7.33 us
    all_to_all x1, waiting for transfers between devices: 0.01 us -> 6.93 us  [local(): back = lax.all_to_all(back, 'exp', split_axis=0, concat_axis=0, tiled=True)]
    ppermute x7, starting transfers between devices: 10.7 us -> 14.9 us  [local(): lax.ppermute(out[k], 'exp', hops_to(chips, k))]
    ppermute x1, waiting for transfers between devices: 3.71 us -> 0.01 us  [local(): seconds = [lax.ppermute(passed, 'rep', hops) for hops in around]]
    ppermute x1, waiting for transfers between devices: 2.87 us -> 6.08 us  [local(): firsts = [lax.ppermute(arrived, 'rep', hops) for hops in around]]
    ppermute x7, waiting for transfers between devices: 13.3 us -> 11.3 us  [local(): lax.ppermute(out[k], 'exp', hops_to(chips, k))]
    ppermute x1, waiting for transfers between devices: 1.11 us -> 0.01 us  [crossed(): return lax.ppermute(piece, ('rep', 'exp'), pairs)]
  transfers between devices with their start and end apart: 13 -> 13, of which waited for: 5 -> 7; matrix products, arithmetic and copies ran while one was open for 0% -> 0% of each run, Pallas kernels for 28% -> 24%
where the time goes in v12:
time: 76.8 us; the launch traced here: 76.4 us
  waiting for transfers between devices  24.3 us (32%)
  starting transfers between devices  23.1 us (30%)
  Pallas kernels  20.9 us (27%)
  local copies, waits for them, and re-layouts  7.33 us (10%)
  between operations  0.81 us (1%)
    pallas_call x10, Pallas kernels, call(): pl.pallas_call(body, name=name, out_shape=outs, in_specs=in_specs, out_sp...  17.8 us
    ppermute x7, starting transfers between devices, local(): lax.ppermute(out[k], 'exp', hops_to(chips, k))  14.9 us
    ppermute x7, waiting for transfers between devices, local(): lax.ppermute(out[k], 'exp', hops_to(chips, k))  11.3 us
    unnamed x24, local copies, waits for them, and re-layouts  7.33 us
    all_to_all x1, waiting for transfers between devices, local(): back = lax.all_to_all(back, 'exp', split_axis=0, concat_axis=0, tiled=True)  6.93 us
    ppermute x1, waiting for transfers between devices, local(): firsts = [lax.ppermute(arrived, 'rep', hops) for hops in around]  6.08 us
    all_to_all x1, starting transfers between devices, local(): back = lax.all_to_all(back, 'exp', split_axis=0, concat_axis=0, tiled=True)  4.53 us
    pallas_call x1, Pallas kernels, local(): pl.pallas_call(functools.partial(sibling_back_kernel, cap, pad, block, [0...  3.1 us
  transfers between devices with their start and end apart: 13, of which 7 were waited for; matrix products, arithmetic and copies ran while one was open for 0% of the time, Pallas kernels for 24%

profile of v12, /device:TPU:0, one launch (start us, length us, event | category | flops | bytes accessed | tf_op | source)
XLA Modules:
  0.0 76.4 jit_solution(11367745503575603970)
XLA Ops:
  0.6 1.6 %slots.1 = (bf16[128,512]{1,0:T(8,128)(2,1)S(1)}, bf16[128,512]{1,0:T(8,128)(2,1)S(1)}, bf16[128,512]{1,0:T(8,128)(2,1)S(1)}, bf16[128,512]{1,0:T(8,128)(2,1)S(1...) custom-call(s32[2,160]{1,0:T(2,128)} %bitcast.3, ...), custom_call_target="tpu_custom_call" | custom-call | flops 167772160 | bytes 1509248 | tf_op jit(solution)/shard_map/slots/pallas_call | solution.py:35
  2.2 4.1 %collective-permute-start = (bf16[128,512]{1,0:T(8,128)(2,1)S(1)}, bf16[128,512]{1,0:T(8,128)(2,1)S(1)}, u32[]{:S(2)}, u32[]{:S(2)}) collective-permute-start(bf16[128,512]{1,0:T(8,128)(2,1)S(1)} %get-tuple-element.29), channel_id=1, source_target_pairs={{0,8},{1,9},{2,10},{3,11},{4,12},{5,13},{6,14},{7,15},{8,0},{9,1},... | collective-permute-start | bytes 393224 | tf_op jit(solution)/shard_map/ppermute | solution.py:354
  6.3 1.5 %collective-permute-start.1 = (bf16[128,512]{1,0:T(8,128)(2,1)S(1)}, bf16[128,512]{1,0:T(8,128)(2,1)S(1)}, u32[]{:S(2)}, u32[]{:S(2)}) collective-permute-start(bf16[128,512]{1,0:T(8,128)(2,1)S(1)} %get-tuple-element.30), channel_id=1, source_target_pairs={{0,16},{1,17},{2,18},{3,19},{4,20},{5,21},{6,22},{7,23},{8,24},{9,... | collective-permute-start | bytes 393224 | tf_op jit(solution)/shard_map/ppermute | solution.py:361
  7.8 1.3 %collective-permute-start.2 = (bf16[128,512]{1,0:T(8,128)(2,1)S(1)}, bf16[128,512]{1,0:T(8,128)(2,1)S(1)}, u32[]{:S(2)}, u32[]{:S(2)}) collective-permute-start(bf16[128,512]{1,0:T(8,128)(2,1)S(1)} %get-tuple-element.31), channel_id=1, source_target_pairs={{0,10},{1,11},{2,8},{3,9},{4,14},{5,15},{6,12},{7,13},{8,2},{9,3},... | collective-permute-start | bytes 393224 | tf_op jit(solution)/shard_map/ppermute | solution.py:354
  9.1 0.5 collective-permute-start.3
  9.6 3.6 %collective-permute-start.4 = (bf16[128,512]{1,0:T(8,128)(2,1)S(1)}, bf16[128,512]{1,0:T(8,128)(2,1)S(1)}, u32[]{:S(2)}, u32[]{:S(2)}) collective-permute-start(bf16[128,512]{1,0:T(8,128)(2,1)S(1)} %get-tuple-element.33), channel_id=1, source_target_pairs={{0,12},{1,13},{2,14},{3,15},{4,8},{5,9},{6,10},{7,11},{8,4},{9,5},... | collective-permute-start | bytes 393224 | tf_op jit(solution)/shard_map/ppermute | solution.py:354
  13.2 5.9 %collective-permute-done.refs_1_ = bf16[128,512]{1,0:T(8,128)(2,1)S(1)} collective-permute-done((bf16[128,512]{1,0:T(8,128)(2,1)S(1)}, bf16[128,512]{1,0:T(8,128)(2,1)S(1)}, u32[]{:S(2)}, u32[]{:S(2)}) %collective-permute-start) | collective-permute-done | bytes 131104 | tf_op jit(solution)/shard_map/ppermute | solution.py:354
  19.1 3.8 %collective-permute-start.5 = (bf16[128,512]{1,0:T(8,128)(2,1)S(1)}, bf16[128,512]{1,0:T(8,128)(2,1)S(1)}, u32[]{:S(2)}, u32[]{:S(2)}) collective-permute-start(bf16[128,512]{1,0:T(8,128)(2,1)S(1)} %get-tuple-element.34), channel_id=1, source_target_pairs={{0,14},{1,15},{2,12},{3,13},{4,10},{5,11},{6,8},{7,9},{8,6},{9,7},... | collective-permute-start | bytes 393224 | tf_op jit(solution)/shard_map/ppermute | solution.py:354
  22.8 0.0 collective-permute-done.1.refs_2_.refs_0_
  22.8 0.0 copy-start
  22.8 0.0 collective-permute-start.6
  22.9 0.3 collective-permute-done.2.refs_3_.refs_2_
  23.2 1.6 %collective-permute-start.7 = (bf16[128,512]{1,0:T(8,128)(2,1)S(1)}, bf16[128,512]{1,0:T(8,128)(2,1)S(1)}, u32[]{:S(2)}, u32[]{:S(2)}) collective-permute-start(bf16[128,512]{1,0:T(8,128)(2,1)S(1)} %get-tuple-element.36), channel_id=1, source_target_pairs={{0,6},{1,7},{2,4},{3,5},{4,2},{5,3},{6,0},{7,1},{8,14},{9,15},{10,... | collective-permute-start | bytes 393224 | tf_op jit(solution)/shard_map/ppermute | solution.py:354
  24.8 2.2 %fetch_weights.1 = (bf16[2048,512]{1,0:T(8,128)(2,1)S(1)}, bf16[2048,512]{1,0:T(8,128)(2,1)S(1)}) custom-call(bf16[1,2048,512]{2,1,0:T(8,128)(2,1)} %refs_4_.1, bf16[1,2048,512]{2,1,0:T(8,128)(2,1)} %refs_5_.1), custom_call_target="tpu_custom_call" | custom-call | tf_op jit(solution)/shard_map/fetch_weights/pallas_call | solution.py:35
  27.1 0.0 collective-permute-done.3.refs_4_.refs_3_
  27.1 0.0 collective-permute-done.4.refs_5_.refs_4_
  27.1 1.1 %collective-permute-done.5.refs_6_.refs_5_ = bf16[128,512]{1,0:T(8,128)(2,1)S(1)} collective-permute-done((bf16[128,512]{1,0:T(8,128)(2,1)S(1)}, bf16[128,512]{1,0:T(8,128)(2,1)S(1)}, u32[]{:S(2)}, u32[]{:S(2)}) %collective-permute-start.5) | collective-permute-done | bytes 131104 | tf_op jit(solution)/shard_map/ppermute | solution.py:354
  28.2 1.9 %collective-permute-done.6.refs_7_.refs_6_ = bf16[128,512]{1,0:T(8,128)(2,1)S(1)} collective-permute-done((bf16[128,512]{1,0:T(8,128)(2,1)S(1)}, bf16[128,512]{1,0:T(8,128)(2,1)S(1)}, u32[]{:S(2)}, u32[]{:S(2)}) %collective-permute-start.6) | collective-permute-done | bytes 131104 | tf_op jit(solution)/shard_map/ppermute | solution.py:354
  30.2 2.0 %collective-permute-done.7.refs_8_.refs_7_ = bf16[128,512]{1,0:T(8,128)(2,1)S(1)} collective-permute-done((bf16[128,512]{1,0:T(8,128)(2,1)S(1)}, bf16[128,512]{1,0:T(8,128)(2,1)S(1)}, u32[]{:S(2)}, u32[]{:S(2)}) %collective-permute-start.7) | collective-permute-done | bytes 131104 | tf_op jit(solution)/shard_map/ppermute | solution.py:354
  32.2 0.1 collective-permute-start.8
  32.3 0.0 copy-done
  32.3 0.8 %arrived_rows.1 = (bf16[448,512]{1,0:T(8,128)(2,1)}, bf16[128,512]{1,0:T(8,128)(2,1)S(1)}) custom-call(bf16[128,512]{1,0:T(8,128)(2,1)S(1)} %get-tuple-element.28.refs_0_, bf16[128,512]{1,0:T(8,128)(2,1)S(1)} %collective-permute-done.refs_1_, bf16[128,512]{1,0:T(8,128)(2,1)S(1)} %collective-permute-done.1.refs_2_.refs_0_, ...), custom_call_target="tpu_custom_call" | custom-call | tf_op jit(solution)/shard_map/arrived_rows/pallas_call | solution.py:35
  33.1 1.5 %collective-permute-start.9 = (bf16[448,512]{1,0:T(8,128)(2,1)}, bf16[448,512]{1,0:T(8,128)(2,1)}, u32[]{:S(2)}, u32[]{:S(2)}) collective-permute-start(bf16[448,512]{1,0:T(8,128)(2,1)} %get-tuple-element.38.refs_10_.refs_1_), channel_id=1, source_target_pairs={{0,16},{16,0},{1,17},{17,1},{2,18},{18,2},{3,19},{19,3},{4,20},{20... | collective-permute-start | bytes 1376264 | tf_op jit(solution)/shard_map/ppermute | solution.py:402
  34.6 2.3 %direct_backward.1.refs_1_ = bf16[8,32,512]{2,1,0:T(8,128)(2,1)S(1)} custom-call(bf16[128,512]{1,0:T(8,128)(2,1)S(1)} %get-tuple-element.28.refs_0_, bf16[128,512]{1,0:T(8,128)(2,1)S(1)} %collective-permute-done.refs_1_, bf16[128,512]{1,0:T(8,128)(2,1)S(1)} %collective-permute-done.2.refs_3_.refs_2_, ...), custom_call_target="tpu_custom_call" | custom-call | flops 99999997952 | bytes 5963776 | tf_op jit(solution)/shard_map/direct_backward/pallas_call | solution.py:35
  36.9 0.0 collective-permute-done.8.refs_0_
  36.9 0.0 copy-start.4
  36.9 0.0 copy-start.5
  36.9 0.6 collective-permute-start.10
  37.5 3.1 %sibling_backward.1.refs_8_.refs_6_ = bf16[16,32,512]{2,1,0:T(8,128)(2,1)} custom-call(bf16[512,512]{1,0:T(8,128)(2,1)S(1)} %collective-permute-done.8.refs_0_, bf16[8,32,512]{2,1,0:T(8,128)(2,1)S(1)} %direct_backward.1.refs_1_, bf16[2048,512]{1,0:T(8,128)(2,1)S(1)} %get-tuple-element.37.refs_9_.refs_8_.refs_2_, ...), custom_call_target="tpu_custom_call" | custom-call | flops 99999997952 | bytes 4194304 | tf_op jit(solution)/shard_map/sibling_backward/pallas_call | solution.py:425
  40.6 6.1 %collective-permute-done.9.refs_3_ = bf16[448,512]{1,0:T(8,128)(2,1)} collective-permute-done((bf16[448,512]{1,0:T(8,128)(2,1)}, bf16[448,512]{1,0:T(8,128)(2,1)}, u32[]{:S(2)}, u32[]{:S(2)}) %collective-permute-start.9) | collective-permute-done | bytes 458784 | tf_op jit(solution)/shard_map/ppermute | solution.py:402
  46.7 0.0 copy-done.4
  46.7 0.0 copy-done.5
  46.7 0.0 copy-start.1
  46.7 6.4 %first_weights.1 = (f32[1,1024,512]{2,1,0:T(8,128)S(1)}, f32[1,1024,512]{2,1,0:T(8,128)S(1)}, bf16[512,160]{1,0:T(8,128)(2,1)S(1)}, f32[2,16,160]{2,1,0:T(8,128)...) custom-call(bf16[512,512]{1,0:T(8,128)(2,1)S(1)} %collective-permute-done.8.ref, ...), custom_call_target="tpu_custom_call" | custom-call | tf_op jit(solution)/shard_map/first_weights/pallas_call | solution.py:35
  53.1 0.0 copy-start.8
  53.1 1.0 %copy-done.8 = bf16[1024,512]{1,0:T(8,128)(2,1)} copy-done((bf16[1024,512]{1,0:T(8,128)(2,1)}, bf16[1024,512]{1,0:T(8,128)(2,1)S(1)}, u32[]{:S(2)}) %copy-start.8) | copy-done | bytes 1048600
  54.1 0.0 copy-start.10
  54.1 1.0 %copy-done.10 = bf16[1024,512]{1,0:T(8,128)(2,1)} copy-done((bf16[1024,512]{1,0:T(8,128)(2,1)}, bf16[1024,512]{1,0:T(8,128)(2,1)S(1)}, u32[]{:S(2)}) %copy-start.10) | copy-done | bytes 1048600
  55.0 0.0 copy-start.2
  55.1 0.0 copy-start.6
  55.1 0.0 copy-done.1
  55.1 0.6 copy-done.2
  55.6 0.8 copy-done.6
  56.4 0.0 collective-permute-start.11
  56.4 4.5 %all-to-all-start = ((bf16[16,32,512]{2,1,0:T(8,128)(2,1)}), bf16[16,32,512]{2,1,0:T(8,128)(2,1)S(1)}, u32[]{:S(2)}, u32[]{:S(2)}) async-start(bf16[16,32,512]{2,1,0:T(8,128)(2,1)} %sibling_backward.1.refs_8_.refs_6_), calls=%async_computation | async-start | bytes 1048576 | tf_op jit(solution)/shard_map/all_to_all | solution.py:438
  60.9 0.0 collective-permute-done.11.refs_1_
  61.0 0.0 collective-permute-done.10.refs_0_
  61.0 0.0 copy-start.7
  61.0 1.6 %copy-done.7 = f32[1,1024,512]{2,1,0:T(8,128)S(1)} copy-done((f32[1,1024,512]{2,1,0:T(8,128)S(1)}, f32[1,1024,512]{2,1,0:T(8,128)}, u32[]{:S(2)}) %copy-start.7) | copy-done | bytes 2097176
  62.6 0.0 copy-start.9
  62.6 1.2 %copy-done.9 = bf16[1024,512]{1,0:T(8,128)(2,1)S(1)} copy-done((bf16[1024,512]{1,0:T(8,128)(2,1)S(1)}, bf16[1024,512]{1,0:T(8,128)(2,1)}, u32[]{:S(2)}) %copy-start.9) | copy-done | bytes 1048600
  63.8 0.0 copy-start.11
  63.8 1.2 %copy-done.11 = bf16[1024,512]{1,0:T(8,128)(2,1)S(1)} copy-done((bf16[1024,512]{1,0:T(8,128)(2,1)S(1)}, bf16[1024,512]{1,0:T(8,128)(2,1)}, u32[]{:S(2)}) %copy-start.11) | copy-done | bytes 1048600
  65.0 0.0 copy-start.3
  65.0 3.5 %last_weights.1 = (bf16[1,1024,512]{2,1,0:T(8,128)(2,1)}, bf16[1,1024,512]{2,1,0:T(8,128)(2,1)}) custom-call(bf16[448,512]{1,0:T(8,128)(2,1)} %collective-permute-done.10.refs_0_, bf16[64,512]{1,0:T(8,128)(2,1)} %collective-permute-done.11.refs_1_, bf16[1024,512]{1,0:T(8,128)(2,1)S(1)} %copy-done.9, bf16[1024,512]{1,0:T(8,128)(2,1)S(1)} %copy-done.11, ...), custom_call_target="tpu_custom_call" | custom-call | flops 99999997952 | bytes 9437184 | tf_op jit(solution)/shard_map/last_weights/pallas_call | solution.py:35
  68.5 6.9 %all-to-all-done.back_ref = bf16[16,32,512]{2,1,0:T(8,128)(2,1)S(1)} async-done(((bf16[16,32,512]{2,1,0:T(8,128)(2,1)}), bf16[16,32,512]{2,1,0:T(8,128)(2,1)S(1)}, u32[]{:S(2)}, u32[]{:S(2)}) %all-to-all-start) | async-done | bytes 524320 | tf_op jit(solution)/shard_map/all_to_all | solution.py:438
  75.4 0.0 copy-done.3
  75.4 0.9 %combine.1 = (bf16[160,512]{1,0:T(8,128)(2,1)}, bf16[2,160]{1,0:T(2,128)(2,1)}) custom-call(bf16[512,160]{1,0:T(8,128)(2,1)S(1)} %get-tuple-element.41.pick_ref, f32[2,16,160]{2,1,0:T(8,128)S(1)} %copy-done.3, bf16[2,128,160]{2,1,0:T(8,128)(2,1)S(1)} %get-tuple-element.43.spot_ref, bf16[16,32,512]{2,1,0:T(8,128)(2,1)S(1)} %all-to-all-done.back_ref), custom_call_target="tpu_custom_call" | custom-call | flops 167772160 | bytes 955008 | tf_op jit(solution)/shard_map/combine/pallas_call | solution.py:35
  (3 shorter events, 0.1 us)
Async XLA Ops:
  2.2 16.9 %collective-permute-start = (bf16[128,512]{1,0:T(8,128)(2,1)S(1)}, bf16[128,512]{1,0:T(8,128)(2,1)S(1)}, u32[]{:S(2)}, u32[]{:S(2)}) collective-permute-start(bf16[128,512]{1,0:T(8,128)(2,1)S(1)} %get-tuple-element.29), channel_id=1, source_target_pairs={{0,8},{1,9},{2,10},{3,11},{4,12},{5,13},{6,14},{7,15},{8,0},{9,1},... | collective-permute-start | bytes 393224 | tf_op jit(solution)/shard_map/ppermute | solution.py:354
  6.3 16.5 %collective-permute-start.1 = (bf16[128,512]{1,0:T(8,128)(2,1)S(1)}, bf16[128,512]{1,0:T(8,128)(2,1)S(1)}, u32[]{:S(2)}, u32[]{:S(2)}) collective-permute-start(bf16[128,512]{1,0:T(8,128)(2,1)S(1)} %get-tuple-element.30), channel_id=1, source_target_pairs={{0,16},{1,17},{2,18},{3,19},{4,20},{5,21},{6,22},{7,23},{8,24},{9,... | collective-permute-start | bytes 393224 | tf_op jit(solution)/shard_map/ppermute | solution.py:361
  7.8 15.4 %collective-permute-start.2 = (bf16[128,512]{1,0:T(8,128)(2,1)S(1)}, bf16[128,512]{1,0:T(8,128)(2,1)S(1)}, u32[]{:S(2)}, u32[]{:S(2)}) collective-permute-start(bf16[128,512]{1,0:T(8,128)(2,1)S(1)} %get-tuple-element.31), channel_id=1, source_target_pairs={{0,10},{1,11},{2,8},{3,9},{4,14},{5,15},{6,12},{7,13},{8,2},{9,3},... | collective-permute-start | bytes 393224 | tf_op jit(solution)/shard_map/ppermute | solution.py:354
  9.1 17.9 %collective-permute-start.3 = (bf16[128,512]{1,0:T(8,128)(2,1)S(1)}, bf16[128,512]{1,0:T(8,128)(2,1)S(1)}, u32[]{:S(2)}, u32[]{:S(2)}) collective-permute-start(bf16[128,512]{1,0:T(8,128)(2,1)S(1)} %get-tuple-element.32), channel_id=1, source_target_pairs={{0,2},{1,3},{2,0},{3,1},{4,6},{5,7},{6,4},{7,5},{8,10},{9,11},{10,... | collective-permute-start | bytes 393224 | tf_op jit(solution)/shard_map/ppermute | solution.py:354
  9.6 17.5 %collective-permute-start.4 = (bf16[128,512]{1,0:T(8,128)(2,1)S(1)}, bf16[128,512]{1,0:T(8,128)(2,1)S(1)}, u32[]{:S(2)}, u32[]{:S(2)}) collective-permute-start(bf16[128,512]{1,0:T(8,128)(2,1)S(1)} %get-tuple-element.33), channel_id=1, source_target_pairs={{0,12},{1,13},{2,14},{3,15},{4,8},{5,9},{6,10},{7,11},{8,4},{9,5},... | collective-permute-start | bytes 393224 | tf_op jit(solution)/shard_map/ppermute | solution.py:354
  19.1 9.1 %collective-permute-start.5 = (bf16[128,512]{1,0:T(8,128)(2,1)S(1)}, bf16[128,512]{1,0:T(8,128)(2,1)S(1)}, u32[]{:S(2)}, u32[]{:S(2)}) collective-permute-start(bf16[128,512]{1,0:T(8,128)(2,1)S(1)} %get-tuple-element.34), channel_id=1, source_target_pairs={{0,14},{1,15},{2,12},{3,13},{4,10},{5,11},{6,8},{7,9},{8,6},{9,7},... | collective-permute-start | bytes 393224 | tf_op jit(solution)/shard_map/ppermute | solution.py:354
  22.8 9.4 %copy-start = (bf16[128,512]{1,0:T(8,128)(2,1)}, bf16[128,512]{1,0:T(8,128)(2,1)S(1)}, u32[]{:S(2)}) copy-start(bf16[128,512]{1,0:T(8,128)(2,1)S(1)} %collective-permute-done.1.refs_2_.refs_0_) | copy-start | bytes 393220
  22.8 7.3 %collective-permute-start.6 = (bf16[128,512]{1,0:T(8,128)(2,1)S(1)}, bf16[128,512]{1,0:T(8,128)(2,1)S(1)}, u32[]{:S(2)}, u32[]{:S(2)}) collective-permute-start(bf16[128,512]{1,0:T(8,128)(2,1)S(1)} %get-tuple-element.35), channel_id=1, source_target_pairs={{0,4},{1,5},{2,6},{3,7},{4,0},{5,1},{6,2},{7,3},{8,12},{9,13},{10,... | collective-permute-start | bytes 393224 | tf_op jit(solution)/shard_map/ppermute | solution.py:354
  23.2 9.0 %collective-permute-start.7 = (bf16[128,512]{1,0:T(8,128)(2,1)S(1)}, bf16[128,512]{1,0:T(8,128)(2,1)S(1)}, u32[]{:S(2)}, u32[]{:S(2)}) collective-permute-start(bf16[128,512]{1,0:T(8,128)(2,1)S(1)} %get-tuple-element.36), channel_id=1, source_target_pairs={{0,6},{1,7},{2,4},{3,5},{4,2},{5,3},{6,0},{7,1},{8,14},{9,15},{10,... | collective-permute-start | bytes 393224 | tf_op jit(solution)/shard_map/ppermute | solution.py:354
  32.2 4.7 %collective-permute-start.8 = (bf16[512,512]{1,0:T(8,128)(2,1)S(1)}, bf16[512,512]{1,0:T(8,128)(2,1)S(1)}, u32[]{:S(2)}, u32[]{:S(2)}) collective-permute-start(bf16[512,512]{1,0:T(8,128)(2,1)S(1)} %hand_on.1.refs_9_), channel_id=1, source_target_pairs={{0,1},{1,0},{2,3},{3,2},{4,5},{5,4},{6,7},{7,6},{8,9},{9,8},{10,11... | collective-permute-start | bytes 1572872 | tf_op jit(solution)/shard_map/ppermute | solution.py:399
  33.1 13.6 %collective-permute-start.9 = (bf16[448,512]{1,0:T(8,128)(2,1)}, bf16[448,512]{1,0:T(8,128)(2,1)}, u32[]{:S(2)}, u32[]{:S(2)}) collective-permute-start(bf16[448,512]{1,0:T(8,128)(2,1)} %get-tuple-element.38.refs_10_.refs_1_), channel_id=1, source_target_pairs={{0,16},{16,0},{1,17},{17,1},{2,18},{18,2},{3,19},{19,3},{4,20},{20... | collective-permute-start | bytes 1376264 | tf_op jit(solution)/shard_map/ppermute | solution.py:402
  36.9 9.8 %copy-start.4 = (s32[160,2]{0,1:T(2,128)S(1)}, s32[160,2]{0,1:T(2,128)}, u32[]{:S(2)}) copy-start(s32[160,2]{0,1:T(2,128)} %param.8) | copy-start | bytes 3844
  36.9 9.8 %copy-start.5 = (bf16[160,2]{0,1:T(2,128)(2,1)S(1)}, bf16[160,2]{0,1:T(2,128)(2,1)}, u32[]{:S(2)}) copy-start(bf16[160,2]{0,1:T(2,128)(2,1)} %param.7) | copy-start | bytes 1924
  36.9 24.0 %collective-permute-start.10 = (bf16[448,512]{1,0:T(8,128)(2,1)S(1)}, bf16[448,512]{1,0:T(8,128)(2,1)}, u32[]{:S(2)}, u32[]{:S(2)}) collective-permute-start(bf16[448,512]{1,0:T(8,128)(2,1)S(1)} %sibling_rows.1), channel_id=1, source_target_pairs={{0,16},{16,0},{1,17},{17,1},{2,18},{18,2},{3,19},{19,3},{4,20},{20... | collective-permute-start | bytes 1376264 | tf_op jit(solution)/shard_map/ppermute | solution.py:405
  46.7 8.3 %copy-start.1 = (bf16[128,512]{1,0:T(8,128)(2,1)S(1)}, bf16[128,512]{1,0:T(8,128)(2,1)}, u32[]{:S(2)}) copy-start(bf16[128,512]{1,0:T(8,128)(2,1)} %copy-done) | copy-start | bytes 393220
  53.1 1.0 %copy-start.8 = (bf16[1024,512]{1,0:T(8,128)(2,1)}, bf16[1024,512]{1,0:T(8,128)(2,1)S(1)}, u32[]{:S(2)}) copy-start(bf16[1024,512]{1,0:T(8,128)(2,1)S(1)} %get-tuple-element.47.refs_2_) | copy-start | bytes 3145732
  54.1 1.0 %copy-start.10 = (bf16[1024,512]{1,0:T(8,128)(2,1)}, bf16[1024,512]{1,0:T(8,128)(2,1)S(1)}, u32[]{:S(2)}) copy-start(bf16[1024,512]{1,0:T(8,128)(2,1)S(1)} %get-tuple-element.48.refs_3_) | copy-start | bytes 3145732
  55.0 0.6 copy-start.2
  55.1 1.4 %copy-start.6 = (f32[1,1024,512]{2,1,0:T(8,128)}, f32[1,1024,512]{2,1,0:T(8,128)S(1)}, u32[]{:S(2)}) copy-start(f32[1,1024,512]{2,1,0:T(8,128)S(1)} %get-tuple-element.49.refs_5_) | copy-start | bytes 6291460
  56.4 4.5 %collective-permute-start.11 = (bf16[64,512]{1,0:T(8,128)(2,1)S(1)}, bf16[64,512]{1,0:T(8,128)(2,1)}, u32[]{:S(2)}, u32[]{:S(2)}) collective-permute-start(bf16[64,512]{1,0:T(8,128)(2,1)S(1)} %hand_on_mirror.1), channel_id=1, source_target_pairs={{0,1},{1,0},{2,3},{3,2},{4,5},{5,4},{6,7},{7,6},{8,9},{9,8},{10,11... | collective-permute-start | bytes 196616 | tf_op jit(solution)/shard_map/ppermute | solution.py:492
  56.4 19.0 %all-to-all-start = ((bf16[16,32,512]{2,1,0:T(8,128)(2,1)}), bf16[16,32,512]{2,1,0:T(8,128)(2,1)S(1)}, u32[]{:S(2)}, u32[]{:S(2)}) async-start(bf16[16,32,512]{2,1,0:T(8,128)(2,1)} %sibling_backward.1.refs_8_.refs_6_), calls=%async_computation | async-start | bytes 1048576 | tf_op jit(solution)/shard_map/all_to_all | solution.py:438
  61.0 1.6 %copy-start.7 = (f32[1,1024,512]{2,1,0:T(8,128)S(1)}, f32[1,1024,512]{2,1,0:T(8,128)}, u32[]{:S(2)}) copy-start(f32[1,1024,512]{2,1,0:T(8,128)} %copy-done.6) | copy-start | bytes 6291460
  62.6 1.2 %copy-start.9 = (bf16[1024,512]{1,0:T(8,128)(2,1)S(1)}, bf16[1024,512]{1,0:T(8,128)(2,1)}, u32[]{:S(2)}) copy-start(bf16[1024,512]{1,0:T(8,128)(2,1)} %copy-done.8) | copy-start | bytes 3145732
  63.8 1.2 %copy-start.11 = (bf16[1024,512]{1,0:T(8,128)(2,1)S(1)}, bf16[1024,512]{1,0:T(8,128)(2,1)}, u32[]{:S(2)}) copy-start(bf16[1024,512]{1,0:T(8,128)(2,1)} %copy-done.10) | copy-start | bytes 3145732
  65.0 10.4 %copy-start.3 = (f32[2,16,160]{2,1,0:T(8,128)S(1)}, f32[2,16,160]{2,1,0:T(8,128)}, u32[]{:S(2)}) copy-start(f32[2,16,160]{2,1,0:T(8,128)} %copy-done.2) | copy-start | bytes 61444

commit v13 on v12

--- a/solution.py
+++ b/solution.py
@@ -1,4 +1,5 @@
 import functools
+import itertools
 import math
 
 import jax
@@ -97,9 +98,9 @@
     return [index == pieces[k : k + 1, :] * pad + slot[k] for k in range(2)]
 
 
-def slots_kernel(pad, chips, twice, routes_hbm, gates_hbm, tok_hbm, cot_hbm, *refs):
-    order = [*range(chips), *twice]
-    out_refs, refs = refs[: len(order)], refs[len(order) :]
+def slots_kernel(pad, routes_hbm, gates_hbm, tok_hbm, cot_hbm, *refs):
+    chips = len(refs) - 5
+    out_refs, refs = refs[:chips], refs[chips:]
     routes_ref, gates_ref, tok_ref, cot_ref, sems = refs
     pairs = [
         (routes_hbm, routes_ref),
@@ -126,7 +127,7 @@
     copies[3].wait()
     rows = dot(plain, tok_ref[...], 1, 0).astype(BF16)
     grads = dot(scaled, cot_ref[...], 1, 0).astype(BF16)
-    for k, out_ref in zip(order, out_refs):
+    for k, out_ref in enumerate(out_refs):
         for i in range(2):
             here = slice((2 * k + i) * pad, (2 * k + i + 1) * pad)
             out_ref[2 * i * pad : (2 * i + 1) * pad, :] = rows[here, :]
@@ -261,7 +262,6 @@
     row_refs, weights = take(number), take(2)
     sums = take(2) if begun else None
     notes = None if begun else take(2)
-    take(1)
     outs = take(2)
     notes_out = None if begun else take(3)
     up_ref, down_ref = weights if begun else take(2)
@@ -334,12 +334,12 @@
     unit = 2 * slots * feat
 
     near, far = list(range(1, chips // 2)), list(range(chips // 2, chips))
-    order = far[:2] + near[:1] + far[2:] + near[1:]
-    twice = [0] if mirrors > 1 else []
+    order = [k for pair in itertools.zip_longest(far[:-1], near[:-1]) for k in pair if k is not None]
+    order += far[-1:] + near[-1:]
     out = call(
-        functools.partial(slots_kernel, pad, chips, twice),
+        functools.partial(slots_kernel, pad),
         "slots",
-        [shape((4 * pad, feat), BF16)] * (chips + len(twice)),
+        [shape((4 * pad, feat), BF16)] * chips,
         [hbm(a) for a in (routes_t, gates_t, tokens, cotangent)],
         [IN_HBM] * 4,
         [
@@ -354,15 +354,6 @@
     pieces = [out[0]] + [lax.ppermute(out[k], "exp", hops_to(chips, k)) for k in order]
     swap = [(i, i ^ 1) for i in range(groups)]
     around = [[(i, (i + s) % mirrors) for i in range(mirrors)] for s in range(1, mirrors)]
-
-    def crossed(piece, k, hops):
-        moves = hops_to(chips, k) if k else [(i, i) for i in range(groups)]
-        pairs = [(m * groups + i, n * groups + j) for m, n in hops for i, j in moves]
-        return lax.ppermute(piece, ("rep", "exp"), pairs)
-
-    doubles = list(zip(out[chips:], twice))
-    straight = [[crossed(piece, k, hops) for hops in around] for piece, k in doubles]
-    arrivals = [*pieces[:2], *sum(straight, []), *pieces[2:]]
 
     w_up, w_down = hbm(w_up), hbm(w_down)
     up_v, down_v = call(
@@ -378,31 +369,24 @@
     )
     whole = 2 * pad
 
-    def join(name, arrays, *lists, after=()):
+    def join(name, arrays, *lists):
         return call(
             functools.partial(join_kernel, whole, lists),
             name,
             [shape((len(blocks) * whole, feat), BF16) for blocks in lists],
-            [*arrays, *after],
-            [IN_VMEM] * len(arrays) + [ANYWHERE] * len(after),
+            arrays,
+            [IN_VMEM] * len(arrays),
             [],
             0,
             0,
             SMALL,
         )
 
-    def places_in(arrays):
-        return [next(i for i, a in enumerate(arrivals) if a is array) for array in arrays]
-
-    own, flat = places_in(pieces), places_in(sum(straight, []))
-    (handed,) = join("hand_on", [*arrivals, up_v], [(i, whole) for i in own])
+    (handed,) = join("hand_on", [*pieces, up_v], [(i, whole) for i in range(chips)])
     sibling = lax.ppermute(handed, "exp", swap)
-    lists = [[(i, 0) for i in own[1:]], [(i, 0) for i in own[:1] + flat]]
-    arrived, early = join("arrived_rows", [*arrivals, handed], *lists)
+    (arrived,) = join("arrived_rows", [*pieces, handed], [(i, 0) for i in range(chips)])
     firsts = [lax.ppermute(arrived, "rep", hops) for hops in around]
-    later = range(1, chips)
-    (passed,) = join("sibling_rows", [sibling], [(0, i * whole) for i in later])
-    seconds = [lax.ppermute(passed, "rep", hops) for hops in around]
+    seconds = [lax.ppermute(sibling, "rep", hops) for hops in around]
 
     block = min(512, hidden)
     scratch = [
@@ -434,7 +418,6 @@
             flops=AHEAD, bytes_accessed=4 * hidden * feat, transcendentals=slots * hidden
         ),
     )(sibling, direct, up_v, down_v)
-    results_out = hbm(back)
     back = lax.all_to_all(back, "exp", split_axis=0, concat_axis=0, tiled=True)
 
     part = min(512, share)
@@ -464,11 +447,8 @@
             ),
             name,
             [grad] * 2 + notes,
-            [*arrays, *weights, *(sums or [routes_t, gates_t]), results_out],
-            [IN_VMEM] * len(arrays)
-            + [IN_VMEM if begun else IN_HBM] * 2
-            + [IN_VMEM] * 2
-            + [IN_HBM],
+            [*arrays, *weights, *(sums or [routes_t, gates_t])],
+            [IN_VMEM] * len(arrays) + [IN_VMEM if begun else IN_HBM] * 2 + [IN_VMEM] * 2,
             scratch,
             flops,
             number * share,
@@ -481,15 +461,10 @@
             (first + i, at) for i, a in enumerate(arrays) for at in range(0, a.shape[0], whole)
         ]
 
-    joined = [sibling, arrived, early, *firsts]
+    joined = [sibling, arrived, *firsts]
     *sums, pick, hot, spot, up_v, down_v = weights_call(
         "first_weights", joined, places_of(joined), [w_up, w_down], [], not seconds, 0
     )
-    if flat:
-        crossers = sum(straight, [])
-        blocks = [(i, whole) for i in range(len(crossers))]
-        (mirrored,) = join("hand_on_mirror", crossers, blocks, after=sums[:1])
-        seconds.append(lax.ppermute(mirrored, "exp", swap))
     if seconds:
         sums = weights_call(
             "last_weights", seconds, places_of(seconds), [up_v, down_v], sums, True, AHEAD

time: 76.8 us -> 59.5 us (0.77)
  waiting for transfers between devices: 24.3 us -> 14.6 us
  local copies, waits for them, and re-layouts: 7.33 us -> 0.01 us
  Pallas kernels: 20.9 us -> 19.8 us
    unnamed x24 -> x4, local copies, waits for them, and re-layouts: 7.33 us -> 0.01 us
    all_to_all x1, waiting for transfers between devices: 6.93 us -> 0.01 us  [local(): back = lax.all_to_all(back, 'exp', split_axis=0, concat_axis=0, tiled=True)]
    ppermute x3 -> x1, waiting for transfers between devices: 0.01 us -> 4.33 us  [local(): seconds = [lax.ppermute(sibling, 'rep', hops) for hops in around]]
    ppermute x1, waiting for transfers between devices: 6.08 us -> 1.81 us  [local(): firsts = [lax.ppermute(arrived, 'rep', hops) for hops in around]]
    ppermute x7, waiting for transfers between devices: 11.3 us -> 8.43 us  [local(): lax.ppermute(out[k], 'exp', hops_to(chips, k))]
    ppermute x3 -> x1, starting transfers between devices: 2.1 us -> 0.6 us  [local(): seconds = [lax.ppermute(sibling, 'rep', hops) for hops in around]]
    all_to_all x1, starting transfers between devices: 4.53 us -> 5.72 us  [local(): back = lax.all_to_all(back, 'exp', split_axis=0, concat_axis=0, tiled=True)]
    pallas_call x10 -> x8, Pallas kernels: 17.8 us -> 16.7 us  [call(): pl.pallas_call(body, name=name, out_shape=outs, in_specs=in_specs, out_sp...]
  transfers between devices with their start and end apart: 13 -> 11, of which waited for: 7 -> 5; matrix products, arithmetic and copies ran while one was open for 0% -> 0% of each run, Pallas kernels for 24% -> 29%
where the time goes in v13:
time: 59.5 us; the launch traced here: 58.9 us
  starting transfers between devices  23.8 us (40%)
  Pallas kernels  19.8 us (33%)
  waiting for transfers between devices  14.6 us (25%)
  between operations  0.76 us (1%)
    pallas_call x8, Pallas kernels, call(): pl.pallas_call(body, name=name, out_shape=outs, in_specs=in_specs, out_sp...  16.7 us
    ppermute x7, starting transfers between devices, local(): lax.ppermute(out[k], 'exp', hops_to(chips, k))  15.9 us
    ppermute x7, waiting for transfers between devices, local(): lax.ppermute(out[k], 'exp', hops_to(chips, k))  8.43 us
    all_to_all x1, starting transfers between devices, local(): back = lax.all_to_all(back, 'exp', split_axis=0, concat_axis=0, tiled=True)  5.72 us
    ppermute x1, waiting for transfers between devices, local(): seconds = [lax.ppermute(sibling, 'rep', hops) for hops in around]  4.33 us
    pallas_call x1, Pallas kernels, local(): pl.pallas_call(functools.partial(sibling_back_kernel, cap, pad, block, [0...  3.07 us
    ppermute x1, waiting for transfers between devices, local(): firsts = [lax.ppermute(arrived, 'rep', hops) for hops in around]  1.81 us
    ppermute x1, starting transfers between devices, local(): firsts = [lax.ppermute(arrived, 'rep', hops) for hops in around]  1.49 us
  transfers between devices with their start and end apart: 11, of which 5 were waited for; matrix products, arithmetic and copies ran while one was open for 0% of the time, Pallas kernels for 29%

profile of v13, /device:TPU:0, one launch (start us, length us, event | category | flops | bytes accessed | tf_op | source)
XLA Modules:
  0.0 58.9 jit_solution(16512362778084938577)
XLA Ops:
  0.6 1.6 %slots.1 = (bf16[128,512]{1,0:T(8,128)(2,1)S(1)}, bf16[128,512]{1,0:T(8,128)(2,1)S(1)}, bf16[128,512]{1,0:T(8,128)(2,1)S(1)}, bf16[128,512]{1,0:T(8,128)(2,1)S(1...) custom-call(s32[2,160]{1,0:T(2,128)} %bitcast.3, ...), custom_call_target="tpu_custom_call" | custom-call | flops 167772160 | bytes 1378176 | tf_op jit(solution)/shard_map/slots/pallas_call | solution.py:36
  2.2 4.1 %collective-permute-start = (bf16[128,512]{1,0:T(8,128)(2,1)S(1)}, bf16[128,512]{1,0:T(8,128)(2,1)S(1)}, u32[]{:S(2)}, u32[]{:S(2)}) collective-permute-start(bf16[128,512]{1,0:T(8,128)(2,1)S(1)} %get-tuple-element.26), channel_id=1, source_target_pairs={{0,8},{1,9},{2,10},{3,11},{4,12},{5,13},{6,14},{7,15},{8,0},{9,1},... | collective-permute-start | bytes 393224 | tf_op jit(solution)/shard_map/ppermute | solution.py:354
  6.3 1.5 %collective-permute-start.1 = (bf16[128,512]{1,0:T(8,128)(2,1)S(1)}, bf16[128,512]{1,0:T(8,128)(2,1)S(1)}, u32[]{:S(2)}, u32[]{:S(2)}) collective-permute-start(bf16[128,512]{1,0:T(8,128)(2,1)S(1)} %get-tuple-element.27), channel_id=1, source_target_pairs={{0,2},{1,3},{2,0},{3,1},{4,6},{5,7},{6,4},{7,5},{8,10},{9,11},{10,... | collective-permute-start | bytes 393224 | tf_op jit(solution)/shard_map/ppermute | solution.py:354
  7.8 0.0 collective-permute-start.2
  7.9 1.8 %collective-permute-start.3 = (bf16[128,512]{1,0:T(8,128)(2,1)S(1)}, bf16[128,512]{1,0:T(8,128)(2,1)S(1)}, u32[]{:S(2)}, u32[]{:S(2)}) collective-permute-start(bf16[128,512]{1,0:T(8,128)(2,1)S(1)} %get-tuple-element.29), channel_id=1, source_target_pairs={{0,4},{1,5},{2,6},{3,7},{4,0},{5,1},{6,2},{7,3},{8,12},{9,13},{10,... | collective-permute-start | bytes 393224 | tf_op jit(solution)/shard_map/ppermute | solution.py:354
  9.7 2.5 %collective-permute-start.4 = (bf16[128,512]{1,0:T(8,128)(2,1)S(1)}, bf16[128,512]{1,0:T(8,128)(2,1)S(1)}, u32[]{:S(2)}, u32[]{:S(2)}) collective-permute-start(bf16[128,512]{1,0:T(8,128)(2,1)S(1)} %get-tuple-element.30), channel_id=1, source_target_pairs={{0,12},{1,13},{2,14},{3,15},{4,8},{5,9},{6,10},{7,11},{8,4},{9,5},... | collective-permute-start | bytes 393224 | tf_op jit(solution)/shard_map/ppermute | solution.py:354
  12.2 4.8 %collective-permute-done.refs_1_ = bf16[128,512]{1,0:T(8,128)(2,1)S(1)} collective-permute-done((bf16[128,512]{1,0:T(8,128)(2,1)S(1)}, bf16[128,512]{1,0:T(8,128)(2,1)S(1)}, u32[]{:S(2)}, u32[]{:S(2)}) %collective-permute-start) | collective-permute-done | bytes 131104 | tf_op jit(solution)/shard_map/ppermute | solution.py:354
  17.0 5.9 %collective-permute-start.5 = (bf16[128,512]{1,0:T(8,128)(2,1)S(1)}, bf16[128,512]{1,0:T(8,128)(2,1)S(1)}, u32[]{:S(2)}, u32[]{:S(2)}) collective-permute-start(bf16[128,512]{1,0:T(8,128)(2,1)S(1)} %get-tuple-element.31), channel_id=1, source_target_pairs={{0,14},{1,15},{2,12},{3,13},{4,10},{5,11},{6,8},{7,9},{8,6},{9,7},... | collective-permute-start | bytes 393224 | tf_op jit(solution)/shard_map/ppermute | solution.py:354
  22.9 0.0 collective-permute-done.1.refs_2_
  22.9 0.0 collective-permute-start.6
  22.9 2.2 %fetch_weights.1 = (bf16[2048,512]{1,0:T(8,128)(2,1)S(1)}, bf16[2048,512]{1,0:T(8,128)(2,1)S(1)}) custom-call(bf16[1,2048,512]{2,1,0:T(8,128)(2,1)} %refs_3_.1, bf16[1,2048,512]{2,1,0:T(8,128)(2,1)} %refs_4_.1), custom_call_target="tpu_custom_call" | custom-call | tf_op jit(solution)/shard_map/fetch_weights/pallas_call | solution.py:36
  25.2 0.0 collective-permute-done.2.refs_3_
  25.2 0.0 collective-permute-done.3.refs_4_
  25.2 0.0 collective-permute-done.4.refs_5_
  25.2 1.0 %collective-permute-done.5.refs_6_ = bf16[128,512]{1,0:T(8,128)(2,1)S(1)} collective-permute-done((bf16[128,512]{1,0:T(8,128)(2,1)S(1)}, bf16[128,512]{1,0:T(8,128)(2,1)S(1)}, u32[]{:S(2)}, u32[]{:S(2)}) %collective-permute-start.5) | collective-permute-done | bytes 131104 | tf_op jit(solution)/shard_map/ppermute | solution.py:354
  26.3 2.5 %collective-permute-done.6.refs_7_ = bf16[128,512]{1,0:T(8,128)(2,1)S(1)} collective-permute-done((bf16[128,512]{1,0:T(8,128)(2,1)S(1)}, bf16[128,512]{1,0:T(8,128)(2,1)S(1)}, u32[]{:S(2)}, u32[]{:S(2)}) %collective-permute-start.6) | collective-permute-done | bytes 131104 | tf_op jit(solution)/shard_map/ppermute | solution.py:354
  28.8 0.1 collective-permute-start.7
  28.9 0.8 %arrived_rows.1.refs_1_.refs_10_ = bf16[512,512]{1,0:T(8,128)(2,1)} custom-call(bf16[128,512]{1,0:T(8,128)(2,1)S(1)} %get-tuple-element.25.refs_0_, bf16[128,512]{1,0:T(8,128)(2,1)S(1)} %collective-permute-done.refs_1_, bf16[128,512]{1,0:T(8,128)(2,1)S(1)} %collective-permute-done.1.refs_2_, bf16[128,512]{1,0:T(8,128)(2,1)S(1)} %collective-permute-done.2.refs_3_, ...), custom_call_target="tpu_custom_call" | custom-call | tf_op jit(solution)/shard_map/arrived_rows/pallas_call | solution.py:36
  29.8 1.5 %collective-permute-start.8 = (bf16[512,512]{1,0:T(8,128)(2,1)}, bf16[512,512]{1,0:T(8,128)(2,1)}, u32[]{:S(2)}, u32[]{:S(2)}) collective-permute-start(bf16[512,512]{1,0:T(8,128)(2,1)} %arrived_rows.1.refs_1_.refs_10_), channel_id=1, source_target_pairs={{0,16},{16,0},{1,17},{17,1},{2,18},{18,2},{3,19},{19,3},{4,20},{20... | collective-permute-start | bytes 1572872 | tf_op jit(solution)/shard_map/ppermute | solution.py:388
  31.2 2.3 %direct_backward.1.refs_1_ = bf16[8,32,512]{2,1,0:T(8,128)(2,1)S(1)} custom-call(bf16[128,512]{1,0:T(8,128)(2,1)S(1)} %get-tuple-element.25.refs_0_, bf16[128,512]{1,0:T(8,128)(2,1)S(1)} %collective-permute-done.refs_1_, bf16[128,512]{1,0:T(8,128)(2,1)S(1)} %collective-permute-done.1.refs_2_, bf16[128,512]{1,0:T(8,128)(2,1)S(1)} %collective-permute-done.2.refs_3_, ...), custom_call_target="tpu_custom_call" | custom-call | flops 99999997952 | bytes 6029312 | tf_op jit(solution)/shard_map/direct_backward/pallas_call | solution.py:36
  33.5 0.0 copy-start
  33.5 0.0 copy-start.1
  33.6 0.0 collective-permute-done.7.refs_0_
  33.6 0.6 %collective-permute-start.9 = (bf16[512,512]{1,0:T(8,128)(2,1)S(1)}, bf16[512,512]{1,0:T(8,128)(2,1)S(1)}, u32[]{:S(2)}, u32[]{:S(2)}) collective-permute-start(bf16[512,512]{1,0:T(8,128)(2,1)S(1)} %collective-permute-done.7.refs_0_), channel_id=1, source_target_pairs={{0,16},{16,0},{1,17},{17,1},{2,18},{18,2},{3,19},{19,3},{4,20},{20... | collective-permute-start | bytes 1572872 | tf_op jit(solution)/shard_map/ppermute | solution.py:389
  34.2 3.1 %sibling_backward.1 = bf16[16,32,512]{2,1,0:T(8,128)(2,1)} custom-call(bf16[512,512]{1,0:T(8,128)(2,1)S(1)} %collective-permute-done.7.refs_0_, bf16[8,32,512]{2,1,0:T(8,128)(2,1)S(1)} %direct_backward.1.refs_1_, bf16[2048,512]{1,0:T(8,128)(2,1)S(1)} %get-tuple-element.33.refs_8_.refs_2_, bf16[2048,512]{1,0:T(8,128)(2,1)S(1)} %get-tuple-element.37.refs_9_.refs_3_), custom_call_target="tpu_custom_call" | custom-call | flops 99999997952 | bytes 4194304 | tf_op jit(solution)/shard_map/sibling_backward/pallas_call | solution.py:409
  37.3 5.7 %all-to-all-start = ((bf16[16,32,512]{2,1,0:T(8,128)(2,1)}), bf16[16,32,512]{2,1,0:T(8,128)(2,1)S(1)}, u32[]{:S(2)}, u32[]{:S(2)}) async-start(bf16[16,32,512]{2,1,0:T(8,128)(2,1)} %sibling_backward.1), calls=%async_computation | async-start | bytes 1048576 | tf_op jit(solution)/shard_map/all_to_all | solution.py:421
  43.0 1.8 %collective-permute-done.8.refs_2_ = bf16[512,512]{1,0:T(8,128)(2,1)} collective-permute-done((bf16[512,512]{1,0:T(8,128)(2,1)}, bf16[512,512]{1,0:T(8,128)(2,1)}, u32[]{:S(2)}, u32[]{:S(2)}) %collective-permute-start.8) | collective-permute-done | bytes 524320 | tf_op jit(solution)/shard_map/ppermute | solution.py:388
  44.8 0.0 copy-done
  44.8 0.0 copy-done.1
  44.8 6.4 %first_weights.1 = (f32[1,1024,512]{2,1,0:T(8,128)S(1)}, f32[1,1024,512]{2,1,0:T(8,128)S(1)}, bf16[512,160]{1,0:T(8,128)(2,1)S(1)}, f32[2,16,160]{2,1,0:T(8,128)...) custom-call(bf16[512,512]{1,0:T(8,128)(2,1)S(1)} %collective-permute-done.7.ref, ...), custom_call_target="tpu_custom_call" | custom-call | tf_op jit(solution)/shard_map/first_weights/pallas_call | solution.py:36
  51.2 4.3 %collective-permute-done.9.refs_0_ = bf16[512,512]{1,0:T(8,128)(2,1)S(1)} collective-permute-done((bf16[512,512]{1,0:T(8,128)(2,1)S(1)}, bf16[512,512]{1,0:T(8,128)(2,1)S(1)}, u32[]{:S(2)}, u32[]{:S(2)}) %collective-permute-start.9) | collective-permute-done | bytes 524320 | tf_op jit(solution)/shard_map/ppermute | solution.py:389
  55.5 2.4 %last_weights.1 = (bf16[1,1024,512]{2,1,0:T(8,128)(2,1)}, bf16[1,1024,512]{2,1,0:T(8,128)(2,1)}) custom-call(bf16[512,512]{1,0:T(8,128)(2,1)S(1)} %collective-permute-done.9.refs_0_, bf16[1024,512]{1,0:T(8,128)(2,1)S(1)} %get-tuple-element.40.refs_1_, bf16[1024,512]{1,0:T(8,128)(2,1)S(1)} %get-tuple-element.41.refs_2_, ...), custom_call_target="tpu_custom_call" | custom-call | flops 99999997952 | bytes 8912896 | tf_op jit(solution)/shard_map/last_weights/pallas_call | solution.py:36
  58.0 0.0 all-to-all-done.back_ref
  58.0 0.9 %combine.1 = (bf16[160,512]{1,0:T(8,128)(2,1)}, bf16[2,160]{1,0:T(2,128)(2,1)}) custom-call(bf16[512,160]{1,0:T(8,128)(2,1)S(1)} %get-tuple-element.34.pick_ref, f32[2,16,160]{2,1,0:T(8,128)S(1)} %get-tuple-element.35.hot_ref, bf16[2,128,160]{2,1,0:T(8,128)(2,1)S(1)} %get-tuple-element.36.spot_ref, bf16[16,32,512]{2,1,0:T(8,128)(2,1)S(1)} %all-to-all-done.back_ref), custom_call_target="tpu_custom_call" | custom-call | flops 167772160 | bytes 955008 | tf_op jit(solution)/shard_map/combine/pallas_call | solution.py:36
  (1 shorter events, 0.0 us)
Async XLA Ops:
  2.2 14.8 %collective-permute-start = (bf16[128,512]{1,0:T(8,128)(2,1)S(1)}, bf16[128,512]{1,0:T(8,128)(2,1)S(1)}, u32[]{:S(2)}, u32[]{:S(2)}) collective-permute-start(bf16[128,512]{1,0:T(8,128)(2,1)S(1)} %get-tuple-element.26), channel_id=1, source_target_pairs={{0,8},{1,9},{2,10},{3,11},{4,12},{5,13},{6,14},{7,15},{8,0},{9,1},... | collective-permute-start | bytes 393224 | tf_op jit(solution)/shard_map/ppermute | solution.py:354
  6.3 16.6 %collective-permute-start.1 = (bf16[128,512]{1,0:T(8,128)(2,1)S(1)}, bf16[128,512]{1,0:T(8,128)(2,1)S(1)}, u32[]{:S(2)}, u32[]{:S(2)}) collective-permute-start(bf16[128,512]{1,0:T(8,128)(2,1)S(1)} %get-tuple-element.27), channel_id=1, source_target_pairs={{0,2},{1,3},{2,0},{3,1},{4,6},{5,7},{6,4},{7,5},{8,10},{9,11},{10,... | collective-permute-start | bytes 393224 | tf_op jit(solution)/shard_map/ppermute | solution.py:354
  7.8 17.3 %collective-permute-start.2 = (bf16[128,512]{1,0:T(8,128)(2,1)S(1)}, bf16[128,512]{1,0:T(8,128)(2,1)S(1)}, u32[]{:S(2)}, u32[]{:S(2)}) collective-permute-start(bf16[128,512]{1,0:T(8,128)(2,1)S(1)} %get-tuple-element.28), channel_id=1, source_target_pairs={{0,10},{1,11},{2,8},{3,9},{4,14},{5,15},{6,12},{7,13},{8,2},{9,3},... | collective-permute-start | bytes 393224 | tf_op jit(solution)/shard_map/ppermute | solution.py:354
  7.9 17.3 %collective-permute-start.3 = (bf16[128,512]{1,0:T(8,128)(2,1)S(1)}, bf16[128,512]{1,0:T(8,128)(2,1)S(1)}, u32[]{:S(2)}, u32[]{:S(2)}) collective-permute-start(bf16[128,512]{1,0:T(8,128)(2,1)S(1)} %get-tuple-element.29), channel_id=1, source_target_pairs={{0,4},{1,5},{2,6},{3,7},{4,0},{5,1},{6,2},{7,3},{8,12},{9,13},{10,... | collective-permute-start | bytes 393224 | tf_op jit(solution)/shard_map/ppermute | solution.py:354
  9.7 15.5 %collective-permute-start.4 = (bf16[128,512]{1,0:T(8,128)(2,1)S(1)}, bf16[128,512]{1,0:T(8,128)(2,1)S(1)}, u32[]{:S(2)}, u32[]{:S(2)}) collective-permute-start(bf16[128,512]{1,0:T(8,128)(2,1)S(1)} %get-tuple-element.30), channel_id=1, source_target_pairs={{0,12},{1,13},{2,14},{3,15},{4,8},{5,9},{6,10},{7,11},{8,4},{9,5},... | collective-permute-start | bytes 393224 | tf_op jit(solution)/shard_map/ppermute | solution.py:354
  17.0 9.2 %collective-permute-start.5 = (bf16[128,512]{1,0:T(8,128)(2,1)S(1)}, bf16[128,512]{1,0:T(8,128)(2,1)S(1)}, u32[]{:S(2)}, u32[]{:S(2)}) collective-permute-start(bf16[128,512]{1,0:T(8,128)(2,1)S(1)} %get-tuple-element.31), channel_id=1, source_target_pairs={{0,14},{1,15},{2,12},{3,13},{4,10},{5,11},{6,8},{7,9},{8,6},{9,7},... | collective-permute-start | bytes 393224 | tf_op jit(solution)/shard_map/ppermute | solution.py:354
  22.9 5.9 %collective-permute-start.6 = (bf16[128,512]{1,0:T(8,128)(2,1)S(1)}, bf16[128,512]{1,0:T(8,128)(2,1)S(1)}, u32[]{:S(2)}, u32[]{:S(2)}) collective-permute-start(bf16[128,512]{1,0:T(8,128)(2,1)S(1)} %get-tuple-element.32), channel_id=1, source_target_pairs={{0,6},{1,7},{2,4},{3,5},{4,2},{5,3},{6,0},{7,1},{8,14},{9,15},{10,... | collective-permute-start | bytes 393224 | tf_op jit(solution)/shard_map/ppermute | solution.py:354
  28.8 4.7 %collective-permute-start.7 = (bf16[512,512]{1,0:T(8,128)(2,1)S(1)}, bf16[512,512]{1,0:T(8,128)(2,1)S(1)}, u32[]{:S(2)}, u32[]{:S(2)}) collective-permute-start(bf16[512,512]{1,0:T(8,128)(2,1)S(1)} %hand_on.1.refs_8_), channel_id=1, source_target_pairs={{0,1},{1,0},{2,3},{3,2},{4,5},{5,4},{6,7},{7,6},{8,9},{9,8},{10,11... | collective-permute-start | bytes 1572872 | tf_op jit(solution)/shard_map/ppermute | solution.py:386
  29.8 15.0 %collective-permute-start.8 = (bf16[512,512]{1,0:T(8,128)(2,1)}, bf16[512,512]{1,0:T(8,128)(2,1)}, u32[]{:S(2)}, u32[]{:S(2)}) collective-permute-start(bf16[512,512]{1,0:T(8,128)(2,1)} %arrived_rows.1.refs_1_.refs_10_), channel_id=1, source_target_pairs={{0,16},{16,0},{1,17},{17,1},{2,18},{18,2},{3,19},{19,3},{4,20},{20... | collective-permute-start | bytes 1572872 | tf_op jit(solution)/shard_map/ppermute | solution.py:388
  33.5 11.3 %copy-start = (s32[160,2]{0,1:T(2,128)S(1)}, s32[160,2]{0,1:T(2,128)}, u32[]{:S(2)}) copy-start(s32[160,2]{0,1:T(2,128)} %param.8) | copy-start | bytes 3844
  33.5 11.2 %copy-start.1 = (bf16[160,2]{0,1:T(2,128)(2,1)S(1)}, bf16[160,2]{0,1:T(2,128)(2,1)}, u32[]{:S(2)}) copy-start(bf16[160,2]{0,1:T(2,128)(2,1)} %param.7) | copy-start | bytes 1924
  33.6 22.0 %collective-permute-start.9 = (bf16[512,512]{1,0:T(8,128)(2,1)S(1)}, bf16[512,512]{1,0:T(8,128)(2,1)S(1)}, u32[]{:S(2)}, u32[]{:S(2)}) collective-permute-start(bf16[512,512]{1,0:T(8,128)(2,1)S(1)} %collective-permute-done.7.refs_0_), channel_id=1, source_target_pairs={{0,16},{16,0},{1,17},{17,1},{2,18},{18,2},{3,19},{19,3},{4,20},{20... | collective-permute-start | bytes 1572872 | tf_op jit(solution)/shard_map/ppermute | solution.py:389
  37.3 20.7 %all-to-all-start = ((bf16[16,32,512]{2,1,0:T(8,128)(2,1)}), bf16[16,32,512]{2,1,0:T(8,128)(2,1)S(1)}, u32[]{:S(2)}, u32[]{:S(2)}) async-start(bf16[16,32,512]{2,1,0:T(8,128)(2,1)} %sibling_backward.1), calls=%async_computation | async-start | bytes 1048576 | tf_op jit(solution)/shard_map/all_to_all | solution.py:421

commit v14 on v13

--- a/solution.py
+++ b/solution.py
@@ -98,7 +98,7 @@
     return [index == pieces[k : k + 1, :] * pad + slot[k] for k in range(2)]
 
 
-def slots_kernel(pad, routes_hbm, gates_hbm, tok_hbm, cot_hbm, *refs):
+def slots_kernel(pad, tight, routes_hbm, gates_hbm, tok_hbm, cot_hbm, *refs):
     chips = len(refs) - 5
     out_refs, refs = refs[:chips], refs[chips:]
     routes_ref, gates_ref, tok_ref, cot_ref, sems = refs
@@ -129,9 +129,9 @@
     grads = dot(scaled, cot_ref[...], 1, 0).astype(BF16)
     for k, out_ref in enumerate(out_refs):
         for i in range(2):
-            here = slice((2 * k + i) * pad, (2 * k + i + 1) * pad)
-            out_ref[2 * i * pad : (2 * i + 1) * pad, :] = rows[here, :]
-            out_ref[(2 * i + 1) * pad : (2 * i + 2) * pad, :] = grads[here, :]
+            here = slice((2 * k + i) * pad, (2 * k + i) * pad + tight)
+            out_ref[2 * i * tight : (2 * i + 1) * tight, :] = rows[here, :]
+            out_ref[(2 * i + 1) * tight : (2 * i + 2) * tight, :] = grads[here, :]
 
 
 def steps_of(size, block):
@@ -179,16 +179,17 @@
             out_ref[i * size : (i + 1) * size, :] = refs[number][at : at + size, :]
 
 
-def gather_rows(pad, blocks, rows_ref, grads_ref):
-    for i, (ref, at) in enumerate(blocks):
-        here = slice(i * pad, (i + 1) * pad)
-        rows_ref[here, :] = ref[at : at + pad, :]
-        grads_ref[here, :] = ref[at + pad : at + 2 * pad, :]
-
-
-def backward(cap, pad, block, blocks, up_ref, down_ref, scratch, put):
+def spread_rows(pad, tight, blocks, rows_ref, grads_ref):
+    feat = rows_ref.shape[1]
+    for i, (ref, row_at, grad_at) in enumerate(blocks):
+        for to_ref, at in [(rows_ref, row_at), (grads_ref, grad_at)]:
+            to_ref[i * pad : i * pad + tight, :] = ref[at : at + tight, :]
+            to_ref[i * pad + tight : (i + 1) * pad, :] = jnp.zeros((pad - tight, feat), BF16)
+
+
+def backward(cap, pad, tight, block, blocks, up_ref, down_ref, scratch, put):
     rows_ref, grads_ref, grad_acc, gate_acc = scratch
-    gather_rows(pad, blocks, rows_ref, grads_ref)
+    spread_rows(pad, tight, blocks, rows_ref, grads_ref)
     slots = rows_ref.shape[0]
     for step in range(up_ref.shape[0] // block):
         part = pl.ds(step * block, block)
@@ -217,22 +218,18 @@
         put(k, first.astype(BF16), grad_acc[here, 128:].astype(BF16))
 
 
-def blocks_of(pad, refs):
-    return [(ref, at) for ref in refs for at in range(0, ref.shape[0], 2 * pad)]
-
-
-def direct_back_kernel(cap, pad, block, chips, *refs):
+def direct_back_kernel(cap, pad, tight, block, chips, *refs):
     pieces, (up_ref, down_ref, _, out_ref, *scratch) = refs[:chips], refs[chips:]
 
     def put(k, first, rest):
         out_ref[k, :, 0:128] = first
         out_ref[k, :, 128:] = rest
 
-    blocks = [(ref, 0) for ref in pieces]
-    backward(cap, pad, block, blocks, up_ref, down_ref, scratch, put)
-
-
-def sibling_back_kernel(cap, pad, block, order, *refs):
+    blocks = [(ref, 0, tight) for ref in pieces]
+    backward(cap, pad, tight, block, blocks, up_ref, down_ref, scratch, put)
+
+
+def sibling_back_kernel(cap, pad, tight, block, order, *refs):
     sibling_ref, direct_ref, up_ref, down_ref, out_hbm, mine_ref, sems, *scratch = refs
     copies = []
 
@@ -250,13 +247,14 @@
         mine_ref[k, :, 128:] = rest
         send(k, 1)
 
-    blocks = blocks_of(pad, [sibling_ref])
-    backward(cap, pad, block, blocks, up_ref, down_ref, scratch, put)
+    chips = len(order)
+    blocks = [(sibling_ref, k * tight, (chips + k) * tight) for k in range(chips)]
+    backward(cap, pad, tight, block, blocks, up_ref, down_ref, scratch, put)
     for copy in copies:
         copy.wait()
 
 
-def weights_kernel(pad, block, share, number, places, begun, ended, *refs):
+def weights_kernel(pad, block, share, number, begun, ended, *refs):
     refs = list(refs)
     take = lambda number: [refs.pop(0) for _ in range(number)]
     row_refs, weights = take(number), take(2)
@@ -269,7 +267,10 @@
     steps = steps_of(share, block)
     if not begun:
         fetch = Fetch(*weights, up_ref, down_ref, sems, lax.axis_index("rep") * share, steps)
-    gather_rows(pad, [(row_refs[i], at) for i, at in places], rows_ref, grads_ref)
+    for i, ref in enumerate(row_refs):
+        size = ref.shape[0] // 2
+        rows_ref[i * size : (i + 1) * size, :] = ref[:size, :]
+        grads_ref[i * size : (i + 1) * size, :] = ref[size:, :]
     copies = []
     for step, (at, size) in enumerate(steps):
         here = pl.ds(at, size)
@@ -326,6 +327,7 @@
     chips = groups // 2
     cap = max(2, 3 * rows // groups)
     pad = (cap // 16 + 1) * 16
+    tight = cap + cap % 2
     slots = chips * pad
     share = hidden // mirrors
     routes_t, gates_t = routes.T, gates.T
@@ -337,9 +339,9 @@
     order = [k for pair in itertools.zip_longest(far[:-1], near[:-1]) for k in pair if k is not None]
     order += far[-1:] + near[-1:]
     out = call(
-        functools.partial(slots_kernel, pad),
+        functools.partial(slots_kernel, pad, tight),
         "slots",
-        [shape((4 * pad, feat), BF16)] * chips,
+        [shape((4 * tight, feat), BF16)] * chips,
         [hbm(a) for a in (routes_t, gates_t, tokens, cotangent)],
         [IN_HBM] * 4,
         [
@@ -367,13 +369,11 @@
         0,
         SMALL,
     )
-    whole = 2 * pad
-
     def join(name, arrays, *lists):
         return call(
-            functools.partial(join_kernel, whole, lists),
+            functools.partial(join_kernel, tight, lists),
             name,
-            [shape((len(blocks) * whole, feat), BF16) for blocks in lists],
+            [shape((len(blocks) * tight, feat), BF16) for blocks in lists],
             arrays,
             [IN_VMEM] * len(arrays),
             [],
@@ -382,9 +382,9 @@
             SMALL,
         )
 
-    (handed,) = join("hand_on", [*pieces, up_v], [(i, whole) for i in range(chips)])
+    (handed,) = join("hand_on", [*pieces, up_v], [(i, at) for at in (2 * tight, 3 * tight) for i in range(chips)])
     sibling = lax.ppermute(handed, "exp", swap)
-    (arrived,) = join("arrived_rows", [*pieces, handed], [(i, 0) for i in range(chips)])
+    (arrived,) = join("arrived_rows", [*pieces, handed], [(i, at) for at in (0, tight) for i in range(chips)])
     firsts = [lax.ppermute(arrived, "rep", hops) for hops in around]
     seconds = [lax.ppermute(sibling, "rep", hops) for hops in around]
 
@@ -397,7 +397,7 @@
     ]
     results = (chips, pad, feat)
     (direct,) = call(
-        functools.partial(direct_back_kernel, cap, pad, block, chips),
+        functools.partial(direct_back_kernel, cap, pad, tight, block, chips),
         "direct_backward",
         [shape(results, BF16)],
         [*pieces, up_v, down_v, arrived],
@@ -407,7 +407,7 @@
         slots * hidden,
     )
     back = pl.pallas_call(
-        functools.partial(sibling_back_kernel, cap, pad, block, [0, *order]),
+        functools.partial(sibling_back_kernel, cap, pad, tight, block, [0, *order]),
         name="sibling_backward",
         out_shape=pltpu.HBM((groups, pad, feat), BF16),
         in_specs=[IN_VMEM] * 4,
@@ -422,9 +422,9 @@
 
     part = min(512, share)
 
-    def weights_call(name, arrays, places, weights, sums, ended, flops):
+    def weights_call(name, arrays, weights, sums, ended, flops):
         begun = bool(sums)
-        number = len(places) * pad
+        number = len(arrays) * chips * tight
         notes = [] if begun else [
             shape((groups * pad, rows), BF16),
             shape((2, groups, rows), F32),
@@ -442,9 +442,7 @@
         if ended:
             scratch += [pltpu.VMEM((share, feat), BF16)] * 2 + [DMA((2 * steps,))]
         return call(
-            functools.partial(
-                weights_kernel, pad, part, share, len(arrays), places, begun, ended
-            ),
+            functools.partial(weights_kernel, pad, part, share, len(arrays), begun, ended),
             name,
             [grad] * 2 + notes,
             [*arrays, *weights, *(sums or [routes_t, gates_t])],
@@ -456,18 +454,13 @@
             [IN_HBM if ended else IN_VMEM] * 2 + [IN_VMEM] * len(notes),
         )
 
-    def places_of(arrays, first=0):
-        return [
-            (first + i, at) for i, a in enumerate(arrays) for at in range(0, a.shape[0], whole)
-        ]
-
     joined = [sibling, arrived, *firsts]
     *sums, pick, hot, spot, up_v, down_v = weights_call(
-        "first_weights", joined, places_of(joined), [w_up, w_down], [], not seconds, 0
+        "first_weights", joined, [w_up, w_down], [], not seconds, 0
     )
     if seconds:
         sums = weights_call(
-            "last_weights", seconds, places_of(seconds), [up_v, down_v], sums, True, AHEAD
+            "last_weights", seconds, [up_v, down_v], sums, True, AHEAD
         )
     grad_up, grad_down = sums
 

time: 59.5 us -> 57.5 us (0.966)
  waiting for transfers between devices: 14.6 us -> 13.3 us
  starting transfers between devices: 23.8 us -> 23.1 us
    ppermute x7, waiting for transfers between devices: 8.43 us -> 7.64 us  [local(): lax.ppermute(out[k], 'exp', hops_to(chips, k))]
    ppermute x1, waiting for transfers between devices: 4.33 us -> 3.65 us  [local(): seconds = [lax.ppermute(sibling, 'rep', hops) for hops in around]]
    all_to_all x1, starting transfers between devices: 5.72 us -> 5.12 us  [local(): back = lax.all_to_all(back, 'exp', split_axis=0, concat_axis=0, tiled=True)]
  transfers between devices with their start and end apart: 11 -> 11, of which waited for: 5 -> 6; matrix products, arithmetic and copies ran while one was open for 0% -> 0% of each run, Pallas kernels for 29% -> 30%
where the time goes in v14:
time: 57.5 us; the launch traced here: 57.2 us
  starting transfers between devices  23.1 us (40%)
  Pallas kernels  20 us (35%)
  waiting for transfers between devices  13.3 us (23%)
  between operations  0.75 us (1%)
    pallas_call x8, Pallas kernels, call(): pl.pallas_call(body, name=name, out_shape=outs, in_specs=in_specs, out_sp...  16.9 us
    ppermute x7, starting transfers between devices, local(): lax.ppermute(out[k], 'exp', hops_to(chips, k))  15.9 us
    ppermute x7, waiting for transfers between devices, local(): lax.ppermute(out[k], 'exp', hops_to(chips, k))  7.64 us
    all_to_all x1, starting transfers between devices, local(): back = lax.all_to_all(back, 'exp', split_axis=0, concat_axis=0, tiled=True)  5.12 us
    ppermute x1, waiting for transfers between devices, local(): seconds = [lax.ppermute(sibling, 'rep', hops) for hops in around]  3.65 us
    pallas_call x1, Pallas kernels, local(): pl.pallas_call(functools.partial(sibling_back_kernel, cap, pad, tight, bl...  3.17 us
    ppermute x1, waiting for transfers between devices, local(): firsts = [lax.ppermute(arrived, 'rep', hops) for hops in around]  1.55 us
    ppermute x1, starting transfers between devices, local(): firsts = [lax.ppermute(arrived, 'rep', hops) for hops in around]  1.49 us
  transfers between devices with their start and end apart: 11, of which 6 were waited for; matrix products, arithmetic and copies ran while one was open for 0% of the time, Pallas kernels for 30%

profile of v14, /device:TPU:0, one launch (start us, length us, event | category | flops | bytes accessed | tf_op | source)
XLA Modules:
  0.0 57.2 jit_solution(11489274850524809912)
XLA Ops:
  0.6 1.6 %slots.1 = (bf16[120,512]{1,0:T(8,128)(2,1)S(1)}, bf16[120,512]{1,0:T(8,128)(2,1)S(1)}, bf16[120,512]{1,0:T(8,128)(2,1)S(1)}, bf16[120,512]{1,0:T(8,128)(2,1)S(1...) custom-call(s32[2,160]{1,0:T(2,128)} %bitcast.3, ...), custom_call_target="tpu_custom_call" | custom-call | flops 167772160 | bytes 1312640 | tf_op jit(solution)/shard_map/slots/pallas_call | solution.py:36
  2.2 4.1 %collective-permute-start = (bf16[120,512]{1,0:T(8,128)(2,1)S(1)}, bf16[120,512]{1,0:T(8,128)(2,1)S(1)}, u32[]{:S(2)}, u32[]{:S(2)}) collective-permute-start(bf16[120,512]{1,0:T(8,128)(2,1)S(1)} %get-tuple-element.26), channel_id=1, source_target_pairs={{0,8},{1,9},{2,10},{3,11},{4,12},{5,13},{6,14},{7,15},{8,0},{9,1},... | collective-permute-start | bytes 368648 | tf_op jit(solution)/shard_map/ppermute | solution.py:356
  6.3 1.5 %collective-permute-start.1 = (bf16[120,512]{1,0:T(8,128)(2,1)S(1)}, bf16[120,512]{1,0:T(8,128)(2,1)S(1)}, u32[]{:S(2)}, u32[]{:S(2)}) collective-permute-start(bf16[120,512]{1,0:T(8,128)(2,1)S(1)} %get-tuple-element.27), channel_id=1, source_target_pairs={{0,2},{1,3},{2,0},{3,1},{4,6},{5,7},{6,4},{7,5},{8,10},{9,11},{10,... | collective-permute-start | bytes 368648 | tf_op jit(solution)/shard_map/ppermute | solution.py:356
  7.9 0.0 collective-permute-start.2
  7.9 1.8 %collective-permute-start.3 = (bf16[120,512]{1,0:T(8,128)(2,1)S(1)}, bf16[120,512]{1,0:T(8,128)(2,1)S(1)}, u32[]{:S(2)}, u32[]{:S(2)}) collective-permute-start(bf16[120,512]{1,0:T(8,128)(2,1)S(1)} %get-tuple-element.29), channel_id=1, source_target_pairs={{0,4},{1,5},{2,6},{3,7},{4,0},{5,1},{6,2},{7,3},{8,12},{9,13},{10,... | collective-permute-start | bytes 368648 | tf_op jit(solution)/shard_map/ppermute | solution.py:356
  9.7 2.5 %collective-permute-start.4 = (bf16[120,512]{1,0:T(8,128)(2,1)S(1)}, bf16[120,512]{1,0:T(8,128)(2,1)S(1)}, u32[]{:S(2)}, u32[]{:S(2)}) collective-permute-start(bf16[120,512]{1,0:T(8,128)(2,1)S(1)} %get-tuple-element.30), channel_id=1, source_target_pairs={{0,12},{1,13},{2,14},{3,15},{4,8},{5,9},{6,10},{7,11},{8,4},{9,5},... | collective-permute-start | bytes 368648 | tf_op jit(solution)/shard_map/ppermute | solution.py:356
  12.2 4.1 %collective-permute-done.refs_1_ = bf16[120,512]{1,0:T(8,128)(2,1)S(1)} collective-permute-done((bf16[120,512]{1,0:T(8,128)(2,1)S(1)}, bf16[120,512]{1,0:T(8,128)(2,1)S(1)}, u32[]{:S(2)}, u32[]{:S(2)}) %collective-permute-start) | collective-permute-done | bytes 122912 | tf_op jit(solution)/shard_map/ppermute | solution.py:356
  16.3 5.9 %collective-permute-start.5 = (bf16[120,512]{1,0:T(8,128)(2,1)S(1)}, bf16[120,512]{1,0:T(8,128)(2,1)S(1)}, u32[]{:S(2)}, u32[]{:S(2)}) collective-permute-start(bf16[120,512]{1,0:T(8,128)(2,1)S(1)} %get-tuple-element.31), channel_id=1, source_target_pairs={{0,14},{1,15},{2,12},{3,13},{4,10},{5,11},{6,8},{7,9},{8,6},{9,7},... | collective-permute-start | bytes 368648 | tf_op jit(solution)/shard_map/ppermute | solution.py:356
  22.2 0.0 collective-permute-done.1.refs_2_
  22.2 0.0 collective-permute-start.6
  22.2 2.2 %fetch_weights.1 = (bf16[2048,512]{1,0:T(8,128)(2,1)S(1)}, bf16[2048,512]{1,0:T(8,128)(2,1)S(1)}) custom-call(bf16[1,2048,512]{2,1,0:T(8,128)(2,1)} %refs_3_.1, bf16[1,2048,512]{2,1,0:T(8,128)(2,1)} %refs_4_.1), custom_call_target="tpu_custom_call" | custom-call | tf_op jit(solution)/shard_map/fetch_weights/pallas_call | solution.py:36
  24.5 0.0 collective-permute-done.2.refs_3_
  24.5 0.0 collective-permute-done.3.refs_4_
  24.5 0.0 collective-permute-done.4.refs_5_
  24.5 0.9 %collective-permute-done.5.refs_6_ = bf16[120,512]{1,0:T(8,128)(2,1)S(1)} collective-permute-done((bf16[120,512]{1,0:T(8,128)(2,1)S(1)}, bf16[120,512]{1,0:T(8,128)(2,1)S(1)}, u32[]{:S(2)}, u32[]{:S(2)}) %collective-permute-start.5) | collective-permute-done | bytes 122912 | tf_op jit(solution)/shard_map/ppermute | solution.py:356
  25.5 2.6 %collective-permute-done.6.refs_7_ = bf16[120,512]{1,0:T(8,128)(2,1)S(1)} collective-permute-done((bf16[120,512]{1,0:T(8,128)(2,1)S(1)}, bf16[120,512]{1,0:T(8,128)(2,1)S(1)}, u32[]{:S(2)}, u32[]{:S(2)}) %collective-permute-start.6) | collective-permute-done | bytes 122912 | tf_op jit(solution)/shard_map/ppermute | solution.py:356
  28.0 0.1 hand_on.1.refs_8_
  28.1 0.1 collective-permute-start.7
  28.2 0.8 %arrived_rows.1.refs_1_.refs_10_ = bf16[480,512]{1,0:T(8,128)(2,1)} custom-call(bf16[120,512]{1,0:T(8,128)(2,1)S(1)} %get-tuple-element.25.refs_0_, bf16[120,512]{1,0:T(8,128)(2,1)S(1)} %collective-permute-done.refs_1_, bf16[120,512]{1,0:T(8,128)(2,1)S(1)} %collective-permute-done.1.refs_2_, bf16[120,512]{1,0:T(8,128)(2,1)S(1)} %collective-permute-done.2.refs_3_, ...), custom_call_target="tpu_custom_call" | custom-call | tf_op jit(solution)/shard_map/arrived_rows/pallas_call | solution.py:36
  29.0 1.5 %collective-permute-start.8 = (bf16[480,512]{1,0:T(8,128)(2,1)}, bf16[480,512]{1,0:T(8,128)(2,1)}, u32[]{:S(2)}, u32[]{:S(2)}) collective-permute-start(bf16[480,512]{1,0:T(8,128)(2,1)} %arrived_rows.1.refs_1_.refs_10_), channel_id=1, source_target_pairs={{0,16},{16,0},{1,17},{17,1},{2,18},{18,2},{3,19},{19,3},{4,20},{20... | collective-permute-start | bytes 1474568 | tf_op jit(solution)/shard_map/ppermute | solution.py:388
  30.5 2.4 %direct_backward.1.refs_1_ = bf16[8,32,512]{2,1,0:T(8,128)(2,1)S(1)} custom-call(bf16[120,512]{1,0:T(8,128)(2,1)S(1)} %get-tuple-element.25.refs_0_, bf16[120,512]{1,0:T(8,128)(2,1)S(1)} %collective-permute-done.refs_1_, bf16[120,512]{1,0:T(8,128)(2,1)S(1)} %collective-permute-done.1.refs_2_, bf16[120,512]{1,0:T(8,128)(2,1)S(1)} %collective-permute-done.2.refs_3_, ...), custom_call_target="tpu_custom_call" | custom-call | flops 99999997952 | bytes 5931008 | tf_op jit(solution)/shard_map/direct_backward/pallas_call | solution.py:36
  32.9 0.0 copy-start
  32.9 0.0 copy-start.1
  32.9 0.0 collective-permute-done.7.refs_0_
  32.9 0.6 %collective-permute-start.9 = (bf16[480,512]{1,0:T(8,128)(2,1)S(1)}, bf16[480,512]{1,0:T(8,128)(2,1)S(1)}, u32[]{:S(2)}, u32[]{:S(2)}) collective-permute-start(bf16[480,512]{1,0:T(8,128)(2,1)S(1)} %collective-permute-done.7.refs_0_), channel_id=1, source_target_pairs={{0,16},{16,0},{1,17},{17,1},{2,18},{18,2},{3,19},{19,3},{4,20},{20... | collective-permute-start | bytes 1474568 | tf_op jit(solution)/shard_map/ppermute | solution.py:389
  33.5 3.2 %sibling_backward.1 = bf16[16,32,512]{2,1,0:T(8,128)(2,1)} custom-call(bf16[480,512]{1,0:T(8,128)(2,1)S(1)} %collective-permute-done.7.refs_0_, bf16[8,32,512]{2,1,0:T(8,128)(2,1)S(1)} %direct_backward.1.refs_1_, bf16[2048,512]{1,0:T(8,128)(2,1)S(1)} %get-tuple-element.33.refs_8_.refs_2_, bf16[2048,512]{1,0:T(8,128)(2,1)S(1)} %get-tuple-element.37.refs_9_.refs_3_), custom_call_target="tpu_custom_call" | custom-call | flops 99999997952 | bytes 4194304 | tf_op jit(solution)/shard_map/sibling_backward/pallas_call | solution.py:409
  36.7 5.1 %all-to-all-start = ((bf16[16,32,512]{2,1,0:T(8,128)(2,1)}), bf16[16,32,512]{2,1,0:T(8,128)(2,1)S(1)}, u32[]{:S(2)}, u32[]{:S(2)}) async-start(bf16[16,32,512]{2,1,0:T(8,128)(2,1)} %sibling_backward.1), calls=%async_computation | async-start | bytes 1048576 | tf_op jit(solution)/shard_map/all_to_all | solution.py:421
  41.8 1.5 %collective-permute-done.8.refs_2_ = bf16[480,512]{1,0:T(8,128)(2,1)} collective-permute-done((bf16[480,512]{1,0:T(8,128)(2,1)}, bf16[480,512]{1,0:T(8,128)(2,1)}, u32[]{:S(2)}, u32[]{:S(2)}) %collective-permute-start.8) | collective-permute-done | bytes 491552 | tf_op jit(solution)/shard_map/ppermute | solution.py:388
  43.3 0.0 copy-done
  43.3 0.0 copy-done.1
  43.3 6.4 %first_weights.1 = (f32[1,1024,512]{2,1,0:T(8,128)S(1)}, f32[1,1024,512]{2,1,0:T(8,128)S(1)}, bf16[512,160]{1,0:T(8,128)(2,1)S(1)}, f32[2,16,160]{2,1,0:T(8,128)...) custom-call(bf16[480,512]{1,0:T(8,128)(2,1)S(1)} %collective-permute-done.7.ref, ...), custom_call_target="tpu_custom_call" | custom-call | tf_op jit(solution)/shard_map/first_weights/pallas_call | solution.py:36
  49.7 3.6 %collective-permute-done.9.refs_0_ = bf16[480,512]{1,0:T(8,128)(2,1)S(1)} collective-permute-done((bf16[480,512]{1,0:T(8,128)(2,1)S(1)}, bf16[480,512]{1,0:T(8,128)(2,1)S(1)}, u32[]{:S(2)}, u32[]{:S(2)}) %collective-permute-start.9) | collective-permute-done | bytes 491552 | tf_op jit(solution)/shard_map/ppermute | solution.py:389
  53.4 2.4 %last_weights.1 = (bf16[1,1024,512]{2,1,0:T(8,128)(2,1)}, bf16[1,1024,512]{2,1,0:T(8,128)(2,1)}) custom-call(bf16[480,512]{1,0:T(8,128)(2,1)S(1)} %collective-permute-done.9.refs_0_, bf16[1024,512]{1,0:T(8,128)(2,1)S(1)} %get-tuple-element.40.refs_1_, bf16[1024,512]{1,0:T(8,128)(2,1)S(1)} %get-tuple-element.41.refs_2_, ...), custom_call_target="tpu_custom_call" | custom-call | flops 99999997952 | bytes 8880128 | tf_op jit(solution)/shard_map/last_weights/pallas_call | solution.py:36
  55.8 0.4 all-to-all-done.back_ref
  56.3 0.9 %combine.1 = (bf16[160,512]{1,0:T(8,128)(2,1)}, bf16[2,160]{1,0:T(2,128)(2,1)}) custom-call(bf16[512,160]{1,0:T(8,128)(2,1)S(1)} %get-tuple-element.34.pick_ref, f32[2,16,160]{2,1,0:T(8,128)S(1)} %get-tuple-element.35.hot_ref, bf16[2,128,160]{2,1,0:T(8,128)(2,1)S(1)} %get-tuple-element.36.spot_ref, bf16[16,32,512]{2,1,0:T(8,128)(2,1)S(1)} %all-to-all-done.back_ref), custom_call_target="tpu_custom_call" | custom-call | flops 167772160 | bytes 955008 | tf_op jit(solution)/shard_map/combine/pallas_call | solution.py:36
Async XLA Ops:
  2.2 14.1 %collective-permute-start = (bf16[120,512]{1,0:T(8,128)(2,1)S(1)}, bf16[120,512]{1,0:T(8,128)(2,1)S(1)}, u32[]{:S(2)}, u32[]{:S(2)}) collective-permute-start(bf16[120,512]{1,0:T(8,128)(2,1)S(1)} %get-tuple-element.26), channel_id=1, source_target_pairs={{0,8},{1,9},{2,10},{3,11},{4,12},{5,13},{6,14},{7,15},{8,0},{9,1},... | collective-permute-start | bytes 368648 | tf_op jit(solution)/shard_map/ppermute | solution.py:356
  6.3 15.9 %collective-permute-start.1 = (bf16[120,512]{1,0:T(8,128)(2,1)S(1)}, bf16[120,512]{1,0:T(8,128)(2,1)S(1)}, u32[]{:S(2)}, u32[]{:S(2)}) collective-permute-start(bf16[120,512]{1,0:T(8,128)(2,1)S(1)} %get-tuple-element.27), channel_id=1, source_target_pairs={{0,2},{1,3},{2,0},{3,1},{4,6},{5,7},{6,4},{7,5},{8,10},{9,11},{10,... | collective-permute-start | bytes 368648 | tf_op jit(solution)/shard_map/ppermute | solution.py:356
  7.9 16.6 %collective-permute-start.2 = (bf16[120,512]{1,0:T(8,128)(2,1)S(1)}, bf16[120,512]{1,0:T(8,128)(2,1)S(1)}, u32[]{:S(2)}, u32[]{:S(2)}) collective-permute-start(bf16[120,512]{1,0:T(8,128)(2,1)S(1)} %get-tuple-element.28), channel_id=1, source_target_pairs={{0,10},{1,11},{2,8},{3,9},{4,14},{5,15},{6,12},{7,13},{8,2},{9,3},... | collective-permute-start | bytes 368648 | tf_op jit(solution)/shard_map/ppermute | solution.py:356
  7.9 16.6 %collective-permute-start.3 = (bf16[120,512]{1,0:T(8,128)(2,1)S(1)}, bf16[120,512]{1,0:T(8,128)(2,1)S(1)}, u32[]{:S(2)}, u32[]{:S(2)}) collective-permute-start(bf16[120,512]{1,0:T(8,128)(2,1)S(1)} %get-tuple-element.29), channel_id=1, source_target_pairs={{0,4},{1,5},{2,6},{3,7},{4,0},{5,1},{6,2},{7,3},{8,12},{9,13},{10,... | collective-permute-start | bytes 368648 | tf_op jit(solution)/shard_map/ppermute | solution.py:356
  9.7 14.8 %collective-permute-start.4 = (bf16[120,512]{1,0:T(8,128)(2,1)S(1)}, bf16[120,512]{1,0:T(8,128)(2,1)S(1)}, u32[]{:S(2)}, u32[]{:S(2)}) collective-permute-start(bf16[120,512]{1,0:T(8,128)(2,1)S(1)} %get-tuple-element.30), channel_id=1, source_target_pairs={{0,12},{1,13},{2,14},{3,15},{4,8},{5,9},{6,10},{7,11},{8,4},{9,5},... | collective-permute-start | bytes 368648 | tf_op jit(solution)/shard_map/ppermute | solution.py:356
  16.3 9.1 %collective-permute-start.5 = (bf16[120,512]{1,0:T(8,128)(2,1)S(1)}, bf16[120,512]{1,0:T(8,128)(2,1)S(1)}, u32[]{:S(2)}, u32[]{:S(2)}) collective-permute-start(bf16[120,512]{1,0:T(8,128)(2,1)S(1)} %get-tuple-element.31), channel_id=1, source_target_pairs={{0,14},{1,15},{2,12},{3,13},{4,10},{5,11},{6,8},{7,9},{8,6},{9,7},... | collective-permute-start | bytes 368648 | tf_op jit(solution)/shard_map/ppermute | solution.py:356
  22.2 5.8 %collective-permute-start.6 = (bf16[120,512]{1,0:T(8,128)(2,1)S(1)}, bf16[120,512]{1,0:T(8,128)(2,1)S(1)}, u32[]{:S(2)}, u32[]{:S(2)}) collective-permute-start(bf16[120,512]{1,0:T(8,128)(2,1)S(1)} %get-tuple-element.32), channel_id=1, source_target_pairs={{0,6},{1,7},{2,4},{3,5},{4,2},{5,3},{6,0},{7,1},{8,14},{9,15},{10,... | collective-permute-start | bytes 368648 | tf_op jit(solution)/shard_map/ppermute | solution.py:356
  28.1 4.8 %collective-permute-start.7 = (bf16[480,512]{1,0:T(8,128)(2,1)S(1)}, bf16[480,512]{1,0:T(8,128)(2,1)S(1)}, u32[]{:S(2)}, u32[]{:S(2)}) collective-permute-start(bf16[480,512]{1,0:T(8,128)(2,1)S(1)} %hand_on.1.refs_8_), channel_id=1, source_target_pairs={{0,1},{1,0},{2,3},{3,2},{4,5},{5,4},{6,7},{7,6},{8,9},{9,8},{10,11... | collective-permute-start | bytes 1474568 | tf_op jit(solution)/shard_map/ppermute | solution.py:386
  29.0 14.3 %collective-permute-start.8 = (bf16[480,512]{1,0:T(8,128)(2,1)}, bf16[480,512]{1,0:T(8,128)(2,1)}, u32[]{:S(2)}, u32[]{:S(2)}) collective-permute-start(bf16[480,512]{1,0:T(8,128)(2,1)} %arrived_rows.1.refs_1_.refs_10_), channel_id=1, source_target_pairs={{0,16},{16,0},{1,17},{17,1},{2,18},{18,2},{3,19},{19,3},{4,20},{20... | collective-permute-start | bytes 1474568 | tf_op jit(solution)/shard_map/ppermute | solution.py:388
  32.9 10.5 %copy-start = (s32[160,2]{0,1:T(2,128)S(1)}, s32[160,2]{0,1:T(2,128)}, u32[]{:S(2)}) copy-start(s32[160,2]{0,1:T(2,128)} %param.8) | copy-start | bytes 3844
  32.9 10.5 %copy-start.1 = (bf16[160,2]{0,1:T(2,128)(2,1)S(1)}, bf16[160,2]{0,1:T(2,128)(2,1)}, u32[]{:S(2)}) copy-start(bf16[160,2]{0,1:T(2,128)(2,1)} %param.7) | copy-start | bytes 1924
  32.9 20.5 %collective-permute-start.9 = (bf16[480,512]{1,0:T(8,128)(2,1)S(1)}, bf16[480,512]{1,0:T(8,128)(2,1)S(1)}, u32[]{:S(2)}, u32[]{:S(2)}) collective-permute-start(bf16[480,512]{1,0:T(8,128)(2,1)S(1)} %collective-permute-done.7.refs_0_), channel_id=1, source_target_pairs={{0,16},{16,0},{1,17},{17,1},{2,18},{18,2},{3,19},{19,3},{4,20},{20... | collective-permute-start | bytes 1474568 | tf_op jit(solution)/shard_map/ppermute | solution.py:389
  36.7 19.6 %all-to-all-start = ((bf16[16,32,512]{2,1,0:T(8,128)(2,1)}), bf16[16,32,512]{2,1,0:T(8,128)(2,1)S(1)}, u32[]{:S(2)}, u32[]{:S(2)}) async-start(bf16[16,32,512]{2,1,0:T(8,128)(2,1)} %sibling_backward.1), calls=%async_computation | async-start | bytes 1048576 | tf_op jit(solution)/shard_map/all_to_all | solution.py:421

commit v15 on v14

--- a/solution.py
+++ b/solution.py
@@ -218,8 +218,8 @@
         put(k, first.astype(BF16), grad_acc[here, 128:].astype(BF16))
 
 
-def direct_back_kernel(cap, pad, tight, block, chips, *refs):
-    pieces, (up_ref, down_ref, _, out_ref, *scratch) = refs[:chips], refs[chips:]
+def early_back_kernel(cap, pad, tight, block, number, *refs):
+    pieces, (up_ref, down_ref, out_ref, *scratch) = refs[:number], refs[number:]
 
     def put(k, first, rest):
         out_ref[k, :, 0:128] = first
@@ -229,26 +229,31 @@
     backward(cap, pad, tight, block, blocks, up_ref, down_ref, scratch, put)
 
 
-def sibling_back_kernel(cap, pad, tight, block, order, *refs):
-    sibling_ref, direct_ref, up_ref, down_ref, out_hbm, mine_ref, sems, *scratch = refs
+def late_back_kernel(cap, pad, tight, block, order, number, *refs):
+    pieces, refs = refs[:number], refs[number:]
+    sibling_ref, early_ref, up_ref, down_ref, _, out_hbm, late_ref, sems, *scratch = refs
+    chips = len(order)
+    begun = chips - number
     copies = []
 
-    def send(i, core):
-        ref = mine_ref if core else direct_ref
-        to = out_hbm.at[origin_of(order[i], core, len(order))]
-        copies.append(pltpu.make_async_copy(ref.at[i], to, sems.at[2 * i + core]))
+    def send(ref, k, core):
+        to = out_hbm.at[origin_of(order[k], core, chips)]
+        copies.append(pltpu.make_async_copy(ref, to, sems.at[2 * k + core]))
         copies[-1].start()
 
-    for i in range(len(order)):
-        send(i, 0)
-
-    def put(k, first, rest):
-        mine_ref[k, :, 0:128] = first
-        mine_ref[k, :, 128:] = rest
-        send(k, 1)
-
-    chips = len(order)
-    blocks = [(sibling_ref, k * tight, (chips + k) * tight) for k in range(chips)]
+    for k in range(begun):
+        send(early_ref.at[k], k, 0)
+
+    def put(i, first, rest):
+        late_ref[i, :, 0:128] = first
+        late_ref[i, :, 128:] = rest
+        if i < number:
+            send(late_ref.at[i], begun + i, 0)
+        else:
+            send(late_ref.at[i], i - number, 1)
+
+    blocks = [(ref, 0, tight) for ref in pieces]
+    blocks += [(sibling_ref, k * tight, (chips + k) * tight) for k in range(chips)]
     backward(cap, pad, tight, block, blocks, up_ref, down_ref, scratch, put)
     for copy in copies:
         copy.wait()
@@ -299,10 +304,17 @@
 def note_routes(pad, routes_ref, gates_ref, pick_ref, hot_ref, spot_ref):
     routes = routes_ref[...]
     gates = gates_ref[...].astype(F32)
-    groups = pick_ref.shape[0] // pad
+    rows, slots = pick_ref.shape
+    groups = slots // pad
     hot, slot = slots_of(routes, groups)
-    pick = picks_of(routes, slot, groups, pad)
-    pick_ref[...] = jnp.where(pick[0] | pick[1], 1.0, 0.0).astype(BF16)
+    same = lax.broadcasted_iota(jnp.int32, (rows, rows), 0) == lax.broadcasted_iota(
+        jnp.int32, (rows, rows), 1
+    )
+    along = jnp.concatenate([routes, *slot, jnp.zeros((4, rows), jnp.int32)], axis=0)
+    down = dot(jnp.where(same, 1.0, 0.0).astype(BF16), along.astype(F32).astype(BF16), 1, 1)
+    index = lax.broadcasted_iota(jnp.int32, (rows, slots), 1)
+    target = [(down[:, k : k + 1] * pad + down[:, 2 + k : 3 + k]).astype(jnp.int32) for k in (0, 1)]
+    pick_ref[...] = jnp.where((index == target[0]) | (index == target[1]), 1.0, 0.0).astype(BF16)
     lane = lax.broadcasted_iota(jnp.int32, (128, routes.shape[1]), 0)
     for k in range(2):
         hot_ref[k] = jnp.where(hot[k], 1.0 / gates[k : k + 1, :], 0.0)
@@ -312,7 +324,7 @@
 def combine_kernel(cap, pick_ref, hot_ref, spot_ref, back_ref, d_tok_ref, d_gate_ref):
     groups, pad, feat = back_ref.shape
     back = back_ref[...]
-    d_tok_ref[...] = dot(pick_ref[...], back.reshape(groups * pad, feat), 0, 0).astype(BF16)
+    d_tok_ref[...] = dot(pick_ref[...], back.reshape(groups * pad, feat), 1, 0).astype(BF16)
     values = back[:, cap, 0:128]
     for k in range(2):
         found = dot(values, spot_ref[k], 1, 0) * hot_ref[k]
@@ -369,6 +381,28 @@
         0,
         SMALL,
     )
+    block = min(512, hidden)
+    late = min(3, chips // 2)
+
+    def scratch(number):
+        return [
+            pltpu.VMEM((number * pad, feat), BF16),
+            pltpu.VMEM((number * pad, feat), BF16),
+            pltpu.VMEM((number * pad, feat), F32),
+            pltpu.VMEM((number * pad, 128), F32),
+        ]
+
+    (early,) = call(
+        functools.partial(early_back_kernel, cap, pad, tight, block, chips - late),
+        "early_backward",
+        [shape((chips - late, pad, feat), BF16)],
+        [*pieces[:-late], up_v, down_v],
+        [IN_VMEM] * (chips - late + 2),
+        scratch(chips - late),
+        3 * unit * hidden,
+        slots * hidden,
+    )
+
     def join(name, arrays, *lists):
         return call(
             functools.partial(join_kernel, tight, lists),
@@ -382,42 +416,28 @@
             SMALL,
         )
 
-    (handed,) = join("hand_on", [*pieces, up_v], [(i, at) for at in (2 * tight, 3 * tight) for i in range(chips)])
+    (handed,) = join("hand_on", [*pieces, early], [(i, at) for at in (2 * tight, 3 * tight) for i in range(chips)])
     sibling = lax.ppermute(handed, "exp", swap)
     (arrived,) = join("arrived_rows", [*pieces, handed], [(i, at) for at in (0, tight) for i in range(chips)])
     firsts = [lax.ppermute(arrived, "rep", hops) for hops in around]
     seconds = [lax.ppermute(sibling, "rep", hops) for hops in around]
 
-    block = min(512, hidden)
-    scratch = [
-        pltpu.VMEM((slots, feat), BF16),
-        pltpu.VMEM((slots, feat), BF16),
-        pltpu.VMEM((slots, feat), F32),
-        pltpu.VMEM((slots, 128), F32),
-    ]
-    results = (chips, pad, feat)
-    (direct,) = call(
-        functools.partial(direct_back_kernel, cap, pad, tight, block, chips),
-        "direct_backward",
-        [shape(results, BF16)],
-        [*pieces, up_v, down_v, arrived],
-        [IN_VMEM] * (chips + 2) + [ANYWHERE],
-        scratch,
-        AHEAD,
-        slots * hidden,
-    )
     back = pl.pallas_call(
-        functools.partial(sibling_back_kernel, cap, pad, tight, block, [0, *order]),
-        name="sibling_backward",
+        functools.partial(late_back_kernel, cap, pad, tight, block, [0, *order], late),
+        name="late_backward",
         out_shape=pltpu.HBM((groups, pad, feat), BF16),
-        in_specs=[IN_VMEM] * 4,
+        in_specs=[IN_VMEM] * (late + 4) + [ANYWHERE],
         out_specs=IN_HBM,
-        scratch_shapes=[pltpu.VMEM(results, BF16), DMA((groups,)), *scratch],
+        scratch_shapes=[
+            pltpu.VMEM((late + chips, pad, feat), BF16),
+            DMA((groups,)),
+            *scratch(late + chips),
+        ],
         compiler_params=pltpu.CompilerParams(vmem_limit_bytes=MEDIUM),
         cost_estimate=pl.CostEstimate(
             flops=AHEAD, bytes_accessed=4 * hidden * feat, transcendentals=slots * hidden
         ),
-    )(sibling, direct, up_v, down_v)
+    )(*pieces[-late:], sibling, early, up_v, down_v, arrived)
     back = lax.all_to_all(back, "exp", split_axis=0, concat_axis=0, tiled=True)
 
     part = min(512, share)
@@ -426,7 +446,7 @@
         begun = bool(sums)
         number = len(arrays) * chips * tight
         notes = [] if begun else [
-            shape((groups * pad, rows), BF16),
+            shape((rows, groups * pad), BF16),
             shape((2, groups, rows), F32),
             shape((2, 128, rows), BF16),
             shape((share, feat), BF16),

time: 57.5 us -> 56.2 us (0.977)
  Pallas kernels: 20 us -> 18.7 us
  starting transfers between devices: 23.1 us -> 24.1 us
  waiting for transfers between devices: 13.3 us -> 12.4 us
    ppermute x7, waiting for transfers between devices: 7.64 us -> 5.38 us  [local(): lax.ppermute(out[k], 'exp', hops_to(chips, k))]
    pallas_call x8, Pallas kernels: 16.9 us -> 15 us  [call(): pl.pallas_call(body, name=name, out_shape=outs, in_specs=in_specs, out_sp...]
    ppermute x1, waiting for transfers between devices: 3.65 us -> 4.75 us  [local(): seconds = [lax.ppermute(sibling, 'rep', hops) for hops in around]]
    ppermute x1, starting transfers between devices: 0.58 us -> 1.49 us  [local(): seconds = [lax.ppermute(sibling, 'rep', hops) for hops in around]]
  transfers between devices with their start and end apart: 11 -> 11, of which waited for: 6 -> 6; matrix products, arithmetic and copies ran while one was open for 0% -> 0% of each run, Pallas kernels for 30% -> 29%
where the time goes in v15:
time: 56.2 us; the launch traced here: 55.9 us
  starting transfers between devices  24.1 us (43%)
  Pallas kernels  18.7 us (33%)
  waiting for transfers between devices  12.4 us (22%)
  between operations  0.75 us (1%)
    ppermute x7, starting transfers between devices, local(): lax.ppermute(out[k], 'exp', hops_to(chips, k))  15.9 us
    pallas_call x8, Pallas kernels, call(): pl.pallas_call(body, name=name, out_shape=outs, in_specs=in_specs, out_sp...  15 us
    ppermute x7, waiting for transfers between devices, local(): lax.ppermute(out[k], 'exp', hops_to(chips, k))  5.38 us
    all_to_all x1, starting transfers between devices, local(): back = lax.all_to_all(back, 'exp', split_axis=0, concat_axis=0, tiled=True)  5.09 us
    ppermute x1, waiting for transfers between devices, local(): seconds = [lax.ppermute(sibling, 'rep', hops) for hops in around]  4.75 us
    pallas_call x1, Pallas kernels, local(): pl.pallas_call(functools.partial(late_back_kernel, cap, pad, tight, block...  3.71 us
    ppermute x1, waiting for transfers between devices, local(): firsts = [lax.ppermute(arrived, 'rep', hops) for hops in around]  2.02 us
    ppermute x1, starting transfers between devices, local(): firsts = [lax.ppermute(arrived, 'rep', hops) for hops in around]  1.56 us
  transfers between devices with their start and end apart: 11, of which 6 were waited for; matrix products, arithmetic and copies ran while one was open for 0% of the time, Pallas kernels for 29%

profile of v15, /device:TPU:0, one launch (start us, length us, event | category | flops | bytes accessed | tf_op | source)
XLA Modules:
  0.0 55.9 jit_solution(10957875421981197159)
XLA Ops:
  0.6 1.6 %slots.1 = (bf16[120,512]{1,0:T(8,128)(2,1)S(1)}, bf16[120,512]{1,0:T(8,128)(2,1)S(1)}, bf16[120,512]{1,0:T(8,128)(2,1)S(1)}, bf16[120,512]{1,0:T(8,128)(2,1)S(1...) custom-call(s32[2,160]{1,0:T(2,128)} %bitcast.3, ...), custom_call_target="tpu_custom_call" | custom-call | flops 167772160 | bytes 1312640 | tf_op jit(solution)/shard_map/slots/pallas_call | solution.py:36
  2.2 4.1 %collective-permute-start = (bf16[120,512]{1,0:T(8,128)(2,1)S(1)}, bf16[120,512]{1,0:T(8,128)(2,1)S(1)}, u32[]{:S(2)}, u32[]{:S(2)}) collective-permute-start(bf16[120,512]{1,0:T(8,128)(2,1)S(1)} %get-tuple-element.26), channel_id=1, source_target_pairs={{0,8},{1,9},{2,10},{3,11},{4,12},{5,13},{6,14},{7,15},{8,0},{9,1},... | collective-permute-start | bytes 368648 | tf_op jit(solution)/shard_map/ppermute | solution.py:368
  6.3 1.5 %collective-permute-start.1 = (bf16[120,512]{1,0:T(8,128)(2,1)S(1)}, bf16[120,512]{1,0:T(8,128)(2,1)S(1)}, u32[]{:S(2)}, u32[]{:S(2)}) collective-permute-start(bf16[120,512]{1,0:T(8,128)(2,1)S(1)} %get-tuple-element.27), channel_id=1, source_target_pairs={{0,2},{1,3},{2,0},{3,1},{4,6},{5,7},{6,4},{7,5},{8,10},{9,11},{10,... | collective-permute-start | bytes 368648 | tf_op jit(solution)/shard_map/ppermute | solution.py:368
  7.9 0.0 collective-permute-start.2
  7.9 1.8 %collective-permute-start.3 = (bf16[120,512]{1,0:T(8,128)(2,1)S(1)}, bf16[120,512]{1,0:T(8,128)(2,1)S(1)}, u32[]{:S(2)}, u32[]{:S(2)}) collective-permute-start(bf16[120,512]{1,0:T(8,128)(2,1)S(1)} %get-tuple-element.29), channel_id=1, source_target_pairs={{0,4},{1,5},{2,6},{3,7},{4,0},{5,1},{6,2},{7,3},{8,12},{9,13},{10,... | collective-permute-start | bytes 368648 | tf_op jit(solution)/shard_map/ppermute | solution.py:368
  9.7 2.5 %collective-permute-start.4 = (bf16[120,512]{1,0:T(8,128)(2,1)S(1)}, bf16[120,512]{1,0:T(8,128)(2,1)S(1)}, u32[]{:S(2)}, u32[]{:S(2)}) collective-permute-start(bf16[120,512]{1,0:T(8,128)(2,1)S(1)} %get-tuple-element.30), channel_id=1, source_target_pairs={{0,12},{1,13},{2,14},{3,15},{4,8},{5,9},{6,10},{7,11},{8,4},{9,5},... | collective-permute-start | bytes 368648 | tf_op jit(solution)/shard_map/ppermute | solution.py:368
  12.2 2.2 %fetch_weights.1 = (bf16[2048,512]{1,0:T(8,128)(2,1)S(1)}, bf16[2048,512]{1,0:T(8,128)(2,1)S(1)}) custom-call(bf16[1,2048,512]{2,1,0:T(8,128)(2,1)} %refs_3_.1, bf16[1,2048,512]{2,1,0:T(8,128)(2,1)} %refs_4_.1), custom_call_target="tpu_custom_call" | custom-call | tf_op jit(solution)/shard_map/fetch_weights/pallas_call | solution.py:36
  14.4 1.9 %collective-permute-done.refs_1_ = bf16[120,512]{1,0:T(8,128)(2,1)S(1)} collective-permute-done((bf16[120,512]{1,0:T(8,128)(2,1)S(1)}, bf16[120,512]{1,0:T(8,128)(2,1)S(1)}, u32[]{:S(2)}, u32[]{:S(2)}) %collective-permute-start) | collective-permute-done | bytes 122912 | tf_op jit(solution)/shard_map/ppermute | solution.py:368
  16.3 5.9 %collective-permute-start.5 = (bf16[120,512]{1,0:T(8,128)(2,1)S(1)}, bf16[120,512]{1,0:T(8,128)(2,1)S(1)}, u32[]{:S(2)}, u32[]{:S(2)}) collective-permute-start(bf16[120,512]{1,0:T(8,128)(2,1)S(1)} %get-tuple-element.31), channel_id=1, source_target_pairs={{0,14},{1,15},{2,12},{3,13},{4,10},{5,11},{6,8},{7,9},{8,6},{9,7},... | collective-permute-start | bytes 368648 | tf_op jit(solution)/shard_map/ppermute | solution.py:368
  22.2 0.0 collective-permute-done.1.refs_2_
  22.2 0.0 collective-permute-start.6
  22.2 1.4 %collective-permute-done.2.refs_3_ = bf16[120,512]{1,0:T(8,128)(2,1)S(1)} collective-permute-done((bf16[120,512]{1,0:T(8,128)(2,1)S(1)}, bf16[120,512]{1,0:T(8,128)(2,1)S(1)}, u32[]{:S(2)}, u32[]{:S(2)}) %collective-permute-start.2) | collective-permute-done | bytes 122912 | tf_op jit(solution)/shard_map/ppermute | solution.py:368
  23.6 0.0 collective-permute-done.3.refs_4_
  23.6 2.3 %early_backward.1.refs_8_.refs_4_ = bf16[5,32,512]{2,1,0:T(8,128)(2,1)S(1)} custom-call(bf16[120,512]{1,0:T(8,128)(2,1)S(1)} %get-tuple-element.25.refs_0_, bf16[120,512]{1,0:T(8,128)(2,1)S(1)} %collective-permute-done.refs_1_, bf16[120,512]{1,0:T(8,128)(2,1)S(1)} %collective-permute-done.1.refs_2_, bf16[120,512]{1,0:T(8,128)(2,1)S(1)} %collective-permute-done.2.refs_3_, ...), custom_call_target="tpu_custom_call" | custom-call | flops 1610612736 | bytes 4972544 | tf_op jit(solution)/shard_map/early_backward/pallas_call | solution.py:36
  25.9 0.0 collective-permute-done.4.refs_5_.refs_0_
  25.9 0.0 collective-permute-done.5.refs_6_.refs_1_
  25.9 2.1 %collective-permute-done.6.refs_7_.refs_2_ = bf16[120,512]{1,0:T(8,128)(2,1)S(1)} collective-permute-done((bf16[120,512]{1,0:T(8,128)(2,1)S(1)}, bf16[120,512]{1,0:T(8,128)(2,1)S(1)}, u32[]{:S(2)}, u32[]{:S(2)}) %collective-permute-start.6) | collective-permute-done | bytes 122912 | tf_op jit(solution)/shard_map/ppermute | solution.py:368
  28.0 0.1 hand_on.1.refs_8_
  28.1 0.1 collective-permute-start.7
  28.2 0.1 arrived_rows.1.refs_1_.refs_7_
  28.2 0.0 copy-start
  28.2 0.0 copy-start.1
  28.3 1.6 %collective-permute-start.8 = (bf16[480,512]{1,0:T(8,128)(2,1)S(1)}, bf16[480,512]{1,0:T(8,128)(2,1)S(1)}, u32[]{:S(2)}, u32[]{:S(2)}) collective-permute-start(bf16[480,512]{1,0:T(8,128)(2,1)S(1)} %arrived_rows.1.refs_1_.refs_7_), channel_id=1, source_target_pairs={{0,16},{16,0},{1,17},{17,1},{2,18},{18,2},{3,19},{19,3},{4,20},{20... | collective-permute-start | bytes 1474568 | tf_op jit(solution)/shard_map/ppermute | solution.py:422
  29.8 0.2 collective-permute-done.7.refs_0_.refs_3_
  30.0 1.5 %collective-permute-start.9 = (bf16[480,512]{1,0:T(8,128)(2,1)S(1)}, bf16[480,512]{1,0:T(8,128)(2,1)S(1)}, u32[]{:S(2)}, u32[]{:S(2)}) collective-permute-start(bf16[480,512]{1,0:T(8,128)(2,1)S(1)} %collective-permute-done.7.refs_0_.refs_3_), channel_id=1, source_target_pairs={{0,16},{16,0},{1,17},{17,1},{2,18},{18,2},{3,19},{19,3},{4,20},{20... | collective-permute-start | bytes 1474568 | tf_op jit(solution)/shard_map/ppermute | solution.py:423
  31.5 3.7 %late_backward.1 = bf16[16,32,512]{2,1,0:T(8,128)(2,1)} custom-call(bf16[120,512]{1,0:T(8,128)(2,1)S(1)} %collective-permute-done.4.refs_5_.refs_0_, bf16[120,512]{1,0:T(8,128)(2,1)S(1)} %collective-permute-done.5.refs_6_.refs_1_, bf16[120,512]{1,0:T(8,128)(2,1)S(1)} %collective-permute-done.6.refs_7_.refs_2_, ...), custom_call_target="tpu_custom_call" | custom-call | flops 99999997952 | bytes 4194304 | tf_op jit(solution)/shard_map/late_backward/pallas_call | solution.py:425
  35.2 5.1 %all-to-all-start = ((bf16[16,32,512]{2,1,0:T(8,128)(2,1)}), bf16[16,32,512]{2,1,0:T(8,128)(2,1)S(1)}, u32[]{:S(2)}, u32[]{:S(2)}) async-start(bf16[16,32,512]{2,1,0:T(8,128)(2,1)} %late_backward.1), calls=%async_computation | async-start | bytes 1048576 | tf_op jit(solution)/shard_map/all_to_all | solution.py:441
  40.3 2.0 %collective-permute-done.8.refs_2_ = bf16[480,512]{1,0:T(8,128)(2,1)S(1)} collective-permute-done((bf16[480,512]{1,0:T(8,128)(2,1)S(1)}, bf16[480,512]{1,0:T(8,128)(2,1)S(1)}, u32[]{:S(2)}, u32[]{:S(2)}) %collective-permute-start.8) | collective-permute-done | bytes 491552 | tf_op jit(solution)/shard_map/ppermute | solution.py:422
  42.3 0.0 copy-done
  42.3 0.0 copy-done.1
  42.3 5.4 %first_weights.1 = (f32[1,1024,512]{2,1,0:T(8,128)S(1)}, f32[1,1024,512]{2,1,0:T(8,128)S(1)}, bf16[160,512]{1,0:T(8,128)(2,1)S(1)}, f32[2,16,160]{2,1,0:T(8,128)...) custom-call(bf16[480,512]{1,0:T(8,128)(2,1)S(1)} %collective-permute-done.7.ref, ...), custom_call_target="tpu_custom_call" | custom-call | tf_op jit(solution)/shard_map/first_weights/pallas_call | solution.py:36
  47.7 4.8 %collective-permute-done.9.refs_0_ = bf16[480,512]{1,0:T(8,128)(2,1)S(1)} collective-permute-done((bf16[480,512]{1,0:T(8,128)(2,1)S(1)}, bf16[480,512]{1,0:T(8,128)(2,1)S(1)}, u32[]{:S(2)}, u32[]{:S(2)}) %collective-permute-start.9) | collective-permute-done | bytes 491552 | tf_op jit(solution)/shard_map/ppermute | solution.py:423
  52.5 2.5 %last_weights.1 = (bf16[1,1024,512]{2,1,0:T(8,128)(2,1)}, bf16[1,1024,512]{2,1,0:T(8,128)(2,1)}) custom-call(bf16[480,512]{1,0:T(8,128)(2,1)S(1)} %collective-permute-done.9.refs_0_, bf16[1024,512]{1,0:T(8,128)(2,1)S(1)} %get-tuple-element.40.refs_1_, bf16[1024,512]{1,0:T(8,128)(2,1)S(1)} %get-tuple-element.41.refs_2_, ...), custom_call_target="tpu_custom_call" | custom-call | flops 99999997952 | bytes 8880128 | tf_op jit(solution)/shard_map/last_weights/pallas_call | solution.py:36
  55.0 0.0 all-to-all-done.back_ref
  55.0 0.9 %combine.1 = (bf16[160,512]{1,0:T(8,128)(2,1)}, bf16[2,160]{1,0:T(2,128)(2,1)}) custom-call(bf16[160,512]{1,0:T(8,128)(2,1)S(1)} %get-tuple-element.35.pick_ref, f32[2,16,160]{2,1,0:T(8,128)S(1)} %get-tuple-element.36.hot_ref, bf16[2,128,160]{2,1,0:T(8,128)(2,1)S(1)} %get-tuple-element.37.spot_ref, bf16[16,32,512]{2,1,0:T(8,128)(2,1)S(1)} %all-to-all-done.back_ref), custom_call_target="tpu_custom_call" | custom-call | flops 167772160 | bytes 955008 | tf_op jit(solution)/shard_map/combine/pallas_call | solution.py:36
Async XLA Ops:
  2.2 14.1 %collective-permute-start = (bf16[120,512]{1,0:T(8,128)(2,1)S(1)}, bf16[120,512]{1,0:T(8,128)(2,1)S(1)}, u32[]{:S(2)}, u32[]{:S(2)}) collective-permute-start(bf16[120,512]{1,0:T(8,128)(2,1)S(1)} %get-tuple-element.26), channel_id=1, source_target_pairs={{0,8},{1,9},{2,10},{3,11},{4,12},{5,13},{6,14},{7,15},{8,0},{9,1},... | collective-permute-start | bytes 368648 | tf_op jit(solution)/shard_map/ppermute | solution.py:368
  6.3 15.9 %collective-permute-start.1 = (bf16[120,512]{1,0:T(8,128)(2,1)S(1)}, bf16[120,512]{1,0:T(8,128)(2,1)S(1)}, u32[]{:S(2)}, u32[]{:S(2)}) collective-permute-start(bf16[120,512]{1,0:T(8,128)(2,1)S(1)} %get-tuple-element.27), channel_id=1, source_target_pairs={{0,2},{1,3},{2,0},{3,1},{4,6},{5,7},{6,4},{7,5},{8,10},{9,11},{10,... | collective-permute-start | bytes 368648 | tf_op jit(solution)/shard_map/ppermute | solution.py:368
  7.9 15.8 %collective-permute-start.2 = (bf16[120,512]{1,0:T(8,128)(2,1)S(1)}, bf16[120,512]{1,0:T(8,128)(2,1)S(1)}, u32[]{:S(2)}, u32[]{:S(2)}) collective-permute-start(bf16[120,512]{1,0:T(8,128)(2,1)S(1)} %get-tuple-element.28), channel_id=1, source_target_pairs={{0,10},{1,11},{2,8},{3,9},{4,14},{5,15},{6,12},{7,13},{8,2},{9,3},... | collective-permute-start | bytes 368648 | tf_op jit(solution)/shard_map/ppermute | solution.py:368
  7.9 15.8 %collective-permute-start.3 = (bf16[120,512]{1,0:T(8,128)(2,1)S(1)}, bf16[120,512]{1,0:T(8,128)(2,1)S(1)}, u32[]{:S(2)}, u32[]{:S(2)}) collective-permute-start(bf16[120,512]{1,0:T(8,128)(2,1)S(1)} %get-tuple-element.29), channel_id=1, source_target_pairs={{0,4},{1,5},{2,6},{3,7},{4,0},{5,1},{6,2},{7,3},{8,12},{9,13},{10,... | collective-permute-start | bytes 368648 | tf_op jit(solution)/shard_map/ppermute | solution.py:368
  9.7 16.2 %collective-permute-start.4 = (bf16[120,512]{1,0:T(8,128)(2,1)S(1)}, bf16[120,512]{1,0:T(8,128)(2,1)S(1)}, u32[]{:S(2)}, u32[]{:S(2)}) collective-permute-start(bf16[120,512]{1,0:T(8,128)(2,1)S(1)} %get-tuple-element.30), channel_id=1, source_target_pairs={{0,12},{1,13},{2,14},{3,15},{4,8},{5,9},{6,10},{7,11},{8,4},{9,5},... | collective-permute-start | bytes 368648 | tf_op jit(solution)/shard_map/ppermute | solution.py:368
  16.3 9.6 %collective-permute-start.5 = (bf16[120,512]{1,0:T(8,128)(2,1)S(1)}, bf16[120,512]{1,0:T(8,128)(2,1)S(1)}, u32[]{:S(2)}, u32[]{:S(2)}) collective-permute-start(bf16[120,512]{1,0:T(8,128)(2,1)S(1)} %get-tuple-element.31), channel_id=1, source_target_pairs={{0,14},{1,15},{2,12},{3,13},{4,10},{5,11},{6,8},{7,9},{8,6},{9,7},... | collective-permute-start | bytes 368648 | tf_op jit(solution)/shard_map/ppermute | solution.py:368
  22.2 5.8 %collective-permute-start.6 = (bf16[120,512]{1,0:T(8,128)(2,1)S(1)}, bf16[120,512]{1,0:T(8,128)(2,1)S(1)}, u32[]{:S(2)}, u32[]{:S(2)}) collective-permute-start(bf16[120,512]{1,0:T(8,128)(2,1)S(1)} %get-tuple-element.32), channel_id=1, source_target_pairs={{0,6},{1,7},{2,4},{3,5},{4,2},{5,3},{6,0},{7,1},{8,14},{9,15},{10,... | collective-permute-start | bytes 368648 | tf_op jit(solution)/shard_map/ppermute | solution.py:368
  28.1 1.9 %collective-permute-start.7 = (bf16[480,512]{1,0:T(8,128)(2,1)S(1)}, bf16[480,512]{1,0:T(8,128)(2,1)S(1)}, u32[]{:S(2)}, u32[]{:S(2)}) collective-permute-start(bf16[480,512]{1,0:T(8,128)(2,1)S(1)} %hand_on.1.refs_8_), channel_id=1, source_target_pairs={{0,1},{1,0},{2,3},{3,2},{4,5},{5,4},{6,7},{7,6},{8,9},{9,8},{10,11... | collective-permute-start | bytes 1474568 | tf_op jit(solution)/shard_map/ppermute | solution.py:420
  28.2 14.1 %copy-start = (s32[160,2]{0,1:T(2,128)S(1)}, s32[160,2]{0,1:T(2,128)}, u32[]{:S(2)}) copy-start(s32[160,2]{0,1:T(2,128)} %param.8) | copy-start | bytes 3844
  28.2 14.1 %copy-start.1 = (bf16[160,2]{0,1:T(2,128)(2,1)S(1)}, bf16[160,2]{0,1:T(2,128)(2,1)}, u32[]{:S(2)}) copy-start(bf16[160,2]{0,1:T(2,128)(2,1)} %param.7) | copy-start | bytes 1924
  28.3 14.1 %collective-permute-start.8 = (bf16[480,512]{1,0:T(8,128)(2,1)S(1)}, bf16[480,512]{1,0:T(8,128)(2,1)S(1)}, u32[]{:S(2)}, u32[]{:S(2)}) collective-permute-start(bf16[480,512]{1,0:T(8,128)(2,1)S(1)} %arrived_rows.1.refs_1_.refs_7_), channel_id=1, source_target_pairs={{0,16},{16,0},{1,17},{17,1},{2,18},{18,2},{3,19},{19,3},{4,20},{20... | collective-permute-start | bytes 1474568 | tf_op jit(solution)/shard_map/ppermute | solution.py:422
  30.0 22.5 %collective-permute-start.9 = (bf16[480,512]{1,0:T(8,128)(2,1)S(1)}, bf16[480,512]{1,0:T(8,128)(2,1)S(1)}, u32[]{:S(2)}, u32[]{:S(2)}) collective-permute-start(bf16[480,512]{1,0:T(8,128)(2,1)S(1)} %collective-permute-done.7.refs_0_.refs_3_), channel_id=1, source_target_pairs={{0,16},{16,0},{1,17},{17,1},{2,18},{18,2},{3,19},{19,3},{4,20},{20... | collective-permute-start | bytes 1474568 | tf_op jit(solution)/shard_map/ppermute | solution.py:423
  35.2 19.7 %all-to-all-start = ((bf16[16,32,512]{2,1,0:T(8,128)(2,1)}), bf16[16,32,512]{2,1,0:T(8,128)(2,1)S(1)}, u32[]{:S(2)}, u32[]{:S(2)}) async-start(bf16[16,32,512]{2,1,0:T(8,128)(2,1)} %late_backward.1), calls=%async_computation | async-start | bytes 1048576 | tf_op jit(solution)/shard_map/all_to_all | solution.py:441

commit v16 on v15

--- a/solution.py
+++ b/solution.py
@@ -272,10 +272,12 @@
     steps = steps_of(share, block)
     if not begun:
         fetch = Fetch(*weights, up_ref, down_ref, sems, lax.axis_index("rep") * share, steps)
-    for i, ref in enumerate(row_refs):
+    begin = 0
+    for ref in row_refs:
         size = ref.shape[0] // 2
-        rows_ref[i * size : (i + 1) * size, :] = ref[:size, :]
-        grads_ref[i * size : (i + 1) * size, :] = ref[size:, :]
+        rows_ref[begin : begin + size, :] = ref[:size, :]
+        grads_ref[begin : begin + size, :] = ref[size:, :]
+        begin += size
     copies = []
     for step, (at, size) in enumerate(steps):
         here = pl.ds(at, size)
@@ -403,23 +405,28 @@
         slots * hidden,
     )
 
-    def join(name, arrays, *lists):
+    def join(name, arrays, *lists, after=()):
         return call(
             functools.partial(join_kernel, tight, lists),
             name,
             [shape((len(blocks) * tight, feat), BF16) for blocks in lists],
-            arrays,
-            [IN_VMEM] * len(arrays),
+            [*arrays, *after],
+            [IN_VMEM] * len(arrays) + [ANYWHERE] * len(after),
             [],
             0,
             0,
             SMALL,
         )
 
-    (handed,) = join("hand_on", [*pieces, early], [(i, at) for at in (2 * tight, 3 * tight) for i in range(chips)])
+    soon = 2
+    (ahead,) = join("first_rows", pieces[:soon], [(i, at) for at in (0, tight) for i in range(soon)])
+    firsts = [lax.ppermute(ahead, "rep", hops) for hops in around]
+    blocks = [(i, at) for at in (2 * tight, 3 * tight) for i in range(chips)]
+    (handed,) = join("hand_on", [*pieces, early], blocks, after=firsts)
     sibling = lax.ppermute(handed, "exp", swap)
-    (arrived,) = join("arrived_rows", [*pieces, handed], [(i, at) for at in (0, tight) for i in range(chips)])
-    firsts = [lax.ppermute(arrived, "rep", hops) for hops in around]
+    blocks = [(i, at) for at in (0, tight) for i in range(soon, chips)]
+    (arrived,) = join("arrived_rows", [*pieces, handed], blocks)
+    firsts += [lax.ppermute(arrived, "rep", hops) for hops in around]
     seconds = [lax.ppermute(sibling, "rep", hops) for hops in around]
 
     back = pl.pallas_call(
@@ -444,7 +451,7 @@
 
     def weights_call(name, arrays, weights, sums, ended, flops):
         begun = bool(sums)
-        number = len(arrays) * chips * tight
+        number = sum(a.shape[0] for a in arrays) // 2
         notes = [] if begun else [
             shape((rows, groups * pad), BF16),
             shape((2, groups, rows), F32),
@@ -474,9 +481,9 @@
             [IN_HBM if ended else IN_VMEM] * 2 + [IN_VMEM] * len(notes),
         )
 
-    joined = [sibling, arrived, *firsts]
+    joined = [sibling, arrived, ahead, *firsts]
     *sums, pick, hot, spot, up_v, down_v = weights_call(
-        "first_weights", joined, [w_up, w_down], [], not seconds, 0
+        "first_weights", joined, [w_up, w_down], [], not seconds, AHEAD
     )
     if seconds:
         sums = weights_call(

time: 56.2 us -> 57.1 us (1.016)
  waiting for transfers between devices: 12.4 us -> 11 us
  starting transfers between devices: 24.1 us -> 25.3 us
  Pallas kernels: 18.7 us -> 19.7 us
    ppermute x1, waiting for transfers between devices: 4.75 us -> 6.55 us  [local(): seconds = [lax.ppermute(sibling, 'rep', hops) for hops in around]]
    ppermute x1 -> x2, waiting for transfers between devices: 2.02 us -> 0.4 us  [the longest x1 0.4 us: local(): firsts = [lax.ppermute(ahead, 'rep', hops) for hops in around]]
    ppermute x7, waiting for transfers between devices: 5.38 us -> 3.88 us  [local(): lax.ppermute(out[k], 'exp', hops_to(chips, k))]
    ppermute x1 -> x2, starting transfers between devices: 1.56 us -> 3.04 us  [the longest x1 1.55 us: local(): firsts += [lax.ppermute(arrived, 'rep', hops) for hops in around]]
    pallas_call x8 -> x9, Pallas kernels: 15 us -> 16 us  [call(): pl.pallas_call(body, name=name, out_shape=outs, in_specs=in_specs, out_sp...]
  transfers between devices with their start and end apart: 11 -> 12, of which waited for: 6 -> 6; matrix products, arithmetic and copies ran while one was open for 0% -> 0% of each run, Pallas kernels for 29% -> 28%
where the time goes in v16:
time: 57.1 us; the launch traced here: 56.8 us
  starting transfers between devices  25.3 us (44%)
  Pallas kernels  19.7 us (35%)
  waiting for transfers between devices  11 us (19%)
  between operations  0.78 us (1%)
    pallas_call x9, Pallas kernels, call(): pl.pallas_call(body, name=name, out_shape=outs, in_specs=in_specs, out_sp...  16 us
    ppermute x7, starting transfers between devices, local(): lax.ppermute(out[k], 'exp', hops_to(chips, k))  15.9 us
    ppermute x1, waiting for transfers between devices, local(): seconds = [lax.ppermute(sibling, 'rep', hops) for hops in around]  6.55 us
    all_to_all x1, starting transfers between devices, local(): back = lax.all_to_all(back, 'exp', split_axis=0, concat_axis=0, tiled=True)  4.67 us
    ppermute x7, waiting for transfers between devices, local(): lax.ppermute(out[k], 'exp', hops_to(chips, k))  3.88 us
    pallas_call x1, Pallas kernels, local(): pl.pallas_call(functools.partial(late_back_kernel, cap, pad, tight, block...  3.68 us
    ppermute x1, starting transfers between devices, local(): firsts += [lax.ppermute(arrived, 'rep', hops) for hops in around]  1.55 us
    ppermute x1, starting transfers between devices, local(): seconds = [lax.ppermute(sibling, 'rep', hops) for hops in around]  1.55 us
  transfers between devices with their start and end apart: 12, of which 6 were waited for; matrix products, arithmetic and copies ran while one was open for 0% of the time, Pallas kernels for 28%

profile of v16, /device:TPU:0, one launch (start us, length us, event | category | flops | bytes accessed | tf_op | source)
XLA Modules:
  0.0 56.8 jit_solution(16100800035166721074)
XLA Ops:
  0.6 1.6 %slots.1 = (bf16[120,512]{1,0:T(8,128)(2,1)S(1)}, bf16[120,512]{1,0:T(8,128)(2,1)S(1)}, bf16[120,512]{1,0:T(8,128)(2,1)S(1)}, bf16[120,512]{1,0:T(8,128)(2,1)S(1...) custom-call(s32[2,160]{1,0:T(2,128)} %bitcast.3, ...), custom_call_target="tpu_custom_call" | custom-call | flops 167772160 | bytes 1312640 | tf_op jit(solution)/shard_map/slots/pallas_call | solution.py:36
  2.2 4.1 %collective-permute-start = (bf16[120,512]{1,0:T(8,128)(2,1)S(1)}, bf16[120,512]{1,0:T(8,128)(2,1)S(1)}, u32[]{:S(2)}, u32[]{:S(2)}) collective-permute-start(bf16[120,512]{1,0:T(8,128)(2,1)S(1)} %get-tuple-element.26), channel_id=1, source_target_pairs={{0,8},{1,9},{2,10},{3,11},{4,12},{5,13},{6,14},{7,15},{8,0},{9,1},... | collective-permute-start | bytes 368648 | tf_op jit(solution)/shard_map/ppermute | solution.py:370
  6.3 1.5 %collective-permute-start.1 = (bf16[120,512]{1,0:T(8,128)(2,1)S(1)}, bf16[120,512]{1,0:T(8,128)(2,1)S(1)}, u32[]{:S(2)}, u32[]{:S(2)}) collective-permute-start(bf16[120,512]{1,0:T(8,128)(2,1)S(1)} %get-tuple-element.27), channel_id=1, source_target_pairs={{0,2},{1,3},{2,0},{3,1},{4,6},{5,7},{6,4},{7,5},{8,10},{9,11},{10,... | collective-permute-start | bytes 368648 | tf_op jit(solution)/shard_map/ppermute | solution.py:370
  7.9 0.0 collective-permute-start.2
  7.9 1.8 %collective-permute-start.3 = (bf16[120,512]{1,0:T(8,128)(2,1)S(1)}, bf16[120,512]{1,0:T(8,128)(2,1)S(1)}, u32[]{:S(2)}, u32[]{:S(2)}) collective-permute-start(bf16[120,512]{1,0:T(8,128)(2,1)S(1)} %get-tuple-element.29), channel_id=1, source_target_pairs={{0,4},{1,5},{2,6},{3,7},{4,0},{5,1},{6,2},{7,3},{8,12},{9,13},{10,... | collective-permute-start | bytes 368648 | tf_op jit(solution)/shard_map/ppermute | solution.py:370
  9.7 2.5 %collective-permute-start.4 = (bf16[120,512]{1,0:T(8,128)(2,1)S(1)}, bf16[120,512]{1,0:T(8,128)(2,1)S(1)}, u32[]{:S(2)}, u32[]{:S(2)}) collective-permute-start(bf16[120,512]{1,0:T(8,128)(2,1)S(1)} %get-tuple-element.30), channel_id=1, source_target_pairs={{0,12},{1,13},{2,14},{3,15},{4,8},{5,9},{6,10},{7,11},{8,4},{9,5},... | collective-permute-start | bytes 368648 | tf_op jit(solution)/shard_map/ppermute | solution.py:370
  12.2 2.2 %fetch_weights.1 = (bf16[2048,512]{1,0:T(8,128)(2,1)S(1)}, bf16[2048,512]{1,0:T(8,128)(2,1)S(1)}) custom-call(bf16[1,2048,512]{2,1,0:T(8,128)(2,1)} %refs_5_.1, bf16[1,2048,512]{2,1,0:T(8,128)(2,1)} %refs_6_.1), custom_call_target="tpu_custom_call" | custom-call | tf_op jit(solution)/shard_map/fetch_weights/pallas_call | solution.py:36
  14.4 1.9 %collective-permute-done.refs_1_ = bf16[120,512]{1,0:T(8,128)(2,1)S(1)} collective-permute-done((bf16[120,512]{1,0:T(8,128)(2,1)S(1)}, bf16[120,512]{1,0:T(8,128)(2,1)S(1)}, u32[]{:S(2)}, u32[]{:S(2)}) %collective-permute-start) | collective-permute-done | bytes 122912 | tf_op jit(solution)/shard_map/ppermute | solution.py:370
  16.3 5.9 %collective-permute-start.5 = (bf16[120,512]{1,0:T(8,128)(2,1)S(1)}, bf16[120,512]{1,0:T(8,128)(2,1)S(1)}, u32[]{:S(2)}, u32[]{:S(2)}) collective-permute-start(bf16[120,512]{1,0:T(8,128)(2,1)S(1)} %get-tuple-element.31), channel_id=1, source_target_pairs={{0,14},{1,15},{2,12},{3,13},{4,10},{5,11},{6,8},{7,9},{8,6},{9,7},... | collective-permute-start | bytes 368648 | tf_op jit(solution)/shard_map/ppermute | solution.py:370
  22.3 0.0 collective-permute-done.1.refs_2_
  22.3 0.1 collective-permute-start.6
  22.4 1.3 %collective-permute-done.2.refs_3_ = bf16[120,512]{1,0:T(8,128)(2,1)S(1)} collective-permute-done((bf16[120,512]{1,0:T(8,128)(2,1)S(1)}, bf16[120,512]{1,0:T(8,128)(2,1)S(1)}, u32[]{:S(2)}, u32[]{:S(2)}) %collective-permute-start.2) | collective-permute-done | bytes 122912 | tf_op jit(solution)/shard_map/ppermute | solution.py:370
  23.6 1.5 %collective-permute-start.7 = (bf16[120,512]{1,0:T(8,128)(2,1)S(1)}, bf16[120,512]{1,0:T(8,128)(2,1)S(1)}, u32[]{:S(2)}, u32[]{:S(2)}) collective-permute-start(bf16[120,512]{1,0:T(8,128)(2,1)S(1)} %first_rows.1.refs_2_), channel_id=1, source_target_pairs={{0,16},{16,0},{1,17},{17,1},{2,18},{18,2},{3,19},{19,3},{4,20},{20... | collective-permute-start | bytes 368648 | tf_op jit(solution)/shard_map/ppermute | solution.py:423
  25.1 0.0 collective-permute-done.3.refs_4_
  25.1 2.3 %early_backward.1.refs_8_.refs_4_ = bf16[5,32,512]{2,1,0:T(8,128)(2,1)S(1)} custom-call(bf16[120,512]{1,0:T(8,128)(2,1)S(1)} %get-tuple-element.25.refs_0_, bf16[120,512]{1,0:T(8,128)(2,1)S(1)} %collective-permute-done.refs_1_, bf16[120,512]{1,0:T(8,128)(2,1)S(1)} %collective-permute-done.1.refs_2_, bf16[120,512]{1,0:T(8,128)(2,1)S(1)} %collective-permute-done.2.refs_3_, ...), custom_call_target="tpu_custom_call" | custom-call | flops 1610612736 | bytes 4972544 | tf_op jit(solution)/shard_map/early_backward/pallas_call | solution.py:36
  27.4 0.0 collective-permute-done.4.refs_5_.refs_0_
  27.4 0.0 collective-permute-done.5.refs_6_.refs_1_
  27.4 0.7 %collective-permute-done.6.refs_7_.refs_2_ = bf16[120,512]{1,0:T(8,128)(2,1)S(1)} collective-permute-done((bf16[120,512]{1,0:T(8,128)(2,1)S(1)}, bf16[120,512]{1,0:T(8,128)(2,1)S(1)}, u32[]{:S(2)}, u32[]{:S(2)}) %collective-permute-start.6) | collective-permute-done | bytes 122912 | tf_op jit(solution)/shard_map/ppermute | solution.py:370
  28.1 0.4 collective-permute-done.7.refs_9_.refs_3_
  28.5 0.1 hand_on.1.refs_8_
  28.6 0.1 collective-permute-start.8
  28.7 0.0 copy-start
  28.7 0.0 copy-start.1
  28.7 1.6 %collective-permute-start.9 = (bf16[360,512]{1,0:T(8,128)(2,1)S(1)}, bf16[360,512]{1,0:T(8,128)(2,1)S(1)}, u32[]{:S(2)}, u32[]{:S(2)}) collective-permute-start(bf16[360,512]{1,0:T(8,128)(2,1)S(1)} %arrived_rows.1.refs_1_.refs_7_), channel_id=1, source_target_pairs={{0,16},{16,0},{1,17},{17,1},{2,18},{18,2},{3,19},{19,3},{4,20},{20... | collective-permute-start | bytes 1105928 | tf_op jit(solution)/shard_map/ppermute | solution.py:429
  30.3 0.2 collective-permute-done.8.refs_0_.refs_3_
  30.5 3.7 %late_backward.1 = bf16[16,32,512]{2,1,0:T(8,128)(2,1)} custom-call(bf16[120,512]{1,0:T(8,128)(2,1)S(1)} %collective-permute-done.4.refs_5_.refs_0_, bf16[120,512]{1,0:T(8,128)(2,1)S(1)} %collective-permute-done.5.refs_6_.refs_1_, bf16[120,512]{1,0:T(8,128)(2,1)S(1)} %collective-permute-done.6.refs_7_.refs_2_, ...), custom_call_target="tpu_custom_call" | custom-call | flops 99999997952 | bytes 4194304 | tf_op jit(solution)/shard_map/late_backward/pallas_call | solution.py:432
  34.2 4.7 %all-to-all-start = ((bf16[16,32,512]{2,1,0:T(8,128)(2,1)}), bf16[16,32,512]{2,1,0:T(8,128)(2,1)}, u32[]{:S(2)}, u32[]{:S(2)}) async-start(bf16[16,32,512]{2,1,0:T(8,128)(2,1)} %late_backward.1), calls=%async_computation | async-start | bytes 1048576 | tf_op jit(solution)/shard_map/all_to_all | solution.py:448
  38.9 1.6 %collective-permute-start.10 = (bf16[480,512]{1,0:T(8,128)(2,1)S(1)}, bf16[480,512]{1,0:T(8,128)(2,1)S(1)}, u32[]{:S(2)}, u32[]{:S(2)}) collective-permute-start(bf16[480,512]{1,0:T(8,128)(2,1)S(1)} %collective-permute-done.8.refs_0_.refs_3_), channel_id=1, source_target_pairs={{0,16},{16,0},{1,17},{17,1},{2,18},{18,2},{3,19},{19,3},{4,20},{20... | collective-permute-start | bytes 1474568 | tf_op jit(solution)/shard_map/ppermute | solution.py:430
  40.4 0.0 collective-permute-done.9.refs_4_
  40.4 0.0 copy-done
  40.4 0.0 copy-done.1
  40.4 5.4 %first_weights.1 = (f32[1,1024,512]{2,1,0:T(8,128)S(1)}, f32[1,1024,512]{2,1,0:T(8,128)S(1)}, bf16[160,512]{1,0:T(8,128)(2,1)S(1)}, f32[2,16,160]{2,1,0:T(8,128)...) custom-call(bf16[480,512]{1,0:T(8,128)(2,1)S(1)} %collective-permute-done.8.ref, ...), custom_call_target="tpu_custom_call" | custom-call | flops 99999997952 | bytes 12228480 | tf_op jit(solution)/shard_map/first_weights/pallas_call | solution.py:36
  45.8 6.5 %collective-permute-done.10.refs_0_ = bf16[480,512]{1,0:T(8,128)(2,1)S(1)} collective-permute-done((bf16[480,512]{1,0:T(8,128)(2,1)S(1)}, bf16[480,512]{1,0:T(8,128)(2,1)S(1)}, u32[]{:S(2)}, u32[]{:S(2)}) %collective-permute-start.10) | collective-permute-done | bytes 491552 | tf_op jit(solution)/shard_map/ppermute | solution.py:430
  52.4 2.4 %last_weights.1 = (bf16[1,1024,512]{2,1,0:T(8,128)(2,1)}, bf16[1,1024,512]{2,1,0:T(8,128)(2,1)}) custom-call(bf16[480,512]{1,0:T(8,128)(2,1)S(1)} %collective-permute-done.10.refs_0_, bf16[1024,512]{1,0:T(8,128)(2,1)S(1)} %get-tuple-element.40.refs_1_, bf16[1024,512]{1,0:T(8,128)(2,1)S(1)} %get-tuple-element.41.refs_2_, ...), custom_call_target="tpu_custom_call" | custom-call | flops 99999997952 | bytes 8880128 | tf_op jit(solution)/shard_map/last_weights/pallas_call | solution.py:36
  54.8 0.0 all-to-all-done.back_ref
  54.8 2.0 %combine.1 = (bf16[160,512]{1,0:T(8,128)(2,1)}, bf16[2,160]{1,0:T(2,128)(2,1)}) custom-call(bf16[160,512]{1,0:T(8,128)(2,1)S(1)} %get-tuple-element.35.pick_ref, f32[2,16,160]{2,1,0:T(8,128)S(1)} %get-tuple-element.36.hot_ref, bf16[2,128,160]{2,1,0:T(8,128)(2,1)S(1)} %get-tuple-element.37.spot_ref, bf16[16,32,512]{2,1,0:T(8,128)(2,1)} %all-to-all-done.back_ref), custom_call_target="tpu_custom_call" | custom-call | flops 167772160 | bytes 955008 | tf_op jit(solution)/shard_map/combine/pallas_call | solution.py:36
  (2 shorter events, 0.1 us)
Async XLA Ops:
  2.2 14.1 %collective-permute-start = (bf16[120,512]{1,0:T(8,128)(2,1)S(1)}, bf16[120,512]{1,0:T(8,128)(2,1)S(1)}, u32[]{:S(2)}, u32[]{:S(2)}) collective-permute-start(bf16[120,512]{1,0:T(8,128)(2,1)S(1)} %get-tuple-element.26), channel_id=1, source_target_pairs={{0,8},{1,9},{2,10},{3,11},{4,12},{5,13},{6,14},{7,15},{8,0},{9,1},... | collective-permute-start | bytes 368648 | tf_op jit(solution)/shard_map/ppermute | solution.py:370
  6.3 15.9 %collective-permute-start.1 = (bf16[120,512]{1,0:T(8,128)(2,1)S(1)}, bf16[120,512]{1,0:T(8,128)(2,1)S(1)}, u32[]{:S(2)}, u32[]{:S(2)}) collective-permute-start(bf16[120,512]{1,0:T(8,128)(2,1)S(1)} %get-tuple-element.27), channel_id=1, source_target_pairs={{0,2},{1,3},{2,0},{3,1},{4,6},{5,7},{6,4},{7,5},{8,10},{9,11},{10,... | collective-permute-start | bytes 368648 | tf_op jit(solution)/shard_map/ppermute | solution.py:370
  7.9 15.8 %collective-permute-start.2 = (bf16[120,512]{1,0:T(8,128)(2,1)S(1)}, bf16[120,512]{1,0:T(8,128)(2,1)S(1)}, u32[]{:S(2)}, u32[]{:S(2)}) collective-permute-start(bf16[120,512]{1,0:T(8,128)(2,1)S(1)} %get-tuple-element.28), channel_id=1, source_target_pairs={{0,10},{1,11},{2,8},{3,9},{4,14},{5,15},{6,12},{7,13},{8,2},{9,3},... | collective-permute-start | bytes 368648 | tf_op jit(solution)/shard_map/ppermute | solution.py:370
  7.9 17.3 %collective-permute-start.3 = (bf16[120,512]{1,0:T(8,128)(2,1)S(1)}, bf16[120,512]{1,0:T(8,128)(2,1)S(1)}, u32[]{:S(2)}, u32[]{:S(2)}) collective-permute-start(bf16[120,512]{1,0:T(8,128)(2,1)S(1)} %get-tuple-element.29), channel_id=1, source_target_pairs={{0,4},{1,5},{2,6},{3,7},{4,0},{5,1},{6,2},{7,3},{8,12},{9,13},{10,... | collective-permute-start | bytes 368648 | tf_op jit(solution)/shard_map/ppermute | solution.py:370
  9.7 17.7 %collective-permute-start.4 = (bf16[120,512]{1,0:T(8,128)(2,1)S(1)}, bf16[120,512]{1,0:T(8,128)(2,1)S(1)}, u32[]{:S(2)}, u32[]{:S(2)}) collective-permute-start(bf16[120,512]{1,0:T(8,128)(2,1)S(1)} %get-tuple-element.30), channel_id=1, source_target_pairs={{0,12},{1,13},{2,14},{3,15},{4,8},{5,9},{6,10},{7,11},{8,4},{9,5},... | collective-permute-start | bytes 368648 | tf_op jit(solution)/shard_map/ppermute | solution.py:370
  16.3 11.1 %collective-permute-start.5 = (bf16[120,512]{1,0:T(8,128)(2,1)S(1)}, bf16[120,512]{1,0:T(8,128)(2,1)S(1)}, u32[]{:S(2)}, u32[]{:S(2)}) collective-permute-start(bf16[120,512]{1,0:T(8,128)(2,1)S(1)} %get-tuple-element.31), channel_id=1, source_target_pairs={{0,14},{1,15},{2,12},{3,13},{4,10},{5,11},{6,8},{7,9},{8,6},{9,7},... | collective-permute-start | bytes 368648 | tf_op jit(solution)/shard_map/ppermute | solution.py:370
  22.3 5.8 %collective-permute-start.6 = (bf16[120,512]{1,0:T(8,128)(2,1)S(1)}, bf16[120,512]{1,0:T(8,128)(2,1)S(1)}, u32[]{:S(2)}, u32[]{:S(2)}) collective-permute-start(bf16[120,512]{1,0:T(8,128)(2,1)S(1)} %get-tuple-element.32), channel_id=1, source_target_pairs={{0,6},{1,7},{2,4},{3,5},{4,2},{5,3},{6,0},{7,1},{8,14},{9,15},{10,... | collective-permute-start | bytes 368648 | tf_op jit(solution)/shard_map/ppermute | solution.py:370
  23.6 4.9 %collective-permute-start.7 = (bf16[120,512]{1,0:T(8,128)(2,1)S(1)}, bf16[120,512]{1,0:T(8,128)(2,1)S(1)}, u32[]{:S(2)}, u32[]{:S(2)}) collective-permute-start(bf16[120,512]{1,0:T(8,128)(2,1)S(1)} %first_rows.1.refs_2_), channel_id=1, source_target_pairs={{0,16},{16,0},{1,17},{17,1},{2,18},{18,2},{3,19},{19,3},{4,20},{20... | collective-permute-start | bytes 368648 | tf_op jit(solution)/shard_map/ppermute | solution.py:423
  28.6 1.9 %collective-permute-start.8 = (bf16[480,512]{1,0:T(8,128)(2,1)S(1)}, bf16[480,512]{1,0:T(8,128)(2,1)S(1)}, u32[]{:S(2)}, u32[]{:S(2)}) collective-permute-start(bf16[480,512]{1,0:T(8,128)(2,1)S(1)} %hand_on.1.refs_8_), channel_id=1, source_target_pairs={{0,1},{1,0},{2,3},{3,2},{4,5},{5,4},{6,7},{7,6},{8,9},{9,8},{10,11... | collective-permute-start | bytes 1474568 | tf_op jit(solution)/shard_map/ppermute | solution.py:426
  28.7 11.7 %copy-start = (s32[160,2]{0,1:T(2,128)S(1)}, s32[160,2]{0,1:T(2,128)}, u32[]{:S(2)}) copy-start(s32[160,2]{0,1:T(2,128)} %param.8) | copy-start | bytes 3844
  28.7 11.7 %copy-start.1 = (bf16[160,2]{0,1:T(2,128)(2,1)S(1)}, bf16[160,2]{0,1:T(2,128)(2,1)}, u32[]{:S(2)}) copy-start(bf16[160,2]{0,1:T(2,128)(2,1)} %param.7) | copy-start | bytes 1924
  28.7 11.7 %collective-permute-start.9 = (bf16[360,512]{1,0:T(8,128)(2,1)S(1)}, bf16[360,512]{1,0:T(8,128)(2,1)S(1)}, u32[]{:S(2)}, u32[]{:S(2)}) collective-permute-start(bf16[360,512]{1,0:T(8,128)(2,1)S(1)} %arrived_rows.1.refs_1_.refs_7_), channel_id=1, source_target_pairs={{0,16},{16,0},{1,17},{17,1},{2,18},{18,2},{3,19},{19,3},{4,20},{20... | collective-permute-start | bytes 1105928 | tf_op jit(solution)/shard_map/ppermute | solution.py:429
  34.2 20.6 %all-to-all-start = ((bf16[16,32,512]{2,1,0:T(8,128)(2,1)}), bf16[16,32,512]{2,1,0:T(8,128)(2,1)}, u32[]{:S(2)}, u32[]{:S(2)}) async-start(bf16[16,32,512]{2,1,0:T(8,128)(2,1)} %late_backward.1), calls=%async_computation | async-start | bytes 1048576 | tf_op jit(solution)/shard_map/all_to_all | solution.py:448
  38.9 13.5 %collective-permute-start.10 = (bf16[480,512]{1,0:T(8,128)(2,1)S(1)}, bf16[480,512]{1,0:T(8,128)(2,1)S(1)}, u32[]{:S(2)}, u32[]{:S(2)}) collective-permute-start(bf16[480,512]{1,0:T(8,128)(2,1)S(1)} %collective-permute-done.8.refs_0_.refs_3_), channel_id=1, source_target_pairs={{0,16},{16,0},{1,17},{17,1},{2,18},{18,2},{3,19},{19,3},{4,20},{20... | collective-permute-start | bytes 1474568 | tf_op jit(solution)/shard_map/ppermute | solution.py:430

commit v17 on v15

--- a/solution.py
+++ b/solution.py
@@ -134,8 +134,11 @@
             out_ref[(2 * i + 1) * tight : (2 * i + 2) * tight, :] = grads[here, :]
 
 
-def steps_of(size, block):
+def steps_of(size, block, begun=False):
     half = block // 2
+    if begun and size > block:
+        last = size - half // 2
+        return [(at, min(block, last - at)) for at in range(0, last, block)] + [(last, half // 2)]
     return [(0, half)] + [(at, block) for at in range(half, size - half, block)] + [(size - half, half)]
 
 
@@ -152,7 +155,8 @@
         if number == len(self.steps):
             return
         at, size = self.steps[number]
-        to, of = pl.ds(at, size), pl.ds(pl.multiple_of(self.base + at, size), size)
+        unit = math.gcd(at, size)
+        to, of = pl.ds(at, size), pl.ds(pl.multiple_of(self.base + at, unit), size)
         self.copies.append([
             pltpu.make_async_copy(src.at[0, of, :], dst.at[to, :], self.sems.at[2 * number + i])
             for i, (src, dst) in enumerate(self.pairs)
@@ -269,7 +273,7 @@
     notes_out = None if begun else take(3)
     up_ref, down_ref = weights if begun else take(2)
     rows_ref, grads_ref, sems, *kept = refs
-    steps = steps_of(share, block)
+    steps = steps_of(share, block, begun)
     if not begun:
         fetch = Fetch(*weights, up_ref, down_ref, sems, lax.axis_index("rep") * share, steps)
     for i, ref in enumerate(row_refs):
@@ -453,7 +457,7 @@
             shape((share, feat), BF16),
         ]
         grad = pltpu.HBM((1, share, feat), BF16) if ended else shape((1, share, feat), F32)
-        steps = len(steps_of(share, part))
+        steps = len(steps_of(share, part, begun))
         scratch = [
             pltpu.VMEM((number, feat), BF16),
             pltpu.VMEM((number, feat), BF16),

time: 56.2 us -> 56.1 us (level)
  no operation moved by 1% of the time
where the time goes in v17:
time: 56.1 us; the launch traced here: 55.9 us
  starting transfers between devices  24.1 us (43%)
  Pallas kernels  18.6 us (33%)
  waiting for transfers between devices  12.4 us (22%)
  between operations  0.75 us (1%)
    ppermute x7, starting transfers between devices, local(): lax.ppermute(out[k], 'exp', hops_to(chips, k))  15.9 us
    pallas_call x8, Pallas kernels, call(): pl.pallas_call(body, name=name, out_shape=outs, in_specs=in_specs, out_sp...  14.9 us
    ppermute x7, waiting for transfers between devices, local(): lax.ppermute(out[k], 'exp', hops_to(chips, k))  5.38 us
    all_to_all x1, starting transfers between devices, local(): back = lax.all_to_all(back, 'exp', split_axis=0, concat_axis=0, tiled=True)  5.09 us
    ppermute x1, waiting for transfers between devices, local(): seconds = [lax.ppermute(sibling, 'rep', hops) for hops in around]  4.75 us
    pallas_call x1, Pallas kernels, local(): pl.pallas_call(functools.partial(late_back_kernel, cap, pad, tight, block...  3.71 us
    ppermute x1, waiting for transfers between devices, local(): firsts = [lax.ppermute(arrived, 'rep', hops) for hops in around]  2.02 us
    ppermute x1, starting transfers between devices, local(): firsts = [lax.ppermute(arrived, 'rep', hops) for hops in around]  1.56 us
  transfers between devices with their start and end apart: 11, of which 6 were waited for; matrix products, arithmetic and copies ran while one was open for 0% of the time, Pallas kernels for 29%

profile of v17, /device:TPU:0, one launch (start us, length us, event | category | flops | bytes accessed | tf_op | source)
XLA Modules:
  0.0 55.9 jit_solution(2985984252311799192)
XLA Ops:
  0.6 1.6 %slots.1 = (bf16[120,512]{1,0:T(8,128)(2,1)S(1)}, bf16[120,512]{1,0:T(8,128)(2,1)S(1)}, bf16[120,512]{1,0:T(8,128)(2,1)S(1)}, bf16[120,512]{1,0:T(8,128)(2,1)S(1...) custom-call(s32[2,160]{1,0:T(2,128)} %bitcast.3, ...), custom_call_target="tpu_custom_call" | custom-call | flops 167772160 | bytes 1312640 | tf_op jit(solution)/shard_map/slots/pallas_call | solution.py:36
  2.2 4.1 %collective-permute-start = (bf16[120,512]{1,0:T(8,128)(2,1)S(1)}, bf16[120,512]{1,0:T(8,128)(2,1)S(1)}, u32[]{:S(2)}, u32[]{:S(2)}) collective-permute-start(bf16[120,512]{1,0:T(8,128)(2,1)S(1)} %get-tuple-element.26), channel_id=1, source_target_pairs={{0,8},{1,9},{2,10},{3,11},{4,12},{5,13},{6,14},{7,15},{8,0},{9,1},... | collective-permute-start | bytes 368648 | tf_op jit(solution)/shard_map/ppermute | solution.py:372
  6.3 1.5 %collective-permute-start.1 = (bf16[120,512]{1,0:T(8,128)(2,1)S(1)}, bf16[120,512]{1,0:T(8,128)(2,1)S(1)}, u32[]{:S(2)}, u32[]{:S(2)}) collective-permute-start(bf16[120,512]{1,0:T(8,128)(2,1)S(1)} %get-tuple-element.27), channel_id=1, source_target_pairs={{0,2},{1,3},{2,0},{3,1},{4,6},{5,7},{6,4},{7,5},{8,10},{9,11},{10,... | collective-permute-start | bytes 368648 | tf_op jit(solution)/shard_map/ppermute | solution.py:372
  7.9 0.0 collective-permute-start.2
  7.9 1.8 %collective-permute-start.3 = (bf16[120,512]{1,0:T(8,128)(2,1)S(1)}, bf16[120,512]{1,0:T(8,128)(2,1)S(1)}, u32[]{:S(2)}, u32[]{:S(2)}) collective-permute-start(bf16[120,512]{1,0:T(8,128)(2,1)S(1)} %get-tuple-element.29), channel_id=1, source_target_pairs={{0,4},{1,5},{2,6},{3,7},{4,0},{5,1},{6,2},{7,3},{8,12},{9,13},{10,... | collective-permute-start | bytes 368648 | tf_op jit(solution)/shard_map/ppermute | solution.py:372
  9.7 2.5 %collective-permute-start.4 = (bf16[120,512]{1,0:T(8,128)(2,1)S(1)}, bf16[120,512]{1,0:T(8,128)(2,1)S(1)}, u32[]{:S(2)}, u32[]{:S(2)}) collective-permute-start(bf16[120,512]{1,0:T(8,128)(2,1)S(1)} %get-tuple-element.30), channel_id=1, source_target_pairs={{0,12},{1,13},{2,14},{3,15},{4,8},{5,9},{6,10},{7,11},{8,4},{9,5},... | collective-permute-start | bytes 368648 | tf_op jit(solution)/shard_map/ppermute | solution.py:372
  12.2 2.2 %fetch_weights.1 = (bf16[2048,512]{1,0:T(8,128)(2,1)S(1)}, bf16[2048,512]{1,0:T(8,128)(2,1)S(1)}) custom-call(bf16[1,2048,512]{2,1,0:T(8,128)(2,1)} %refs_3_.1, bf16[1,2048,512]{2,1,0:T(8,128)(2,1)} %refs_4_.1), custom_call_target="tpu_custom_call" | custom-call | tf_op jit(solution)/shard_map/fetch_weights/pallas_call | solution.py:36
  14.4 1.9 %collective-permute-done.refs_1_ = bf16[120,512]{1,0:T(8,128)(2,1)S(1)} collective-permute-done((bf16[120,512]{1,0:T(8,128)(2,1)S(1)}, bf16[120,512]{1,0:T(8,128)(2,1)S(1)}, u32[]{:S(2)}, u32[]{:S(2)}) %collective-permute-start) | collective-permute-done | bytes 122912 | tf_op jit(solution)/shard_map/ppermute | solution.py:372
  16.3 5.9 %collective-permute-start.5 = (bf16[120,512]{1,0:T(8,128)(2,1)S(1)}, bf16[120,512]{1,0:T(8,128)(2,1)S(1)}, u32[]{:S(2)}, u32[]{:S(2)}) collective-permute-start(bf16[120,512]{1,0:T(8,128)(2,1)S(1)} %get-tuple-element.31), channel_id=1, source_target_pairs={{0,14},{1,15},{2,12},{3,13},{4,10},{5,11},{6,8},{7,9},{8,6},{9,7},... | collective-permute-start | bytes 368648 | tf_op jit(solution)/shard_map/ppermute | solution.py:372
  22.2 0.0 collective-permute-done.1.refs_2_
  22.2 0.0 collective-permute-start.6
  22.2 1.4 %collective-permute-done.2.refs_3_ = bf16[120,512]{1,0:T(8,128)(2,1)S(1)} collective-permute-done((bf16[120,512]{1,0:T(8,128)(2,1)S(1)}, bf16[120,512]{1,0:T(8,128)(2,1)S(1)}, u32[]{:S(2)}, u32[]{:S(2)}) %collective-permute-start.2) | collective-permute-done | bytes 122912 | tf_op jit(solution)/shard_map/ppermute | solution.py:372
  23.6 0.0 collective-permute-done.3.refs_4_
  23.6 2.3 %early_backward.1.refs_8_.refs_4_ = bf16[5,32,512]{2,1,0:T(8,128)(2,1)S(1)} custom-call(bf16[120,512]{1,0:T(8,128)(2,1)S(1)} %get-tuple-element.25.refs_0_, bf16[120,512]{1,0:T(8,128)(2,1)S(1)} %collective-permute-done.refs_1_, bf16[120,512]{1,0:T(8,128)(2,1)S(1)} %collective-permute-done.1.refs_2_, bf16[120,512]{1,0:T(8,128)(2,1)S(1)} %collective-permute-done.2.refs_3_, ...), custom_call_target="tpu_custom_call" | custom-call | flops 1610612736 | bytes 4972544 | tf_op jit(solution)/shard_map/early_backward/pallas_call | solution.py:36
  25.9 0.0 collective-permute-done.4.refs_5_.refs_0_
  25.9 0.0 collective-permute-done.5.refs_6_.refs_1_
  25.9 2.1 %collective-permute-done.6.refs_7_.refs_2_ = bf16[120,512]{1,0:T(8,128)(2,1)S(1)} collective-permute-done((bf16[120,512]{1,0:T(8,128)(2,1)S(1)}, bf16[120,512]{1,0:T(8,128)(2,1)S(1)}, u32[]{:S(2)}, u32[]{:S(2)}) %collective-permute-start.6) | collective-permute-done | bytes 122912 | tf_op jit(solution)/shard_map/ppermute | solution.py:372
  28.0 0.1 hand_on.1.refs_8_
  28.1 0.1 collective-permute-start.7
  28.2 0.1 arrived_rows.1.refs_1_.refs_7_
  28.2 0.0 copy-start
  28.2 0.0 copy-start.1
  28.3 1.6 %collective-permute-start.8 = (bf16[480,512]{1,0:T(8,128)(2,1)S(1)}, bf16[480,512]{1,0:T(8,128)(2,1)S(1)}, u32[]{:S(2)}, u32[]{:S(2)}) collective-permute-start(bf16[480,512]{1,0:T(8,128)(2,1)S(1)} %arrived_rows.1.refs_1_.refs_7_), channel_id=1, source_target_pairs={{0,16},{16,0},{1,17},{17,1},{2,18},{18,2},{3,19},{19,3},{4,20},{20... | collective-permute-start | bytes 1474568 | tf_op jit(solution)/shard_map/ppermute | solution.py:426
  29.8 0.2 collective-permute-done.7.refs_0_.refs_3_
  30.0 1.5 %collective-permute-start.9 = (bf16[480,512]{1,0:T(8,128)(2,1)S(1)}, bf16[480,512]{1,0:T(8,128)(2,1)S(1)}, u32[]{:S(2)}, u32[]{:S(2)}) collective-permute-start(bf16[480,512]{1,0:T(8,128)(2,1)S(1)} %collective-permute-done.7.refs_0_.refs_3_), channel_id=1, source_target_pairs={{0,16},{16,0},{1,17},{17,1},{2,18},{18,2},{3,19},{19,3},{4,20},{20... | collective-permute-start | bytes 1474568 | tf_op jit(solution)/shard_map/ppermute | solution.py:427
  31.5 3.7 %late_backward.1 = bf16[16,32,512]{2,1,0:T(8,128)(2,1)} custom-call(bf16[120,512]{1,0:T(8,128)(2,1)S(1)} %collective-permute-done.4.refs_5_.refs_0_, bf16[120,512]{1,0:T(8,128)(2,1)S(1)} %collective-permute-done.5.refs_6_.refs_1_, bf16[120,512]{1,0:T(8,128)(2,1)S(1)} %collective-permute-done.6.refs_7_.refs_2_, ...), custom_call_target="tpu_custom_call" | custom-call | flops 99999997952 | bytes 4194304 | tf_op jit(solution)/shard_map/late_backward/pallas_call | solution.py:429
  35.2 5.1 %all-to-all-start = ((bf16[16,32,512]{2,1,0:T(8,128)(2,1)}), bf16[16,32,512]{2,1,0:T(8,128)(2,1)S(1)}, u32[]{:S(2)}, u32[]{:S(2)}) async-start(bf16[16,32,512]{2,1,0:T(8,128)(2,1)} %late_backward.1), calls=%async_computation | async-start | bytes 1048576 | tf_op jit(solution)/shard_map/all_to_all | solution.py:445
  40.3 2.0 %collective-permute-done.8.refs_2_ = bf16[480,512]{1,0:T(8,128)(2,1)S(1)} collective-permute-done((bf16[480,512]{1,0:T(8,128)(2,1)S(1)}, bf16[480,512]{1,0:T(8,128)(2,1)S(1)}, u32[]{:S(2)}, u32[]{:S(2)}) %collective-permute-start.8) | collective-permute-done | bytes 491552 | tf_op jit(solution)/shard_map/ppermute | solution.py:426
  42.3 0.0 copy-done
  42.3 0.0 copy-done.1
  42.3 5.4 %first_weights.1 = (f32[1,1024,512]{2,1,0:T(8,128)S(1)}, f32[1,1024,512]{2,1,0:T(8,128)S(1)}, bf16[160,512]{1,0:T(8,128)(2,1)S(1)}, f32[2,16,160]{2,1,0:T(8,128)...) custom-call(bf16[480,512]{1,0:T(8,128)(2,1)S(1)} %collective-permute-done.7.ref, ...), custom_call_target="tpu_custom_call" | custom-call | tf_op jit(solution)/shard_map/first_weights/pallas_call | solution.py:36
  47.7 4.8 %collective-permute-done.9.refs_0_ = bf16[480,512]{1,0:T(8,128)(2,1)S(1)} collective-permute-done((bf16[480,512]{1,0:T(8,128)(2,1)S(1)}, bf16[480,512]{1,0:T(8,128)(2,1)S(1)}, u32[]{:S(2)}, u32[]{:S(2)}) %collective-permute-start.9) | collective-permute-done | bytes 491552 | tf_op jit(solution)/shard_map/ppermute | solution.py:427
  52.5 2.4 %last_weights.1 = (bf16[1,1024,512]{2,1,0:T(8,128)(2,1)}, bf16[1,1024,512]{2,1,0:T(8,128)(2,1)}) custom-call(bf16[480,512]{1,0:T(8,128)(2,1)S(1)} %collective-permute-done.9.refs_0_, bf16[1024,512]{1,0:T(8,128)(2,1)S(1)} %get-tuple-element.40.refs_1_, bf16[1024,512]{1,0:T(8,128)(2,1)S(1)} %get-tuple-element.41.refs_2_, ...), custom_call_target="tpu_custom_call" | custom-call | flops 99999997952 | bytes 8880128 | tf_op jit(solution)/shard_map/last_weights/pallas_call | solution.py:36
  54.9 0.0 all-to-all-done.back_ref
  54.9 0.9 %combine.1 = (bf16[160,512]{1,0:T(8,128)(2,1)}, bf16[2,160]{1,0:T(2,128)(2,1)}) custom-call(bf16[160,512]{1,0:T(8,128)(2,1)S(1)} %get-tuple-element.35.pick_ref, f32[2,16,160]{2,1,0:T(8,128)S(1)} %get-tuple-element.36.hot_ref, bf16[2,128,160]{2,1,0:T(8,128)(2,1)S(1)} %get-tuple-element.37.spot_ref, bf16[16,32,512]{2,1,0:T(8,128)(2,1)S(1)} %all-to-all-done.back_ref), custom_call_target="tpu_custom_call" | custom-call | flops 167772160 | bytes 955008 | tf_op jit(solution)/shard_map/combine/pallas_call | solution.py:36
Async XLA Ops:
  2.2 14.1 %collective-permute-start = (bf16[120,512]{1,0:T(8,128)(2,1)S(1)}, bf16[120,512]{1,0:T(8,128)(2,1)S(1)}, u32[]{:S(2)}, u32[]{:S(2)}) collective-permute-start(bf16[120,512]{1,0:T(8,128)(2,1)S(1)} %get-tuple-element.26), channel_id=1, source_target_pairs={{0,8},{1,9},{2,10},{3,11},{4,12},{5,13},{6,14},{7,15},{8,0},{9,1},... | collective-permute-start | bytes 368648 | tf_op jit(solution)/shard_map/ppermute | solution.py:372
  6.3 15.9 %collective-permute-start.1 = (bf16[120,512]{1,0:T(8,128)(2,1)S(1)}, bf16[120,512]{1,0:T(8,128)(2,1)S(1)}, u32[]{:S(2)}, u32[]{:S(2)}) collective-permute-start(bf16[120,512]{1,0:T(8,128)(2,1)S(1)} %get-tuple-element.27), channel_id=1, source_target_pairs={{0,2},{1,3},{2,0},{3,1},{4,6},{5,7},{6,4},{7,5},{8,10},{9,11},{10,... | collective-permute-start | bytes 368648 | tf_op jit(solution)/shard_map/ppermute | solution.py:372
  7.9 15.8 %collective-permute-start.2 = (bf16[120,512]{1,0:T(8,128)(2,1)S(1)}, bf16[120,512]{1,0:T(8,128)(2,1)S(1)}, u32[]{:S(2)}, u32[]{:S(2)}) collective-permute-start(bf16[120,512]{1,0:T(8,128)(2,1)S(1)} %get-tuple-element.28), channel_id=1, source_target_pairs={{0,10},{1,11},{2,8},{3,9},{4,14},{5,15},{6,12},{7,13},{8,2},{9,3},... | collective-permute-start | bytes 368648 | tf_op jit(solution)/shard_map/ppermute | solution.py:372
  7.9 15.8 %collective-permute-start.3 = (bf16[120,512]{1,0:T(8,128)(2,1)S(1)}, bf16[120,512]{1,0:T(8,128)(2,1)S(1)}, u32[]{:S(2)}, u32[]{:S(2)}) collective-permute-start(bf16[120,512]{1,0:T(8,128)(2,1)S(1)} %get-tuple-element.29), channel_id=1, source_target_pairs={{0,4},{1,5},{2,6},{3,7},{4,0},{5,1},{6,2},{7,3},{8,12},{9,13},{10,... | collective-permute-start | bytes 368648 | tf_op jit(solution)/shard_map/ppermute | solution.py:372
  9.7 16.2 %collective-permute-start.4 = (bf16[120,512]{1,0:T(8,128)(2,1)S(1)}, bf16[120,512]{1,0:T(8,128)(2,1)S(1)}, u32[]{:S(2)}, u32[]{:S(2)}) collective-permute-start(bf16[120,512]{1,0:T(8,128)(2,1)S(1)} %get-tuple-element.30), channel_id=1, source_target_pairs={{0,12},{1,13},{2,14},{3,15},{4,8},{5,9},{6,10},{7,11},{8,4},{9,5},... | collective-permute-start | bytes 368648 | tf_op jit(solution)/shard_map/ppermute | solution.py:372
  16.3 9.6 %collective-permute-start.5 = (bf16[120,512]{1,0:T(8,128)(2,1)S(1)}, bf16[120,512]{1,0:T(8,128)(2,1)S(1)}, u32[]{:S(2)}, u32[]{:S(2)}) collective-permute-start(bf16[120,512]{1,0:T(8,128)(2,1)S(1)} %get-tuple-element.31), channel_id=1, source_target_pairs={{0,14},{1,15},{2,12},{3,13},{4,10},{5,11},{6,8},{7,9},{8,6},{9,7},... | collective-permute-start | bytes 368648 | tf_op jit(solution)/shard_map/ppermute | solution.py:372
  22.2 5.8 %collective-permute-start.6 = (bf16[120,512]{1,0:T(8,128)(2,1)S(1)}, bf16[120,512]{1,0:T(8,128)(2,1)S(1)}, u32[]{:S(2)}, u32[]{:S(2)}) collective-permute-start(bf16[120,512]{1,0:T(8,128)(2,1)S(1)} %get-tuple-element.32), channel_id=1, source_target_pairs={{0,6},{1,7},{2,4},{3,5},{4,2},{5,3},{6,0},{7,1},{8,14},{9,15},{10,... | collective-permute-start | bytes 368648 | tf_op jit(solution)/shard_map/ppermute | solution.py:372
  28.1 1.9 %collective-permute-start.7 = (bf16[480,512]{1,0:T(8,128)(2,1)S(1)}, bf16[480,512]{1,0:T(8,128)(2,1)S(1)}, u32[]{:S(2)}, u32[]{:S(2)}) collective-permute-start(bf16[480,512]{1,0:T(8,128)(2,1)S(1)} %hand_on.1.refs_8_), channel_id=1, source_target_pairs={{0,1},{1,0},{2,3},{3,2},{4,5},{5,4},{6,7},{7,6},{8,9},{9,8},{10,11... | collective-permute-start | bytes 1474568 | tf_op jit(solution)/shard_map/ppermute | solution.py:424
  28.2 14.1 %copy-start = (s32[160,2]{0,1:T(2,128)S(1)}, s32[160,2]{0,1:T(2,128)}, u32[]{:S(2)}) copy-start(s32[160,2]{0,1:T(2,128)} %param.8) | copy-start | bytes 3844
  28.2 14.1 %copy-start.1 = (bf16[160,2]{0,1:T(2,128)(2,1)S(1)}, bf16[160,2]{0,1:T(2,128)(2,1)}, u32[]{:S(2)}) copy-start(bf16[160,2]{0,1:T(2,128)(2,1)} %param.7) | copy-start | bytes 1924
  28.3 14.1 %collective-permute-start.8 = (bf16[480,512]{1,0:T(8,128)(2,1)S(1)}, bf16[480,512]{1,0:T(8,128)(2,1)S(1)}, u32[]{:S(2)}, u32[]{:S(2)}) collective-permute-start(bf16[480,512]{1,0:T(8,128)(2,1)S(1)} %arrived_rows.1.refs_1_.refs_7_), channel_id=1, source_target_pairs={{0,16},{16,0},{1,17},{17,1},{2,18},{18,2},{3,19},{19,3},{4,20},{20... | collective-permute-start | bytes 1474568 | tf_op jit(solution)/shard_map/ppermute | solution.py:426
  30.0 22.5 %collective-permute-start.9 = (bf16[480,512]{1,0:T(8,128)(2,1)S(1)}, bf16[480,512]{1,0:T(8,128)(2,1)S(1)}, u32[]{:S(2)}, u32[]{:S(2)}) collective-permute-start(bf16[480,512]{1,0:T(8,128)(2,1)S(1)} %collective-permute-done.7.refs_0_.refs_3_), channel_id=1, source_target_pairs={{0,16},{16,0},{1,17},{17,1},{2,18},{18,2},{3,19},{19,3},{4,20},{20... | collective-permute-start | bytes 1474568 | tf_op jit(solution)/shard_map/ppermute | solution.py:427
  35.2 19.7 %all-to-all-start = ((bf16[16,32,512]{2,1,0:T(8,128)(2,1)}), bf16[16,32,512]{2,1,0:T(8,128)(2,1)S(1)}, u32[]{:S(2)}, u32[]{:S(2)}) async-start(bf16[16,32,512]{2,1,0:T(8,128)(2,1)} %late_backward.1), calls=%async_computation | async-start | bytes 1048576 | tf_op jit(solution)/shard_map/all_to_all | solution.py:445

commit v18 on v17

--- a/solution.py
+++ b/solution.py
@@ -11,7 +11,7 @@
 
 F32 = jnp.float32
 BF16 = jnp.bfloat16
-SMALL, MEDIUM, LARGE = 8 << 20, 12 << 20, 24 << 20
+SMALL, MEDIUM, LARGE = 8 << 20, 12 << 20, 16 << 20
 AHEAD = 10**11
 IN_HBM = pl.BlockSpec(memory_space=pltpu.HBM)
 IN_VMEM = pl.BlockSpec(memory_space=pltpu.VMEM)
@@ -72,17 +72,18 @@
     return 2 * ((me // 2 - k + chips) % chips) + (me + core) % 2
 
 
-def slots_of(pieces, number_of):
+def before_of(rows):
+    first = lax.broadcasted_iota(jnp.int32, (rows, rows), 0)
+    second = lax.broadcasted_iota(jnp.int32, (rows, rows), 1)
+    return jnp.where(first < second, 1.0, 0.0).astype(BF16)
+
+
+def slots_of(pieces, number_of, before=None):
     rows = pieces.shape[1]
     number = lax.broadcasted_iota(jnp.int32, (number_of, rows), 0)
     hot = [number == pieces[k : k + 1, :] for k in range(2)]
     as_num = [jnp.where(h, 1.0, 0.0).astype(F32) for h in hot]
-    before = jnp.where(
-        lax.broadcasted_iota(jnp.int32, (rows, rows), 0)
-        < lax.broadcasted_iota(jnp.int32, (rows, rows), 1),
-        1.0,
-        0.0,
-    ).astype(BF16)
+    before = before_of(rows) if before is None else before
     count = dot(jnp.concatenate(as_num, axis=0).astype(BF16), before, 1, 0)
     total = jnp.sum(as_num[0], axis=1, keepdims=True)
     place = [count[:number_of], count[number_of:] + total]
@@ -113,11 +114,12 @@
     ]
     for copy in copies:
         copy.start()
+    before = before_of(tok_hbm.shape[0])
     copies[0].wait()
     copies[1].wait()
     pieces = pieces_of(routes_ref[...], chips)
     gates = gates_ref[...].astype(F32)
-    _, slot = slots_of(pieces, 2 * chips)
+    _, slot = slots_of(pieces, 2 * chips, before)
     pick = picks_of(pieces, slot, 2 * chips, pad)
     plain = jnp.where(pick[0] | pick[1], 1.0, 0.0).astype(BF16)
     scaled = (
@@ -276,6 +278,10 @@
     steps = steps_of(share, block, begun)
     if not begun:
         fetch = Fetch(*weights, up_ref, down_ref, sems, lax.axis_index("rep") * share, steps)
+    if len(row_refs) == 1:
+        size = row_refs[0].shape[0] // 2
+        rows_ref, grads_ref = row_refs[0].at[0:size, :], row_refs[0].at[size : 2 * size, :]
+        row_refs = []
     for i, ref in enumerate(row_refs):
         size = ref.shape[0] // 2
         rows_ref[i * size : (i + 1) * size, :] = ref[:size, :]
@@ -480,7 +486,7 @@
 
     joined = [sibling, arrived, *firsts]
     *sums, pick, hot, spot, up_v, down_v = weights_call(
-        "first_weights", joined, [w_up, w_down], [], not seconds, 0
+        "first_weights", joined, [w_up, w_down], [], not seconds, AHEAD
     )
     if seconds:
         sums = weights_call(

time: 56.1 us -> 57.2 us (1.020)
  Pallas kernels: 18.6 us -> 19.6 us
    pallas_call x8, Pallas kernels: 14.9 us -> 16 us  [call(): pl.pallas_call(body, name=name, out_shape=outs, in_specs=in_specs, out_sp...]
  transfers between devices with their start and end apart: 11 -> 11, of which waited for: 6 -> 6; matrix products, arithmetic and copies ran while one was open for 0% -> 0% of each run, Pallas kernels for 29% -> 28%
where the time goes in v18:
time: 57.2 us; the launch traced here: 56.9 us
  starting transfers between devices  24.2 us (42%)
  Pallas kernels  19.6 us (34%)
  waiting for transfers between devices  12.3 us (22%)
  between operations  0.75 us (1%)
    pallas_call x8, Pallas kernels, call(): pl.pallas_call(body, name=name, out_shape=outs, in_specs=in_specs, out_sp...  16 us
    ppermute x7, starting transfers between devices, local(): lax.ppermute(out[k], 'exp', hops_to(chips, k))  15.9 us
    ppermute x7, waiting for transfers between devices, local(): lax.ppermute(out[k], 'exp', hops_to(chips, k))  5.38 us
    all_to_all x1, starting transfers between devices, local(): back = lax.all_to_all(back, 'exp', split_axis=0, concat_axis=0, tiled=True)  5.16 us
    ppermute x1, waiting for transfers between devices, local(): seconds = [lax.ppermute(sibling, 'rep', hops) for hops in around]  5.08 us
    pallas_call x1, Pallas kernels, local(): pl.pallas_call(functools.partial(late_back_kernel, cap, pad, tight, block...  3.66 us
    ppermute x1, waiting for transfers between devices, local(): firsts = [lax.ppermute(arrived, 'rep', hops) for hops in around]  1.61 us
    ppermute x1, starting transfers between devices, local(): firsts = [lax.ppermute(arrived, 'rep', hops) for hops in around]  1.56 us
  transfers between devices with their start and end apart: 11, of which 6 were waited for; matrix products, arithmetic and copies ran while one was open for 0% of the time, Pallas kernels for 28%

profile of v18, /device:TPU:0, one launch (start us, length us, event | category | flops | bytes accessed | tf_op | source)
XLA Modules:
  0.0 56.9 jit_solution(7996202599430010165)
XLA Ops:
  0.6 1.6 %slots.1 = (bf16[120,512]{1,0:T(8,128)(2,1)S(1)}, bf16[120,512]{1,0:T(8,128)(2,1)S(1)}, bf16[120,512]{1,0:T(8,128)(2,1)S(1)}, bf16[120,512]{1,0:T(8,128)(2,1)S(1...) custom-call(s32[2,160]{1,0:T(2,128)} %bitcast.3, ...), custom_call_target="tpu_custom_call" | custom-call | flops 167772160 | bytes 1312640 | tf_op jit(solution)/shard_map/slots/pallas_call | solution.py:36
  2.2 4.1 %collective-permute-start = (bf16[120,512]{1,0:T(8,128)(2,1)S(1)}, bf16[120,512]{1,0:T(8,128)(2,1)S(1)}, u32[]{:S(2)}, u32[]{:S(2)}) collective-permute-start(bf16[120,512]{1,0:T(8,128)(2,1)S(1)} %get-tuple-element.26), channel_id=1, source_target_pairs={{0,8},{1,9},{2,10},{3,11},{4,12},{5,13},{6,14},{7,15},{8,0},{9,1},... | collective-permute-start | bytes 368648 | tf_op jit(solution)/shard_map/ppermute | solution.py:378
  6.3 1.5 %collective-permute-start.1 = (bf16[120,512]{1,0:T(8,128)(2,1)S(1)}, bf16[120,512]{1,0:T(8,128)(2,1)S(1)}, u32[]{:S(2)}, u32[]{:S(2)}) collective-permute-start(bf16[120,512]{1,0:T(8,128)(2,1)S(1)} %get-tuple-element.27), channel_id=1, source_target_pairs={{0,2},{1,3},{2,0},{3,1},{4,6},{5,7},{6,4},{7,5},{8,10},{9,11},{10,... | collective-permute-start | bytes 368648 | tf_op jit(solution)/shard_map/ppermute | solution.py:378
  7.8 0.0 collective-permute-start.2
  7.9 1.8 %collective-permute-start.3 = (bf16[120,512]{1,0:T(8,128)(2,1)S(1)}, bf16[120,512]{1,0:T(8,128)(2,1)S(1)}, u32[]{:S(2)}, u32[]{:S(2)}) collective-permute-start(bf16[120,512]{1,0:T(8,128)(2,1)S(1)} %get-tuple-element.29), channel_id=1, source_target_pairs={{0,4},{1,5},{2,6},{3,7},{4,0},{5,1},{6,2},{7,3},{8,12},{9,13},{10,... | collective-permute-start | bytes 368648 | tf_op jit(solution)/shard_map/ppermute | solution.py:378
  9.7 2.5 %collective-permute-start.4 = (bf16[120,512]{1,0:T(8,128)(2,1)S(1)}, bf16[120,512]{1,0:T(8,128)(2,1)S(1)}, u32[]{:S(2)}, u32[]{:S(2)}) collective-permute-start(bf16[120,512]{1,0:T(8,128)(2,1)S(1)} %get-tuple-element.30), channel_id=1, source_target_pairs={{0,12},{1,13},{2,14},{3,15},{4,8},{5,9},{6,10},{7,11},{8,4},{9,5},... | collective-permute-start | bytes 368648 | tf_op jit(solution)/shard_map/ppermute | solution.py:378
  12.2 2.2 %fetch_weights.1 = (bf16[2048,512]{1,0:T(8,128)(2,1)S(1)}, bf16[2048,512]{1,0:T(8,128)(2,1)S(1)}) custom-call(bf16[1,2048,512]{2,1,0:T(8,128)(2,1)} %refs_3_.1, bf16[1,2048,512]{2,1,0:T(8,128)(2,1)} %refs_4_.1), custom_call_target="tpu_custom_call" | custom-call | tf_op jit(solution)/shard_map/fetch_weights/pallas_call | solution.py:36
  14.4 1.9 %collective-permute-done.refs_1_ = bf16[120,512]{1,0:T(8,128)(2,1)S(1)} collective-permute-done((bf16[120,512]{1,0:T(8,128)(2,1)S(1)}, bf16[120,512]{1,0:T(8,128)(2,1)S(1)}, u32[]{:S(2)}, u32[]{:S(2)}) %collective-permute-start) | collective-permute-done | bytes 122912 | tf_op jit(solution)/shard_map/ppermute | solution.py:378
  16.3 5.9 %collective-permute-start.5 = (bf16[120,512]{1,0:T(8,128)(2,1)S(1)}, bf16[120,512]{1,0:T(8,128)(2,1)S(1)}, u32[]{:S(2)}, u32[]{:S(2)}) collective-permute-start(bf16[120,512]{1,0:T(8,128)(2,1)S(1)} %get-tuple-element.31), channel_id=1, source_target_pairs={{0,14},{1,15},{2,12},{3,13},{4,10},{5,11},{6,8},{7,9},{8,6},{9,7},... | collective-permute-start | bytes 368648 | tf_op jit(solution)/shard_map/ppermute | solution.py:378
  22.2 0.0 collective-permute-done.1.refs_2_
  22.2 0.0 collective-permute-start.6
  22.2 1.4 %collective-permute-done.2.refs_3_ = bf16[120,512]{1,0:T(8,128)(2,1)S(1)} collective-permute-done((bf16[120,512]{1,0:T(8,128)(2,1)S(1)}, bf16[120,512]{1,0:T(8,128)(2,1)S(1)}, u32[]{:S(2)}, u32[]{:S(2)}) %collective-permute-start.2) | collective-permute-done | bytes 122912 | tf_op jit(solution)/shard_map/ppermute | solution.py:378
  23.6 0.0 collective-permute-done.3.refs_4_
  23.6 2.3 %early_backward.1.refs_8_.refs_4_ = bf16[5,32,512]{2,1,0:T(8,128)(2,1)S(1)} custom-call(bf16[120,512]{1,0:T(8,128)(2,1)S(1)} %get-tuple-element.25.refs_0_, bf16[120,512]{1,0:T(8,128)(2,1)S(1)} %collective-permute-done.refs_1_, bf16[120,512]{1,0:T(8,128)(2,1)S(1)} %collective-permute-done.1.refs_2_, bf16[120,512]{1,0:T(8,128)(2,1)S(1)} %collective-permute-done.2.refs_3_, ...), custom_call_target="tpu_custom_call" | custom-call | flops 1610612736 | bytes 4972544 | tf_op jit(solution)/shard_map/early_backward/pallas_call | solution.py:36
  25.9 0.0 collective-permute-done.4.refs_5_.refs_0_
  25.9 0.0 collective-permute-done.5.refs_6_.refs_1_
  25.9 2.1 %collective-permute-done.6.refs_7_.refs_2_ = bf16[120,512]{1,0:T(8,128)(2,1)S(1)} collective-permute-done((bf16[120,512]{1,0:T(8,128)(2,1)S(1)}, bf16[120,512]{1,0:T(8,128)(2,1)S(1)}, u32[]{:S(2)}, u32[]{:S(2)}) %collective-permute-start.6) | collective-permute-done | bytes 122912 | tf_op jit(solution)/shard_map/ppermute | solution.py:378
  28.0 0.1 hand_on.1.refs_8_
  28.1 0.1 collective-permute-start.7
  28.2 0.1 arrived_rows.1.refs_1_.refs_7_
  28.2 0.0 copy-start
  28.2 0.0 copy-start.1
  28.3 1.6 %collective-permute-start.8 = (bf16[480,512]{1,0:T(8,128)(2,1)S(1)}, bf16[480,512]{1,0:T(8,128)(2,1)S(1)}, u32[]{:S(2)}, u32[]{:S(2)}) collective-permute-start(bf16[480,512]{1,0:T(8,128)(2,1)S(1)} %arrived_rows.1.refs_1_.refs_7_), channel_id=1, source_target_pairs={{0,16},{16,0},{1,17},{17,1},{2,18},{18,2},{3,19},{19,3},{4,20},{20... | collective-permute-start | bytes 1474568 | tf_op jit(solution)/shard_map/ppermute | solution.py:432
  29.8 0.2 collective-permute-done.7.refs_0_.refs_3_
  30.0 3.7 %late_backward.1 = bf16[16,32,512]{2,1,0:T(8,128)(2,1)} custom-call(bf16[120,512]{1,0:T(8,128)(2,1)S(1)} %collective-permute-done.4.refs_5_.refs_0_, bf16[120,512]{1,0:T(8,128)(2,1)S(1)} %collective-permute-done.5.refs_6_.refs_1_, bf16[120,512]{1,0:T(8,128)(2,1)S(1)} %collective-permute-done.6.refs_7_.refs_2_, ...), custom_call_target="tpu_custom_call" | custom-call | flops 99999997952 | bytes 4194304 | tf_op jit(solution)/shard_map/late_backward/pallas_call | solution.py:435
  33.7 5.2 %all-to-all-start = ((bf16[16,32,512]{2,1,0:T(8,128)(2,1)}), bf16[16,32,512]{2,1,0:T(8,128)(2,1)}, u32[]{:S(2)}, u32[]{:S(2)}) async-start(bf16[16,32,512]{2,1,0:T(8,128)(2,1)} %late_backward.1), calls=%async_computation | async-start | bytes 1048576 | tf_op jit(solution)/shard_map/all_to_all | solution.py:451
  38.8 1.5 %collective-permute-start.9 = (bf16[480,512]{1,0:T(8,128)(2,1)S(1)}, bf16[480,512]{1,0:T(8,128)(2,1)S(1)}, u32[]{:S(2)}, u32[]{:S(2)}) collective-permute-start(bf16[480,512]{1,0:T(8,128)(2,1)S(1)} %collective-permute-done.7.refs_0_.refs_3_), channel_id=1, source_target_pairs={{0,16},{16,0},{1,17},{17,1},{2,18},{18,2},{3,19},{19,3},{4,20},{20... | collective-permute-start | bytes 1474568 | tf_op jit(solution)/shard_map/ppermute | solution.py:433
  40.4 1.6 %collective-permute-done.8.refs_2_ = bf16[480,512]{1,0:T(8,128)(2,1)S(1)} collective-permute-done((bf16[480,512]{1,0:T(8,128)(2,1)S(1)}, bf16[480,512]{1,0:T(8,128)(2,1)S(1)}, u32[]{:S(2)}, u32[]{:S(2)}) %collective-permute-start.8) | collective-permute-done | bytes 491552 | tf_op jit(solution)/shard_map/ppermute | solution.py:432
  42.0 0.0 copy-done
  42.0 0.0 copy-done.1
  42.0 5.4 %first_weights.1 = (f32[1,1024,512]{2,1,0:T(8,128)S(1)}, f32[1,1024,512]{2,1,0:T(8,128)S(1)}, bf16[160,512]{1,0:T(8,128)(2,1)S(1)}, f32[2,16,160]{2,1,0:T(8,128)...) custom-call(bf16[480,512]{1,0:T(8,128)(2,1)S(1)} %collective-permute-done.7.ref, ...), custom_call_target="tpu_custom_call" | custom-call | flops 99999997952 | bytes 12228480 | tf_op jit(solution)/shard_map/first_weights/pallas_call | solution.py:36
  47.4 5.1 %collective-permute-done.9.refs_0_ = bf16[480,512]{1,0:T(8,128)(2,1)S(1)} collective-permute-done((bf16[480,512]{1,0:T(8,128)(2,1)S(1)}, bf16[480,512]{1,0:T(8,128)(2,1)S(1)}, u32[]{:S(2)}, u32[]{:S(2)}) %collective-permute-start.9) | collective-permute-done | bytes 491552 | tf_op jit(solution)/shard_map/ppermute | solution.py:433
  52.5 2.4 %last_weights.1 = (bf16[1,1024,512]{2,1,0:T(8,128)(2,1)}, bf16[1,1024,512]{2,1,0:T(8,128)(2,1)}) custom-call(bf16[480,512]{1,0:T(8,128)(2,1)S(1)} %collective-permute-done.9.refs_0_, bf16[1024,512]{1,0:T(8,128)(2,1)S(1)} %get-tuple-element.40.refs_1_, bf16[1024,512]{1,0:T(8,128)(2,1)S(1)} %get-tuple-element.41.refs_2_, ...), custom_call_target="tpu_custom_call" | custom-call | flops 99999997952 | bytes 8880128 | tf_op jit(solution)/shard_map/last_weights/pallas_call | solution.py:36
  54.9 0.0 all-to-all-done.back_ref
  54.9 2.0 %combine.1 = (bf16[160,512]{1,0:T(8,128)(2,1)}, bf16[2,160]{1,0:T(2,128)(2,1)}) custom-call(bf16[160,512]{1,0:T(8,128)(2,1)S(1)} %get-tuple-element.35.pick_ref, f32[2,16,160]{2,1,0:T(8,128)S(1)} %get-tuple-element.36.hot_ref, bf16[2,128,160]{2,1,0:T(8,128)(2,1)S(1)} %get-tuple-element.37.spot_ref, bf16[16,32,512]{2,1,0:T(8,128)(2,1)} %all-to-all-done.back_ref), custom_call_target="tpu_custom_call" | custom-call | flops 167772160 | bytes 955008 | tf_op jit(solution)/shard_map/combine/pallas_call | solution.py:36
Async XLA Ops:
  2.2 14.1 %collective-permute-start = (bf16[120,512]{1,0:T(8,128)(2,1)S(1)}, bf16[120,512]{1,0:T(8,128)(2,1)S(1)}, u32[]{:S(2)}, u32[]{:S(2)}) collective-permute-start(bf16[120,512]{1,0:T(8,128)(2,1)S(1)} %get-tuple-element.26), channel_id=1, source_target_pairs={{0,8},{1,9},{2,10},{3,11},{4,12},{5,13},{6,14},{7,15},{8,0},{9,1},... | collective-permute-start | bytes 368648 | tf_op jit(solution)/shard_map/ppermute | solution.py:378
  6.3 15.9 %collective-permute-start.1 = (bf16[120,512]{1,0:T(8,128)(2,1)S(1)}, bf16[120,512]{1,0:T(8,128)(2,1)S(1)}, u32[]{:S(2)}, u32[]{:S(2)}) collective-permute-start(bf16[120,512]{1,0:T(8,128)(2,1)S(1)} %get-tuple-element.27), channel_id=1, source_target_pairs={{0,2},{1,3},{2,0},{3,1},{4,6},{5,7},{6,4},{7,5},{8,10},{9,11},{10,... | collective-permute-start | bytes 368648 | tf_op jit(solution)/shard_map/ppermute | solution.py:378
  7.8 15.8 %collective-permute-start.2 = (bf16[120,512]{1,0:T(8,128)(2,1)S(1)}, bf16[120,512]{1,0:T(8,128)(2,1)S(1)}, u32[]{:S(2)}, u32[]{:S(2)}) collective-permute-start(bf16[120,512]{1,0:T(8,128)(2,1)S(1)} %get-tuple-element.28), channel_id=1, source_target_pairs={{0,10},{1,11},{2,8},{3,9},{4,14},{5,15},{6,12},{7,13},{8,2},{9,3},... | collective-permute-start | bytes 368648 | tf_op jit(solution)/shard_map/ppermute | solution.py:378
  7.9 15.8 %collective-permute-start.3 = (bf16[120,512]{1,0:T(8,128)(2,1)S(1)}, bf16[120,512]{1,0:T(8,128)(2,1)S(1)}, u32[]{:S(2)}, u32[]{:S(2)}) collective-permute-start(bf16[120,512]{1,0:T(8,128)(2,1)S(1)} %get-tuple-element.29), channel_id=1, source_target_pairs={{0,4},{1,5},{2,6},{3,7},{4,0},{5,1},{6,2},{7,3},{8,12},{9,13},{10,... | collective-permute-start | bytes 368648 | tf_op jit(solution)/shard_map/ppermute | solution.py:378
  9.7 16.2 %collective-permute-start.4 = (bf16[120,512]{1,0:T(8,128)(2,1)S(1)}, bf16[120,512]{1,0:T(8,128)(2,1)S(1)}, u32[]{:S(2)}, u32[]{:S(2)}) collective-permute-start(bf16[120,512]{1,0:T(8,128)(2,1)S(1)} %get-tuple-element.30), channel_id=1, source_target_pairs={{0,12},{1,13},{2,14},{3,15},{4,8},{5,9},{6,10},{7,11},{8,4},{9,5},... | collective-permute-start | bytes 368648 | tf_op jit(solution)/shard_map/ppermute | solution.py:378
  16.3 9.6 %collective-permute-start.5 = (bf16[120,512]{1,0:T(8,128)(2,1)S(1)}, bf16[120,512]{1,0:T(8,128)(2,1)S(1)}, u32[]{:S(2)}, u32[]{:S(2)}) collective-permute-start(bf16[120,512]{1,0:T(8,128)(2,1)S(1)} %get-tuple-element.31), channel_id=1, source_target_pairs={{0,14},{1,15},{2,12},{3,13},{4,10},{5,11},{6,8},{7,9},{8,6},{9,7},... | collective-permute-start | bytes 368648 | tf_op jit(solution)/shard_map/ppermute | solution.py:378
  22.2 5.8 %collective-permute-start.6 = (bf16[120,512]{1,0:T(8,128)(2,1)S(1)}, bf16[120,512]{1,0:T(8,128)(2,1)S(1)}, u32[]{:S(2)}, u32[]{:S(2)}) collective-permute-start(bf16[120,512]{1,0:T(8,128)(2,1)S(1)} %get-tuple-element.32), channel_id=1, source_target_pairs={{0,6},{1,7},{2,4},{3,5},{4,2},{5,3},{6,0},{7,1},{8,14},{9,15},{10,... | collective-permute-start | bytes 368648 | tf_op jit(solution)/shard_map/ppermute | solution.py:378
  28.1 1.9 %collective-permute-start.7 = (bf16[480,512]{1,0:T(8,128)(2,1)S(1)}, bf16[480,512]{1,0:T(8,128)(2,1)S(1)}, u32[]{:S(2)}, u32[]{:S(2)}) collective-permute-start(bf16[480,512]{1,0:T(8,128)(2,1)S(1)} %hand_on.1.refs_8_), channel_id=1, source_target_pairs={{0,1},{1,0},{2,3},{3,2},{4,5},{5,4},{6,7},{7,6},{8,9},{9,8},{10,11... | collective-permute-start | bytes 1474568 | tf_op jit(solution)/shard_map/ppermute | solution.py:430
  28.2 13.8 %copy-start = (s32[160,2]{0,1:T(2,128)S(1)}, s32[160,2]{0,1:T(2,128)}, u32[]{:S(2)}) copy-start(s32[160,2]{0,1:T(2,128)} %param.8) | copy-start | bytes 3844
  28.2 13.8 %copy-start.1 = (bf16[160,2]{0,1:T(2,128)(2,1)S(1)}, bf16[160,2]{0,1:T(2,128)(2,1)}, u32[]{:S(2)}) copy-start(bf16[160,2]{0,1:T(2,128)(2,1)} %param.7) | copy-start | bytes 1924
  28.3 13.7 %collective-permute-start.8 = (bf16[480,512]{1,0:T(8,128)(2,1)S(1)}, bf16[480,512]{1,0:T(8,128)(2,1)S(1)}, u32[]{:S(2)}, u32[]{:S(2)}) collective-permute-start(bf16[480,512]{1,0:T(8,128)(2,1)S(1)} %arrived_rows.1.refs_1_.refs_7_), channel_id=1, source_target_pairs={{0,16},{16,0},{1,17},{17,1},{2,18},{18,2},{3,19},{19,3},{4,20},{20... | collective-permute-start | bytes 1474568 | tf_op jit(solution)/shard_map/ppermute | solution.py:432
  33.7 21.2 %all-to-all-start = ((bf16[16,32,512]{2,1,0:T(8,128)(2,1)}), bf16[16,32,512]{2,1,0:T(8,128)(2,1)}, u32[]{:S(2)}, u32[]{:S(2)}) async-start(bf16[16,32,512]{2,1,0:T(8,128)(2,1)} %late_backward.1), calls=%async_computation | async-start | bytes 1048576 | tf_op jit(solution)/shard_map/all_to_all | solution.py:451
  38.8 13.6 %collective-permute-start.9 = (bf16[480,512]{1,0:T(8,128)(2,1)S(1)}, bf16[480,512]{1,0:T(8,128)(2,1)S(1)}, u32[]{:S(2)}, u32[]{:S(2)}) collective-permute-start(bf16[480,512]{1,0:T(8,128)(2,1)S(1)} %collective-permute-done.7.refs_0_.refs_3_), channel_id=1, source_target_pairs={{0,16},{16,0},{1,17},{17,1},{2,18},{18,2},{3,19},{19,3},{4,20},{20... | collective-permute-start | bytes 1474568 | tf_op jit(solution)/shard_map/ppermute | solution.py:433
